TPU v7x, 32 devices: a whole 2x2x4 slice. The times are simulated.
32 devices in a mesh: groups: 2 (over y), dp: 4 (over z), feat: 2 (over x), test: 2 (over core).
Axes of the slice: x: 2, y: 2, z: 4, core: 2. Of those that a mesh axis runs over, the one named last changes fastest.
Arguments:
- train_inputs: bfloat16 [128, 96, 4096], P(('groups', 'dp', 'test'), None, 'feat'), parts along dimension 0, may hold values from -6 to 6
- train_grads: bfloat16 [128, 96, 14336], P(('groups', 'dp', 'test'), None, 'feat'), parts along dimension 0, may hold values from -6 to 6
- proj_in: bfloat16 [4096, 64], P('feat'), as said below
- proj_out: bfloat16 [14336, 64], P('feat'), as said below
- lengths: int32 [128], P(('groups', 'dp', 'test')), parts along dimension 0, may hold values from 24 to 96
- loss_mask: int32 [128, 96], P(('groups', 'dp', 'test')), parts along dimension 0, may hold values 0 or 1
- test_feats: bfloat16 [2048, 64, 64], P(('groups', 'dp', 'test'), 'feat'), parts along dimension 0, may hold values from -0.29882812 to 0.29882812
Outputs:
- scores: float32 [128, 8, 128], P(('groups', 'dp', 'test'), None, 'feat'), parts along dimension 0
There are 2 independent parts, one for each index of `groups`. A program takes and returns all parts, laid end to end along the dimension named above; an argument that names none is the same for every part. Nothing has to cross between parts.
Inputs may be any that keep to these rules, and one draw needn't show every extreme that they name: `proj_in`: entries of order 4096 ** -0.5. `proj_out`: entries of order 14336 ** -0.5.
All inputs are finite; a program needn't handle non-finite values. No bound on the sum of `loss_mask` on one device may be relied on, other than what follows from the above.
Results may differ from a plain program's by a relative error of at most 0.0095.
Values may be sent and summed in bfloat16 or wider, within the bound.
No kernel may reach another device: no remote copies, remote signals or barrier semaphores. Data moves between devices by JAX's collectives and lax.ppermute only.
A program may use at most 64 MiB of HBM per device.

v0:
```python
import jax
import jax.numpy as jnp
from jax import lax
from jax.sharding import PartitionSpec as P


def damped_inverse(factor):
    order_size = factor.shape[0]
    identity = jnp.eye(order_size, dtype=jnp.float32)
    damped = factor + (0.1 * jnp.trace(factor) / order_size + 1e-06) * identity
    lower_factor = jnp.linalg.cholesky(damped)
    inverse_lower = lax.linalg.triangular_solve(lower_factor, identity, left_side=True, lower=True)
    return jnp.dot(inverse_lower.T, inverse_lower, precision=lax.Precision.HIGHEST)


def on_device(train_inputs, train_grads, proj_in, proj_out, lengths, loss_mask, test_feats):
    examples, seq_len, in_width = train_inputs.shape
    out_width = train_grads.shape[2]
    in_rank = proj_in.shape[1]
    grad_rank = proj_out.shape[1]
    tokens = examples * seq_len
    feat_count = lax.axis_size("feat")
    feat_index = lax.axis_index("feat")
    blocks = lax.axis_size(("dp", "test"))
    own_grad = grad_rank // feat_count
    partial_in = jnp.dot(
        train_inputs.reshape(tokens, in_width), proj_in, preferred_element_type=jnp.float32
    )
    partial_grad = jnp.dot(
        train_grads.reshape(tokens, out_width), proj_out, preferred_element_type=jnp.float32
    )
    summed_in, summed_grad = lax.psum((partial_in, partial_grad), "feat")
    in_flat = summed_in.astype(jnp.bfloat16)
    grad_flat = summed_grad.astype(jnp.bfloat16)
    positions = jnp.arange(seq_len, dtype=jnp.int32)
    live_mask = ((loss_mask > 0) & (positions[None, :] < lengths[:, None])).astype(jnp.bfloat16)
    masked_in = (in_flat.reshape(examples, seq_len, in_rank) * live_mask[:, :, None]).reshape(
        tokens, in_rank
    )
    masked_grad = (grad_flat.reshape(examples, seq_len, grad_rank) * live_mask[:, :, None]).reshape(
        tokens, grad_rank
    )
    grad_block = lax.dynamic_slice_in_dim(masked_grad, feat_index * own_grad, own_grad, 1)
    sums = jnp.einsum(
        "etg,etx->egx",
        grad_block.reshape(examples, seq_len, own_grad),
        in_flat.reshape(examples, seq_len, in_rank),
        preferred_element_type=jnp.float32,
    )
    features = (sums / lengths.astype(jnp.float32)[:, None, None]).astype(jnp.bfloat16)
    total_tokens = float(tokens * blocks)
    in_whole = jnp.dot(masked_in.T, in_flat, preferred_element_type=jnp.float32)
    grad_whole = jnp.dot(masked_grad.T, grad_flat, preferred_element_type=jnp.float32)
    in_factor, grad_factor = lax.psum((in_whole, grad_whole), ("dp", "test"))
    in_inverse = damped_inverse(in_factor / total_tokens)
    grad_inverse = damped_inverse(grad_factor / total_tokens)
    full_tests = lax.all_gather(test_feats, "feat", axis=1, tiled=True)
    inverse_rows = lax.dynamic_slice_in_dim(grad_inverse, feat_index * own_grad, own_grad, 0)
    left_solved = jnp.einsum(
        "gk,ekx->egx", inverse_rows, full_tests.astype(jnp.float32), precision=lax.Precision.HIGHEST
    )
    solved = jnp.einsum(
        "egx,xy->egy", left_solved, in_inverse, precision=lax.Precision.HIGHEST
    ).astype(jnp.bfloat16)
    test_count = solved.shape[0]
    feature_flat = features.reshape(examples, own_grad * in_rank)
    solved_flat = solved.reshape(test_count, own_grad * in_rank)
    partial_scores = jnp.einsum(
        "ef,kf->ek",
        feature_flat,
        lax.all_gather(solved_flat, ("dp", "test"), axis=0, tiled=True),
        preferred_element_type=jnp.float32,
    )
    scores = lax.psum_scatter(
        partial_scores.reshape(examples, blocks, test_count).astype(jnp.bfloat16),
        "feat",
        scatter_dimension=2,
        tiled=True,
    ).astype(jnp.float32)
    return scores


def solution(mesh):
    return jax.shard_map(
        on_device,
        mesh=mesh,
        in_specs=(
            P(("groups", "dp", "test"), None, "feat"),
            P(("groups", "dp", "test"), None, "feat"),
            P("feat", None),
            P("feat", None),
            P(("groups", "dp", "test")),
            P(("groups", "dp", "test"), None),
            P(("groups", "dp", "test"), "feat", None),
        ),
        out_specs=P(("groups", "dp", "test"), None, "feat"),
        check_vma=False,
    )
```

profile of v0, /device:TPU:0, one launch (start us, length us, event | category | flops | bytes accessed | tf_op | source)
XLA Modules:
  0.0 175.7 jit_solution(4841471499461707111)
XLA Ops:
  6.5 0.7 all-gather.3.cloned.1.call-update
  7.3 0.9 fusion.23
  8.4 2.1 %fusion.26 = f32[768,64]{0,1:T(8,128)S(1)} fusion(bf16[768,2048]{1,0:T(8,128)(2,1)S(1)} %bitcast.49, bf16[2048,64]{0,1:T(8,128)(2,1)} %param.12), kind=kOutput, calls=%fused_computation.49 | convolution fusion | flops 201326592 | bytes 3604480 | tf_op jit(solution)/shard_map/dot_general | solution.py:26
  10.5 8.3 %fusion.25 = f32[768,64]{0,1:T(8,128)} fusion(bf16[768,7168]{1,0:T(8,128)(2,1)} %bitcast.51, bf16[7168,64]{0,1:T(8,128)(2,1)S(1)} %copy-done.1), kind=kOutput, calls=%fused_computation.48 | convolution fusion | flops 704643072 | bytes 12124160 | tf_op jit(solution)/shard_map/dot_general | solution.py:29
  18.8 22.7 %all-reduce.3 = (bf16[768,64]{0,1:T(8,128)(2,1)S(1)}, bf16[768,64]{0,1:T(8,128)(2,1)S(1)}) all-reduce(f32[768,64]{0,1:T(8,128)S(1)} %fusion.26, f32[768,64]{0,1:T(8,128)} %fusion.25), channel_id=1, replica_groups=mesh['groups'=2,'dp'=4,'feat'=2,'test'=2] {'feat'}, use_global_device_ids=true, to_apply=%region_1.0 | all-reduce | flops 98304 | bytes 589824 | tf_op jit(solution)/shard_map/psum | solution.py:32
  41.9 28.5 %all-reduce = (f32[64,64]{0,1:T(8,128)S(1)}, f32[64,64]{0,1:T(8,128)S(1)}) all-reduce(f32[64,64]{0,1:T(8,128)S(1)} %fusion.3, f32[64,64]{0,1:T(8,128)S(1)} %fusion.8), channel_id=1, replica_groups=mesh['groups'=2,'dp'=4,'feat'=2,'test'=2] {'dp','test'}, use_global_device_ids=true, to_apply=%region_6.9 | all-reduce | flops 8192 | bytes 65536 | tf_op jit(solution)/shard_map/psum | solution.py:54
  70.4 0.7 select_reduce_fusion.3
  73.2 5.8 %cholesky.55 = f32[64,64]{1,0:T(8,128)S(1)} custom-call(f32[64,64]{1,0:T(8,128)S(1)} %fusion.17), custom_call_target="Cholesky" | custom-call | tf_op jit(solution)/shard_map/jit(cholesky)/cholesky | solution.py:11
  79.0 0.6 compare_reduce_fusion
  79.7 0.7 fusion.15
  80.4 5.8 %cholesky.44 = f32[64,64]{1,0:T(8,128)S(1)} custom-call(f32[64,64]{1,0:T(8,128)S(1)} %fusion.19), custom_call_target="Cholesky" | custom-call | tf_op jit(solution)/shard_map/jit(cholesky)/cholesky | solution.py:11
  86.3 0.6 compare_reduce_fusion.1
  87.0 4.9 %custom-call.7 = f32[1,64,64]{1,2,0:T(8,128)S(1)} custom-call(f32[1,64,64]{2,1,0:T(8,128)S(1)} %fusion.15), custom_call_target="InvertDiagBlocksLowerTriangular" | custom-call | tf_op jit(solution)/shard_map/triangular_solve/custom-call.0 | solution.py:12
  91.9 0.7 fusion.14
  92.5 4.9 %custom-call.6 = f32[1,64,64]{1,2,0:T(8,128)S(1)} custom-call(f32[1,64,64]{2,1,0:T(8,128)S(1)} %fusion.14), custom_call_target="InvertDiagBlocksLowerTriangular" | custom-call | tf_op jit(solution)/shard_map/triangular_solve/custom-call.0 | solution.py:12
  98.4 2.3 %convolution_bitcast_fusion = f32[128,32,64]{0,1,2:T(8,128)S(1)} fusion(bf16[128,64,64]{0,2,1:T(8,128)(2,1)} %all-gather.3.cloned.1.call-done, f32[64,64]{1,0:T(8,128)S(1)} %fusion.27, s32[]{:T(128)S(6)} %select_n.15), kind=kOutput, calls=%fused_computation | convolution fusion | flops 201326592 | bytes 2113540 | tf_op jit(solution)/shard_map/gk,ekx->egx/dot_general | solution.py:59
  100.8 2.5 %convolution_convert_fusion = bf16[128,32,64]{0,2,1:T(8,128)(2,1)} fusion(f32[64,64,1]{0,1,2:T(8,128)S(1)} %convolution_bitcast_fusion.1, f32[128,32,64]{0,1,2:T(8,128)S(1)} %convolution_bitcast_fusion), kind=kOutput, calls=%fused_computation.1 | convolution fusion | flops 201588736 | bytes 1589248 | tf_op jit(solution)/shard_map/egx,xy->egy/dot_general | solution.py:62
  104.0 44.4 %all-gather.5.cloned.1.call-done = bf16[1024,2048]{0,1:T(8,128)(2,1)} async-done(((bf16[128,2048]{0,1:T(8,128)(2,1)}), bf16[1024,2048]{0,1:T(8,128)(2,1)}) %all-gather.5.cloned.1.call-update) | async-done | bytes 4194320 | tf_op jit(solution)/shard_map/all_gather | solution.py:71
  148.5 6.5 %copy.32 = bf16[1024,2048]{1,0:T(8,128)(2,1)} copy(bf16[1024,2048]{0,1:T(8,128)(2,1)} %all-gather.5.cloned.1.call-done) | data formatting | bytes 8388608 | tf_op jit(solution)/shard_map/all_gather | solution.py:71
  155.0 3.4 %convolution_convert_fusion.1 = bf16[8,8,128]{2,0,1:T(8,128)(2,1)S(1)} fusion(bf16[8,2048,1]{1,0,2:T(8,128)(2,1)S(1)} %reshape.57, bf16[8,128,2048]{2,1,0:T(8,128)(2,1)} %bitcast.50), kind=kOutput, calls=%fused_computation.5 | convolution fusion | flops 33562624 | bytes 4243456 | tf_op jit(solution)/shard_map/ef,kf->ek/dot_general | solution.py:68
  158.6 0.8 reshape.59
  159.4 8.2 %reduce-scatter.4.cloned.1.call-done = bf16[64,64]{1,0:T(8,128)(2,1)} async-done(((bf16[128,64]{1,0:T(8,128)(2,1)}), bf16[64,64]{1,0:T(8,128)(2,1)}) %reduce-scatter.4.cloned.1.call-update) | async-done | bytes 8208
  167.6 0.8 reshape.60
  168.5 0.6 copy.33
  (36 shorter events, 3.4 us)
Async XLA Ops:
  6.5 1.9 %copy-start = (bf16[8,96,2048]{2,1,0:T(8,128)(2,1)S(1)}, bf16[8,96,2048]{2,1,0:T(8,128)(2,1)}, u32[]{:S(2)}) copy-start(bf16[8,96,2048]{2,1,0:T(8,128)(2,1)} %param.10) | copy-start | bytes 9437188
  6.5 91.9 %all-gather.3.cloned.1.call-start = ((), (), s32[]{:S(2)}) async-start(), calls=%async_computation.1 | async-start | bytes 1572864 | tf_op jit(solution)/shard_map/all_gather | solution.py:57
  7.3 141.2 %all-gather.5.cloned.1.call-start = ((), (), s32[]{:S(2)}) async-start(), calls=%async_computation.2 | async-start | bytes 4718592 | tf_op jit(solution)/shard_map/all_gather | solution.py:71
  8.4 2.1 %copy-start.1 = (bf16[7168,64]{0,1:T(8,128)(2,1)S(1)}, bf16[7168,64]{0,1:T(8,128)(2,1)}, u32[]{:S(2)}) copy-start(bf16[7168,64]{0,1:T(8,128)(2,1)} %param.13) | copy-start | bytes 2752516
  18.8 84.5 %copy-start.2 = (s32[8]{0:T(128)S(1)}, s32[8]{0:T(128)}, u32[]{:S(2)}) copy-start(s32[8]{0:T(128)} %param.14) | copy-start | bytes 100
  103.3 64.3 %reduce-scatter.4.cloned.1.call-start = ((), (), s32[]{:S(2)}) async-start(), calls=%async_computation.3 | async-start | bytes 49152
Sparse Core Ops, SparseCore 0:
  8.9 29.0 all-gather.2
  103.4 45.0 all-gather.4
  159.5 8.0 reduce-scatter.3
where the time goes:
time: 176 us
  waiting for transfers between devices  53.4 us (30%)
  blocking collectives  51.2 us (29%)
  other arithmetic  26.4 us (15%)
  matrix products  20 us (11%)
  between operations  14.7 us (8%)
  local copies, waits for them, and re-layouts  9.89 us (6%)
    all_gather x1, waiting for transfers between devices, on_device(): lax.all_gather(solved_flat, ('dp', 'test'), axis=0, tiled=True)  44.4 us
    psum x1, blocking collectives, on_device(): in_factor, grad_factor = lax.psum((in_whole, grad_whole), ('dp', 'test'))  28.5 us
    psum x1, blocking collectives, on_device(): summed_in, summed_grad = lax.psum((partial_in, partial_grad), 'feat')  22.7 us
    another operation x6, other arithmetic, damped_inverse(): lower_factor = jnp.linalg.cholesky(damped)  13 us
    another operation x4, other arithmetic, damped_inverse(): lax.linalg.triangular_solve(lower_factor, identity, left_side=True, lower...  11.1 us
    unnamed x4, waiting for transfers between devices  8.92 us
    dot_general x1, matrix products, on_device(): jnp.dot(train_grads.reshape(tokens, out_width), proj_out, preferred_eleme...  8.27 us
    all_gather x1, local copies, waits for them, and re-layouts, on_device(): lax.all_gather(solved_flat, ('dp', 'test'), axis=0, tiled=True)  6.52 us
  transfers between devices with their start and end apart: 3, of which 2 were waited for; matrix products, arithmetic and copies ran while one was open for 22% of the time, Pallas kernels for 0%

commit v1 on v0

v1 whole, which is shorter than its diff:
```python
import functools

import jax
import jax.numpy as jnp
from jax import lax
from jax.experimental import pallas as pl
from jax.experimental.pallas import tpu as pltpu
from jax.sharding import PartitionSpec as P

f32 = jnp.float32
bf16 = jnp.bfloat16
VMEM_BYTES = 48 * 1024 * 1024


def xor_permute(values, axis, mask):
    size = lax.axis_size(axis)
    return lax.ppermute(values, axis, [(i, i ^ mask) for i in range(size)])


def chunk_of(width):
    for size in (1024, 512, 256, 128):
        if width % size == 0:
            return size
    return width


def project_body(start, rows, x_chunk, g_chunk, x_hbm, g_hbm, pin_hbm, pout_hbm, own_ref, sent_ref, x_buf, g_buf, pin_buf, pout_buf, sems):
    x_steps = x_buf.shape[0]
    g_steps = g_buf.shape[0]

    def copies(step):
        if step < x_steps:
            src, dst, wsrc, wdst, at, size = x_hbm, x_buf, pin_hbm, pin_buf, step, x_chunk
        else:
            src, dst, wsrc, wdst, at, size = g_hbm, g_buf, pout_hbm, pout_buf, step - x_steps, g_chunk
        return (
            pltpu.make_async_copy(wsrc.at[pl.ds(at * size, size), :], wdst.at[at], sems.at[0, step]),
            pltpu.make_async_copy(src.at[pl.ds(start, rows), pl.ds(at * size, size)], dst.at[at], sems.at[1, step]),
        )

    steps = x_steps + g_steps
    for step in range(steps):
        for copy in copies(step):
            copy.start()
    totals = []
    for first, last, buf, weights in ((0, x_steps, x_buf, pin_buf), (x_steps, steps, g_buf, pout_buf)):
        total = None
        for step in range(first, last):
            for copy in copies(step):
                copy.wait()
            term = jnp.dot(buf[step - first], weights[step - first], preferred_element_type=f32)
            total = term if total is None else total + term
        totals.append(total)
    both = jnp.concatenate(totals, axis=1)
    own_ref[...] = both
    sent_ref[...] = both.astype(bf16)


def project(x, g, pin, pout, start, rows):
    in_width, out_width = x.shape[1], g.shape[1]
    x_chunk, g_chunk = chunk_of(in_width), chunk_of(out_width)
    x_steps, g_steps = in_width // x_chunk, out_width // g_chunk
    rank = pin.shape[1]
    any_spec = pl.BlockSpec(memory_space=pl.ANY)
    return pl.pallas_call(
        functools.partial(project_body, start, rows, x_chunk, g_chunk),
        out_shape=(
            jax.ShapeDtypeStruct((rows, 2 * rank), f32),
            jax.ShapeDtypeStruct((rows, 2 * rank), bf16),
        ),
        in_specs=[any_spec] * 4,
        scratch_shapes=[
            pltpu.VMEM((x_steps, rows, x_chunk), bf16),
            pltpu.VMEM((g_steps, rows, g_chunk), bf16),
            pltpu.VMEM((x_steps, x_chunk, rank), bf16),
            pltpu.VMEM((g_steps, g_chunk, rank), bf16),
            pltpu.SemaphoreType.DMA((2, x_steps + g_steps)),
        ],
        compiler_params=pltpu.CompilerParams(vmem_limit_bytes=VMEM_BYTES),
        cost_estimate=pl.CostEstimate(
            flops=2 * rows * (in_width + out_width) * rank,
            bytes_accessed=2 * (rows + rank) * (in_width + out_width),
            transcendentals=0,
        ),
        name="project",
    )(x, g, pin, pout)


def gram_body(first, count, received, lengths_ref, mask_ref, own_ref, *refs):
    received_refs = refs[:received]
    gram_ref, feats_ref = refs[received:]
    seq_len = mask_ref.shape[1]
    rank = gram_ref.shape[0]
    positions = lax.broadcasted_iota(jnp.int32, (1, seq_len), 1)
    total = None
    feats = []
    for local in range(count):
        rows = pl.ds(local * seq_len, seq_len)
        summed = own_ref[rows, :]
        for ref in received_refs:
            summed = summed + ref[rows, :].astype(f32)
        rounded = summed.astype(bf16)
        length = lengths_ref[first + local]
        live = (mask_ref[first + local : first + local + 1, :] > 0) & (positions < length)
        turned = jnp.where(live, rounded.astype(f32).T, 0.0).astype(bf16)
        products = jnp.dot(turned, rounded, preferred_element_type=f32)
        total = products if total is None else total + products
        feats.append(products[rank:, :] / length.astype(f32))
    lane = lax.broadcasted_iota(jnp.int32, (rank, 2 * rank), 1)
    gram_ref[...] = jnp.where(lane < rank, total[:rank, :], total[rank:, :])
    half = count // 2
    for pair in range(half):
        other = pltpu.roll(feats[half + pair], rank, 1)
        feats_ref[pair] = jnp.where(lane < rank, feats[pair], other).astype(bf16)


def gram(lengths, mask, own, received, first, count):
    rank = own.shape[1] // 2
    vmem = pl.BlockSpec(memory_space=pltpu.VMEM)
    return pl.pallas_call(
        functools.partial(gram_body, first, count, len(received)),
        out_shape=(
            jax.ShapeDtypeStruct((rank, 2 * rank), f32),
            jax.ShapeDtypeStruct((count // 2, rank, 2 * rank), bf16),
        ),
        in_specs=[pl.BlockSpec(memory_space=pltpu.SMEM), vmem, vmem] + [vmem] * len(received),
        name="gram",
    )(lengths, mask, own, *received)


def flatten_body(tests_ref, out_ref, wide):
    count, rows, width = tests_ref.shape
    wide[...] = tests_ref[...].reshape(count * rows, width).astype(f32)
    for pair in range(rows // 2):
        low = wide[pl.ds(2 * pair, count, stride=rows), :]
        high = wide[pl.ds(2 * pair + 1, count, stride=rows), :]
        out_ref[:, 2 * width * pair : 2 * width * (pair + 1)] = jnp.concatenate([low, high], axis=1).astype(bf16)


def flatten(tests):
    count, rows, width = tests.shape
    vmem = pl.BlockSpec(memory_space=pltpu.VMEM)
    return pl.pallas_call(
        flatten_body,
        out_shape=jax.ShapeDtypeStruct((count, rows * width), bf16),
        in_specs=[vmem],
        out_specs=vmem,
        scratch_shapes=[pltpu.VMEM((count * rows, width), f32)],
        name="flatten",
    )(tests)


def both_inverses(total_tokens, packed):
    rank = packed.shape[0]
    lane = lax.broadcasted_iota(jnp.int32, (rank, 2 * rank), 1)
    sub = lax.broadcasted_iota(jnp.int32, (rank, 2 * rank), 0)
    left = lane < rank
    column = jnp.where(left, lane, lane - rank)
    diagonal = column == sub
    packed = packed / total_tokens
    on_diagonal = jnp.sum(jnp.where(diagonal, packed, 0.0), axis=0, keepdims=True)
    trace_in = jnp.sum(jnp.where(left[:1], on_diagonal, 0.0), axis=1, keepdims=True)
    trace_grad = jnp.sum(jnp.where(left[:1], 0.0, on_diagonal), axis=1, keepdims=True)
    damping = 0.1 * jnp.where(left[:1], trace_in, trace_grad) / rank + 1e-06
    packed = packed + jnp.where(diagonal, damping, 0.0)
    for k in range(rank):
        pivot_column = jnp.where(left, packed[:, k : k + 1], packed[:, rank + k : rank + k + 1])
        row = packed[k : k + 1, :]
        inverse = 1.0 / pivot_column[k : k + 1, :]
        at_pivot = column[:1] == k
        row = jnp.where(at_pivot, inverse, row * inverse)
        packed = jnp.where(sub == k, row, jnp.where(at_pivot, 0.0, packed) - pivot_column * row)
    return packed


def split(values):
    high = values.astype(bf16)
    return high, (values - high.astype(f32)).astype(bf16)


def product(left, right):
    left_high, left_low = split(left)
    right_high, right_low = split(right)
    dot = functools.partial(jnp.dot, preferred_element_type=f32)
    return dot(left_high, right_high) + dot(left_high, right_low) + dot(left_low, right_high)


def scores_body(total_tokens, blocks, chunks, gram_a_ref, gram_b_ref, tests_ref, *refs):
    feats_refs, (out_ref, inverse_buf, turned_buf, line_buf) = refs[:-4], refs[-4:]
    feat = lax.axis_index("feat")
    test = lax.axis_index("test")
    dp = lax.axis_index("dp")
    feat_count = lax.axis_size("feat")
    test_count = lax.axis_size("test")
    rank = gram_a_ref.shape[0]
    own_rows = rank // feat_count
    inverses = both_inverses(total_tokens, gram_a_ref[...] + gram_b_ref[...])
    inverse_buf[...] = pltpu.roll(inverses, rank, 1)
    grad_rows = inverse_buf[pl.ds(pl.multiple_of(feat * own_rows, 8), own_rows), :][:, :rank]
    in_inverse = inverses[:, :rank]
    zero = jnp.zeros_like(in_inverse)
    in_pair = jnp.concatenate(
        [jnp.concatenate([in_inverse, zero], axis=1), jnp.concatenate([zero, in_inverse], axis=1)], axis=0
    )
    grad_high, grad_low = split(grad_rows)
    in_high, in_low = split(in_pair)
    pairs = [ref[i] for ref in feats_refs for i in range(ref.shape[0])]
    count = len(pairs)
    for at in range(count):
        solved = jnp.dot(grad_high, pairs[at], preferred_element_type=f32) + jnp.dot(
            grad_low, pairs[at], preferred_element_type=f32
        )
        high, low = split(solved)
        turned_buf[at * own_rows : (at + 1) * own_rows, :] = (
            jnp.dot(high, in_high, preferred_element_type=f32)
            + jnp.dot(high, in_low, preferred_element_type=f32)
            + jnp.dot(low, in_high, preferred_element_type=f32)
        )
    lane = lax.broadcasted_iota(jnp.int32, (count, 2 * rank), 1)
    for g in range(0, own_rows, 2):
        low = turned_buf[pl.ds(g, count, stride=own_rows), :]
        high = turned_buf[pl.ds(g + 1, count, stride=own_rows), :]
        first = jnp.where(lane < rank, low, pltpu.roll(high, rank, 1))
        second = jnp.where(lane < rank, pltpu.roll(low, rank, 1), high)
        line_buf[:, g * rank : (g + 2) * rank] = jnp.concatenate([first, second], axis=0).astype(bf16)
    lines = line_buf[...]
    test_block = tests_ref.shape[0] // feat_count
    half = count // len(blocks)
    run = half // chunks
    for target in range(feat_count):
        part = lax.dot_general(
            lines,
            tests_ref[target * test_block : (target + 1) * test_block, :],
            (((1,), (1,)), ((), ())),
            preferred_element_type=f32,
        )
        for at, (dp_mask, test_mask) in enumerate(blocks):
            place = ((dp ^ dp_mask) * feat_count + target) * test_count + (test ^ test_mask)
            for chunk in range(chunks):
                begin = at * half + chunk * run
                for second in range(2):
                    to = (2 * chunk + second) * run
                    out_ref[place, to : to + run, :] = part[second * count + begin : second * count + begin + run, :]


def partial_scores(total_tokens, blocks, chunks, gram_a, gram_b, tests, feats, examples):
    rank = gram_a.shape[0]
    feat_count = lax.axis_size("feat")
    own_rows = rank // feat_count
    count = sum(f.shape[0] for f in feats)
    vmem = pl.BlockSpec(memory_space=pltpu.VMEM)
    return pl.pallas_call(
        functools.partial(scores_body, total_tokens, blocks, chunks),
        out_shape=jax.ShapeDtypeStruct((len(blocks) * feat_count, examples, tests.shape[0] // feat_count), f32),
        in_specs=[vmem] * (3 + len(feats)),
        out_specs=vmem,
        scratch_shapes=[
            pltpu.VMEM((rank, 2 * rank), f32),
            pltpu.VMEM((count * own_rows, 2 * rank), f32),
            pltpu.VMEM((2 * count, own_rows * rank), bf16),
        ],
        compiler_params=pltpu.CompilerParams(vmem_limit_bytes=VMEM_BYTES),
        name="scores",
    )(gram_a, gram_b, tests, *feats)


def masks_of(size):
    masks, mask = [], 1
    while mask < size:
        masks.append(mask)
        mask *= 2
    return masks


def on_device(train_inputs, train_grads, proj_in, proj_out, lengths, loss_mask, test_feats):
    examples, seq_len, in_width = train_inputs.shape
    out_width = train_grads.shape[2]
    tokens = examples * seq_len
    feat_count = lax.axis_size("feat")
    dp_count = lax.axis_size("dp")
    test_count = lax.axis_size("test")
    x = train_inputs.reshape(tokens, in_width)
    g = train_grads.reshape(tokens, out_width)
    part = examples // 2
    owns, gots = [], []
    for first in (0, part):
        own, sent = project(x, g, proj_in, proj_out, first * seq_len, part * seq_len)
        owns.append(own)
        gots.append([xor_permute(sent, "feat", mask) for mask in range(1, feat_count)])
    tests = flatten(test_feats)
    grams, feats = [], []
    for at, first in enumerate((0, part)):
        share, features = gram(lengths, loss_mask, owns[at], gots[at], first, part)
        grams.append(share)
        feats.append(features)
    factor = grams[0] + grams[1]
    features = jnp.concatenate(feats, axis=0)
    steps = [("test", m) for m in masks_of(test_count)] + [("dp", m) for m in masks_of(dp_count)]
    for at, (axis, mask) in enumerate(steps):
        other = xor_permute(factor, axis, mask)
        if at < len(steps) - 1:
            factor = factor + other
    blocks = [(0, 0)]
    for axis, mask in reversed(steps):
        features = jnp.concatenate([features, xor_permute(features, axis, mask)], axis=0)
        blocks = blocks + [(d ^ mask, t) if axis == "dp" else (d, t ^ mask) for d, t in blocks]
    total_tokens = float(tokens * dp_count * test_count)
    shares = partial_scores(total_tokens, blocks, 2, factor, other, tests, [features], examples)
    arrived = lax.all_to_all(shares, ("dp", "feat", "test"), split_axis=0, concat_axis=0)
    arrived = arrived.reshape((dp_count, feat_count, test_count) + arrived.shape[1:])
    scores = jnp.sum(arrived, axis=1)
    return scores.reshape((dp_count * test_count,) + scores.shape[2:]).transpose(1, 0, 2)


def solution(mesh):
    return jax.shard_map(
        on_device,
        mesh=mesh,
        in_specs=(
            P(("groups", "dp", "test"), None, "feat"),
            P(("groups", "dp", "test"), None, "feat"),
            P("feat", None),
            P("feat", None),
            P(("groups", "dp", "test")),
            P(("groups", "dp", "test"), None),
            P(("groups", "dp", "test"), "feat", None),
        ),
        out_specs=P(("groups", "dp", "test"), None, "feat"),
        check_vma=False,
    )
```

time: 176 us -> 74.9 us (0.43)
  waiting for transfers between devices: 53.4 us -> 10.9 us
  blocking collectives: 51.2 us -> 10.7 us
  Pallas kernels: 0 us -> 26.5 us
  other arithmetic: 26.4 us -> 2.4 us
  matrix products: 20 us -> 0 us
  between operations: 14.7 us -> 0.18 us
  starting transfers between devices: 0.08 us -> 11 us
  local copies, waits for them, and re-layouts: 9.89 us -> 12.6 us
    psum x2 -> x0, blocking collectives: 51.2 us -> none  [the longest x1 28.5 us: on_device(): in_factor, grad_factor = lax.psum((in_whole, grad_whole), ('dp', 'test'))]
    all_gather x2 -> x0, waiting for transfers between devices: 44.5 us -> none  [the longest x1 44.4 us: on_device(): lax.all_gather(solved_flat, ('dp', 'test'), axis=0, tiled=True)]
    pallas_call x0 -> x6, Pallas kernels: none -> 26.5 us  [the longest x2 9.85 us: project(): pl.pallas_call(functools.partial(project_body, start, rows, x_chunk, g_ch...]
    another operation x10 -> x0, other arithmetic: 24.2 us -> none  [the longest x6 13 us: damped_inverse(): lower_factor = jnp.linalg.cholesky(damped)]
    dot_general x10 -> x0, matrix products: 19.5 us -> none  [the longest x1 8.27 us: on_device(): jnp.dot(train_grads.reshape(tokens, out_width), proj_out, preferred_eleme...]
    ppermute x0 -> x8, starting transfers between devices: none -> 11 us  [xor_permute(): return lax.ppermute(values, axis, [(i, i ^ mask) for i in range(size)])]
    ppermute x0 -> x8, waiting for transfers between devices: none -> 10.9 us  [xor_permute(): return lax.ppermute(values, axis, [(i, i ^ mask) for i in range(size)])]
    all_to_all x0 -> x1, blocking collectives: none -> 10.7 us  [on_device(): lax.all_to_all(shares, ('dp', 'feat', 'test'), split_axis=0, concat_axis=0)]
  transfers between devices with their start and end apart: 3 -> 8, of which waited for: 2 -> 5; matrix products, arithmetic and copies ran while one was open for 22% -> 4% of each run, Pallas kernels for 0% -> 14%
where the time goes in v1:
time: 74.9 us; the launch traced here: 74.4 us
  Pallas kernels  26.5 us (35%)
  local copies, waits for them, and re-layouts  12.6 us (17%)
  starting transfers between devices  11 us (15%)
  waiting for transfers between devices  10.9 us (15%)
  blocking collectives  10.7 us (14%)
  other arithmetic  2.4 us (3%)
    unnamed x31, local copies, waits for them, and re-layouts  11.4 us
    ppermute x8, starting transfers between devices, xor_permute(): return lax.ppermute(values, axis, [(i, i ^ mask) for i in range(size)])  11 us
    ppermute x8, waiting for transfers between devices, xor_permute(): return lax.ppermute(values, axis, [(i, i ^ mask) for i in range(size)])  10.9 us
    all_to_all x1, blocking collectives, on_device(): lax.all_to_all(shares, ('dp', 'feat', 'test'), split_axis=0, concat_axis=0)  10.7 us
    pallas_call x2, Pallas kernels, project(): pl.pallas_call(functools.partial(project_body, start, rows, x_chunk, g_ch...  9.85 us
    pallas_call x1, Pallas kernels, partial_scores(): pl.pallas_call(functools.partial(scores_body, total_tokens, blocks, chunk...  9.23 us
    pallas_call x2, Pallas kernels, gram(): pl.pallas_call(functools.partial(gram_body, first, count, len(received)),...  3.85 us
    pallas_call x1, Pallas kernels, flatten(): pl.pallas_call(flatten_body, out_shape=jax.ShapeDtypeStruct((count, rows...  3.62 us
  transfers between devices with their start and end apart: 8, of which 5 were waited for; matrix products, arithmetic and copies ran while one was open for 4% of the time, Pallas kernels for 14%

profile of v1, /device:TPU:0, one launch (start us, length us, event | category | flops | bytes accessed | tf_op | source)
XLA Modules:
  0.0 74.4 jit_solution(12166754180143969321)
XLA Ops:
  0.0 1.2 %copy.13.pin_hbm = bf16[2048,64]{1,0:T(8,128)(2,1)S(1)} copy(bf16[2048,64]{0,1:T(8,128)(2,1)} %param.9) | data formatting | bytes 524288 | tf_op args[2]
  1.2 1.9 %copy.14.pout_hbm = bf16[7168,64]{1,0:T(8,128)(2,1)S(1)} copy(bf16[7168,64]{0,1:T(8,128)(2,1)} %param.10) | data formatting | bytes 1835008 | tf_op args[3]
  3.2 1.9 %copy-done = bf16[8,96,2048]{2,1,0:T(8,128)(2,1)S(1)} copy-done((bf16[8,96,2048]{2,1,0:T(8,128)(2,1)S(1)}, bf16[8,96,2048]{2,1,0:T(8,128)(2,1)}, u32[]{:S(2)}) %copy-start) | copy-done | bytes 3145752
  5.0 4.9 %project.2 = (f32[384,128]{1,0:T(8,128)S(1)}, bf16[384,128]{1,0:T(8,128)(2,1)S(1)}) custom-call(bf16[768,2048]{1,0:T(8,128)(2,1)S(1)} %bitcast.7, bf16[768,7168]{1,0:T(8,128)(2,1)} %bitcast.9, bf16[2048,64]{1,0:T(8,128)(2,1)S(1)} %copy.13.pin_hbm, bf16[7168,64]{1,0:T(8,128)(2,1)S(1)} %copy.14.pout_hbm), custom_call_target="tpu_custom_call" | custom-call | flops 452984832 | bytes 8257536 | tf_op jit(solution)/shard_map/project/pallas_call | solution.py:65
  10.6 2.9 %collective-permute-start = (bf16[384,128]{1,0:T(8,128)(2,1)S(1)}, bf16[384,128]{1,0:T(8,128)(2,1)S(1)}, u32[]{:S(2)}, u32[]{:S(2)}) collective-permute-start(bf16[384,128]{1,0:T(8,128)(2,1)S(1)} %get-tuple-element.14), channel_id=1, source_target_pairs={{0,2},{2,0},{1,3},{3,1},{4,6},{6,4},{5,7},{7,5},{8,10},{10,8},{9,1... | collective-permute-start | bytes 294920 | tf_op jit(solution)/shard_map/ppermute | solution.py:17
  13.5 5.0 %project.3 = (f32[384,128]{1,0:T(8,128)S(1)}, bf16[384,128]{1,0:T(8,128)(2,1)S(1)}) custom-call(bf16[768,2048]{1,0:T(8,128)(2,1)S(1)} %bitcast.8, bf16[768,7168]{1,0:T(8,128)(2,1)} %bitcast.10, bf16[2048,64]{1,0:T(8,128)(2,1)S(1)} %copy.13.pin_hbm, bf16[7168,64]{1,0:T(8,128)(2,1)S(1)} %copy.14.pout_hbm), custom_call_target="tpu_custom_call" | custom-call | flops 452984832 | bytes 8257536 | tf_op jit(solution)/shard_map/project/pallas_call | solution.py:65
  19.8 1.9 %gram.2 = (f32[64,128]{1,0:T(8,128)}, bf16[2,64,128]{2,1,0:T(8,128)(2,1)}) custom-call(s32[8]{0:T(128)} %lengths_ref.3, s32[8,96]{1,0:T(8,128)} %mask_ref.3, f32[384,128]{1,0:T(8,128)} %copy-done.3, bf16[384,128]{1,0:T(8,128)(2,1)} %copy-done.8), custom_call_target="tpu_custom_call" | custom-call | tf_op jit(solution)/shard_map/gram/pallas_call | solution.py:120
  21.8 2.1 %collective-permute-done.1.refs_0_ = bf16[384,128]{1,0:T(8,128)(2,1)S(1)} collective-permute-done((bf16[384,128]{1,0:T(8,128)(2,1)S(1)}, bf16[384,128]{1,0:T(8,128)(2,1)S(1)}, u32[]{:S(2)}, u32[]{:S(2)}) %collective-permute-start.1) | collective-permute-done | bytes 98336 | tf_op jit(solution)/shard_map/ppermute | solution.py:17
  24.4 1.9 %gram.3 = (f32[64,128]{1,0:T(8,128)}, bf16[2,64,128]{2,1,0:T(8,128)(2,1)}) custom-call(s32[8]{0:T(128)} %lengths_ref.3, s32[8,96]{1,0:T(8,128)} %mask_ref.3, f32[384,128]{1,0:T(8,128)} %copy-done.2, bf16[384,128]{1,0:T(8,128)(2,1)} %copy-done.7), custom_call_target="tpu_custom_call" | custom-call | tf_op jit(solution)/shard_map/gram/pallas_call | solution.py:120
  26.4 0.8 %pad_maximum_fusion.2 = bf16[4,64,128]{2,1,0:T(8,128)(2,1)S(1)} fusion(bf16[2,64,128]{2,1,0:T(8,128)(2,1)} %get-tuple-element.20, bf16[2,64,128]{2,1,0:T(8,128)(2,1)} %get-tuple-element.19), kind=kLoop, calls=%fused_computation.2 | loop fusion | flops 32768 | bytes 131072 | tf_op jit(solution)/shard_map/concatenate | solution.py:297
  27.2 2.7 %collective-permute-start.5 = (bf16[4,64,128]{2,1,0:T(8,128)(2,1)S(1)}, bf16[4,64,128]{2,1,0:T(8,128)(2,1)S(1)}, u32[]{:S(2)}, u32[]{:S(2)}) collective-permute-start(bf16[4,64,128]{2,1,0:T(8,128)(2,1)S(1)} %pad_maximum_fusion.2), channel_id=1, source_target_pairs={{0,8},{4,12},{8,0},{12,4},{1,9},{5,13},{9,1},{13,5},{2,10},{6,14},... | collective-permute-start | bytes 196616 | tf_op jit(solution)/shard_map/ppermute | solution.py:17
  29.9 2.6 %collective-permute-done.5 = bf16[4,64,128]{2,1,0:T(8,128)(2,1)S(1)} collective-permute-done((bf16[4,64,128]{2,1,0:T(8,128)(2,1)S(1)}, bf16[4,64,128]{2,1,0:T(8,128)(2,1)S(1)}, u32[]{:S(2)}, u32[]{:S(2)}) %collective-permute-start.5) | collective-permute-done | bytes 65568 | tf_op jit(solution)/shard_map/ppermute | solution.py:17
  32.4 0.8 %pad_maximum_fusion.1 = bf16[8,64,128]{2,1,0:T(8,128)(2,1)S(1)} fusion(bf16[4,64,128]{2,1,0:T(8,128)(2,1)S(1)} %collective-permute-done.5, bf16[2,64,128]{2,1,0:T(8,128)(2,1)} %get-tuple-element.20, bf16[2,64,128]{2,1,0:T(8,128)(2,1)} %get-tuple-element.19), kind=kLoop, calls=%fused_computation.1 | loop fusion | flops 131072 | bytes 262144 | tf_op jit(solution)/shard_map/concatenate | solution.py:305
  33.2 1.6 %collective-permute-start.6 = (bf16[8,64,128]{2,1,0:T(8,128)(2,1)S(1)}, bf16[8,64,128]{2,1,0:T(8,128)(2,1)S(1)}, u32[]{:S(2)}, u32[]{:S(2)}) collective-permute-start(bf16[8,64,128]{2,1,0:T(8,128)(2,1)S(1)} %pad_maximum_fusion.1), channel_id=1, source_target_pairs={{0,4},{4,0},{8,12},{12,8},{1,5},{5,1},{9,13},{13,9},{2,6},{6,2},{1... | collective-permute-start | bytes 393224 | tf_op jit(solution)/shard_map/ppermute | solution.py:17
  34.9 2.5 %copy.17.tests_ref = bf16[128,32,64]{2,1,0:T(8,128)(2,1)} copy(bf16[128,32,64]{0,2,1:T(8,128)(2,1)S(1)} %copy-done.4) | data formatting | bytes 1048576 | tf_op args[6]
  37.4 3.6 %flatten.1.tests_ref = bf16[128,2048]{1,0:T(8,128)(2,1)} custom-call(bf16[128,32,64]{2,1,0:T(8,128)(2,1)} %copy.17.tests_ref), custom_call_target="tpu_custom_call" | custom-call | tf_op jit(solution)/shard_map/flatten/pallas_call | solution.py:143
  41.1 1.2 %collective-permute-done.2 = f32[64,128]{1,0:T(8,128)S(1)} collective-permute-done((f32[64,128]{1,0:T(8,128)S(1)}, f32[64,128]{1,0:T(8,128)S(1)}, u32[]{:S(2)}, u32[]{:S(2)}) %collective-permute-start.2) | collective-permute-done | bytes 32800 | tf_op jit(solution)/shard_map/ppermute | solution.py:17
  42.9 3.3 %collective-permute-done.3 = f32[64,128]{1,0:T(8,128)S(1)} collective-permute-done((f32[64,128]{1,0:T(8,128)S(1)}, f32[64,128]{1,0:T(8,128)S(1)}, u32[]{:S(2)}, u32[]{:S(2)}) %collective-permute-start.3) | collective-permute-done | bytes 32800 | tf_op jit(solution)/shard_map/ppermute | solution.py:17
  46.2 3.2 %collective-permute-start.4 = (f32[64,128]{1,0:T(8,128)S(1)}, f32[64,128]{1,0:T(8,128)S(1)}, u32[]{:S(2)}, u32[]{:S(2)}) collective-permute-start(f32[64,128]{1,0:T(8,128)S(1)} %add.11.gram_a_ref), channel_id=1, source_target_pairs={{0,8},{4,12},{8,0},{12,4},{1,9},{5,13},{9,1},{13,5},{2,10},{6,14},... | collective-permute-start | bytes 98312 | tf_op jit(solution)/shard_map/ppermute | solution.py:17
  49.5 1.8 %collective-permute-done.4.gram_b_ref = f32[64,128]{1,0:T(8,128)S(1)} collective-permute-done((f32[64,128]{1,0:T(8,128)S(1)}, f32[64,128]{1,0:T(8,128)S(1)}, u32[]{:S(2)}, u32[]{:S(2)}) %collective-permute-start.4) | collective-permute-done | bytes 32800 | tf_op jit(solution)/shard_map/ppermute | solution.py:17
  51.3 1.0 %copy-done.1 = bf16[128,2048]{1,0:T(8,128)(2,1)S(1)} copy-done((bf16[128,2048]{1,0:T(8,128)(2,1)S(1)}, bf16[128,2048]{1,0:T(8,128)(2,1)}, u32[]{:S(2)}) %copy-start.1) | copy-done | bytes 524312
  52.4 9.2 %scores.1 = f32[16,8,64]{2,1,0:T(8,128)S(1)} custom-call(f32[64,128]{1,0:T(8,128)S(1)} %add.11.gram_a_ref, f32[64,128]{1,0:T(8,128)S(1)} %collective-permute-done.4.gram_b_ref, bf16[128,2048]{1,0:T(8,128)(2,1)S(1)} %copy-done.1, bf16[32,64,128]{2,1,0:T(8,128)(2,1)S(1)} %constant_dynamic-update-slice_fusion.refs_0_), custom_call_target="tpu_custom_call" | custom-call | tf_op jit(solution)/shard_map/scores/pallas_call | solution.py:252
  61.7 10.7 %all_to_all.5 = f32[16,1,512]{2,1,0:T(1,128)S(1)} all-to-all(f32[16,1,512]{2,1,0:T(1,128)S(1)} %reshape.16), channel_id=1, replica_groups=mesh['groups'=2,'dp'=4,'feat'=2,'test'=2] {'dp','feat','test'}, dimensions={0} | all-to-all | bytes 65536 | tf_op jit(solution)/shard_map/all_to_all | solution.py:309
  72.9 0.7 reduce
  (41 shorter events, 4.7 us)
Async XLA Ops:
  3.1 1.9 %copy-start = (bf16[8,96,2048]{2,1,0:T(8,128)(2,1)S(1)}, bf16[8,96,2048]{2,1,0:T(8,128)(2,1)}, u32[]{:S(2)}) copy-start(bf16[8,96,2048]{2,1,0:T(8,128)(2,1)} %param.7) | copy-start | bytes 9437188
  9.9 0.7 copy-start.3
  10.6 24.3 %copy-start.4 = (bf16[128,32,64]{0,2,1:T(8,128)(2,1)S(1)}, bf16[128,32,64]{0,2,1:T(8,128)(2,1)}, u32[]{:S(2)}) copy-start(bf16[128,32,64]{0,2,1:T(8,128)(2,1)} %param.13) | copy-start | bytes 1572868
  10.6 8.6 %collective-permute-start = (bf16[384,128]{1,0:T(8,128)(2,1)S(1)}, bf16[384,128]{1,0:T(8,128)(2,1)S(1)}, u32[]{:S(2)}, u32[]{:S(2)}) collective-permute-start(bf16[384,128]{1,0:T(8,128)(2,1)S(1)} %get-tuple-element.14), channel_id=1, source_target_pairs={{0,2},{2,0},{1,3},{3,1},{4,6},{6,4},{5,7},{7,5},{8,10},{10,8},{9,1... | collective-permute-start | bytes 294920 | tf_op jit(solution)/shard_map/ppermute | solution.py:17
  18.5 0.7 copy-start.2
  19.2 4.6 %collective-permute-start.1 = (bf16[384,128]{1,0:T(8,128)(2,1)S(1)}, bf16[384,128]{1,0:T(8,128)(2,1)S(1)}, u32[]{:S(2)}, u32[]{:S(2)}) collective-permute-start(bf16[384,128]{1,0:T(8,128)(2,1)S(1)} %get-tuple-element.17), channel_id=1, source_target_pairs={{0,2},{2,0},{1,3},{3,1},{4,6},{6,4},{5,7},{7,5},{8,10},{10,8},{9,1... | collective-permute-start | bytes 294920 | tf_op jit(solution)/shard_map/ppermute | solution.py:17
  19.2 0.6 copy-start.8
  21.8 19.3 %copy-start.9 = (f32[64,128]{1,0:T(8,128)S(1)}, f32[64,128]{1,0:T(8,128)}, u32[]{:S(2)}) copy-start(f32[64,128]{1,0:T(8,128)} %get-tuple-element.15) | copy-start | bytes 98308
  21.8 19.4 %copy-start.5 = (bf16[2,64,128]{2,1,0:T(8,128)(2,1)S(1)}, bf16[2,64,128]{2,1,0:T(8,128)(2,1)}, u32[]{:S(2)}) copy-start(bf16[2,64,128]{2,1,0:T(8,128)(2,1)} %get-tuple-element.19) | copy-start | bytes 98308
  23.8 0.6 copy-start.7
  26.4 14.7 %copy-start.10 = (f32[64,128]{1,0:T(8,128)S(1)}, f32[64,128]{1,0:T(8,128)}, u32[]{:S(2)}) copy-start(f32[64,128]{1,0:T(8,128)} %get-tuple-element.18) | copy-start | bytes 98308
  26.4 16.4 %copy-start.6 = (bf16[2,64,128]{2,1,0:T(8,128)(2,1)S(1)}, bf16[2,64,128]{2,1,0:T(8,128)(2,1)}, u32[]{:S(2)}) copy-start(bf16[2,64,128]{2,1,0:T(8,128)(2,1)} %get-tuple-element.20) | copy-start | bytes 98308
  27.2 5.2 %collective-permute-start.5 = (bf16[4,64,128]{2,1,0:T(8,128)(2,1)S(1)}, bf16[4,64,128]{2,1,0:T(8,128)(2,1)S(1)}, u32[]{:S(2)}, u32[]{:S(2)}) collective-permute-start(bf16[4,64,128]{2,1,0:T(8,128)(2,1)S(1)} %pad_maximum_fusion.2), channel_id=1, source_target_pairs={{0,8},{4,12},{8,0},{12,4},{1,9},{5,13},{9,1},{13,5},{2,10},{6,14},... | collective-permute-start | bytes 196616 | tf_op jit(solution)/shard_map/ppermute | solution.py:17
  33.2 9.5 %collective-permute-start.6 = (bf16[8,64,128]{2,1,0:T(8,128)(2,1)S(1)}, bf16[8,64,128]{2,1,0:T(8,128)(2,1)S(1)}, u32[]{:S(2)}, u32[]{:S(2)}) collective-permute-start(bf16[8,64,128]{2,1,0:T(8,128)(2,1)S(1)} %pad_maximum_fusion.1), channel_id=1, source_target_pairs={{0,4},{4,0},{8,12},{12,8},{1,5},{5,1},{9,13},{13,9},{2,6},{6,2},{1... | collective-permute-start | bytes 393224 | tf_op jit(solution)/shard_map/ppermute | solution.py:17
  41.0 1.3 %collective-permute-start.2 = (f32[64,128]{1,0:T(8,128)S(1)}, f32[64,128]{1,0:T(8,128)S(1)}, u32[]{:S(2)}, u32[]{:S(2)}) collective-permute-start(f32[64,128]{1,0:T(8,128)S(1)} %add.9), channel_id=1, source_target_pairs={{0,1},{1,0},{2,3},{3,2},{4,5},{5,4},{6,7},{7,6},{8,9},{9,8},{10,11... | collective-permute-start | bytes 98312 | tf_op jit(solution)/shard_map/ppermute | solution.py:17
  42.3 3.9 %collective-permute-start.3 = (f32[64,128]{1,0:T(8,128)S(1)}, f32[64,128]{1,0:T(8,128)S(1)}, u32[]{:S(2)}, u32[]{:S(2)}) collective-permute-start(f32[64,128]{1,0:T(8,128)S(1)} %add.10), channel_id=1, source_target_pairs={{0,4},{4,0},{8,12},{12,8},{1,5},{5,1},{9,13},{13,9},{2,6},{6,2},{1... | collective-permute-start | bytes 98312 | tf_op jit(solution)/shard_map/ppermute | solution.py:17
  42.8 6.7 %collective-permute-start.7 = (bf16[16,64,128]{2,1,0:T(8,128)(2,1)S(1)}, bf16[16,64,128]{2,1,0:T(8,128)(2,1)S(1)}, u32[]{:S(2)}, u32[]{:S(2)}) collective-permute-start(bf16[16,64,128]{2,1,0:T(8,128)(2,1)S(1)} %pad_maximum_fusion), channel_id=1, source_target_pairs={{0,1},{1,0},{2,3},{3,2},{4,5},{5,4},{6,7},{7,6},{8,9},{9,8},{10,11... | collective-permute-start | bytes 786440 | tf_op jit(solution)/shard_map/ppermute | solution.py:17
  46.2 5.1 %collective-permute-start.4 = (f32[64,128]{1,0:T(8,128)S(1)}, f32[64,128]{1,0:T(8,128)S(1)}, u32[]{:S(2)}, u32[]{:S(2)}) collective-permute-start(f32[64,128]{1,0:T(8,128)S(1)} %add.11.gram_a_ref), channel_id=1, source_target_pairs={{0,8},{4,12},{8,0},{12,4},{1,9},{5,13},{9,1},{13,5},{2,10},{6,14},... | collective-permute-start | bytes 98312 | tf_op jit(solution)/shard_map/ppermute | solution.py:17
  51.3 1.0 %copy-start.1 = (bf16[128,2048]{1,0:T(8,128)(2,1)S(1)}, bf16[128,2048]{1,0:T(8,128)(2,1)}, u32[]{:S(2)}) copy-start(bf16[128,2048]{1,0:T(8,128)(2,1)} %flatten.1.tests_ref) | copy-start | bytes 1572868

commit v2 on v0

v2 whole, which is shorter than its diff:
```python
import functools

import jax
import jax.numpy as jnp
from jax import lax
from jax.experimental import pallas as pl
from jax.experimental.pallas import tpu as pltpu
from jax.sharding import PartitionSpec as P

f32 = jnp.float32
bf16 = jnp.bfloat16
MIB = 1024 * 1024
NT = (((1,), (1,)), ((), ()))
VMEM = pl.BlockSpec(memory_space=pltpu.VMEM)
SMEM = pl.BlockSpec(memory_space=pltpu.SMEM)
ANY = pl.BlockSpec(memory_space=pl.ANY)


def xor_permute(values, axis, mask):
    size = lax.axis_size(axis)
    return lax.ppermute(values, axis, [(i, i ^ mask) for i in range(size)])


def masks_of(size):
    masks, mask = [], 1
    while mask < size:
        masks.append(mask)
        mask *= 2
    return masks


def project_body(rows, x_hbm, g_hbm, pin_hbm, pout_hbm, own_ref, sent_ref, x_buf, g_buf, pin_buf, pout_buf, sems):
    steps = x_hbm.shape[0] // rows
    rank = pin_hbm.shape[0]
    pin_copy = pltpu.make_async_copy(pin_hbm, pin_buf, sems.at[0])
    x_copy = pltpu.make_async_copy(x_hbm, x_buf, sems.at[1])
    pout_copy = pltpu.make_async_copy(pout_hbm, pout_buf, sems.at[2])

    def g_copy(step):
        begin = step * rows if isinstance(step, int) else pl.multiple_of(step * rows, rows)
        block = pl.ds(begin, rows)
        return pltpu.make_async_copy(g_hbm.at[block, :], g_buf.at[block, :], sems.at[3 + step])

    pin_copy.start()
    x_copy.start()
    pout_copy.start()
    for step in range(steps):
        g_copy(step).start()
    pin_copy.wait()
    x_copy.wait()
    own_ref[:, :rank] = lax.dot_general(x_buf[...], pin_buf[...], NT, preferred_element_type=f32)
    pout_copy.wait()

    @pl.loop(0, steps)
    def _(step):
        g_copy(step).wait()
        block = pl.ds(pl.multiple_of(step * rows, rows), rows)
        right = lax.dot_general(g_buf[block, :], pout_buf[...], NT, preferred_element_type=f32)
        both = jnp.concatenate([own_ref[block, :rank], right], axis=1)
        own_ref[block, :] = both
        sent_ref[block, :] = both.astype(bf16)


def project(x, g, pin, pout, rows):
    tokens, in_width = x.shape
    out_width = g.shape[1]
    rank = pin.shape[0]
    return pl.pallas_call(
        functools.partial(project_body, rows),
        out_shape=(
            jax.ShapeDtypeStruct((tokens, 2 * rank), f32),
            jax.ShapeDtypeStruct((tokens, 2 * rank), bf16),
        ),
        in_specs=[ANY] * 4,
        out_specs=(VMEM, VMEM),
        scratch_shapes=[
            pltpu.VMEM(x.shape, bf16),
            pltpu.VMEM(g.shape, bf16),
            pltpu.VMEM(pin.shape, bf16),
            pltpu.VMEM(pout.shape, bf16),
            pltpu.SemaphoreType.DMA((3 + tokens // rows,)),
        ],
        compiler_params=pltpu.CompilerParams(vmem_limit_bytes=60 * MIB),
        cost_estimate=pl.CostEstimate(
            flops=2 * tokens * (in_width + out_width) * rank,
            bytes_accessed=2 * (tokens + rank) * (in_width + out_width),
            transcendentals=0,
        ),
        name="project",
    )(x, g, pin, pout)


def factors_body(received, lengths_ref, mask_ref, own_ref, *refs):
    received_refs = refs[:received]
    factor_ref, rounded_ref, turned_ref = refs[received:]
    examples, seq_len = mask_ref.shape
    rank = factor_ref.shape[0]
    positions = lax.broadcasted_iota(jnp.int32, (1, seq_len), 1)
    total = None
    for example in range(examples):
        rows = pl.ds(example * seq_len, seq_len)
        summed = own_ref[rows, :]
        for ref in received_refs:
            summed = summed + ref[rows, :].astype(f32)
        rounded = summed.astype(bf16)
        rounded_ref[rows, :] = rounded
        live = (mask_ref[example : example + 1, :] > 0) & (positions < lengths_ref[example])
        turned = jnp.where(live, rounded.astype(f32).T, 0.0).astype(bf16)
        turned_ref[example] = turned
        products = jnp.dot(turned, rounded, preferred_element_type=f32)
        total = products if total is None else total + products
    lane = lax.broadcasted_iota(jnp.int32, (rank, 2 * rank), 1)
    factor_ref[...] = jnp.where(lane < rank, total[:rank, :], total[rank:, :])


def factors(lengths, mask, own, received):
    tokens, width = own.shape
    examples, seq_len = mask.shape
    return pl.pallas_call(
        functools.partial(factors_body, len(received)),
        out_shape=(
            jax.ShapeDtypeStruct((width // 2, width), f32),
            jax.ShapeDtypeStruct((tokens, width), bf16),
            jax.ShapeDtypeStruct((examples, width, seq_len), bf16),
        ),
        in_specs=[SMEM, VMEM, VMEM] + [VMEM] * len(received),
        out_specs=(VMEM, VMEM, VMEM),
        compiler_params=pltpu.CompilerParams(vmem_limit_bytes=4 * MIB),
        name="factors",
    )(lengths, mask, own, *received)


def features_body(lengths_ref, rounded_ref, turned_ref, feats_ref):
    half, rank, _ = feats_ref.shape
    examples, _, seq_len = turned_ref.shape
    lane = lax.broadcasted_iota(jnp.int32, (rank, 2 * rank), 1)

    def features(example):
        products = jnp.dot(
            turned_ref[example, rank:, :], rounded_ref[pl.ds(example * seq_len, seq_len), :], preferred_element_type=f32
        )
        return products / lengths_ref[example].astype(f32)

    for pair in range(half):
        other = pltpu.roll(features(half + pair), rank, 1)
        feats_ref[pair] = jnp.where(lane < rank, features(pair), other).astype(bf16)


def features_of(lengths, rounded, turned):
    examples, width, seq_len = turned.shape
    return pl.pallas_call(
        features_body,
        out_shape=jax.ShapeDtypeStruct((examples // 2, width // 2, width), bf16),
        in_specs=[SMEM, VMEM, VMEM],
        out_specs=VMEM,
        compiler_params=pltpu.CompilerParams(vmem_limit_bytes=4 * MIB),
        cost_estimate=pl.CostEstimate(flops=2 * examples * seq_len * width * width, bytes_accessed=8 * MIB, transcendentals=0),
        name="features",
    )(lengths, rounded, turned)


def split(values):
    high = values.astype(bf16)
    return high, (values - high.astype(f32)).astype(bf16)


def inverses_body(total_tokens, factor_a_ref, factor_b_ref, grad_ref, in_ref, inverse_buf):
    rank = factor_a_ref.shape[0]
    own_rows = grad_ref.shape[1]
    lane = lax.broadcasted_iota(jnp.int32, (rank, 2 * rank), 1)
    sub = lax.broadcasted_iota(jnp.int32, (rank, 2 * rank), 0)
    left = lane < rank
    column = jnp.where(left, lane, lane - rank)
    diagonal = column == sub
    packed = (factor_a_ref[...] + factor_b_ref[...]) / total_tokens
    on_diagonal = jnp.sum(jnp.where(diagonal, packed, 0.0), axis=0, keepdims=True)
    trace_in = jnp.sum(jnp.where(left[:1], on_diagonal, 0.0), axis=1, keepdims=True)
    trace_grad = jnp.sum(jnp.where(left[:1], 0.0, on_diagonal), axis=1, keepdims=True)
    damping = 0.1 * jnp.where(left[:1], trace_in, trace_grad) / rank + 1e-06
    packed = packed + jnp.where(diagonal, damping, 0.0)
    for k in range(rank):
        pivot_column = jnp.where(left, packed[:, k : k + 1], packed[:, rank + k : rank + k + 1])
        row = packed[k : k + 1, :]
        inverse = 1.0 / pivot_column[k : k + 1, :]
        at_pivot = column[:1] == k
        row = jnp.where(at_pivot, inverse, row * inverse)
        packed = jnp.where(sub == k, row, jnp.where(at_pivot, 0.0, packed) - pivot_column * row)
    inverse_buf[...] = pltpu.roll(packed, rank, 1)
    first_row = pl.multiple_of(lax.axis_index("feat") * own_rows, 8)
    grad_ref[0], grad_ref[1] = split(inverse_buf[pl.ds(first_row, own_rows), :][:, :rank])
    twice = pltpu.roll(packed, rank, 1)
    in_ref[0, :rank, :], in_ref[1, :rank, :] = split(jnp.where(left, packed, 0.0))
    in_ref[0, rank:, :], in_ref[1, rank:, :] = split(jnp.where(left, 0.0, twice))


def inverses(total_tokens, factor_a, factor_b, own_rows):
    rank, width = factor_a.shape
    return pl.pallas_call(
        functools.partial(inverses_body, total_tokens),
        out_shape=(
            jax.ShapeDtypeStruct((2, own_rows, rank), bf16),
            jax.ShapeDtypeStruct((2, width, width), bf16),
        ),
        in_specs=[VMEM, VMEM],
        out_specs=(VMEM, VMEM),
        scratch_shapes=[pltpu.VMEM((rank, width), f32)],
        compiler_params=pltpu.CompilerParams(vmem_limit_bytes=4 * MIB),
        cost_estimate=pl.CostEstimate(flops=4 * MIB, bytes_accessed=16 * MIB, transcendentals=0),
        name="inverses",
    )(factor_a, factor_b)


def scores_body(dp_masks, grad_ref, in_ref, own_tests_ref, other_tests_ref, *refs):
    feats_refs, (out_ref, solved_buf, line_buf) = refs[:-3], refs[-3:]
    feat_count = lax.axis_size("feat")
    dp = lax.axis_index("dp")
    own_rows, rank = grad_ref.shape[1:]
    pairs = [ref[i] for ref in feats_refs for i in range(ref.shape[0])]
    count = len(pairs)
    half = count // len(dp_masks)
    dot = functools.partial(jnp.dot, preferred_element_type=f32)
    for at in range(count):
        high, low = split(dot(grad_ref[0], pairs[at]) + dot(grad_ref[1], pairs[at]))
        solved_buf[at * own_rows : (at + 1) * own_rows, :] = dot(high, in_ref[0]) + dot(high, in_ref[1]) + dot(low, in_ref[0])
    lane = lax.broadcasted_iota(jnp.int32, (count, 2 * rank), 1)
    for g in range(0, own_rows, 2):
        low = solved_buf[pl.ds(g, count, stride=own_rows), :]
        high = solved_buf[pl.ds(g + 1, count, stride=own_rows), :]
        first = jnp.where(lane < rank, low, pltpu.roll(high, rank, 1))
        second = jnp.where(lane < rank, pltpu.roll(low, rank, 1), high)
        line_buf[:, g * rank : (g + 2) * rank] = jnp.concatenate([first, second], axis=0).astype(bf16)
    lines = line_buf[...]
    own = dot(lines, own_tests_ref[...])
    other = dot(lines, other_tests_ref[...])
    is_first = lax.axis_index("test") == 0
    parts = (jnp.where(is_first, own, other), jnp.where(is_first, other, own))
    block = own.shape[1] // feat_count
    for target in range(feat_count):
        columns = slice(target * block, (target + 1) * block)
        both = jnp.concatenate([part[:, columns] for part in parts], axis=1)
        for at, mask in enumerate(dp_masks):
            place = (dp ^ mask) * feat_count + target
            out_ref[place, :half, :] = both[at * half : (at + 1) * half, :]
            out_ref[place, half:, :] = both[count + at * half : count + (at + 1) * half, :]


def partial_scores(dp_masks, grad, in_pair, own_tests, other_tests, feats):
    feat_count = lax.axis_size("feat")
    own_rows, rank = grad.shape[1:]
    count = sum(f.shape[0] for f in feats)
    rows = 2 * count // len(dp_masks)
    return pl.pallas_call(
        functools.partial(scores_body, dp_masks),
        out_shape=jax.ShapeDtypeStruct((len(dp_masks) * feat_count, rows, 2 * own_tests.shape[1] // feat_count), f32),
        in_specs=[VMEM] * (4 + len(feats)),
        out_specs=VMEM,
        scratch_shapes=[
            pltpu.VMEM((count * own_rows, 2 * rank), f32),
            pltpu.VMEM((2 * count, own_rows * rank), bf16),
        ],
        compiler_params=pltpu.CompilerParams(vmem_limit_bytes=16 * MIB),
        name="scores",
    )(grad, in_pair, own_tests, other_tests, *feats)


def finish_body(feat_count, arrived_ref, out_ref):
    blocks, examples, width = arrived_ref.shape
    dp_count = blocks // feat_count
    half = width // 2
    for dp in range(dp_count):
        total = arrived_ref[dp * feat_count]
        for feat in range(1, feat_count):
            total = total + arrived_ref[dp * feat_count + feat]
        for test in range(2):
            out_ref[pl.ds(2 * dp + test, examples, stride=2 * dp_count), :] = total[:, test * half : (test + 1) * half]


def finish(arrived, feat_count):
    blocks, examples, width = arrived.shape
    queries = 2 * blocks // feat_count
    out = pl.pallas_call(
        functools.partial(finish_body, feat_count),
        out_shape=jax.ShapeDtypeStruct((examples * queries, width // 2), f32),
        in_specs=[VMEM],
        out_specs=VMEM,
        compiler_params=pltpu.CompilerParams(vmem_limit_bytes=4 * MIB),
        name="finish",
    )(arrived)
    return out.reshape(examples, queries, width // 2)


def on_device(train_inputs, train_grads, proj_in, proj_out, lengths, loss_mask, test_feats):
    examples, seq_len, in_width = train_inputs.shape
    out_width = train_grads.shape[2]
    tokens = examples * seq_len
    feat_count = lax.axis_size("feat")
    dp_count = lax.axis_size("dp")
    test_count = lax.axis_size("test")
    own_rows = test_feats.shape[1]
    x = train_inputs.reshape(tokens, in_width)
    g = train_grads.reshape(tokens, out_width)
    own, sent = project(x, g, proj_in.T, proj_out.T, tokens // 3)
    received = [xor_permute(sent, "feat", mask) for mask in range(1, feat_count)]
    own_tests = test_feats.transpose(1, 2, 0).reshape(own_rows * test_feats.shape[2], test_feats.shape[0])
    other_tests = xor_permute(own_tests, "test", 1)
    factor, rounded, turned = factors(lengths, loss_mask, own, received)
    feats = [features_of(lengths, rounded, turned)]
    dp_masks = [0]
    steps = [("dp", m) for m in reversed(masks_of(dp_count))]
    steps = steps[:-1] + [("test", 1)] + steps[-1:]
    for at, (axis, mask) in enumerate(steps):
        other = xor_permute(factor, axis, mask)
        if at < len(steps) - 1:
            factor = factor + other
        if axis == "dp":
            moved = feats[0] if len(feats) == 1 else jnp.concatenate(feats, axis=0)
            feats = feats + [xor_permute(moved, axis, mask)]
            dp_masks = dp_masks + [d ^ mask for d in dp_masks]
    total_tokens = float(tokens * dp_count * test_count)
    grad, in_pair = inverses(total_tokens, factor, other, own_rows)
    shares = partial_scores(dp_masks, grad, in_pair, own_tests, other_tests, feats)
    arrived = lax.all_to_all(shares, ("dp", "feat"), split_axis=0, concat_axis=0)
    return finish(arrived, feat_count)


def solution(mesh):
    return jax.shard_map(
        on_device,
        mesh=mesh,
        in_specs=(
            P(("groups", "dp", "test"), None, "feat"),
            P(("groups", "dp", "test"), None, "feat"),
            P("feat", None),
            P("feat", None),
            P(("groups", "dp", "test")),
            P(("groups", "dp", "test"), None),
            P(("groups", "dp", "test"), "feat", None),
        ),
        out_specs=P(("groups", "dp", "test"), None, "feat"),
        check_vma=False,
    )
```

time: 176 us -> 57.2 us (0.33)
  blocking collectives: 51.2 us -> 11.6 us
  waiting for transfers between devices: 53.4 us -> 14.3 us
  other arithmetic: 26.4 us -> 0.02 us
  matrix products: 20 us -> 0 us
  Pallas kernels: 0 us -> 18 us
  between operations: 14.7 us -> 0.08 us
  starting transfers between devices: 0.08 us -> 11.9 us
  local copies, waits for them, and re-layouts: 9.89 us -> 1.01 us
    psum x2 -> x0, blocking collectives: 51.2 us -> none  [the longest x1 28.5 us: on_device(): in_factor, grad_factor = lax.psum((in_whole, grad_whole), ('dp', 'test'))]
    all_gather x2 -> x0, waiting for transfers between devices: 44.5 us -> none  [the longest x1 44.4 us: on_device(): lax.all_gather(solved_flat, ('dp', 'test'), axis=0, tiled=True)]
    another operation x10 -> x0, other arithmetic: 24.2 us -> none  [the longest x6 13 us: damped_inverse(): lower_factor = jnp.linalg.cholesky(damped)]
    dot_general x10 -> x0, matrix products: 19.5 us -> none  [the longest x1 8.27 us: on_device(): jnp.dot(train_grads.reshape(tokens, out_width), proj_out, preferred_eleme...]
    pallas_call x0 -> x6, Pallas kernels: none -> 18 us  [the longest x1 7.7 us: project(): pl.pallas_call(functools.partial(project_body, rows), out_shape=(jax.Shap...]
    ppermute x0 -> x7, waiting for transfers between devices: none -> 14.3 us  [xor_permute(): return lax.ppermute(values, axis, [(i, i ^ mask) for i in range(size)])]
    ppermute x0 -> x7, starting transfers between devices: none -> 11.9 us  [xor_permute(): return lax.ppermute(values, axis, [(i, i ^ mask) for i in range(size)])]
    all_to_all x0 -> x1, blocking collectives: none -> 11.6 us  [on_device(): lax.all_to_all(shares, ('dp', 'feat'), split_axis=0, concat_axis=0)]
  transfers between devices with their start and end apart: 3 -> 7, of which waited for: 2 -> 5; matrix products, arithmetic and copies ran while one was open for 22% -> 0% of each run, Pallas kernels for 0% -> 27%
where the time goes in v2:
time: 57.2 us; the launch traced here: 57 us
  Pallas kernels  18 us (31%)
  waiting for transfers between devices  14.3 us (25%)
  starting transfers between devices  11.9 us (21%)
  blocking collectives  11.6 us (20%)
  local copies, waits for them, and re-layouts  1.01 us (2%)
    ppermute x7, waiting for transfers between devices, xor_permute(): return lax.ppermute(values, axis, [(i, i ^ mask) for i in range(size)])  14.3 us
    ppermute x7, starting transfers between devices, xor_permute(): return lax.ppermute(values, axis, [(i, i ^ mask) for i in range(size)])  11.9 us
    all_to_all x1, blocking collectives, on_device(): lax.all_to_all(shares, ('dp', 'feat'), split_axis=0, concat_axis=0)  11.6 us
    pallas_call x1, Pallas kernels, project(): pl.pallas_call(functools.partial(project_body, rows), out_shape=(jax.Shap...  7.7 us
    pallas_call x1, Pallas kernels, inverses(): pl.pallas_call(functools.partial(inverses_body, total_tokens), out_shape=...  6.05 us
    pallas_call x1, Pallas kernels, partial_scores(): pl.pallas_call(functools.partial(scores_body, dp_masks), out_shape=jax.Sh...  1.94 us
  transfers between devices with their start and end apart: 7, of which 5 were waited for; matrix products, arithmetic and copies ran while one was open for 0% of the time, Pallas kernels for 27%

profile of v2, /device:TPU:0, one launch (start us, length us, event | category | flops | bytes accessed | tf_op | source)
XLA Modules:
  0.0 57.0 jit_solution(7100906415769020427)
XLA Ops:
  0.0 0.5 collective-permute-start.4
  0.5 7.7 %project.1 = (f32[768,128]{1,0:T(8,128)}, bf16[768,128]{1,0:T(8,128)(2,1)}) custom-call(bf16[768,2048]{1,0:T(8,128)(2,1)} %bitcast.11, bf16[768,7168]{1,0:T(8,128)(2,1)} %bitcast.10, bf16[64,2048]{1,0:T(8,128)(2,1)} %bitcast.13, bf16[64,7168]{1,0:T(8,128)(2,1)} %bitcast.12), custom_call_target="tpu_custom_call" | custom-call | flops 905969664 | bytes 15335424 | tf_op jit(solution)/shard_map/project/pallas_call | solution.py:68
  8.2 2.6 %collective-permute-start = (bf16[768,128]{1,0:T(8,128)(2,1)}, bf16[768,128]{1,0:T(8,128)(2,1)S(1)}, u32[]{:S(2)}, u32[]{:S(2)}) collective-permute-start(bf16[768,128]{1,0:T(8,128)(2,1)} %get-tuple-element.13), channel_id=1, source_target_pairs={{0,2},{2,0},{1,3},{3,1},{4,6},{6,4},{5,7},{7,5},{8,10},{10,8},{9,1... | collective-permute-start | bytes 589832 | tf_op jit(solution)/shard_map/ppermute | solution.py:21
  10.9 5.7 %collective-permute-done.refs_0_ = bf16[768,128]{1,0:T(8,128)(2,1)S(1)} collective-permute-done((bf16[768,128]{1,0:T(8,128)(2,1)}, bf16[768,128]{1,0:T(8,128)(2,1)S(1)}, u32[]{:S(2)}, u32[]{:S(2)}) %collective-permute-start) | collective-permute-done | bytes 196640 | tf_op jit(solution)/shard_map/ppermute | solution.py:21
  16.6 0.0 copy-done.3
  16.6 0.0 copy-done.2
  16.6 1.0 %copy-done.1 = f32[768,128]{1,0:T(8,128)S(1)} copy-done((f32[768,128]{1,0:T(8,128)S(1)}, f32[768,128]{1,0:T(8,128)}, u32[]{:S(2)}) %copy-start.1) | copy-done | bytes 393240
  17.6 0.8 %factors.1 = (f32[64,128]{1,0:T(8,128)S(1)}, bf16[768,128]{1,0:T(8,128)(2,1)S(1)}, bf16[8,128,96]{2,1,0:T(8,128)(2,1)S(1)}) custom-call(s32[8]{0:T(128)S(1)} %copy-done.3, s32[8,96]{1,0:T(8,128)S(1)} %copy-done.2, f32[768,128]{1,0:T(8,128)S(1)} %copy-done.1, bf16[768,128]{1,0:T(8,128)(2,1)S(1)} %collective-permute-done.refs_0_), custom_call_target="tpu_custom_call" | custom-call | tf_op jit(solution)/shard_map/factors/pallas_call | solution.py:119
  18.4 0.8 %features.1.refs_0_ = bf16[4,64,128]{2,1,0:T(8,128)(2,1)S(1)} custom-call(s32[8]{0:T(128)S(1)} %copy-done.3, bf16[768,128]{1,0:T(8,128)(2,1)S(1)} %get-tuple-element.17.rounded_ref, bf16[8,128,96]{2,1,0:T(8,128)(2,1)S(1)} %get-tuple-element.18.turned_ref), custom_call_target="tpu_custom_call" | custom-call | flops 25165824 | bytes 8388608 | tf_op jit(solution)/shard_map/features/pallas_call | solution.py:151
  19.2 2.9 %collective-permute-start.5 = (bf16[4,64,128]{2,1,0:T(8,128)(2,1)S(1)}, bf16[4,64,128]{2,1,0:T(8,128)(2,1)S(1)}, u32[]{:S(2)}, u32[]{:S(2)}) collective-permute-start(bf16[4,64,128]{2,1,0:T(8,128)(2,1)S(1)} %features.1.refs_0_), channel_id=1, source_target_pairs={{0,8},{4,12},{8,0},{12,4},{1,9},{5,13},{9,1},{13,5},{2,10},{6,14},... | collective-permute-start | bytes 196616 | tf_op jit(solution)/shard_map/ppermute | solution.py:21
  22.1 3.0 %collective-permute-done.5.refs_1_ = bf16[4,64,128]{2,1,0:T(8,128)(2,1)S(1)} collective-permute-done((bf16[4,64,128]{2,1,0:T(8,128)(2,1)S(1)}, bf16[4,64,128]{2,1,0:T(8,128)(2,1)S(1)}, u32[]{:S(2)}, u32[]{:S(2)}) %collective-permute-start.5) | collective-permute-done | bytes 65568 | tf_op jit(solution)/shard_map/ppermute | solution.py:21
  25.1 1.3 %collective-permute-start.6 = (bf16[8,64,128]{2,1,0:T(8,128)(2,1)S(1)}, bf16[8,64,128]{2,1,0:T(8,128)(2,1)S(1)}, u32[]{:S(2)}, u32[]{:S(2)}) collective-permute-start(bf16[8,64,128]{2,1,0:T(8,128)(2,1)S(1)} %pad_maximum_fusion), channel_id=1, source_target_pairs={{0,4},{4,0},{8,12},{12,8},{1,5},{5,1},{9,13},{13,9},{2,6},{6,2},{1... | collective-permute-start | bytes 393224 | tf_op jit(solution)/shard_map/ppermute | solution.py:21
  26.5 3.2 %collective-permute-start.1 = (f32[64,128]{1,0:T(8,128)S(1)}, f32[64,128]{1,0:T(8,128)S(1)}, u32[]{:S(2)}, u32[]{:S(2)}) collective-permute-start(f32[64,128]{1,0:T(8,128)S(1)} %get-tuple-element.14), channel_id=1, source_target_pairs={{0,8},{4,12},{8,0},{12,4},{1,9},{5,13},{9,1},{13,5},{2,10},{6,14},... | collective-permute-start | bytes 98312 | tf_op jit(solution)/shard_map/ppermute | solution.py:21
  29.6 1.9 %collective-permute-done.1 = f32[64,128]{1,0:T(8,128)S(1)} collective-permute-done((f32[64,128]{1,0:T(8,128)S(1)}, f32[64,128]{1,0:T(8,128)S(1)}, u32[]{:S(2)}, u32[]{:S(2)}) %collective-permute-start.1) | collective-permute-done | bytes 32800 | tf_op jit(solution)/shard_map/ppermute | solution.py:21
  31.5 0.0 collective-permute-start.2
  31.6 1.2 %collective-permute-done.2 = f32[64,128]{1,0:T(8,128)S(1)} collective-permute-done((f32[64,128]{1,0:T(8,128)S(1)}, f32[64,128]{1,0:T(8,128)S(1)}, u32[]{:S(2)}, u32[]{:S(2)}) %collective-permute-start.2) | collective-permute-done | bytes 32800 | tf_op jit(solution)/shard_map/ppermute | solution.py:21
  32.8 1.4 %collective-permute-start.3 = (f32[64,128]{1,0:T(8,128)S(1)}, f32[64,128]{1,0:T(8,128)S(1)}, u32[]{:S(2)}, u32[]{:S(2)}) collective-permute-start(f32[64,128]{1,0:T(8,128)S(1)} %add.7.factor_a_ref), channel_id=1, source_target_pairs={{0,4},{4,0},{8,12},{12,8},{1,5},{5,1},{9,13},{13,9},{2,6},{6,2},{1... | collective-permute-start | bytes 98312 | tf_op jit(solution)/shard_map/ppermute | solution.py:21
  34.2 2.5 %collective-permute-done.3.factor_b_ref = f32[64,128]{1,0:T(8,128)S(1)} collective-permute-done((f32[64,128]{1,0:T(8,128)S(1)}, f32[64,128]{1,0:T(8,128)S(1)}, u32[]{:S(2)}, u32[]{:S(2)}) %collective-permute-start.3) | collective-permute-done | bytes 32800 | tf_op jit(solution)/shard_map/ppermute | solution.py:21
  36.7 6.1 %inverses.1 = (bf16[2,32,64]{2,1,0:T(8,128)(2,1)S(1)}, bf16[2,128,128]{2,1,0:T(8,128)(2,1)S(1)}) custom-call(f32[64,128]{1,0:T(8,128)S(1)} %add.7.factor_a_ref, f32[64,128]{1,0:T(8,128)S(1)} %collective-permute-done.3.factor_b_ref), custom_call_target="tpu_custom_call" | custom-call | flops 4194304 | bytes 16777216 | tf_op jit(solution)/shard_map/inverses/pallas_call | solution.py:198
  42.7 0.0 collective-permute-done.6.refs_2_
  42.7 0.0 collective-permute-done.4.other_tests_ref
  42.8 1.9 %scores.1 = f32[8,8,128]{2,1,0:T(8,128)S(1)} custom-call(bf16[2,32,64]{2,1,0:T(8,128)(2,1)S(1)} %get-tuple-element.15.grad_ref, bf16[2,128,128]{2,1,0:T(8,128)(2,1)S(1)} %get-tuple-element.16.in_ref, bf16[2048,128]{1,0:T(8,128)(2,1)S(1)} %bitcast.9, bf16[2048,128]{1,0:T(8,128)(2,1)S(1)} %collective-permute-done.4.other_tests_ref, ...), custom_call_target="tpu_custom_call" | custom-call | tf_op jit(solution)/shard_map/scores/pallas_call | solution.py:252
  44.7 11.6 %all_to_all.5.arrived_ref = f32[8,8,128]{2,1,0:T(8,128)S(1)} all-to-all(f32[8,8,128]{2,1,0:T(8,128)S(1)} %scores.1), channel_id=1, replica_groups=mesh['groups'=2,'dp'=4,'feat'=2,'test'=2] {'dp','feat'}, dimensions={0} | all-to-all | bytes 65536 | tf_op jit(solution)/shard_map/all_to_all | solution.py:322
  56.3 0.7 %finish.1 = f32[64,64]{1,0:T(8,128)} custom-call(f32[8,8,128]{2,1,0:T(8,128)S(1)} %all_to_all.5.arrived_ref), custom_call_target="tpu_custom_call" | custom-call | tf_op jit(solution)/shard_map/finish/pallas_call | solution.py:281
  (8 shorter events, 0.0 us)
Async XLA Ops:
  0.0 42.8 %copy-start = (bf16[128,32,64]{0,2,1:T(8,128)(2,1)S(1)}, bf16[128,32,64]{0,2,1:T(8,128)(2,1)}, u32[]{:S(2)}) copy-start(bf16[128,32,64]{0,2,1:T(8,128)(2,1)} %param.13) | copy-start | bytes 1572868
  0.0 16.6 %copy-start.3 = (s32[8]{0:T(128)S(1)}, s32[8]{0:T(128)}, u32[]{:S(2)}) copy-start(s32[8]{0:T(128)} %lengths_ref.3) | copy-start | bytes 100
  0.0 16.6 %copy-start.2 = (s32[8,96]{1,0:T(8,128)S(1)}, s32[8,96]{1,0:T(8,128)}, u32[]{:S(2)}) copy-start(s32[8,96]{1,0:T(8,128)} %mask_ref.1) | copy-start | bytes 9220
  0.0 42.7 %collective-permute-start.4 = (bf16[2048,128]{1,0:T(8,128)(2,1)}, bf16[2048,128]{1,0:T(8,128)(2,1)S(1)}, u32[]{:S(2)}, u32[]{:S(2)}) collective-permute-start(bf16[2048,128]{1,0:T(8,128)(2,1)} %bitcast.8), channel_id=1, source_target_pairs={{0,1},{1,0},{2,3},{3,2},{4,5},{5,4},{6,7},{7,6},{8,9},{9,8},{10,11... | collective-permute-start | bytes 1572872 | tf_op jit(solution)/shard_map/ppermute | solution.py:21
  8.2 8.3 %collective-permute-start = (bf16[768,128]{1,0:T(8,128)(2,1)}, bf16[768,128]{1,0:T(8,128)(2,1)S(1)}, u32[]{:S(2)}, u32[]{:S(2)}) collective-permute-start(bf16[768,128]{1,0:T(8,128)(2,1)} %get-tuple-element.13), channel_id=1, source_target_pairs={{0,2},{2,0},{1,3},{3,1},{4,6},{6,4},{5,7},{7,5},{8,10},{10,8},{9,1... | collective-permute-start | bytes 589832 | tf_op jit(solution)/shard_map/ppermute | solution.py:21
  16.6 1.0 %copy-start.1 = (f32[768,128]{1,0:T(8,128)S(1)}, f32[768,128]{1,0:T(8,128)}, u32[]{:S(2)}) copy-start(f32[768,128]{1,0:T(8,128)} %get-tuple-element.12.own_ref) | copy-start | bytes 1179652
  19.2 5.9 %collective-permute-start.5 = (bf16[4,64,128]{2,1,0:T(8,128)(2,1)S(1)}, bf16[4,64,128]{2,1,0:T(8,128)(2,1)S(1)}, u32[]{:S(2)}, u32[]{:S(2)}) collective-permute-start(bf16[4,64,128]{2,1,0:T(8,128)(2,1)S(1)} %features.1.refs_0_), channel_id=1, source_target_pairs={{0,8},{4,12},{8,0},{12,4},{1,9},{5,13},{9,1},{13,5},{2,10},{6,14},... | collective-permute-start | bytes 196616 | tf_op jit(solution)/shard_map/ppermute | solution.py:21
  25.1 17.6 %collective-permute-start.6 = (bf16[8,64,128]{2,1,0:T(8,128)(2,1)S(1)}, bf16[8,64,128]{2,1,0:T(8,128)(2,1)S(1)}, u32[]{:S(2)}, u32[]{:S(2)}) collective-permute-start(bf16[8,64,128]{2,1,0:T(8,128)(2,1)S(1)} %pad_maximum_fusion), channel_id=1, source_target_pairs={{0,4},{4,0},{8,12},{12,8},{1,5},{5,1},{9,13},{13,9},{2,6},{6,2},{1... | collective-permute-start | bytes 393224 | tf_op jit(solution)/shard_map/ppermute | solution.py:21
  26.5 5.1 %collective-permute-start.1 = (f32[64,128]{1,0:T(8,128)S(1)}, f32[64,128]{1,0:T(8,128)S(1)}, u32[]{:S(2)}, u32[]{:S(2)}) collective-permute-start(f32[64,128]{1,0:T(8,128)S(1)} %get-tuple-element.14), channel_id=1, source_target_pairs={{0,8},{4,12},{8,0},{12,4},{1,9},{5,13},{9,1},{13,5},{2,10},{6,14},... | collective-permute-start | bytes 98312 | tf_op jit(solution)/shard_map/ppermute | solution.py:21
  31.5 1.2 %collective-permute-start.2 = (f32[64,128]{1,0:T(8,128)S(1)}, f32[64,128]{1,0:T(8,128)S(1)}, u32[]{:S(2)}, u32[]{:S(2)}) collective-permute-start(f32[64,128]{1,0:T(8,128)S(1)} %add.6), channel_id=1, source_target_pairs={{0,1},{1,0},{2,3},{3,2},{4,5},{5,4},{6,7},{7,6},{8,9},{9,8},{10,11... | collective-permute-start | bytes 98312 | tf_op jit(solution)/shard_map/ppermute | solution.py:21
  32.8 3.9 %collective-permute-start.3 = (f32[64,128]{1,0:T(8,128)S(1)}, f32[64,128]{1,0:T(8,128)S(1)}, u32[]{:S(2)}, u32[]{:S(2)}) collective-permute-start(f32[64,128]{1,0:T(8,128)S(1)} %add.7.factor_a_ref), channel_id=1, source_target_pairs={{0,4},{4,0},{8,12},{12,8},{1,5},{5,1},{9,13},{13,9},{2,6},{6,2},{1... | collective-permute-start | bytes 98312 | tf_op jit(solution)/shard_map/ppermute | solution.py:21

commit v3 on v2

--- a/solution.py
+++ b/solution.py
@@ -13,7 +13,7 @@
 NT = (((1,), (1,)), ((), ()))
 VMEM = pl.BlockSpec(memory_space=pltpu.VMEM)
 SMEM = pl.BlockSpec(memory_space=pltpu.SMEM)
-ANY = pl.BlockSpec(memory_space=pl.ANY)
+HBM = pl.BlockSpec(memory_space=pltpu.HBM)
 
 
 def xor_permute(values, axis, mask):
@@ -71,7 +71,7 @@
             jax.ShapeDtypeStruct((tokens, 2 * rank), f32),
             jax.ShapeDtypeStruct((tokens, 2 * rank), bf16),
         ),
-        in_specs=[ANY] * 4,
+        in_specs=[HBM] * 4,
         out_specs=(VMEM, VMEM),
         scratch_shapes=[
             pltpu.VMEM(x.shape, bf16),
@@ -164,9 +164,65 @@
     return high, (values - high.astype(f32)).astype(bf16)
 
 
-def inverses_body(total_tokens, factor_a_ref, factor_b_ref, grad_ref, in_ref, inverse_buf):
+def invert(packed):
+    rank, width = packed.shape
+    run = 8
+    blocks = [packed[run * r : run * (r + 1), :] for r in range(rank // run)]
+    lane = lax.broadcasted_iota(jnp.int32, (run, width), 1)
+    sub = lax.broadcasted_iota(jnp.int32, (run, width), 0)
+    column = jnp.where(lane < rank, lane, lane - rank)
+    base = jnp.where(lane < rank, 0, rank)
+
+    def pick(values, at):
+        return jnp.take_along_axis(values, base + at, axis=1)
+
+    for p in range(len(blocks)):
+        first = run * p
+        rows = [jnp.broadcast_to(blocks[p][i : i + 1, :], (run, width)) for i in range(run)]
+        entry = [[None] * run for _ in range(run)]
+        for i in range(run):
+            for j in range(i, run):
+                entry[i][j] = entry[j][i] = pick(rows[i], first + j)
+        columns = [[pick(block, first + j) for j in range(run)] for block in blocks]
+        for j in range(0, run, 2):
+            a, b, c = entry[j][j], entry[j][j + 1], entry[j + 1][j + 1]
+            scale = 1.0 / (a * c - b * b)
+            ia, ib, ic = c * scale, -(b * scale), a * scale
+            at_first, at_second = column == first + j, column == first + j + 1
+            low = jnp.where(at_first, ia, jnp.where(at_second, ib, ia * rows[j] + ib * rows[j + 1]))
+            high = jnp.where(at_first, ib, jnp.where(at_second, ic, ib * rows[j] + ic * rows[j + 1]))
+            later = range(j + 2, run)
+            low_entry = {k: ia * entry[j][k] + ib * entry[j + 1][k] for k in later}
+            high_entry = {k: ib * entry[j][k] + ic * entry[j + 1][k] for k in later}
+            for i in range(run):
+                if i in (j, j + 1):
+                    continue
+                from_low, from_high = entry[i][j], entry[i][j + 1]
+                rows[i] = jnp.where(at_first | at_second, 0.0, rows[i]) - (from_low * low + from_high * high)
+                for k in later:
+                    if j + 1 < i and k < i:
+                        entry[i][k] = entry[k][i]
+                    else:
+                        entry[i][k] = entry[i][k] - (from_low * low_entry[k] + from_high * high_entry[k])
+            rows[j], rows[j + 1] = low, high
+            for k in later:
+                entry[j][k], entry[j + 1][k] = low_entry[k], high_entry[k]
+        pivots = (column >= first) & (column < first + run)
+        for r in range(len(blocks)):
+            if r != p:
+                terms = [columns[r][i] * rows[i] for i in range(run)]
+                while len(terms) > 1:
+                    terms = [terms[i] + terms[i + 1] for i in range(0, len(terms), 2)]
+                blocks[r] = jnp.where(pivots, 0.0, blocks[r]) - terms[0]
+        turned = rows[0]
+        for i in range(1, run):
+            turned = jnp.where(sub == i, rows[i], turned)
+        blocks[p] = turned
+    return jnp.concatenate(blocks, axis=0)
+
+
+def inverses_body(total_tokens, factor_a_ref, factor_b_ref, grad_ref, in_ref):
     rank = factor_a_ref.shape[0]
-    own_rows = grad_ref.shape[1]
     lane = lax.broadcasted_iota(jnp.int32, (rank, 2 * rank), 1)
     sub = lax.broadcasted_iota(jnp.int32, (rank, 2 * rank), 0)
     left = lane < rank
@@ -178,115 +234,164 @@
     trace_grad = jnp.sum(jnp.where(left[:1], 0.0, on_diagonal), axis=1, keepdims=True)
     damping = 0.1 * jnp.where(left[:1], trace_in, trace_grad) / rank + 1e-06
     packed = packed + jnp.where(diagonal, damping, 0.0)
-    for k in range(rank):
-        pivot_column = jnp.where(left, packed[:, k : k + 1], packed[:, rank + k : rank + k + 1])
-        row = packed[k : k + 1, :]
-        inverse = 1.0 / pivot_column[k : k + 1, :]
-        at_pivot = column[:1] == k
-        row = jnp.where(at_pivot, inverse, row * inverse)
-        packed = jnp.where(sub == k, row, jnp.where(at_pivot, 0.0, packed) - pivot_column * row)
-    inverse_buf[...] = pltpu.roll(packed, rank, 1)
-    first_row = pl.multiple_of(lax.axis_index("feat") * own_rows, 8)
-    grad_ref[0], grad_ref[1] = split(inverse_buf[pl.ds(first_row, own_rows), :][:, :rank])
+    packed = invert(packed)
     twice = pltpu.roll(packed, rank, 1)
+    grad_ref[0], grad_ref[1] = split(twice[:, :rank])
     in_ref[0, :rank, :], in_ref[1, :rank, :] = split(jnp.where(left, packed, 0.0))
     in_ref[0, rank:, :], in_ref[1, rank:, :] = split(jnp.where(left, 0.0, twice))
 
 
-def inverses(total_tokens, factor_a, factor_b, own_rows):
+def inverses(total_tokens, factor_a, factor_b):
     rank, width = factor_a.shape
     return pl.pallas_call(
         functools.partial(inverses_body, total_tokens),
         out_shape=(
-            jax.ShapeDtypeStruct((2, own_rows, rank), bf16),
+            jax.ShapeDtypeStruct((2, rank, rank), bf16),
             jax.ShapeDtypeStruct((2, width, width), bf16),
         ),
         in_specs=[VMEM, VMEM],
         out_specs=(VMEM, VMEM),
-        scratch_shapes=[pltpu.VMEM((rank, width), f32)],
         compiler_params=pltpu.CompilerParams(vmem_limit_bytes=4 * MIB),
-        cost_estimate=pl.CostEstimate(flops=4 * MIB, bytes_accessed=16 * MIB, transcendentals=0),
+        cost_estimate=pl.CostEstimate(flops=0, bytes_accessed=0, transcendentals=0),
         name="inverses",
     )(factor_a, factor_b)
 
 
-def scores_body(dp_masks, grad_ref, in_ref, own_tests_ref, other_tests_ref, *refs):
-    feats_refs, (out_ref, solved_buf, line_buf) = refs[:-3], refs[-3:]
+def pack_body(tests_ref, *out_refs):
+    feat_count = len(out_refs)
+    rows, width = tests_ref.shape
+    fold, block = rows // feat_count, width // feat_count
+    feat = lax.axis_index("feat")
+    pieces = []
+    for target in range(feat_count):
+        columns = slice(target * block, (target + 1) * block)
+        parts = [tests_ref[j * fold : (j + 1) * fold, columns] for j in range(feat_count)]
+        pieces.append(jnp.concatenate(parts, axis=1))
+    for mask, out_ref in enumerate(out_refs):
+        piece = pieces[0]
+        for target in range(1, feat_count):
+            piece = jnp.where((feat ^ mask) == target, pieces[target], piece)
+        out_ref[...] = piece
+
+
+def pack(tests):
+    rows, width = tests.shape
     feat_count = lax.axis_size("feat")
-    dp = lax.axis_index("dp")
-    own_rows, rank = grad_ref.shape[1:]
+    return pl.pallas_call(
+        pack_body,
+        out_shape=[jax.ShapeDtypeStruct((rows // feat_count, width), bf16)] * feat_count,
+        in_specs=[VMEM],
+        out_specs=[VMEM] * feat_count,
+        compiler_params=pltpu.CompilerParams(vmem_limit_bytes=8 * MIB),
+        cost_estimate=pl.CostEstimate(flops=4 * MIB, bytes_accessed=4 * MIB, transcendentals=0),
+        name="pack",
+    )(tests)
+
+
+def scores_body(blocks, grad_ref, in_ref, *refs):
+    feat_count = lax.axis_size("feat")
+    feat = lax.axis_index("feat")
+    pieces, refs = refs[: 4 * feat_count], refs[4 * feat_count :]
+    feats_refs, out_refs, (solved_buf, line_buf) = refs[:blocks], refs[blocks : 2 * blocks], refs[2 * blocks :]
+    rank = grad_ref.shape[1]
     pairs = [ref[i] for ref in feats_refs for i in range(ref.shape[0])]
     count = len(pairs)
-    half = count // len(dp_masks)
+    half = count // blocks
+    fold, width = pieces[0].shape
+    block = width // feat_count
     dot = functools.partial(jnp.dot, preferred_element_type=f32)
     for at in range(count):
         high, low = split(dot(grad_ref[0], pairs[at]) + dot(grad_ref[1], pairs[at]))
-        solved_buf[at * own_rows : (at + 1) * own_rows, :] = dot(high, in_ref[0]) + dot(high, in_ref[1]) + dot(low, in_ref[0])
+        solved_buf[at * rank : (at + 1) * rank, :] = dot(high, in_ref[0]) + dot(high, in_ref[1]) + dot(low, in_ref[0])
     lane = lax.broadcasted_iota(jnp.int32, (count, 2 * rank), 1)
-    for g in range(0, own_rows, 2):
-        low = solved_buf[pl.ds(g, count, stride=own_rows), :]
-        high = solved_buf[pl.ds(g + 1, count, stride=own_rows), :]
+    for g in range(0, rank, 2):
+        low = solved_buf[pl.ds(g, count, stride=rank), :]
+        high = solved_buf[pl.ds(g + 1, count, stride=rank), :]
         first = jnp.where(lane < rank, low, pltpu.roll(high, rank, 1))
         second = jnp.where(lane < rank, pltpu.roll(low, rank, 1), high)
-        line_buf[:, g * rank : (g + 2) * rank] = jnp.concatenate([first, second], axis=0).astype(bf16)
-    lines = line_buf[...]
-    own = dot(lines, own_tests_ref[...])
-    other = dot(lines, other_tests_ref[...])
+        line = jnp.concatenate([first, second], axis=0).astype(bf16)
+        step = min(fold, 2 * rank)
+        for begin in range(0, 2 * rank, step):
+            at = (g * rank + begin) // fold
+            to = (g * rank + begin) % fold
+            line_buf[at // feat_count, at % feat_count, :, to : to + step] = line[:, begin : begin + step]
+    lines = []
+    for mask in range(feat_count):
+        owner = feat ^ mask
+        lines.append(jnp.concatenate([line_buf[owner, j] for j in range(feat_count)], axis=0))
     is_first = lax.axis_index("test") == 0
-    parts = (jnp.where(is_first, own, other), jnp.where(is_first, other, own))
-    block = own.shape[1] // feat_count
-    for target in range(feat_count):
-        columns = slice(target * block, (target + 1) * block)
-        both = jnp.concatenate([part[:, columns] for part in parts], axis=1)
-        for at, mask in enumerate(dp_masks):
-            place = (dp ^ mask) * feat_count + target
-            out_ref[place, :half, :] = both[at * half : (at + 1) * half, :]
-            out_ref[place, half:, :] = both[count + at * half : count + (at + 1) * half, :]
-
-
-def partial_scores(dp_masks, grad, in_pair, own_tests, other_tests, feats):
+    odd = lax.rem(lax.axis_index("dp"), 2)
+    for dp_bit in range(2):
+        parts = []
+        for test_bit in range(2):
+            at = (2 * dp_bit + test_bit) * feat_count
+            total = dot(lines[0], pieces[at][...])
+            for mask in range(1, feat_count):
+                total = total + dot(lines[mask], pieces[at + mask][...])
+            part = total[: 2 * count, :block]
+            for j in range(1, feat_count):
+                part = part + total[2 * count * j : 2 * count * (j + 1), block * j : block * (j + 1)]
+            parts.append(part)
+        both = jnp.concatenate(
+            [jnp.where(is_first, parts[0], parts[1]), jnp.where(is_first, parts[1], parts[0])], axis=1
+        )
+        for at, out_ref in enumerate(out_refs):
+            out_ref[odd ^ dp_bit, :half, :] = both[at * half : (at + 1) * half, :]
+            out_ref[odd ^ dp_bit, half:, :] = both[count + at * half : count + (at + 1) * half, :]
+
+
+def scores_of(grad, in_pair, pieces, feats):
     feat_count = lax.axis_size("feat")
-    own_rows, rank = grad.shape[1:]
-    count = sum(f.shape[0] for f in feats)
-    rows = 2 * count // len(dp_masks)
-    return pl.pallas_call(
-        functools.partial(scores_body, dp_masks),
-        out_shape=jax.ShapeDtypeStruct((len(dp_masks) * feat_count, rows, 2 * own_tests.shape[1] // feat_count), f32),
-        in_specs=[VMEM] * (4 + len(feats)),
-        out_specs=VMEM,
+    rank = grad.shape[1]
+    fold, width = pieces[0].shape
+    half = feats[0].shape[0]
+    count = half * len(feats)
+    return pl.pallas_call(
+        functools.partial(scores_body, len(feats)),
+        out_shape=[jax.ShapeDtypeStruct((2, 2 * half, 2 * width // feat_count), f32)] * len(feats),
+        in_specs=[VMEM] * (2 + len(pieces) + len(feats)),
+        out_specs=[VMEM] * len(feats),
         scratch_shapes=[
-            pltpu.VMEM((count * own_rows, 2 * rank), f32),
-            pltpu.VMEM((2 * count, own_rows * rank), bf16),
+            pltpu.VMEM((count * rank, 2 * rank), f32),
+            pltpu.VMEM((feat_count, feat_count, 2 * count, fold), bf16),
         ],
         compiler_params=pltpu.CompilerParams(vmem_limit_bytes=16 * MIB),
         name="scores",
-    )(grad, in_pair, own_tests, other_tests, *feats)
-
-
-def finish_body(feat_count, arrived_ref, out_ref):
-    blocks, examples, width = arrived_ref.shape
-    dp_count = blocks // feat_count
+    )(grad, in_pair, *pieces, *feats)
+
+
+def finish_body(*refs):
+    block_refs, out_ref = refs[:-1], refs[-1]
+    count = len(block_refs)
+    _, examples, width = block_refs[0].shape
     half = width // 2
-    for dp in range(dp_count):
-        total = arrived_ref[dp * feat_count]
-        for feat in range(1, feat_count):
-            total = total + arrived_ref[dp * feat_count + feat]
-        for test in range(2):
-            out_ref[pl.ds(2 * dp + test, examples, stride=2 * dp_count), :] = total[:, test * half : (test + 1) * half]
-
-
-def finish(arrived, feat_count):
-    blocks, examples, width = arrived.shape
-    queries = 2 * blocks // feat_count
+    own = lax.div(lax.axis_index("dp"), 2)
+    for place in range(count):
+        for odd in range(2):
+            block = block_refs[0][odd]
+            for mask in range(1, count):
+                block = jnp.where((own ^ mask) == place, block_refs[mask][odd], block)
+            for test in range(2):
+                rows = pl.ds(4 * place + 2 * odd + test, examples, stride=4 * count)
+                out_ref[rows, :] = block[:, test * half : (test + 1) * half]
+
+
+def finish(blocks):
+    _, examples, width = blocks[0].shape
+    queries = 4 * len(blocks)
     out = pl.pallas_call(
-        functools.partial(finish_body, feat_count),
+        finish_body,
         out_shape=jax.ShapeDtypeStruct((examples * queries, width // 2), f32),
-        in_specs=[VMEM],
+        in_specs=[VMEM] * len(blocks),
         out_specs=VMEM,
         compiler_params=pltpu.CompilerParams(vmem_limit_bytes=4 * MIB),
         name="finish",
-    )(arrived)
+    )(*blocks)
     return out.reshape(examples, queries, width // 2)
+
+
+def after(values, *others):
+    return lax.optimization_barrier((values, *others))[0]
 
 
 def on_device(train_inputs, train_grads, proj_in, proj_out, lengths, loss_mask, test_feats):
@@ -301,26 +406,32 @@
     g = train_grads.reshape(tokens, out_width)
     own, sent = project(x, g, proj_in.T, proj_out.T, tokens // 3)
     received = [xor_permute(sent, "feat", mask) for mask in range(1, feat_count)]
-    own_tests = test_feats.transpose(1, 2, 0).reshape(own_rows * test_feats.shape[2], test_feats.shape[0])
-    other_tests = xor_permute(own_tests, "test", 1)
+    tests = test_feats.transpose(1, 2, 0).reshape(own_rows * test_feats.shape[2], test_feats.shape[0])
+    cut = pack(after(tests, sent))
+    near = [cut[0]] + [xor_permute(cut[mask], "feat", mask) for mask in range(1, feat_count)]
     factor, rounded, turned = factors(lengths, loss_mask, own, received)
     feats = [features_of(lengths, rounded, turned)]
-    dp_masks = [0]
-    steps = [("dp", m) for m in reversed(masks_of(dp_count))]
-    steps = steps[:-1] + [("test", 1)] + steps[-1:]
-    for at, (axis, mask) in enumerate(steps):
-        other = xor_permute(factor, axis, mask)
-        if at < len(steps) - 1:
-            factor = factor + other
-        if axis == "dp":
-            moved = feats[0] if len(feats) == 1 else jnp.concatenate(feats, axis=0)
-            feats = feats + [xor_permute(moved, axis, mask)]
-            dp_masks = dp_masks + [d ^ mask for d in dp_masks]
-    total_tokens = float(tokens * dp_count * test_count)
-    grad, in_pair = inverses(total_tokens, factor, other, own_rows)
-    shares = partial_scores(dp_masks, grad, in_pair, own_tests, other_tests, feats)
-    arrived = lax.all_to_all(shares, ("dp", "feat"), split_axis=0, concat_axis=0)
-    return finish(arrived, feat_count)
+    even_masks = range(2, dp_count, 2)
+    steps = [("test", 1)] + [("dp", m) for m in masks_of(dp_count)]
+    sums = [factor]
+    for axis, mask in steps:
+        if len(sums) == len(steps):
+            sums[-1] = after(sums[-1], feats[0])
+        other = xor_permute(sums[-1], axis, mask)
+        sums.append(sums[-1] + other)
+    factor = sums[-2]
+    far = [xor_permute(near[0], "dp", 1)]
+    if feat_count > 1:
+        far += [xor_permute(piece, "dp", 1) for piece in after(tuple(near[1:]), sums[1])]
+    shared = after(tuple(near), sums[2])
+    pieces = near + [xor_permute(piece, "test", 1) for piece in shared]
+    shared = after(tuple(far), other)
+    pieces += far + [xor_permute(piece, "test", 1) for piece in shared]
+    feats += [xor_permute(feats[0], "dp", mask) for mask in even_masks]
+    grad, in_pair = inverses(float(tokens * dp_count * test_count), factor, other)
+    blocks = scores_of(grad, in_pair, pieces, feats)
+    blocks = [blocks[0]] + [xor_permute(blocks[at + 1], "dp", mask) for at, mask in enumerate(even_masks)]
+    return finish(blocks)
 
 
 def solution(mesh):

time: 57.2 us -> 57.7 us (level)
  waiting for transfers between devices: 14.3 us -> 27.1 us
  blocking collectives: 11.6 us -> 0 us
  Pallas kernels: 18 us -> 14.6 us
  starting transfers between devices: 11.9 us -> 14.7 us
    ppermute x7 -> x13, waiting for transfers between devices: 14.3 us -> 27.1 us  [xor_permute(): return lax.ppermute(values, axis, [(i, i ^ mask) for i in range(size)])]
    all_to_all x1 -> x0, blocking collectives: 11.6 us -> none  [on_device(): lax.all_to_all(shares, ('dp', 'feat'), split_axis=0, concat_axis=0)]
    pallas_call x1, Pallas kernels: 6.05 us -> 2.81 us  [inverses(): pl.pallas_call(functools.partial(inverses_body, total_tokens), out_shape=...]
    ppermute x7 -> x13, starting transfers between devices: 11.9 us -> 14.7 us  [xor_permute(): return lax.ppermute(values, axis, [(i, i ^ mask) for i in range(size)])]
    pallas_call x2 -> x3, Pallas kernels: 2.63 us -> 2.42 us  [the longest x1 1.52 us: scores_of(): pl.pallas_call(functools.partial(scores_body, len(feats)), out_shape=[jax...]
  transfers between devices with their start and end apart: 7 -> 13, of which waited for: 5 -> 5; matrix products, arithmetic and copies ran while one was open for 0% -> 0% of each run, Pallas kernels for 27% -> 8%
where the time goes in v3:
time: 57.7 us; the launch traced here: 57.5 us
  waiting for transfers between devices  27.1 us (47%)
  starting transfers between devices  14.7 us (25%)
  Pallas kernels  14.6 us (25%)
  local copies, waits for them, and re-layouts  1.01 us (2%)
    ppermute x13, waiting for transfers between devices, xor_permute(): return lax.ppermute(values, axis, [(i, i ^ mask) for i in range(size)])  27.1 us
    ppermute x13, starting transfers between devices, xor_permute(): return lax.ppermute(values, axis, [(i, i ^ mask) for i in range(size)])  14.7 us
    pallas_call x1, Pallas kernels, project(): pl.pallas_call(functools.partial(project_body, rows), out_shape=(jax.Shap...  7.77 us
    pallas_call x1, Pallas kernels, inverses(): pl.pallas_call(functools.partial(inverses_body, total_tokens), out_shape=...  2.81 us
    pallas_call x1, Pallas kernels, scores_of(): pl.pallas_call(functools.partial(scores_body, len(feats)), out_shape=[jax...  1.52 us
  transfers between devices with their start and end apart: 13, of which 5 were waited for; matrix products, arithmetic and copies ran while one was open for 0% of the time, Pallas kernels for 8%

profile of v3, /device:TPU:0, one launch (start us, length us, event | category | flops | bytes accessed | tf_op | source)
XLA Modules:
  0.0 57.5 jit_solution(3191156617780521756)
XLA Ops:
  0.0 7.8 %project.1 = (f32[768,128]{1,0:T(8,128)}, bf16[768,128]{1,0:T(8,128)(2,1)}) custom-call(bf16[768,2048]{1,0:T(8,128)(2,1)} %bitcast.10, bf16[768,7168]{1,0:T(8,128)(2,1)} %bitcast.9, bf16[64,2048]{1,0:T(8,128)(2,1)} %bitcast.12, bf16[64,7168]{1,0:T(8,128)(2,1)} %bitcast.11), custom_call_target="tpu_custom_call" | custom-call | flops 905969664 | bytes 15335424 | tf_op jit(solution)/shard_map/project/pallas_call | solution.py:68
  7.8 0.2 pack.1
  8.0 3.0 %collective-permute-start.4 = (bf16[1024,128]{1,0:T(8,128)(2,1)S(1)}, bf16[1024,128]{1,0:T(8,128)(2,1)S(1)}, u32[]{:S(2)}, u32[]{:S(2)}) collective-permute-start(bf16[1024,128]{1,0:T(8,128)(2,1)S(1)} %get-tuple-element.33), channel_id=1, source_target_pairs={{0,2},{2,0},{1,3},{3,1},{4,6},{6,4},{5,7},{7,5},{8,10},{10,8},{9,1... | collective-permute-start | bytes 786440 | tf_op jit(solution)/shard_map/ppermute | solution.py:21
  11.0 0.1 collective-permute-start
  11.1 10.4 %collective-permute-done.refs_0_ = bf16[768,128]{1,0:T(8,128)(2,1)S(1)} collective-permute-done((bf16[768,128]{1,0:T(8,128)(2,1)}, bf16[768,128]{1,0:T(8,128)(2,1)S(1)}, u32[]{:S(2)}, u32[]{:S(2)}) %collective-permute-start) | collective-permute-done | bytes 196640 | tf_op jit(solution)/shard_map/ppermute | solution.py:21
  21.5 1.0 %copy-done.1 = f32[768,128]{1,0:T(8,128)S(1)} copy-done((f32[768,128]{1,0:T(8,128)S(1)}, f32[768,128]{1,0:T(8,128)}, u32[]{:S(2)}) %copy-start.1) | copy-done | bytes 393240
  22.5 0.8 %factors.1 = (f32[64,128]{1,0:T(8,128)S(1)}, bf16[768,128]{1,0:T(8,128)(2,1)S(1)}, bf16[8,128,96]{2,1,0:T(8,128)(2,1)S(1)}) custom-call(s32[8]{0:T(128)S(1)} %copy-done.3, s32[8,96]{1,0:T(8,128)S(1)} %copy-done.2, f32[768,128]{1,0:T(8,128)S(1)} %copy-done.1, bf16[768,128]{1,0:T(8,128)(2,1)S(1)} %collective-permute-done.refs_0_), custom_call_target="tpu_custom_call" | custom-call | tf_op jit(solution)/shard_map/factors/pallas_call | solution.py:119
  23.4 0.1 collective-permute-start.1
  23.5 1.9 %collective-permute-start.7 = (bf16[1024,128]{1,0:T(8,128)(2,1)S(1)}, bf16[1024,128]{1,0:T(8,128)(2,1)S(1)}, u32[]{:S(2)}, u32[]{:S(2)}) collective-permute-start(bf16[1024,128]{1,0:T(8,128)(2,1)S(1)} %get-tuple-element.34.refs_0_), channel_id=1, source_target_pairs={{0,4},{4,0},{8,12},{12,8},{1,5},{5,1},{9,13},{13,9},{2,6},{6,2},{1... | collective-permute-start | bytes 786440 | tf_op jit(solution)/shard_map/ppermute | solution.py:21
  25.4 1.2 %collective-permute-start.8 = (bf16[1024,128]{1,0:T(8,128)(2,1)S(1)}, bf16[1024,128]{1,0:T(8,128)(2,1)S(1)}, u32[]{:S(2)}, u32[]{:S(2)}) collective-permute-start(bf16[1024,128]{1,0:T(8,128)(2,1)S(1)} %collective-permute-done.4.refs_1_), channel_id=1, source_target_pairs={{0,4},{4,0},{8,12},{12,8},{1,5},{5,1},{9,13},{13,9},{2,6},{6,2},{1... | collective-permute-start | bytes 786440 | tf_op jit(solution)/shard_map/ppermute | solution.py:21
  26.6 0.9 %collective-permute-start.2 = (f32[64,128]{1,0:T(8,128)S(1)}, f32[64,128]{1,0:T(8,128)S(1)}, u32[]{:S(2)}, u32[]{:S(2)}) collective-permute-start(f32[64,128]{1,0:T(8,128)S(1)} %add.6), channel_id=1, source_target_pairs={{0,4},{4,0},{8,12},{12,8},{1,5},{5,1},{9,13},{13,9},{2,6},{6,2},{1... | collective-permute-start | bytes 98312 | tf_op jit(solution)/shard_map/ppermute | solution.py:21
  27.5 0.8 %features.1.refs_8_ = bf16[4,64,128]{2,1,0:T(8,128)(2,1)S(1)} custom-call(s32[8]{0:T(128)S(1)} %copy-done.3, bf16[768,128]{1,0:T(8,128)(2,1)S(1)} %get-tuple-element.26.rounded_ref, bf16[8,128,96]{2,1,0:T(8,128)(2,1)S(1)} %get-tuple-element.27.turned_ref), custom_call_target="tpu_custom_call" | custom-call | flops 25165824 | bytes 8388608 | tf_op jit(solution)/shard_map/features/pallas_call | solution.py:151
  28.3 10.3 %collective-permute-done.2 = f32[64,128]{1,0:T(8,128)S(1)} collective-permute-done((f32[64,128]{1,0:T(8,128)S(1)}, f32[64,128]{1,0:T(8,128)S(1)}, u32[]{:S(2)}, u32[]{:S(2)}) %collective-permute-start.2) | collective-permute-done | bytes 32800 | tf_op jit(solution)/shard_map/ppermute | solution.py:21
  38.6 2.8 %collective-permute-start.3 = (f32[64,128]{1,0:T(8,128)S(1)}, f32[64,128]{1,0:T(8,128)S(1)}, u32[]{:S(2)}, u32[]{:S(2)}) collective-permute-start(f32[64,128]{1,0:T(8,128)S(1)} %add.7.factor_a_ref), channel_id=1, source_target_pairs={{0,8},{4,12},{8,0},{12,4},{1,9},{5,13},{9,1},{13,5},{2,10},{6,14},... | collective-permute-start | bytes 98312 | tf_op jit(solution)/shard_map/ppermute | solution.py:21
  41.4 0.5 collective-permute-start.6
  41.9 1.8 %collective-permute-done.3.factor_b_ref = f32[64,128]{1,0:T(8,128)S(1)} collective-permute-done((f32[64,128]{1,0:T(8,128)S(1)}, f32[64,128]{1,0:T(8,128)S(1)}, u32[]{:S(2)}, u32[]{:S(2)}) %collective-permute-start.3) | collective-permute-done | bytes 32800 | tf_op jit(solution)/shard_map/ppermute | solution.py:21
  43.6 0.5 collective-permute-start.10
  44.2 2.6 %collective-permute-start.11 = (bf16[4,64,128]{2,1,0:T(8,128)(2,1)S(1)}, bf16[4,64,128]{2,1,0:T(8,128)(2,1)S(1)}, u32[]{:S(2)}, u32[]{:S(2)}) collective-permute-start(bf16[4,64,128]{2,1,0:T(8,128)(2,1)S(1)} %features.1.refs_8_), channel_id=1, source_target_pairs={{0,8},{4,12},{8,0},{12,4},{1,9},{5,13},{9,1},{13,5},{2,10},{6,14},... | collective-permute-start | bytes 196616 | tf_op jit(solution)/shard_map/ppermute | solution.py:21
  46.7 2.8 %inverses.1 = (bf16[2,64,64]{2,1,0:T(8,128)(2,1)S(1)}, bf16[2,128,128]{2,1,0:T(8,128)(2,1)S(1)}) custom-call(f32[64,128]{1,0:T(8,128)S(1)} %add.7.factor_a_ref, f32[64,128]{1,0:T(8,128)S(1)} %collective-permute-done.3.factor_b_ref), custom_call_target="tpu_custom_call" | custom-call | tf_op jit(solution)/shard_map/inverses/pallas_call | solution.py:246
  49.5 1.2 %collective-permute-done.11.refs_9_ = bf16[4,64,128]{2,1,0:T(8,128)(2,1)S(1)} collective-permute-done((bf16[4,64,128]{2,1,0:T(8,128)(2,1)S(1)}, bf16[4,64,128]{2,1,0:T(8,128)(2,1)S(1)}, u32[]{:S(2)}, u32[]{:S(2)}) %collective-permute-start.11) | collective-permute-done | bytes 65568 | tf_op jit(solution)/shard_map/ppermute | solution.py:21
  50.7 1.5 %scores.1 = (f32[2,8,128]{2,1,0:T(8,128)S(1)}, f32[2,8,128]{2,1,0:T(8,128)S(1)}) custom-call(bf16[2,64,64]{2,1,0:T(8,128)(2,1)S(1)} %get-tuple-element.29.grad_ref, bf16[2,128,128]{2,1,0:T(8,128)(2,1)S(1)} %get-tuple-element.30.in_ref, bf16[1024,128]{1,0:T(8,128)(2,1)S(1)} %get-tuple-element.34.refs_0_, ...), custom_call_target="tpu_custom_call" | custom-call | tf_op jit(solution)/shard_map/scores/pallas_call | solution.py:349
  52.3 1.2 %collective-permute-start.12 = (f32[2,8,128]{2,1,0:T(8,128)S(1)}, f32[2,8,128]{2,1,0:T(8,128)S(1)}, u32[]{:S(2)}, u32[]{:S(2)}) collective-permute-start(f32[2,8,128]{2,1,0:T(8,128)S(1)} %get-tuple-element.40), channel_id=1, source_target_pairs={{0,8},{4,12},{8,0},{12,4},{1,9},{5,13},{9,1},{13,5},{2,10},{6,14},... | collective-permute-start | bytes 24584 | tf_op jit(solution)/shard_map/ppermute | solution.py:21
  53.4 3.4 %collective-permute-done.12.refs_1_ = f32[2,8,128]{2,1,0:T(8,128)S(1)} collective-permute-done((f32[2,8,128]{2,1,0:T(8,128)S(1)}, f32[2,8,128]{2,1,0:T(8,128)S(1)}, u32[]{:S(2)}, u32[]{:S(2)}) %collective-permute-start.12) | collective-permute-done | bytes 8224 | tf_op jit(solution)/shard_map/ppermute | solution.py:21
  56.8 0.7 %finish.1 = f32[64,64]{1,0:T(8,128)} custom-call(f32[2,8,128]{2,1,0:T(8,128)S(1)} %get-tuple-element.39.refs_0_, f32[2,8,128]{2,1,0:T(8,128)S(1)} %collective-permute-done.12.refs_1_), custom_call_target="tpu_custom_call" | custom-call | tf_op jit(solution)/shard_map/finish/pallas_call | solution.py:382
  (19 shorter events, 0.0 us)
Async XLA Ops:
  0.0 7.8 %copy-start = (bf16[128,32,64]{0,2,1:T(8,128)(2,1)S(1)}, bf16[128,32,64]{0,2,1:T(8,128)(2,1)}, u32[]{:S(2)}) copy-start(bf16[128,32,64]{0,2,1:T(8,128)(2,1)} %param.13) | copy-start | bytes 1572868
  0.0 21.5 %copy-start.3 = (s32[8]{0:T(128)S(1)}, s32[8]{0:T(128)}, u32[]{:S(2)}) copy-start(s32[8]{0:T(128)} %lengths_ref.3) | copy-start | bytes 100
  0.0 21.5 %copy-start.2 = (s32[8,96]{1,0:T(8,128)S(1)}, s32[8,96]{1,0:T(8,128)}, u32[]{:S(2)}) copy-start(s32[8,96]{1,0:T(8,128)} %mask_ref.1) | copy-start | bytes 9220
  8.0 17.4 %collective-permute-start.4 = (bf16[1024,128]{1,0:T(8,128)(2,1)S(1)}, bf16[1024,128]{1,0:T(8,128)(2,1)S(1)}, u32[]{:S(2)}, u32[]{:S(2)}) collective-permute-start(bf16[1024,128]{1,0:T(8,128)(2,1)S(1)} %get-tuple-element.33), channel_id=1, source_target_pairs={{0,2},{2,0},{1,3},{3,1},{4,6},{6,4},{5,7},{7,5},{8,10},{10,8},{9,1... | collective-permute-start | bytes 786440 | tf_op jit(solution)/shard_map/ppermute | solution.py:21
  11.0 10.5 %collective-permute-start = (bf16[768,128]{1,0:T(8,128)(2,1)}, bf16[768,128]{1,0:T(8,128)(2,1)S(1)}, u32[]{:S(2)}, u32[]{:S(2)}) collective-permute-start(bf16[768,128]{1,0:T(8,128)(2,1)} %get-tuple-element.24), channel_id=1, source_target_pairs={{0,2},{2,0},{1,3},{3,1},{4,6},{6,4},{5,7},{7,5},{8,10},{10,8},{9,1... | collective-permute-start | bytes 589832 | tf_op jit(solution)/shard_map/ppermute | solution.py:21
  21.5 1.0 %copy-start.1 = (f32[768,128]{1,0:T(8,128)S(1)}, f32[768,128]{1,0:T(8,128)}, u32[]{:S(2)}) copy-start(f32[768,128]{1,0:T(8,128)} %get-tuple-element.23.own_ref) | copy-start | bytes 1179652
  23.4 2.0 %collective-permute-start.1 = (f32[64,128]{1,0:T(8,128)S(1)}, f32[64,128]{1,0:T(8,128)S(1)}, u32[]{:S(2)}, u32[]{:S(2)}) collective-permute-start(f32[64,128]{1,0:T(8,128)S(1)} %get-tuple-element.25), channel_id=1, source_target_pairs={{0,1},{1,0},{2,3},{3,2},{4,5},{5,4},{6,7},{7,6},{8,9},{9,8},{10,11... | collective-permute-start | bytes 98312 | tf_op jit(solution)/shard_map/ppermute | solution.py:21
  23.5 18.4 %collective-permute-start.7 = (bf16[1024,128]{1,0:T(8,128)(2,1)S(1)}, bf16[1024,128]{1,0:T(8,128)(2,1)S(1)}, u32[]{:S(2)}, u32[]{:S(2)}) collective-permute-start(bf16[1024,128]{1,0:T(8,128)(2,1)S(1)} %get-tuple-element.34.refs_0_), channel_id=1, source_target_pairs={{0,4},{4,0},{8,12},{12,8},{1,5},{5,1},{9,13},{13,9},{2,6},{6,2},{1... | collective-permute-start | bytes 786440 | tf_op jit(solution)/shard_map/ppermute | solution.py:21
  25.4 18.3 %collective-permute-start.8 = (bf16[1024,128]{1,0:T(8,128)(2,1)S(1)}, bf16[1024,128]{1,0:T(8,128)(2,1)S(1)}, u32[]{:S(2)}, u32[]{:S(2)}) collective-permute-start(bf16[1024,128]{1,0:T(8,128)(2,1)S(1)} %collective-permute-done.4.refs_1_), channel_id=1, source_target_pairs={{0,4},{4,0},{8,12},{12,8},{1,5},{5,1},{9,13},{13,9},{2,6},{6,2},{1... | collective-permute-start | bytes 786440 | tf_op jit(solution)/shard_map/ppermute | solution.py:21
  26.6 12.0 %collective-permute-start.2 = (f32[64,128]{1,0:T(8,128)S(1)}, f32[64,128]{1,0:T(8,128)S(1)}, u32[]{:S(2)}, u32[]{:S(2)}) collective-permute-start(f32[64,128]{1,0:T(8,128)S(1)} %add.6), channel_id=1, source_target_pairs={{0,4},{4,0},{8,12},{12,8},{1,5},{5,1},{9,13},{13,9},{2,6},{6,2},{1... | collective-permute-start | bytes 98312 | tf_op jit(solution)/shard_map/ppermute | solution.py:21
  38.6 5.0 %collective-permute-start.3 = (f32[64,128]{1,0:T(8,128)S(1)}, f32[64,128]{1,0:T(8,128)S(1)}, u32[]{:S(2)}, u32[]{:S(2)}) collective-permute-start(f32[64,128]{1,0:T(8,128)S(1)} %add.7.factor_a_ref), channel_id=1, source_target_pairs={{0,8},{4,12},{8,0},{12,4},{1,9},{5,13},{9,1},{13,5},{2,10},{6,14},... | collective-permute-start | bytes 98312 | tf_op jit(solution)/shard_map/ppermute | solution.py:21
  41.4 9.4 %collective-permute-start.5 = (bf16[1024,128]{1,0:T(8,128)(2,1)S(1)}, bf16[1024,128]{1,0:T(8,128)(2,1)S(1)}, u32[]{:S(2)}, u32[]{:S(2)}) collective-permute-start(bf16[1024,128]{1,0:T(8,128)(2,1)S(1)} %get-tuple-element.34.refs_0_), channel_id=1, source_target_pairs={{0,1},{1,0},{2,3},{3,2},{4,5},{5,4},{6,7},{7,6},{8,9},{9,8},{10,11... | collective-permute-start | bytes 786440 | tf_op jit(solution)/shard_map/ppermute | solution.py:21
  41.4 9.4 %collective-permute-start.6 = (bf16[1024,128]{1,0:T(8,128)(2,1)S(1)}, bf16[1024,128]{1,0:T(8,128)(2,1)S(1)}, u32[]{:S(2)}, u32[]{:S(2)}) collective-permute-start(bf16[1024,128]{1,0:T(8,128)(2,1)S(1)} %collective-permute-done.4.refs_1_), channel_id=1, source_target_pairs={{0,1},{1,0},{2,3},{3,2},{4,5},{5,4},{6,7},{7,6},{8,9},{9,8},{10,11... | collective-permute-start | bytes 786440 | tf_op jit(solution)/shard_map/ppermute | solution.py:21
  43.6 7.1 %collective-permute-start.9 = (bf16[1024,128]{1,0:T(8,128)(2,1)S(1)}, bf16[1024,128]{1,0:T(8,128)(2,1)S(1)}, u32[]{:S(2)}, u32[]{:S(2)}) collective-permute-start(bf16[1024,128]{1,0:T(8,128)(2,1)S(1)} %collective-permute-done.7.refs_4_), channel_id=1, source_target_pairs={{0,1},{1,0},{2,3},{3,2},{4,5},{5,4},{6,7},{7,6},{8,9},{9,8},{10,11... | collective-permute-start | bytes 786440 | tf_op jit(solution)/shard_map/ppermute | solution.py:21
  43.6 7.1 %collective-permute-start.10 = (bf16[1024,128]{1,0:T(8,128)(2,1)S(1)}, bf16[1024,128]{1,0:T(8,128)(2,1)S(1)}, u32[]{:S(2)}, u32[]{:S(2)}) collective-permute-start(bf16[1024,128]{1,0:T(8,128)(2,1)S(1)} %collective-permute-done.8.refs_5_), channel_id=1, source_target_pairs={{0,1},{1,0},{2,3},{3,2},{4,5},{5,4},{6,7},{7,6},{8,9},{9,8},{10,11... | collective-permute-start | bytes 786440 | tf_op jit(solution)/shard_map/ppermute | solution.py:21
  44.2 6.6 %collective-permute-start.11 = (bf16[4,64,128]{2,1,0:T(8,128)(2,1)S(1)}, bf16[4,64,128]{2,1,0:T(8,128)(2,1)S(1)}, u32[]{:S(2)}, u32[]{:S(2)}) collective-permute-start(bf16[4,64,128]{2,1,0:T(8,128)(2,1)S(1)} %features.1.refs_8_), channel_id=1, source_target_pairs={{0,8},{4,12},{8,0},{12,4},{1,9},{5,13},{9,1},{13,5},{2,10},{6,14},... | collective-permute-start | bytes 196616 | tf_op jit(solution)/shard_map/ppermute | solution.py:21
  52.3 4.6 %collective-permute-start.12 = (f32[2,8,128]{2,1,0:T(8,128)S(1)}, f32[2,8,128]{2,1,0:T(8,128)S(1)}, u32[]{:S(2)}, u32[]{:S(2)}) collective-permute-start(f32[2,8,128]{2,1,0:T(8,128)S(1)} %get-tuple-element.40), channel_id=1, source_target_pairs={{0,8},{4,12},{8,0},{12,4},{1,9},{5,13},{9,1},{13,5},{2,10},{6,14},... | collective-permute-start | bytes 24584 | tf_op jit(solution)/shard_map/ppermute | solution.py:21

commit v4 on v3

--- a/solution.py
+++ b/solution.py
@@ -13,7 +13,8 @@
 NT = (((1,), (1,)), ((), ()))
 VMEM = pl.BlockSpec(memory_space=pltpu.VMEM)
 SMEM = pl.BlockSpec(memory_space=pltpu.SMEM)
-HBM = pl.BlockSpec(memory_space=pltpu.HBM)
+ANY = pl.BlockSpec(memory_space=pl.ANY)
+PROJECT_MIB = 60
 
 
 def xor_permute(values, axis, mask):
@@ -71,7 +72,7 @@
             jax.ShapeDtypeStruct((tokens, 2 * rank), f32),
             jax.ShapeDtypeStruct((tokens, 2 * rank), bf16),
         ),
-        in_specs=[HBM] * 4,
+        in_specs=[ANY] * 4,
         out_specs=(VMEM, VMEM),
         scratch_shapes=[
             pltpu.VMEM(x.shape, bf16),
@@ -80,7 +81,7 @@
             pltpu.VMEM(pout.shape, bf16),
             pltpu.SemaphoreType.DMA((3 + tokens // rows,)),
         ],
-        compiler_params=pltpu.CompilerParams(vmem_limit_bytes=60 * MIB),
+        compiler_params=pltpu.CompilerParams(vmem_limit_bytes=PROJECT_MIB * MIB),
         cost_estimate=pl.CostEstimate(
             flops=2 * tokens * (in_width + out_width) * rank,
             bytes_accessed=2 * (tokens + rank) * (in_width + out_width),
@@ -88,6 +89,22 @@
         ),
         name="project",
     )(x, g, pin, pout)
+
+
+def fetch_body(values_ref, out_ref):
+    out_ref[...] = values_ref[...]
+
+
+def fetch(values):
+    return pl.pallas_call(
+        fetch_body,
+        out_shape=jax.ShapeDtypeStruct(values.shape, values.dtype),
+        in_specs=[VMEM],
+        out_specs=VMEM,
+        compiler_params=pltpu.CompilerParams(vmem_limit_bytes=4 * MIB),
+        cost_estimate=pl.CostEstimate(flops=values.size, bytes_accessed=8 * values.size, transcendentals=0),
+        name="fetch",
+    )(values)
 
 
 def factors_body(received, lengths_ref, mask_ref, own_ref, *refs):
@@ -404,31 +421,29 @@
     own_rows = test_feats.shape[1]
     x = train_inputs.reshape(tokens, in_width)
     g = train_grads.reshape(tokens, out_width)
-    own, sent = project(x, g, proj_in.T, proj_out.T, tokens // 3)
+    tests = test_feats.transpose(1, 2, 0).reshape(own_rows * test_feats.shape[2], test_feats.shape[0])
+    cut = pack(tests)
+    near = [cut[0]] + [xor_permute(cut[mask], "feat", mask) for mask in range(1, feat_count)]
+    far = [xor_permute(near[0], "dp", 1)]
+    own, sent = project(x, g, after(proj_in.T, cut[0]), proj_out.T, tokens // 3)
+    far += [xor_permute(piece, "dp", 1) for piece in after(tuple(near[1:]), sent)]
     received = [xor_permute(sent, "feat", mask) for mask in range(1, feat_count)]
-    tests = test_feats.transpose(1, 2, 0).reshape(own_rows * test_feats.shape[2], test_feats.shape[0])
-    cut = pack(after(tests, sent))
-    near = [cut[0]] + [xor_permute(cut[mask], "feat", mask) for mask in range(1, feat_count)]
-    factor, rounded, turned = factors(lengths, loss_mask, own, received)
+    factor, rounded, turned = factors(lengths, loss_mask, fetch(own), received)
     feats = [features_of(lengths, rounded, turned)]
     even_masks = range(2, dp_count, 2)
-    steps = [("test", 1)] + [("dp", m) for m in masks_of(dp_count)]
+    steps = [("test", 1)] + [("dp", m) for m in reversed(masks_of(dp_count))]
     sums = [factor]
     for axis, mask in steps:
         if len(sums) == len(steps):
             sums[-1] = after(sums[-1], feats[0])
         other = xor_permute(sums[-1], axis, mask)
         sums.append(sums[-1] + other)
-    factor = sums[-2]
-    far = [xor_permute(near[0], "dp", 1)]
-    if feat_count > 1:
-        far += [xor_permute(piece, "dp", 1) for piece in after(tuple(near[1:]), sums[1])]
-    shared = after(tuple(near), sums[2])
-    pieces = near + [xor_permute(piece, "test", 1) for piece in shared]
-    shared = after(tuple(far), other)
-    pieces += far + [xor_permute(piece, "test", 1) for piece in shared]
+    pieces = []
+    for part in (near, far):
+        pieces += part + [xor_permute(piece, "test", 1) for piece in after(tuple(part), sums[2])]
     feats += [xor_permute(feats[0], "dp", mask) for mask in even_masks]
-    grad, in_pair = inverses(float(tokens * dp_count * test_count), factor, other)
+    total_tokens = float(tokens * dp_count * test_count)
+    grad, in_pair = inverses(total_tokens, sums[-2], other)
     blocks = scores_of(grad, in_pair, pieces, feats)
     blocks = [blocks[0]] + [xor_permute(blocks[at + 1], "dp", mask) for at, mask in enumerate(even_masks)]
     return finish(blocks)

time: 57.7 us -> 44.2 us (0.77)
  waiting for transfers between devices: 27.1 us -> 11.3 us
  starting transfers between devices: 14.7 us -> 16 us
  local copies, waits for them, and re-layouts: 1.01 us -> 2.06 us
    ppermute x13, waiting for transfers between devices: 27.1 us -> 11.3 us  [xor_permute(): return lax.ppermute(values, axis, [(i, i ^ mask) for i in range(size)])]
    ppermute x13, starting transfers between devices: 14.7 us -> 16 us  [xor_permute(): return lax.ppermute(values, axis, [(i, i ^ mask) for i in range(size)])]
    unnamed x8, local copies, waits for them, and re-layouts: 1.01 us -> 2.06 us
  transfers between devices with their start and end apart: 13 -> 13, of which waited for: 5 -> 7; matrix products, arithmetic and copies ran while one was open for 0% -> 0% of each run, Pallas kernels for 8% -> 28%
where the time goes in v4:
time: 44.2 us; the launch traced here: 44 us
  starting transfers between devices  16 us (36%)
  Pallas kernels  14.6 us (33%)
  waiting for transfers between devices  11.3 us (26%)
  local copies, waits for them, and re-layouts  2.06 us (5%)
    ppermute x13, starting transfers between devices, xor_permute(): return lax.ppermute(values, axis, [(i, i ^ mask) for i in range(size)])  16 us
    ppermute x13, waiting for transfers between devices, xor_permute(): return lax.ppermute(values, axis, [(i, i ^ mask) for i in range(size)])  11.3 us
    pallas_call x1, Pallas kernels, project(): pl.pallas_call(functools.partial(project_body, rows), out_shape=(jax.Shap...  7.71 us
    pallas_call x1, Pallas kernels, inverses(): pl.pallas_call(functools.partial(inverses_body, total_tokens), out_shape=...  2.81 us
    unnamed x8, local copies, waits for them, and re-layouts  2.06 us
    pallas_call x1, Pallas kernels, scores_of(): pl.pallas_call(functools.partial(scores_body, len(feats)), out_shape=[jax...  1.52 us
  transfers between devices with their start and end apart: 13, of which 7 were waited for; matrix products, arithmetic and copies ran while one was open for 0% of the time, Pallas kernels for 28%

profile of v4, /device:TPU:0, one launch (start us, length us, event | category | flops | bytes accessed | tf_op | source)
XLA Modules:
  0.0 44.0 jit_solution(13467951418663739656)
XLA Ops:
  0.0 1.1 %copy-done = bf16[128,32,64]{0,2,1:T(8,128)(2,1)S(1)} copy-done((bf16[128,32,64]{0,2,1:T(8,128)(2,1)S(1)}, bf16[128,32,64]{0,2,1:T(8,128)(2,1)}, u32[]{:S(2)}) %copy-start) | copy-done | bytes 524312
  1.1 0.2 pack.1
  1.3 3.0 %collective-permute-start.4 = (bf16[1024,128]{1,0:T(8,128)(2,1)S(1)}, bf16[1024,128]{1,0:T(8,128)(2,1)S(1)}, u32[]{:S(2)}, u32[]{:S(2)}) collective-permute-start(bf16[1024,128]{1,0:T(8,128)(2,1)S(1)} %get-tuple-element.33), channel_id=1, source_target_pairs={{0,2},{2,0},{1,3},{3,1},{4,6},{6,4},{5,7},{7,5},{8,10},{10,8},{9,1... | collective-permute-start | bytes 786440 | tf_op jit(solution)/shard_map/ppermute | solution.py:22
  4.3 7.7 %project.1 = (f32[768,128]{1,0:T(8,128)}, bf16[768,128]{1,0:T(8,128)(2,1)}) custom-call(bf16[768,2048]{1,0:T(8,128)(2,1)} %bitcast.10, bf16[768,7168]{1,0:T(8,128)(2,1)} %bitcast.9, bf16[64,2048]{1,0:T(8,128)(2,1)} %bitcast.12, bf16[64,7168]{1,0:T(8,128)(2,1)} %bitcast.11), custom_call_target="tpu_custom_call" | custom-call | flops 905969664 | bytes 15335424 | tf_op jit(solution)/shard_map/project/pallas_call | solution.py:69
  12.1 2.1 %collective-permute-start.7 = (bf16[1024,128]{1,0:T(8,128)(2,1)S(1)}, bf16[1024,128]{1,0:T(8,128)(2,1)S(1)}, u32[]{:S(2)}, u32[]{:S(2)}) collective-permute-start(bf16[1024,128]{1,0:T(8,128)(2,1)S(1)} %get-tuple-element.34.refs_0_), channel_id=1, source_target_pairs={{0,4},{4,0},{8,12},{12,8},{1,5},{5,1},{9,13},{13,9},{2,6},{6,2},{1... | collective-permute-start | bytes 786440 | tf_op jit(solution)/shard_map/ppermute | solution.py:22
  14.2 1.0 %copy-done.1 = f32[768,128]{1,0:T(8,128)S(1)} copy-done((f32[768,128]{1,0:T(8,128)S(1)}, f32[768,128]{1,0:T(8,128)}, u32[]{:S(2)}) %copy-start.1) | copy-done | bytes 393240
  15.2 3.4 %collective-permute-done.refs_0_ = bf16[768,128]{1,0:T(8,128)(2,1)S(1)} collective-permute-done((bf16[768,128]{1,0:T(8,128)(2,1)}, bf16[768,128]{1,0:T(8,128)(2,1)S(1)}, u32[]{:S(2)}, u32[]{:S(2)}) %collective-permute-start) | collective-permute-done | bytes 196640 | tf_op jit(solution)/shard_map/ppermute | solution.py:22
  18.7 0.8 %factors.1 = (f32[64,128]{1,0:T(8,128)S(1)}, bf16[768,128]{1,0:T(8,128)(2,1)S(1)}, bf16[8,128,96]{2,1,0:T(8,128)(2,1)S(1)}) custom-call(s32[8]{0:T(128)S(1)} %copy-done.3, s32[8,96]{1,0:T(8,128)S(1)} %copy-done.2, f32[768,128]{1,0:T(8,128)S(1)} %fetch.1.own_ref, bf16[768,128]{1,0:T(8,128)(2,1)S(1)} %collective-permute-done.refs_0_), custom_call_target="tpu_custom_call" | custom-call | tf_op jit(solution)/shard_map/factors/pallas_call | solution.py:136
  19.6 1.2 %collective-permute-done.1 = f32[64,128]{1,0:T(8,128)S(1)} collective-permute-done((f32[64,128]{1,0:T(8,128)S(1)}, f32[64,128]{1,0:T(8,128)S(1)}, u32[]{:S(2)}, u32[]{:S(2)}) %collective-permute-start.1) | collective-permute-done | bytes 32800 | tf_op jit(solution)/shard_map/ppermute | solution.py:22
  20.8 2.6 %collective-permute-start.2 = (f32[64,128]{1,0:T(8,128)S(1)}, f32[64,128]{1,0:T(8,128)S(1)}, u32[]{:S(2)}, u32[]{:S(2)}) collective-permute-start(f32[64,128]{1,0:T(8,128)S(1)} %add.6), channel_id=1, source_target_pairs={{0,8},{4,12},{8,0},{12,4},{1,9},{5,13},{9,1},{13,5},{2,10},{6,14},... | collective-permute-start | bytes 98312 | tf_op jit(solution)/shard_map/ppermute | solution.py:22
  23.4 0.8 %features.1.refs_8_ = bf16[4,64,128]{2,1,0:T(8,128)(2,1)S(1)} custom-call(s32[8]{0:T(128)S(1)} %copy-done.3, bf16[768,128]{1,0:T(8,128)(2,1)S(1)} %get-tuple-element.28.rounded_ref, bf16[8,128,96]{2,1,0:T(8,128)(2,1)S(1)} %get-tuple-element.29.turned_ref), custom_call_target="tpu_custom_call" | custom-call | flops 25165824 | bytes 8388608 | tf_op jit(solution)/shard_map/features/pallas_call | solution.py:168
  24.2 1.5 %collective-permute-done.2 = f32[64,128]{1,0:T(8,128)S(1)} collective-permute-done((f32[64,128]{1,0:T(8,128)S(1)}, f32[64,128]{1,0:T(8,128)S(1)}, u32[]{:S(2)}, u32[]{:S(2)}) %collective-permute-start.2) | collective-permute-done | bytes 32800 | tf_op jit(solution)/shard_map/ppermute | solution.py:22
  25.6 0.5 %collective-permute-start.6 = (bf16[1024,128]{1,0:T(8,128)(2,1)S(1)}, bf16[1024,128]{1,0:T(8,128)(2,1)S(1)}, u32[]{:S(2)}, u32[]{:S(2)}) collective-permute-start(bf16[1024,128]{1,0:T(8,128)(2,1)S(1)} %collective-permute-done.4.refs_1_), channel_id=1, source_target_pairs={{0,1},{1,0},{2,3},{3,2},{4,5},{5,4},{6,7},{7,6},{8,9},{9,8},{10,11... | collective-permute-start | bytes 786440 | tf_op jit(solution)/shard_map/ppermute | solution.py:22
  26.2 0.1 collective-permute-done.8.refs_5_
  26.2 0.5 %collective-permute-start.10 = (bf16[1024,128]{1,0:T(8,128)(2,1)S(1)}, bf16[1024,128]{1,0:T(8,128)(2,1)S(1)}, u32[]{:S(2)}, u32[]{:S(2)}) collective-permute-start(bf16[1024,128]{1,0:T(8,128)(2,1)S(1)} %collective-permute-done.8.refs_5_), channel_id=1, source_target_pairs={{0,1},{1,0},{2,3},{3,2},{4,5},{5,4},{6,7},{7,6},{8,9},{9,8},{10,11... | collective-permute-start | bytes 786440 | tf_op jit(solution)/shard_map/ppermute | solution.py:22
  26.8 3.3 %collective-permute-start.3 = (f32[64,128]{1,0:T(8,128)S(1)}, f32[64,128]{1,0:T(8,128)S(1)}, u32[]{:S(2)}, u32[]{:S(2)}) collective-permute-start(f32[64,128]{1,0:T(8,128)S(1)} %add.7.factor_a_ref), channel_id=1, source_target_pairs={{0,4},{4,0},{8,12},{12,8},{1,5},{5,1},{9,13},{13,9},{2,6},{6,2},{1... | collective-permute-start | bytes 98312 | tf_op jit(solution)/shard_map/ppermute | solution.py:22
  30.0 1.9 %collective-permute-done.3.factor_b_ref = f32[64,128]{1,0:T(8,128)S(1)} collective-permute-done((f32[64,128]{1,0:T(8,128)S(1)}, f32[64,128]{1,0:T(8,128)S(1)}, u32[]{:S(2)}, u32[]{:S(2)}) %collective-permute-start.3) | collective-permute-done | bytes 32800 | tf_op jit(solution)/shard_map/ppermute | solution.py:22
  31.9 1.9 %collective-permute-start.11 = (bf16[4,64,128]{2,1,0:T(8,128)(2,1)S(1)}, bf16[4,64,128]{2,1,0:T(8,128)(2,1)S(1)}, u32[]{:S(2)}, u32[]{:S(2)}) collective-permute-start(bf16[4,64,128]{2,1,0:T(8,128)(2,1)S(1)} %features.1.refs_8_), channel_id=1, source_target_pairs={{0,8},{4,12},{8,0},{12,4},{1,9},{5,13},{9,1},{13,5},{2,10},{6,14},... | collective-permute-start | bytes 196616 | tf_op jit(solution)/shard_map/ppermute | solution.py:22
  33.8 2.8 %inverses.1 = (bf16[2,64,64]{2,1,0:T(8,128)(2,1)S(1)}, bf16[2,128,128]{2,1,0:T(8,128)(2,1)S(1)}) custom-call(f32[64,128]{1,0:T(8,128)S(1)} %add.7.factor_a_ref, f32[64,128]{1,0:T(8,128)S(1)} %collective-permute-done.3.factor_b_ref), custom_call_target="tpu_custom_call" | custom-call | tf_op jit(solution)/shard_map/inverses/pallas_call | solution.py:263
  36.6 0.6 %collective-permute-done.11.refs_9_ = bf16[4,64,128]{2,1,0:T(8,128)(2,1)S(1)} collective-permute-done((bf16[4,64,128]{2,1,0:T(8,128)(2,1)S(1)}, bf16[4,64,128]{2,1,0:T(8,128)(2,1)S(1)}, u32[]{:S(2)}, u32[]{:S(2)}) %collective-permute-start.11) | collective-permute-done | bytes 65568 | tf_op jit(solution)/shard_map/ppermute | solution.py:22
  37.2 1.5 %scores.1 = (f32[2,8,128]{2,1,0:T(8,128)S(1)}, f32[2,8,128]{2,1,0:T(8,128)S(1)}) custom-call(bf16[2,64,64]{2,1,0:T(8,128)(2,1)S(1)} %get-tuple-element.31.grad_ref, bf16[2,128,128]{2,1,0:T(8,128)(2,1)S(1)} %get-tuple-element.32.in_ref, bf16[1024,128]{1,0:T(8,128)(2,1)S(1)} %get-tuple-element.34.refs_0_, ...), custom_call_target="tpu_custom_call" | custom-call | tf_op jit(solution)/shard_map/scores/pallas_call | solution.py:366
  38.8 1.9 %collective-permute-start.12 = (f32[2,8,128]{2,1,0:T(8,128)S(1)}, f32[2,8,128]{2,1,0:T(8,128)S(1)}, u32[]{:S(2)}, u32[]{:S(2)}) collective-permute-start(f32[2,8,128]{2,1,0:T(8,128)S(1)} %get-tuple-element.40), channel_id=1, source_target_pairs={{0,8},{4,12},{8,0},{12,4},{1,9},{5,13},{9,1},{13,5},{2,10},{6,14},... | collective-permute-start | bytes 24584 | tf_op jit(solution)/shard_map/ppermute | solution.py:22
  40.7 2.7 %collective-permute-done.12.refs_1_ = f32[2,8,128]{2,1,0:T(8,128)S(1)} collective-permute-done((f32[2,8,128]{2,1,0:T(8,128)S(1)}, f32[2,8,128]{2,1,0:T(8,128)S(1)}, u32[]{:S(2)}, u32[]{:S(2)}) %collective-permute-start.12) | collective-permute-done | bytes 8224 | tf_op jit(solution)/shard_map/ppermute | solution.py:22
  43.3 0.7 %finish.1 = f32[64,64]{1,0:T(8,128)} custom-call(f32[2,8,128]{2,1,0:T(8,128)S(1)} %get-tuple-element.39.refs_0_, f32[2,8,128]{2,1,0:T(8,128)S(1)} %collective-permute-done.12.refs_1_), custom_call_target="tpu_custom_call" | custom-call | tf_op jit(solution)/shard_map/finish/pallas_call | solution.py:399
  (20 shorter events, 0.3 us)
Async XLA Ops:
  0.0 18.6 %copy-start.3 = (s32[8]{0:T(128)S(1)}, s32[8]{0:T(128)}, u32[]{:S(2)}) copy-start(s32[8]{0:T(128)} %lengths_ref.3) | copy-start | bytes 100
  0.0 1.1 %copy-start = (bf16[128,32,64]{0,2,1:T(8,128)(2,1)S(1)}, bf16[128,32,64]{0,2,1:T(8,128)(2,1)}, u32[]{:S(2)}) copy-start(bf16[128,32,64]{0,2,1:T(8,128)(2,1)} %param.13) | copy-start | bytes 1572868
  1.1 17.6 %copy-start.2 = (s32[8,96]{1,0:T(8,128)S(1)}, s32[8,96]{1,0:T(8,128)}, u32[]{:S(2)}) copy-start(s32[8,96]{1,0:T(8,128)} %mask_ref.1) | copy-start | bytes 9220
  1.3 12.9 %collective-permute-start.4 = (bf16[1024,128]{1,0:T(8,128)(2,1)S(1)}, bf16[1024,128]{1,0:T(8,128)(2,1)S(1)}, u32[]{:S(2)}, u32[]{:S(2)}) collective-permute-start(bf16[1024,128]{1,0:T(8,128)(2,1)S(1)} %get-tuple-element.33), channel_id=1, source_target_pairs={{0,2},{2,0},{1,3},{3,1},{4,6},{6,4},{5,7},{7,5},{8,10},{10,8},{9,1... | collective-permute-start | bytes 786440 | tf_op jit(solution)/shard_map/ppermute | solution.py:22
  12.0 6.6 %collective-permute-start = (bf16[768,128]{1,0:T(8,128)(2,1)}, bf16[768,128]{1,0:T(8,128)(2,1)S(1)}, u32[]{:S(2)}, u32[]{:S(2)}) collective-permute-start(bf16[768,128]{1,0:T(8,128)(2,1)} %get-tuple-element.26), channel_id=1, source_target_pairs={{0,2},{2,0},{1,3},{3,1},{4,6},{6,4},{5,7},{7,5},{8,10},{10,8},{9,1... | collective-permute-start | bytes 589832 | tf_op jit(solution)/shard_map/ppermute | solution.py:22
  12.1 14.1 %collective-permute-start.7 = (bf16[1024,128]{1,0:T(8,128)(2,1)S(1)}, bf16[1024,128]{1,0:T(8,128)(2,1)S(1)}, u32[]{:S(2)}, u32[]{:S(2)}) collective-permute-start(bf16[1024,128]{1,0:T(8,128)(2,1)S(1)} %get-tuple-element.34.refs_0_), channel_id=1, source_target_pairs={{0,4},{4,0},{8,12},{12,8},{1,5},{5,1},{9,13},{13,9},{2,6},{6,2},{1... | collective-permute-start | bytes 786440 | tf_op jit(solution)/shard_map/ppermute | solution.py:22
  14.2 12.1 %collective-permute-start.8 = (bf16[1024,128]{1,0:T(8,128)(2,1)S(1)}, bf16[1024,128]{1,0:T(8,128)(2,1)S(1)}, u32[]{:S(2)}, u32[]{:S(2)}) collective-permute-start(bf16[1024,128]{1,0:T(8,128)(2,1)S(1)} %collective-permute-done.4.refs_1_), channel_id=1, source_target_pairs={{0,4},{4,0},{8,12},{12,8},{1,5},{5,1},{9,13},{13,9},{2,6},{6,2},{1... | collective-permute-start | bytes 786440 | tf_op jit(solution)/shard_map/ppermute | solution.py:22
  14.2 1.0 %copy-start.1 = (f32[768,128]{1,0:T(8,128)S(1)}, f32[768,128]{1,0:T(8,128)}, u32[]{:S(2)}) copy-start(f32[768,128]{1,0:T(8,128)} %get-tuple-element.25.values_ref) | copy-start | bytes 1179652
  19.5 1.3 %collective-permute-start.1 = (f32[64,128]{1,0:T(8,128)S(1)}, f32[64,128]{1,0:T(8,128)S(1)}, u32[]{:S(2)}, u32[]{:S(2)}) collective-permute-start(f32[64,128]{1,0:T(8,128)S(1)} %get-tuple-element.27), channel_id=1, source_target_pairs={{0,1},{1,0},{2,3},{3,2},{4,5},{5,4},{6,7},{7,6},{8,9},{9,8},{10,11... | collective-permute-start | bytes 98312 | tf_op jit(solution)/shard_map/ppermute | solution.py:22
  20.8 4.9 %collective-permute-start.2 = (f32[64,128]{1,0:T(8,128)S(1)}, f32[64,128]{1,0:T(8,128)S(1)}, u32[]{:S(2)}, u32[]{:S(2)}) collective-permute-start(f32[64,128]{1,0:T(8,128)S(1)} %add.6), channel_id=1, source_target_pairs={{0,8},{4,12},{8,0},{12,4},{1,9},{5,13},{9,1},{13,5},{2,10},{6,14},... | collective-permute-start | bytes 98312 | tf_op jit(solution)/shard_map/ppermute | solution.py:22
  25.6 11.6 %collective-permute-start.5 = (bf16[1024,128]{1,0:T(8,128)(2,1)S(1)}, bf16[1024,128]{1,0:T(8,128)(2,1)S(1)}, u32[]{:S(2)}, u32[]{:S(2)}) collective-permute-start(bf16[1024,128]{1,0:T(8,128)(2,1)S(1)} %get-tuple-element.34.refs_0_), channel_id=1, source_target_pairs={{0,1},{1,0},{2,3},{3,2},{4,5},{5,4},{6,7},{7,6},{8,9},{9,8},{10,11... | collective-permute-start | bytes 786440 | tf_op jit(solution)/shard_map/ppermute | solution.py:22
  25.6 11.6 %collective-permute-start.6 = (bf16[1024,128]{1,0:T(8,128)(2,1)S(1)}, bf16[1024,128]{1,0:T(8,128)(2,1)S(1)}, u32[]{:S(2)}, u32[]{:S(2)}) collective-permute-start(bf16[1024,128]{1,0:T(8,128)(2,1)S(1)} %collective-permute-done.4.refs_1_), channel_id=1, source_target_pairs={{0,1},{1,0},{2,3},{3,2},{4,5},{5,4},{6,7},{7,6},{8,9},{9,8},{10,11... | collective-permute-start | bytes 786440 | tf_op jit(solution)/shard_map/ppermute | solution.py:22
  26.2 11.0 %collective-permute-start.9 = (bf16[1024,128]{1,0:T(8,128)(2,1)S(1)}, bf16[1024,128]{1,0:T(8,128)(2,1)S(1)}, u32[]{:S(2)}, u32[]{:S(2)}) collective-permute-start(bf16[1024,128]{1,0:T(8,128)(2,1)S(1)} %collective-permute-done.7.refs_4_), channel_id=1, source_target_pairs={{0,1},{1,0},{2,3},{3,2},{4,5},{5,4},{6,7},{7,6},{8,9},{9,8},{10,11... | collective-permute-start | bytes 786440 | tf_op jit(solution)/shard_map/ppermute | solution.py:22
  26.2 11.0 %collective-permute-start.10 = (bf16[1024,128]{1,0:T(8,128)(2,1)S(1)}, bf16[1024,128]{1,0:T(8,128)(2,1)S(1)}, u32[]{:S(2)}, u32[]{:S(2)}) collective-permute-start(bf16[1024,128]{1,0:T(8,128)(2,1)S(1)} %collective-permute-done.8.refs_5_), channel_id=1, source_target_pairs={{0,1},{1,0},{2,3},{3,2},{4,5},{5,4},{6,7},{7,6},{8,9},{9,8},{10,11... | collective-permute-start | bytes 786440 | tf_op jit(solution)/shard_map/ppermute | solution.py:22
  26.8 5.2 %collective-permute-start.3 = (f32[64,128]{1,0:T(8,128)S(1)}, f32[64,128]{1,0:T(8,128)S(1)}, u32[]{:S(2)}, u32[]{:S(2)}) collective-permute-start(f32[64,128]{1,0:T(8,128)S(1)} %add.7.factor_a_ref), channel_id=1, source_target_pairs={{0,4},{4,0},{8,12},{12,8},{1,5},{5,1},{9,13},{13,9},{2,6},{6,2},{1... | collective-permute-start | bytes 98312 | tf_op jit(solution)/shard_map/ppermute | solution.py:22
  31.9 5.3 %collective-permute-start.11 = (bf16[4,64,128]{2,1,0:T(8,128)(2,1)S(1)}, bf16[4,64,128]{2,1,0:T(8,128)(2,1)S(1)}, u32[]{:S(2)}, u32[]{:S(2)}) collective-permute-start(bf16[4,64,128]{2,1,0:T(8,128)(2,1)S(1)} %features.1.refs_8_), channel_id=1, source_target_pairs={{0,8},{4,12},{8,0},{12,4},{1,9},{5,13},{9,1},{13,5},{2,10},{6,14},... | collective-permute-start | bytes 196616 | tf_op jit(solution)/shard_map/ppermute | solution.py:22
  38.8 4.6 %collective-permute-start.12 = (f32[2,8,128]{2,1,0:T(8,128)S(1)}, f32[2,8,128]{2,1,0:T(8,128)S(1)}, u32[]{:S(2)}, u32[]{:S(2)}) collective-permute-start(f32[2,8,128]{2,1,0:T(8,128)S(1)} %get-tuple-element.40), channel_id=1, source_target_pairs={{0,8},{4,12},{8,0},{12,4},{1,9},{5,13},{9,1},{13,5},{2,10},{6,14},... | collective-permute-start | bytes 24584 | tf_op jit(solution)/shard_map/ppermute | solution.py:22

commit v5 on v4

--- a/solution.py
+++ b/solution.py
@@ -238,40 +238,21 @@
     return jnp.concatenate(blocks, axis=0)
 
 
-def inverses_body(total_tokens, factor_a_ref, factor_b_ref, grad_ref, in_ref):
-    rank = factor_a_ref.shape[0]
+def damped_inverses(total_tokens, packed):
+    rank = packed.shape[0]
     lane = lax.broadcasted_iota(jnp.int32, (rank, 2 * rank), 1)
     sub = lax.broadcasted_iota(jnp.int32, (rank, 2 * rank), 0)
     left = lane < rank
-    column = jnp.where(left, lane, lane - rank)
-    diagonal = column == sub
-    packed = (factor_a_ref[...] + factor_b_ref[...]) / total_tokens
+    diagonal = jnp.where(left, lane, lane - rank) == sub
+    packed = packed / total_tokens
     on_diagonal = jnp.sum(jnp.where(diagonal, packed, 0.0), axis=0, keepdims=True)
     trace_in = jnp.sum(jnp.where(left[:1], on_diagonal, 0.0), axis=1, keepdims=True)
     trace_grad = jnp.sum(jnp.where(left[:1], 0.0, on_diagonal), axis=1, keepdims=True)
     damping = 0.1 * jnp.where(left[:1], trace_in, trace_grad) / rank + 1e-06
-    packed = packed + jnp.where(diagonal, damping, 0.0)
-    packed = invert(packed)
-    twice = pltpu.roll(packed, rank, 1)
-    grad_ref[0], grad_ref[1] = split(twice[:, :rank])
-    in_ref[0, :rank, :], in_ref[1, :rank, :] = split(jnp.where(left, packed, 0.0))
-    in_ref[0, rank:, :], in_ref[1, rank:, :] = split(jnp.where(left, 0.0, twice))
-
-
-def inverses(total_tokens, factor_a, factor_b):
-    rank, width = factor_a.shape
-    return pl.pallas_call(
-        functools.partial(inverses_body, total_tokens),
-        out_shape=(
-            jax.ShapeDtypeStruct((2, rank, rank), bf16),
-            jax.ShapeDtypeStruct((2, width, width), bf16),
-        ),
-        in_specs=[VMEM, VMEM],
-        out_specs=(VMEM, VMEM),
-        compiler_params=pltpu.CompilerParams(vmem_limit_bytes=4 * MIB),
-        cost_estimate=pl.CostEstimate(flops=0, bytes_accessed=0, transcendentals=0),
-        name="inverses",
-    )(factor_a, factor_b)
+    packed = invert(packed + jnp.where(diagonal, damping, 0.0))
+    other = pltpu.roll(packed, rank, 1)
+    in_pair = jnp.concatenate([jnp.where(left, packed, 0.0), jnp.where(left, 0.0, other)], axis=0)
+    return other[:, :rank], in_pair
 
 
 def pack_body(tests_ref, *out_refs):
@@ -305,12 +286,15 @@
     )(tests)
 
 
-def scores_body(blocks, grad_ref, in_ref, *refs):
+def scores_body(total_tokens, blocks, factor_a_ref, factor_b_ref, *refs):
     feat_count = lax.axis_size("feat")
     feat = lax.axis_index("feat")
     pieces, refs = refs[: 4 * feat_count], refs[4 * feat_count :]
     feats_refs, out_refs, (solved_buf, line_buf) = refs[:blocks], refs[blocks : 2 * blocks], refs[2 * blocks :]
-    rank = grad_ref.shape[1]
+    rank = factor_a_ref.shape[0]
+    grad, in_pair = damped_inverses(total_tokens, factor_a_ref[...] + factor_b_ref[...])
+    grad_high, grad_low = split(grad)
+    in_high, in_low = split(in_pair)
     pairs = [ref[i] for ref in feats_refs for i in range(ref.shape[0])]
     count = len(pairs)
     half = count // blocks
@@ -318,8 +302,8 @@
     block = width // feat_count
     dot = functools.partial(jnp.dot, preferred_element_type=f32)
     for at in range(count):
-        high, low = split(dot(grad_ref[0], pairs[at]) + dot(grad_ref[1], pairs[at]))
-        solved_buf[at * rank : (at + 1) * rank, :] = dot(high, in_ref[0]) + dot(high, in_ref[1]) + dot(low, in_ref[0])
+        high, low = split(dot(grad_high, pairs[at]) + dot(grad_low, pairs[at]))
+        solved_buf[at * rank : (at + 1) * rank, :] = dot(high, in_high) + dot(high, in_low) + dot(low, in_high)
     lane = lax.broadcasted_iota(jnp.int32, (count, 2 * rank), 1)
     for g in range(0, rank, 2):
         low = solved_buf[pl.ds(g, count, stride=rank), :]
@@ -341,10 +325,10 @@
     for dp_bit in range(2):
         parts = []
         for test_bit in range(2):
-            at = (2 * dp_bit + test_bit) * feat_count
-            total = dot(lines[0], pieces[at][...])
-            for mask in range(1, feat_count):
-                total = total + dot(lines[mask], pieces[at + mask][...])
+            total = None
+            for mask in range(feat_count):
+                term = dot(lines[mask], pieces[(2 * dp_bit + test_bit) * feat_count + mask][...])
+                total = term if total is None else total + term
             part = total[: 2 * count, :block]
             for j in range(1, feat_count):
                 part = part + total[2 * count * j : 2 * count * (j + 1), block * j : block * (j + 1)]
@@ -357,14 +341,14 @@
             out_ref[odd ^ dp_bit, half:, :] = both[count + at * half : count + (at + 1) * half, :]
 
 
-def scores_of(grad, in_pair, pieces, feats):
+def scores_of(total_tokens, factor_a, factor_b, pieces, feats):
     feat_count = lax.axis_size("feat")
-    rank = grad.shape[1]
+    rank = factor_a.shape[0]
     fold, width = pieces[0].shape
     half = feats[0].shape[0]
     count = half * len(feats)
     return pl.pallas_call(
-        functools.partial(scores_body, len(feats)),
+        functools.partial(scores_body, total_tokens, len(feats)),
         out_shape=[jax.ShapeDtypeStruct((2, 2 * half, 2 * width // feat_count), f32)] * len(feats),
         in_specs=[VMEM] * (2 + len(pieces) + len(feats)),
         out_specs=[VMEM] * len(feats),
@@ -374,7 +358,7 @@
         ],
         compiler_params=pltpu.CompilerParams(vmem_limit_bytes=16 * MIB),
         name="scores",
-    )(grad, in_pair, *pieces, *feats)
+    )(factor_a, factor_b, *pieces, *feats)
 
 
 def finish_body(*refs):
@@ -428,23 +412,23 @@
     own, sent = project(x, g, after(proj_in.T, cut[0]), proj_out.T, tokens // 3)
     far += [xor_permute(piece, "dp", 1) for piece in after(tuple(near[1:]), sent)]
     received = [xor_permute(sent, "feat", mask) for mask in range(1, feat_count)]
+    shared = [xor_permute(piece, "test", 1) for piece in after(tuple(near), sent)]
     factor, rounded, turned = factors(lengths, loss_mask, fetch(own), received)
     feats = [features_of(lengths, rounded, turned)]
     even_masks = range(2, dp_count, 2)
     steps = [("test", 1)] + [("dp", m) for m in reversed(masks_of(dp_count))]
     sums = [factor]
     for axis, mask in steps:
+        if len(sums) == 3:
+            sums[-1] = after(sums[-1], *shared)
         if len(sums) == len(steps):
             sums[-1] = after(sums[-1], feats[0])
         other = xor_permute(sums[-1], axis, mask)
         sums.append(sums[-1] + other)
-    pieces = []
-    for part in (near, far):
-        pieces += part + [xor_permute(piece, "test", 1) for piece in after(tuple(part), sums[2])]
+    pieces = near + shared + far + [xor_permute(piece, "test", 1) for piece in after(tuple(far), *(sums[2],))]
     feats += [xor_permute(feats[0], "dp", mask) for mask in even_masks]
     total_tokens = float(tokens * dp_count * test_count)
-    grad, in_pair = inverses(total_tokens, sums[-2], other)
-    blocks = scores_of(grad, in_pair, pieces, feats)
+    blocks = scores_of(total_tokens, sums[-2], other, pieces, feats)
     blocks = [blocks[0]] + [xor_permute(blocks[at + 1], "dp", mask) for at, mask in enumerate(even_masks)]
     return finish(blocks)
 

time: 44.2 us -> 44.5 us (level)
  waiting for transfers between devices: 11.3 us -> 12.4 us
  starting transfers between devices: 16 us -> 15.1 us
    ppermute x13, waiting for transfers between devices: 11.3 us -> 12.4 us  [xor_permute(): return lax.ppermute(values, axis, [(i, i ^ mask) for i in range(size)])]
    ppermute x13, starting transfers between devices: 16 us -> 15.1 us  [xor_permute(): return lax.ppermute(values, axis, [(i, i ^ mask) for i in range(size)])]
    pallas_call x2 -> x1, Pallas kernels: 4.33 us -> 4.44 us  [scores_of(): pl.pallas_call(functools.partial(scores_body, total_tokens, len(feats)),...]
  transfers between devices with their start and end apart: 13 -> 13, of which waited for: 7 -> 7; matrix products, arithmetic and copies ran while one was open for 0% -> 0% of each run, Pallas kernels for 28% -> 21%
where the time goes in v5:
time: 44.5 us; the launch traced here: 44.4 us
  starting transfers between devices  15.1 us (34%)
  Pallas kernels  14.7 us (33%)
  waiting for transfers between devices  12.4 us (28%)
  local copies, waits for them, and re-layouts  2.06 us (5%)
    ppermute x13, starting transfers between devices, xor_permute(): return lax.ppermute(values, axis, [(i, i ^ mask) for i in range(size)])  15.1 us
    ppermute x13, waiting for transfers between devices, xor_permute(): return lax.ppermute(values, axis, [(i, i ^ mask) for i in range(size)])  12.4 us
    pallas_call x1, Pallas kernels, project(): pl.pallas_call(functools.partial(project_body, rows), out_shape=(jax.Shap...  7.72 us
    pallas_call x1, Pallas kernels, scores_of(): pl.pallas_call(functools.partial(scores_body, total_tokens, len(feats)),...  4.44 us
    unnamed x8, local copies, waits for them, and re-layouts  2.06 us
  transfers between devices with their start and end apart: 13, of which 7 were waited for; matrix products, arithmetic and copies ran while one was open for 0% of the time, Pallas kernels for 21%

profile of v5, /device:TPU:0, one launch (start us, length us, event | category | flops | bytes accessed | tf_op | source)
XLA Modules:
  0.0 44.4 jit_solution(1360653465228903532)
XLA Ops:
  0.0 1.1 %copy-done = bf16[128,32,64]{0,2,1:T(8,128)(2,1)S(1)} copy-done((bf16[128,32,64]{0,2,1:T(8,128)(2,1)S(1)}, bf16[128,32,64]{0,2,1:T(8,128)(2,1)}, u32[]{:S(2)}) %copy-start) | copy-done | bytes 524312
  1.1 0.2 pack.1
  1.3 3.0 %collective-permute-start.3 = (bf16[1024,128]{1,0:T(8,128)(2,1)S(1)}, bf16[1024,128]{1,0:T(8,128)(2,1)S(1)}, u32[]{:S(2)}, u32[]{:S(2)}) collective-permute-start(bf16[1024,128]{1,0:T(8,128)(2,1)S(1)} %get-tuple-element.27), channel_id=1, source_target_pairs={{0,2},{2,0},{1,3},{3,1},{4,6},{6,4},{5,7},{7,5},{8,10},{10,8},{9,1... | collective-permute-start | bytes 786440 | tf_op jit(solution)/shard_map/ppermute | solution.py:22
  4.3 7.7 %project.1 = (f32[768,128]{1,0:T(8,128)}, bf16[768,128]{1,0:T(8,128)(2,1)}) custom-call(bf16[768,2048]{1,0:T(8,128)(2,1)} %bitcast.10, bf16[768,7168]{1,0:T(8,128)(2,1)} %bitcast.9, bf16[64,2048]{1,0:T(8,128)(2,1)} %bitcast.12, bf16[64,7168]{1,0:T(8,128)(2,1)} %bitcast.11), custom_call_target="tpu_custom_call" | custom-call | flops 905969664 | bytes 15335424 | tf_op jit(solution)/shard_map/project/pallas_call | solution.py:69
  12.0 0.1 collective-permute-start
  12.2 0.5 %collective-permute-start.5 = (bf16[1024,128]{1,0:T(8,128)(2,1)S(1)}, bf16[1024,128]{1,0:T(8,128)(2,1)S(1)}, u32[]{:S(2)}, u32[]{:S(2)}) collective-permute-start(bf16[1024,128]{1,0:T(8,128)(2,1)S(1)} %collective-permute-done.3.refs_1_), channel_id=1, source_target_pairs={{0,1},{1,0},{2,3},{3,2},{4,5},{5,4},{6,7},{7,6},{8,9},{9,8},{10,11... | collective-permute-start | bytes 786440 | tf_op jit(solution)/shard_map/ppermute | solution.py:22
  12.7 2.0 %collective-permute-start.7 = (bf16[1024,128]{1,0:T(8,128)(2,1)S(1)}, bf16[1024,128]{1,0:T(8,128)(2,1)S(1)}, u32[]{:S(2)}, u32[]{:S(2)}) collective-permute-start(bf16[1024,128]{1,0:T(8,128)(2,1)S(1)} %get-tuple-element.28.refs_0_), channel_id=1, source_target_pairs={{0,4},{4,0},{8,12},{12,8},{1,5},{5,1},{9,13},{13,9},{2,6},{6,2},{1... | collective-permute-start | bytes 786440 | tf_op jit(solution)/shard_map/ppermute | solution.py:22
  14.7 1.0 %copy-done.1 = f32[768,128]{1,0:T(8,128)S(1)} copy-done((f32[768,128]{1,0:T(8,128)S(1)}, f32[768,128]{1,0:T(8,128)}, u32[]{:S(2)}) %copy-start.1) | copy-done | bytes 393240
  15.8 2.9 %collective-permute-done.refs_0_ = bf16[768,128]{1,0:T(8,128)(2,1)S(1)} collective-permute-done((bf16[768,128]{1,0:T(8,128)(2,1)}, bf16[768,128]{1,0:T(8,128)(2,1)S(1)}, u32[]{:S(2)}, u32[]{:S(2)}) %collective-permute-start) | collective-permute-done | bytes 196640 | tf_op jit(solution)/shard_map/ppermute | solution.py:22
  18.7 0.8 %factors.1 = (f32[64,128]{1,0:T(8,128)S(1)}, bf16[768,128]{1,0:T(8,128)(2,1)S(1)}, bf16[8,128,96]{2,1,0:T(8,128)(2,1)S(1)}) custom-call(s32[8]{0:T(128)S(1)} %copy-done.3, s32[8,96]{1,0:T(8,128)S(1)} %copy-done.2, f32[768,128]{1,0:T(8,128)S(1)} %fetch.1.own_ref, bf16[768,128]{1,0:T(8,128)(2,1)S(1)} %collective-permute-done.refs_0_), custom_call_target="tpu_custom_call" | custom-call | tf_op jit(solution)/shard_map/factors/pallas_call | solution.py:136
  19.6 1.2 %collective-permute-done.1 = f32[64,128]{1,0:T(8,128)S(1)} collective-permute-done((f32[64,128]{1,0:T(8,128)S(1)}, f32[64,128]{1,0:T(8,128)S(1)}, u32[]{:S(2)}, u32[]{:S(2)}) %collective-permute-start.1) | collective-permute-done | bytes 32800 | tf_op jit(solution)/shard_map/ppermute | solution.py:22
  20.8 2.6 %collective-permute-start.2 = (f32[64,128]{1,0:T(8,128)S(1)}, f32[64,128]{1,0:T(8,128)S(1)}, u32[]{:S(2)}, u32[]{:S(2)}) collective-permute-start(f32[64,128]{1,0:T(8,128)S(1)} %add.6), channel_id=1, source_target_pairs={{0,8},{4,12},{8,0},{12,4},{1,9},{5,13},{9,1},{13,5},{2,10},{6,14},... | collective-permute-start | bytes 98312 | tf_op jit(solution)/shard_map/ppermute | solution.py:22
  23.4 0.8 %features.1.refs_8_ = bf16[4,64,128]{2,1,0:T(8,128)(2,1)S(1)} custom-call(s32[8]{0:T(128)S(1)} %copy-done.3, bf16[768,128]{1,0:T(8,128)(2,1)S(1)} %get-tuple-element.31.rounded_ref, bf16[8,128,96]{2,1,0:T(8,128)(2,1)S(1)} %get-tuple-element.32.turned_ref), custom_call_target="tpu_custom_call" | custom-call | flops 25165824 | bytes 8388608 | tf_op jit(solution)/shard_map/features/pallas_call | solution.py:168
  24.2 2.6 %collective-permute-done.2 = f32[64,128]{1,0:T(8,128)S(1)} collective-permute-done((f32[64,128]{1,0:T(8,128)S(1)}, f32[64,128]{1,0:T(8,128)S(1)}, u32[]{:S(2)}, u32[]{:S(2)}) %collective-permute-start.2) | collective-permute-done | bytes 32800 | tf_op jit(solution)/shard_map/ppermute | solution.py:22
  26.8 0.7 %collective-permute-done.8.refs_5_ = bf16[1024,128]{1,0:T(8,128)(2,1)S(1)} collective-permute-done((bf16[1024,128]{1,0:T(8,128)(2,1)S(1)}, bf16[1024,128]{1,0:T(8,128)(2,1)S(1)}, u32[]{:S(2)}, u32[]{:S(2)}) %collective-permute-start.8) | collective-permute-done | bytes 262176 | tf_op jit(solution)/shard_map/ppermute | solution.py:22
  27.5 0.5 %collective-permute-start.10 = (bf16[1024,128]{1,0:T(8,128)(2,1)S(1)}, bf16[1024,128]{1,0:T(8,128)(2,1)S(1)}, u32[]{:S(2)}, u32[]{:S(2)}) collective-permute-start(bf16[1024,128]{1,0:T(8,128)(2,1)S(1)} %collective-permute-done.8.refs_5_), channel_id=1, source_target_pairs={{0,1},{1,0},{2,3},{3,2},{4,5},{5,4},{6,7},{7,6},{8,9},{9,8},{10,11... | collective-permute-start | bytes 786440 | tf_op jit(solution)/shard_map/ppermute | solution.py:22
  28.0 2.8 %collective-permute-start.11 = (bf16[4,64,128]{2,1,0:T(8,128)(2,1)S(1)}, bf16[4,64,128]{2,1,0:T(8,128)(2,1)S(1)}, u32[]{:S(2)}, u32[]{:S(2)}) collective-permute-start(bf16[4,64,128]{2,1,0:T(8,128)(2,1)S(1)} %features.1.refs_8_), channel_id=1, source_target_pairs={{0,8},{4,12},{8,0},{12,4},{1,9},{5,13},{9,1},{13,5},{2,10},{6,14},... | collective-permute-start | bytes 196616 | tf_op jit(solution)/shard_map/ppermute | solution.py:22
  30.8 1.6 %collective-permute-start.6 = (f32[64,128]{1,0:T(8,128)S(1)}, f32[64,128]{1,0:T(8,128)S(1)}, u32[]{:S(2)}, u32[]{:S(2)}) collective-permute-start(f32[64,128]{1,0:T(8,128)S(1)} %add.7.factor_a_ref), channel_id=1, source_target_pairs={{0,4},{4,0},{8,12},{12,8},{1,5},{5,1},{9,13},{13,9},{2,6},{6,2},{1... | collective-permute-start | bytes 98312 | tf_op jit(solution)/shard_map/ppermute | solution.py:22
  32.3 0.8 %collective-permute-done.11.refs_9_ = bf16[4,64,128]{2,1,0:T(8,128)(2,1)S(1)} collective-permute-done((bf16[4,64,128]{2,1,0:T(8,128)(2,1)S(1)}, bf16[4,64,128]{2,1,0:T(8,128)(2,1)S(1)}, u32[]{:S(2)}, u32[]{:S(2)}) %collective-permute-start.11) | collective-permute-done | bytes 65568 | tf_op jit(solution)/shard_map/ppermute | solution.py:22
  33.2 1.5 %collective-permute-done.6.factor_b_ref = f32[64,128]{1,0:T(8,128)S(1)} collective-permute-done((f32[64,128]{1,0:T(8,128)S(1)}, f32[64,128]{1,0:T(8,128)S(1)}, u32[]{:S(2)}, u32[]{:S(2)}) %collective-permute-start.6) | collective-permute-done | bytes 32800 | tf_op jit(solution)/shard_map/ppermute | solution.py:22
  34.7 4.4 %scores.1 = (f32[2,8,128]{2,1,0:T(8,128)S(1)}, f32[2,8,128]{2,1,0:T(8,128)S(1)}) custom-call(f32[64,128]{1,0:T(8,128)S(1)} %add.7.factor_a_ref, f32[64,128]{1,0:T(8,128)S(1)} %collective-permute-done.6.factor_b_ref, bf16[1024,128]{1,0:T(8,128)(2,1)S(1)} %get-tuple-element.28.refs_0_, bf16[1024,128]{1,0:T(8,128)(2,1)S(1)} %collective-permute-done.3.refs_1_, ...), custom_call_target="tpu_custom_call" | custom-call | tf_op jit(solution)/shard_map/scores/pallas_call | solution.py:350
  39.1 1.9 %collective-permute-start.12 = (f32[2,8,128]{2,1,0:T(8,128)S(1)}, f32[2,8,128]{2,1,0:T(8,128)S(1)}, u32[]{:S(2)}, u32[]{:S(2)}) collective-permute-start(f32[2,8,128]{2,1,0:T(8,128)S(1)} %get-tuple-element.38), channel_id=1, source_target_pairs={{0,8},{4,12},{8,0},{12,4},{1,9},{5,13},{9,1},{13,5},{2,10},{6,14},... | collective-permute-start | bytes 24584 | tf_op jit(solution)/shard_map/ppermute | solution.py:22
  41.0 2.7 %collective-permute-done.12.refs_1_ = f32[2,8,128]{2,1,0:T(8,128)S(1)} collective-permute-done((f32[2,8,128]{2,1,0:T(8,128)S(1)}, f32[2,8,128]{2,1,0:T(8,128)S(1)}, u32[]{:S(2)}, u32[]{:S(2)}) %collective-permute-start.12) | collective-permute-done | bytes 8224 | tf_op jit(solution)/shard_map/ppermute | solution.py:22
  43.7 0.7 %finish.1 = f32[64,64]{1,0:T(8,128)} custom-call(f32[2,8,128]{2,1,0:T(8,128)S(1)} %get-tuple-element.37.refs_0_, f32[2,8,128]{2,1,0:T(8,128)S(1)} %collective-permute-done.12.refs_1_), custom_call_target="tpu_custom_call" | custom-call | tf_op jit(solution)/shard_map/finish/pallas_call | solution.py:383
  (19 shorter events, 0.2 us)
Async XLA Ops:
  0.0 18.7 %copy-start.3 = (s32[8]{0:T(128)S(1)}, s32[8]{0:T(128)}, u32[]{:S(2)}) copy-start(s32[8]{0:T(128)} %lengths_ref.3) | copy-start | bytes 100
  0.0 1.1 %copy-start = (bf16[128,32,64]{0,2,1:T(8,128)(2,1)S(1)}, bf16[128,32,64]{0,2,1:T(8,128)(2,1)}, u32[]{:S(2)}) copy-start(bf16[128,32,64]{0,2,1:T(8,128)(2,1)} %param.13) | copy-start | bytes 1572868
  1.1 17.6 %copy-start.2 = (s32[8,96]{1,0:T(8,128)S(1)}, s32[8,96]{1,0:T(8,128)}, u32[]{:S(2)}) copy-start(s32[8,96]{1,0:T(8,128)} %mask_ref.1) | copy-start | bytes 9220
  1.3 10.8 %collective-permute-start.3 = (bf16[1024,128]{1,0:T(8,128)(2,1)S(1)}, bf16[1024,128]{1,0:T(8,128)(2,1)S(1)}, u32[]{:S(2)}, u32[]{:S(2)}) collective-permute-start(bf16[1024,128]{1,0:T(8,128)(2,1)S(1)} %get-tuple-element.27), channel_id=1, source_target_pairs={{0,2},{2,0},{1,3},{3,1},{4,6},{6,4},{5,7},{7,5},{8,10},{10,8},{9,1... | collective-permute-start | bytes 786440 | tf_op jit(solution)/shard_map/ppermute | solution.py:22
  12.0 6.6 %collective-permute-start = (bf16[768,128]{1,0:T(8,128)(2,1)}, bf16[768,128]{1,0:T(8,128)(2,1)S(1)}, u32[]{:S(2)}, u32[]{:S(2)}) collective-permute-start(bf16[768,128]{1,0:T(8,128)(2,1)} %get-tuple-element.25), channel_id=1, source_target_pairs={{0,2},{2,0},{1,3},{3,1},{4,6},{6,4},{5,7},{7,5},{8,10},{10,8},{9,1... | collective-permute-start | bytes 589832 | tf_op jit(solution)/shard_map/ppermute | solution.py:22
  12.1 14.7 %collective-permute-start.4 = (bf16[1024,128]{1,0:T(8,128)(2,1)S(1)}, bf16[1024,128]{1,0:T(8,128)(2,1)S(1)}, u32[]{:S(2)}, u32[]{:S(2)}) collective-permute-start(bf16[1024,128]{1,0:T(8,128)(2,1)S(1)} %get-tuple-element.28.refs_0_), channel_id=1, source_target_pairs={{0,1},{1,0},{2,3},{3,2},{4,5},{5,4},{6,7},{7,6},{8,9},{9,8},{10,11... | collective-permute-start | bytes 786440 | tf_op jit(solution)/shard_map/ppermute | solution.py:22
  12.2 14.6 %collective-permute-start.5 = (bf16[1024,128]{1,0:T(8,128)(2,1)S(1)}, bf16[1024,128]{1,0:T(8,128)(2,1)S(1)}, u32[]{:S(2)}, u32[]{:S(2)}) collective-permute-start(bf16[1024,128]{1,0:T(8,128)(2,1)S(1)} %collective-permute-done.3.refs_1_), channel_id=1, source_target_pairs={{0,1},{1,0},{2,3},{3,2},{4,5},{5,4},{6,7},{7,6},{8,9},{9,8},{10,11... | collective-permute-start | bytes 786440 | tf_op jit(solution)/shard_map/ppermute | solution.py:22
  12.7 14.1 %collective-permute-start.7 = (bf16[1024,128]{1,0:T(8,128)(2,1)S(1)}, bf16[1024,128]{1,0:T(8,128)(2,1)S(1)}, u32[]{:S(2)}, u32[]{:S(2)}) collective-permute-start(bf16[1024,128]{1,0:T(8,128)(2,1)S(1)} %get-tuple-element.28.refs_0_), channel_id=1, source_target_pairs={{0,4},{4,0},{8,12},{12,8},{1,5},{5,1},{9,13},{13,9},{2,6},{6,2},{1... | collective-permute-start | bytes 786440 | tf_op jit(solution)/shard_map/ppermute | solution.py:22
  14.7 12.8 %collective-permute-start.8 = (bf16[1024,128]{1,0:T(8,128)(2,1)S(1)}, bf16[1024,128]{1,0:T(8,128)(2,1)S(1)}, u32[]{:S(2)}, u32[]{:S(2)}) collective-permute-start(bf16[1024,128]{1,0:T(8,128)(2,1)S(1)} %collective-permute-done.3.refs_1_), channel_id=1, source_target_pairs={{0,4},{4,0},{8,12},{12,8},{1,5},{5,1},{9,13},{13,9},{2,6},{6,2},{1... | collective-permute-start | bytes 786440 | tf_op jit(solution)/shard_map/ppermute | solution.py:22
  14.7 1.0 %copy-start.1 = (f32[768,128]{1,0:T(8,128)S(1)}, f32[768,128]{1,0:T(8,128)}, u32[]{:S(2)}) copy-start(f32[768,128]{1,0:T(8,128)} %get-tuple-element.24.values_ref) | copy-start | bytes 1179652
  19.5 1.3 %collective-permute-start.1 = (f32[64,128]{1,0:T(8,128)S(1)}, f32[64,128]{1,0:T(8,128)S(1)}, u32[]{:S(2)}, u32[]{:S(2)}) collective-permute-start(f32[64,128]{1,0:T(8,128)S(1)} %get-tuple-element.26), channel_id=1, source_target_pairs={{0,1},{1,0},{2,3},{3,2},{4,5},{5,4},{6,7},{7,6},{8,9},{9,8},{10,11... | collective-permute-start | bytes 98312 | tf_op jit(solution)/shard_map/ppermute | solution.py:22
  20.8 6.0 %collective-permute-start.2 = (f32[64,128]{1,0:T(8,128)S(1)}, f32[64,128]{1,0:T(8,128)S(1)}, u32[]{:S(2)}, u32[]{:S(2)}) collective-permute-start(f32[64,128]{1,0:T(8,128)S(1)} %add.6), channel_id=1, source_target_pairs={{0,8},{4,12},{8,0},{12,4},{1,9},{5,13},{9,1},{13,5},{2,10},{6,14},... | collective-permute-start | bytes 98312 | tf_op jit(solution)/shard_map/ppermute | solution.py:22
  27.5 7.2 %collective-permute-start.9 = (bf16[1024,128]{1,0:T(8,128)(2,1)S(1)}, bf16[1024,128]{1,0:T(8,128)(2,1)S(1)}, u32[]{:S(2)}, u32[]{:S(2)}) collective-permute-start(bf16[1024,128]{1,0:T(8,128)(2,1)S(1)} %collective-permute-done.7.refs_4_), channel_id=1, source_target_pairs={{0,1},{1,0},{2,3},{3,2},{4,5},{5,4},{6,7},{7,6},{8,9},{9,8},{10,11... | collective-permute-start | bytes 786440 | tf_op jit(solution)/shard_map/ppermute | solution.py:22
  27.5 7.2 %collective-permute-start.10 = (bf16[1024,128]{1,0:T(8,128)(2,1)S(1)}, bf16[1024,128]{1,0:T(8,128)(2,1)S(1)}, u32[]{:S(2)}, u32[]{:S(2)}) collective-permute-start(bf16[1024,128]{1,0:T(8,128)(2,1)S(1)} %collective-permute-done.8.refs_5_), channel_id=1, source_target_pairs={{0,1},{1,0},{2,3},{3,2},{4,5},{5,4},{6,7},{7,6},{8,9},{9,8},{10,11... | collective-permute-start | bytes 786440 | tf_op jit(solution)/shard_map/ppermute | solution.py:22
  28.0 5.2 %collective-permute-start.11 = (bf16[4,64,128]{2,1,0:T(8,128)(2,1)S(1)}, bf16[4,64,128]{2,1,0:T(8,128)(2,1)S(1)}, u32[]{:S(2)}, u32[]{:S(2)}) collective-permute-start(bf16[4,64,128]{2,1,0:T(8,128)(2,1)S(1)} %features.1.refs_8_), channel_id=1, source_target_pairs={{0,8},{4,12},{8,0},{12,4},{1,9},{5,13},{9,1},{13,5},{2,10},{6,14},... | collective-permute-start | bytes 196616 | tf_op jit(solution)/shard_map/ppermute | solution.py:22
  30.8 3.9 %collective-permute-start.6 = (f32[64,128]{1,0:T(8,128)S(1)}, f32[64,128]{1,0:T(8,128)S(1)}, u32[]{:S(2)}, u32[]{:S(2)}) collective-permute-start(f32[64,128]{1,0:T(8,128)S(1)} %add.7.factor_a_ref), channel_id=1, source_target_pairs={{0,4},{4,0},{8,12},{12,8},{1,5},{5,1},{9,13},{13,9},{2,6},{6,2},{1... | collective-permute-start | bytes 98312 | tf_op jit(solution)/shard_map/ppermute | solution.py:22
  39.1 4.6 %collective-permute-start.12 = (f32[2,8,128]{2,1,0:T(8,128)S(1)}, f32[2,8,128]{2,1,0:T(8,128)S(1)}, u32[]{:S(2)}, u32[]{:S(2)}) collective-permute-start(f32[2,8,128]{2,1,0:T(8,128)S(1)} %get-tuple-element.38), channel_id=1, source_target_pairs={{0,8},{4,12},{8,0},{12,4},{1,9},{5,13},{9,1},{13,5},{2,10},{6,14},... | collective-permute-start | bytes 24584 | tf_op jit(solution)/shard_map/ppermute | solution.py:22

commit v6 on v4

--- a/solution.py
+++ b/solution.py
@@ -14,7 +14,7 @@
 VMEM = pl.BlockSpec(memory_space=pltpu.VMEM)
 SMEM = pl.BlockSpec(memory_space=pltpu.SMEM)
 ANY = pl.BlockSpec(memory_space=pl.ANY)
-PROJECT_MIB = 60
+PROJECT_MIB = 48
 
 
 def xor_permute(values, axis, mask):
@@ -30,33 +30,24 @@
     return masks
 
 
-def project_body(rows, x_hbm, g_hbm, pin_hbm, pout_hbm, own_ref, sent_ref, x_buf, g_buf, pin_buf, pout_buf, sems):
-    steps = x_hbm.shape[0] // rows
-    rank = pin_hbm.shape[0]
-    pin_copy = pltpu.make_async_copy(pin_hbm, pin_buf, sems.at[0])
-    x_copy = pltpu.make_async_copy(x_hbm, x_buf, sems.at[1])
-    pout_copy = pltpu.make_async_copy(pout_hbm, pout_buf, sems.at[2])
+def project_body(rows, x_ref, g_hbm, pin_ref, pout_ref, own_ref, sent_ref, g_buf, sems):
+    steps = x_ref.shape[0] // rows
+    rank = pin_ref.shape[0]
 
     def g_copy(step):
         begin = step * rows if isinstance(step, int) else pl.multiple_of(step * rows, rows)
         block = pl.ds(begin, rows)
-        return pltpu.make_async_copy(g_hbm.at[block, :], g_buf.at[block, :], sems.at[3 + step])
-
-    pin_copy.start()
-    x_copy.start()
-    pout_copy.start()
+        return pltpu.make_async_copy(g_hbm.at[block, :], g_buf.at[block, :], sems.at[step])
+
     for step in range(steps):
         g_copy(step).start()
-    pin_copy.wait()
-    x_copy.wait()
-    own_ref[:, :rank] = lax.dot_general(x_buf[...], pin_buf[...], NT, preferred_element_type=f32)
-    pout_copy.wait()
+    own_ref[:, :rank] = lax.dot_general(x_ref[...], pin_ref[...], NT, preferred_element_type=f32)
 
     @pl.loop(0, steps)
     def _(step):
         g_copy(step).wait()
         block = pl.ds(pl.multiple_of(step * rows, rows), rows)
-        right = lax.dot_general(g_buf[block, :], pout_buf[...], NT, preferred_element_type=f32)
+        right = lax.dot_general(g_buf[block, :], pout_ref[...], NT, preferred_element_type=f32)
         both = jnp.concatenate([own_ref[block, :rank], right], axis=1)
         own_ref[block, :] = both
         sent_ref[block, :] = both.astype(bf16)
@@ -72,15 +63,9 @@
             jax.ShapeDtypeStruct((tokens, 2 * rank), f32),
             jax.ShapeDtypeStruct((tokens, 2 * rank), bf16),
         ),
-        in_specs=[ANY] * 4,
+        in_specs=[VMEM, ANY, VMEM, VMEM],
         out_specs=(VMEM, VMEM),
-        scratch_shapes=[
-            pltpu.VMEM(x.shape, bf16),
-            pltpu.VMEM(g.shape, bf16),
-            pltpu.VMEM(pin.shape, bf16),
-            pltpu.VMEM(pout.shape, bf16),
-            pltpu.SemaphoreType.DMA((3 + tokens // rows,)),
-        ],
+        scratch_shapes=[pltpu.VMEM(g.shape, bf16), pltpu.SemaphoreType.DMA((tokens // rows,))],
         compiler_params=pltpu.CompilerParams(vmem_limit_bytes=PROJECT_MIB * MIB),
         cost_estimate=pl.CostEstimate(
             flops=2 * tokens * (in_width + out_width) * rank,
@@ -300,7 +285,7 @@
         in_specs=[VMEM],
         out_specs=[VMEM] * feat_count,
         compiler_params=pltpu.CompilerParams(vmem_limit_bytes=8 * MIB),
-        cost_estimate=pl.CostEstimate(flops=4 * MIB, bytes_accessed=4 * MIB, transcendentals=0),
+        cost_estimate=pl.CostEstimate(flops=40960 * MIB, bytes_accessed=4 * MIB, transcendentals=0),
         name="pack",
     )(tests)
 
@@ -428,19 +413,20 @@
     own, sent = project(x, g, after(proj_in.T, cut[0]), proj_out.T, tokens // 3)
     far += [xor_permute(piece, "dp", 1) for piece in after(tuple(near[1:]), sent)]
     received = [xor_permute(sent, "feat", mask) for mask in range(1, feat_count)]
-    factor, rounded, turned = factors(lengths, loss_mask, fetch(own), received)
+    shared = [xor_permute(piece, "test", 1) for piece in after(tuple(near), sent)]
+    factor, rounded, turned = factors(lengths, loss_mask, own, received)
     feats = [features_of(lengths, rounded, turned)]
     even_masks = range(2, dp_count, 2)
     steps = [("test", 1)] + [("dp", m) for m in reversed(masks_of(dp_count))]
     sums = [factor]
     for axis, mask in steps:
+        if len(sums) == 3:
+            sums[-1] = after(sums[-1], *shared)
         if len(sums) == len(steps):
             sums[-1] = after(sums[-1], feats[0])
         other = xor_permute(sums[-1], axis, mask)
         sums.append(sums[-1] + other)
-    pieces = []
-    for part in (near, far):
-        pieces += part + [xor_permute(piece, "test", 1) for piece in after(tuple(part), sums[2])]
+    pieces = near + shared + far + [xor_permute(piece, "test", 1) for piece in after(tuple(far), *(other,))]
     feats += [xor_permute(feats[0], "dp", mask) for mask in even_masks]
     total_tokens = float(tokens * dp_count * test_count)
     grad, in_pair = inverses(total_tokens, sums[-2], other)

time: 44.2 us -> 44.7 us (1.011)
  Pallas kernels: 14.6 us -> 12.4 us
  waiting for transfers between devices: 11.3 us -> 13.4 us
  starting transfers between devices: 16 us -> 17.6 us
  local copies, waits for them, and re-layouts: 2.06 us -> 1.06 us
    pallas_call x1, Pallas kernels: 7.71 us -> 5.56 us  [project(): pl.pallas_call(functools.partial(project_body, rows), out_shape=(jax.Shap...]
    ppermute x13, waiting for transfers between devices: 11.3 us -> 13.4 us  [xor_permute(): return lax.ppermute(values, axis, [(i, i ^ mask) for i in range(size)])]
    ppermute x13, starting transfers between devices: 16 us -> 17.6 us  [xor_permute(): return lax.ppermute(values, axis, [(i, i ^ mask) for i in range(size)])]
    unnamed x8 -> x12, local copies, waits for them, and re-layouts: 2.06 us -> 1.06 us
  transfers between devices with their start and end apart: 13 -> 13, of which waited for: 7 -> 6; matrix products, arithmetic and copies ran while one was open for 0% -> 0% of each run, Pallas kernels for 28% -> 22%
where the time goes in v6:
time: 44.7 us; the launch traced here: 44.6 us
  starting transfers between devices  17.6 us (39%)
  waiting for transfers between devices  13.4 us (30%)
  Pallas kernels  12.4 us (28%)
  local copies, waits for them, and re-layouts  1.06 us (2%)
    ppermute x13, starting transfers between devices, xor_permute(): return lax.ppermute(values, axis, [(i, i ^ mask) for i in range(size)])  17.6 us
    ppermute x13, waiting for transfers between devices, xor_permute(): return lax.ppermute(values, axis, [(i, i ^ mask) for i in range(size)])  13.4 us
    pallas_call x1, Pallas kernels, project(): pl.pallas_call(functools.partial(project_body, rows), out_shape=(jax.Shap...  5.56 us
    pallas_call x1, Pallas kernels, inverses(): pl.pallas_call(functools.partial(inverses_body, total_tokens), out_shape=...  2.81 us
    pallas_call x1, Pallas kernels, scores_of(): pl.pallas_call(functools.partial(scores_body, len(feats)), out_shape=[jax...  1.52 us
    unnamed x12, local copies, waits for them, and re-layouts  1.06 us
  transfers between devices with their start and end apart: 13, of which 6 were waited for; matrix products, arithmetic and copies ran while one was open for 0% of the time, Pallas kernels for 22%

profile of v6, /device:TPU:0, one launch (start us, length us, event | category | flops | bytes accessed | tf_op | source)
XLA Modules:
  0.0 44.6 jit_solution(16039301173006582706)
XLA Ops:
  0.0 1.0 %copy-done.5 = bf16[128,32,64]{0,2,1:T(8,128)(2,1)S(1)} copy-done((bf16[128,32,64]{0,2,1:T(8,128)(2,1)S(1)}, bf16[128,32,64]{0,2,1:T(8,128)(2,1)}, u32[]{:S(2)}) %copy-start.5) | copy-done | bytes 524312
  1.0 0.2 pack.1
  1.3 3.0 %collective-permute-start.3 = (bf16[1024,128]{1,0:T(8,128)(2,1)S(1)}, bf16[1024,128]{1,0:T(8,128)(2,1)S(1)}, u32[]{:S(2)}, u32[]{:S(2)}) collective-permute-start(bf16[1024,128]{1,0:T(8,128)(2,1)S(1)} %get-tuple-element.29), channel_id=1, source_target_pairs={{0,2},{2,0},{1,3},{3,1},{4,6},{6,4},{5,7},{7,5},{8,10},{10,8},{9,1... | collective-permute-start | bytes 786440 | tf_op jit(solution)/shard_map/ppermute | solution.py:22
  4.3 5.6 %project.1 = (f32[768,128]{1,0:T(8,128)S(1)}, bf16[768,128]{1,0:T(8,128)(2,1)S(1)}) custom-call(bf16[768,2048]{1,0:T(8,128)(2,1)S(1)} %bitcast.8, bf16[768,7168]{1,0:T(8,128)(2,1)} %bitcast.12, bf16[64,2048]{1,0:T(8,128)(2,1)S(1)} %bitcast.10, bf16[64,7168]{1,0:T(8,128)(2,1)S(1)} %bitcast.9), custom_call_target="tpu_custom_call" | custom-call | flops 905969664 | bytes 15335424 | tf_op jit(solution)/shard_map/project/pallas_call | solution.py:60
  9.9 1.9 %collective-permute-start = (bf16[768,128]{1,0:T(8,128)(2,1)S(1)}, bf16[768,128]{1,0:T(8,128)(2,1)S(1)}, u32[]{:S(2)}, u32[]{:S(2)}) collective-permute-start(bf16[768,128]{1,0:T(8,128)(2,1)S(1)} %get-tuple-element.27), channel_id=1, source_target_pairs={{0,2},{2,0},{1,3},{3,1},{4,6},{6,4},{5,7},{7,5},{8,10},{10,8},{9,1... | collective-permute-start | bytes 589832 | tf_op jit(solution)/shard_map/ppermute | solution.py:22
  11.8 0.5 %collective-permute-start.5 = (bf16[1024,128]{1,0:T(8,128)(2,1)S(1)}, bf16[1024,128]{1,0:T(8,128)(2,1)S(1)}, u32[]{:S(2)}, u32[]{:S(2)}) collective-permute-start(bf16[1024,128]{1,0:T(8,128)(2,1)S(1)} %collective-permute-done.3.refs_1_), channel_id=1, source_target_pairs={{0,1},{1,0},{2,3},{3,2},{4,5},{5,4},{6,7},{7,6},{8,9},{9,8},{10,11... | collective-permute-start | bytes 786440 | tf_op jit(solution)/shard_map/ppermute | solution.py:22
  12.3 1.6 %collective-permute-start.7 = (bf16[1024,128]{1,0:T(8,128)(2,1)S(1)}, bf16[1024,128]{1,0:T(8,128)(2,1)S(1)}, u32[]{:S(2)}, u32[]{:S(2)}) collective-permute-start(bf16[1024,128]{1,0:T(8,128)(2,1)S(1)} %get-tuple-element.30.refs_0_), channel_id=1, source_target_pairs={{0,4},{4,0},{8,12},{12,8},{1,5},{5,1},{9,13},{13,9},{2,6},{6,2},{1... | collective-permute-start | bytes 786440 | tf_op jit(solution)/shard_map/ppermute | solution.py:22
  13.9 0.4 collective-permute-start.8
  14.3 2.4 %collective-permute-done.refs_0_ = bf16[768,128]{1,0:T(8,128)(2,1)S(1)} collective-permute-done((bf16[768,128]{1,0:T(8,128)(2,1)S(1)}, bf16[768,128]{1,0:T(8,128)(2,1)S(1)}, u32[]{:S(2)}, u32[]{:S(2)}) %collective-permute-start) | collective-permute-done | bytes 196640 | tf_op jit(solution)/shard_map/ppermute | solution.py:22
  16.7 0.8 %factors.1 = (f32[64,128]{1,0:T(8,128)S(1)}, bf16[768,128]{1,0:T(8,128)(2,1)S(1)}, bf16[8,128,96]{2,1,0:T(8,128)(2,1)S(1)}) custom-call(s32[8]{0:T(128)S(1)} %copy-done.4, s32[8,96]{1,0:T(8,128)S(1)} %copy-done.3, f32[768,128]{1,0:T(8,128)S(1)} %get-tuple-element.26.own_ref, bf16[768,128]{1,0:T(8,128)(2,1)S(1)} %collective-permute-done.refs_0_), custom_call_target="tpu_custom_call" | custom-call | tf_op jit(solution)/shard_map/factors/pallas_call | solution.py:121
  17.6 1.2 %collective-permute-done.1 = f32[64,128]{1,0:T(8,128)S(1)} collective-permute-done((f32[64,128]{1,0:T(8,128)S(1)}, f32[64,128]{1,0:T(8,128)S(1)}, u32[]{:S(2)}, u32[]{:S(2)}) %collective-permute-start.1) | collective-permute-done | bytes 32800 | tf_op jit(solution)/shard_map/ppermute | solution.py:22
  18.8 2.8 %collective-permute-start.2 = (f32[64,128]{1,0:T(8,128)S(1)}, f32[64,128]{1,0:T(8,128)S(1)}, u32[]{:S(2)}, u32[]{:S(2)}) collective-permute-start(f32[64,128]{1,0:T(8,128)S(1)} %add.6), channel_id=1, source_target_pairs={{0,8},{4,12},{8,0},{12,4},{1,9},{5,13},{9,1},{13,5},{2,10},{6,14},... | collective-permute-start | bytes 98312 | tf_op jit(solution)/shard_map/ppermute | solution.py:22
  21.7 0.8 %features.1.refs_8_ = bf16[4,64,128]{2,1,0:T(8,128)(2,1)S(1)} custom-call(s32[8]{0:T(128)S(1)} %copy-done.4, bf16[768,128]{1,0:T(8,128)(2,1)S(1)} %get-tuple-element.33.rounded_ref, bf16[8,128,96]{2,1,0:T(8,128)(2,1)S(1)} %get-tuple-element.34.turned_ref), custom_call_target="tpu_custom_call" | custom-call | flops 25165824 | bytes 8388608 | tf_op jit(solution)/shard_map/features/pallas_call | solution.py:153
  22.4 3.5 %collective-permute-done.2 = f32[64,128]{1,0:T(8,128)S(1)} collective-permute-done((f32[64,128]{1,0:T(8,128)S(1)}, f32[64,128]{1,0:T(8,128)S(1)}, u32[]{:S(2)}, u32[]{:S(2)}) %collective-permute-start.2) | collective-permute-done | bytes 32800 | tf_op jit(solution)/shard_map/ppermute | solution.py:22
  26.0 3.6 %collective-permute-start.6 = (f32[64,128]{1,0:T(8,128)S(1)}, f32[64,128]{1,0:T(8,128)S(1)}, u32[]{:S(2)}, u32[]{:S(2)}) collective-permute-start(f32[64,128]{1,0:T(8,128)S(1)} %add.7.factor_a_ref), channel_id=1, source_target_pairs={{0,4},{4,0},{8,12},{12,8},{1,5},{5,1},{9,13},{13,9},{2,6},{6,2},{1... | collective-permute-start | bytes 98312 | tf_op jit(solution)/shard_map/ppermute | solution.py:22
  29.5 1.9 %collective-permute-done.6.factor_b_ref = f32[64,128]{1,0:T(8,128)S(1)} collective-permute-done((f32[64,128]{1,0:T(8,128)S(1)}, f32[64,128]{1,0:T(8,128)S(1)}, u32[]{:S(2)}, u32[]{:S(2)}) %collective-permute-start.6) | collective-permute-done | bytes 32800 | tf_op jit(solution)/shard_map/ppermute | solution.py:22
  31.4 0.5 %collective-permute-start.10 = (bf16[1024,128]{1,0:T(8,128)(2,1)S(1)}, bf16[1024,128]{1,0:T(8,128)(2,1)S(1)}, u32[]{:S(2)}, u32[]{:S(2)}) collective-permute-start(bf16[1024,128]{1,0:T(8,128)(2,1)S(1)} %collective-permute-done.8.refs_5_), channel_id=1, source_target_pairs={{0,1},{1,0},{2,3},{3,2},{4,5},{5,4},{6,7},{7,6},{8,9},{9,8},{10,11... | collective-permute-start | bytes 786440 | tf_op jit(solution)/shard_map/ppermute | solution.py:22
  31.9 1.9 %collective-permute-start.11 = (bf16[4,64,128]{2,1,0:T(8,128)(2,1)S(1)}, bf16[4,64,128]{2,1,0:T(8,128)(2,1)S(1)}, u32[]{:S(2)}, u32[]{:S(2)}) collective-permute-start(bf16[4,64,128]{2,1,0:T(8,128)(2,1)S(1)} %features.1.refs_8_), channel_id=1, source_target_pairs={{0,8},{4,12},{8,0},{12,4},{1,9},{5,13},{9,1},{13,5},{2,10},{6,14},... | collective-permute-start | bytes 196616 | tf_op jit(solution)/shard_map/ppermute | solution.py:22
  33.8 2.8 %inverses.1 = (bf16[2,64,64]{2,1,0:T(8,128)(2,1)S(1)}, bf16[2,128,128]{2,1,0:T(8,128)(2,1)S(1)}) custom-call(f32[64,128]{1,0:T(8,128)S(1)} %add.7.factor_a_ref, f32[64,128]{1,0:T(8,128)S(1)} %collective-permute-done.6.factor_b_ref), custom_call_target="tpu_custom_call" | custom-call | tf_op jit(solution)/shard_map/inverses/pallas_call | solution.py:248
  36.6 1.1 %collective-permute-done.11.refs_9_ = bf16[4,64,128]{2,1,0:T(8,128)(2,1)S(1)} collective-permute-done((bf16[4,64,128]{2,1,0:T(8,128)(2,1)S(1)}, bf16[4,64,128]{2,1,0:T(8,128)(2,1)S(1)}, u32[]{:S(2)}, u32[]{:S(2)}) %collective-permute-start.11) | collective-permute-done | bytes 65568 | tf_op jit(solution)/shard_map/ppermute | solution.py:22
  37.8 1.5 %scores.1 = (f32[2,8,128]{2,1,0:T(8,128)S(1)}, f32[2,8,128]{2,1,0:T(8,128)S(1)}) custom-call(bf16[2,64,64]{2,1,0:T(8,128)(2,1)S(1)} %get-tuple-element.36.grad_ref, bf16[2,128,128]{2,1,0:T(8,128)(2,1)S(1)} %get-tuple-element.37.in_ref, bf16[1024,128]{1,0:T(8,128)(2,1)S(1)} %get-tuple-element.30.refs_0_, ...), custom_call_target="tpu_custom_call" | custom-call | tf_op jit(solution)/shard_map/scores/pallas_call | solution.py:351
  39.3 1.2 %collective-permute-start.12 = (f32[2,8,128]{2,1,0:T(8,128)S(1)}, f32[2,8,128]{2,1,0:T(8,128)S(1)}, u32[]{:S(2)}, u32[]{:S(2)}) collective-permute-start(f32[2,8,128]{2,1,0:T(8,128)S(1)} %get-tuple-element.42), channel_id=1, source_target_pairs={{0,8},{4,12},{8,0},{12,4},{1,9},{5,13},{9,1},{13,5},{2,10},{6,14},... | collective-permute-start | bytes 24584 | tf_op jit(solution)/shard_map/ppermute | solution.py:22
  40.5 3.3 %collective-permute-done.12.refs_1_ = f32[2,8,128]{2,1,0:T(8,128)S(1)} collective-permute-done((f32[2,8,128]{2,1,0:T(8,128)S(1)}, f32[2,8,128]{2,1,0:T(8,128)S(1)}, u32[]{:S(2)}, u32[]{:S(2)}) %collective-permute-start.12) | collective-permute-done | bytes 8224 | tf_op jit(solution)/shard_map/ppermute | solution.py:22
  43.9 0.7 %finish.1 = f32[64,64]{1,0:T(8,128)} custom-call(f32[2,8,128]{2,1,0:T(8,128)S(1)} %get-tuple-element.41.refs_0_, f32[2,8,128]{2,1,0:T(8,128)S(1)} %collective-permute-done.12.refs_1_), custom_call_target="tpu_custom_call" | custom-call | tf_op jit(solution)/shard_map/finish/pallas_call | solution.py:384
  (23 shorter events, 0.1 us)
Async XLA Ops:
  0.0 1.0 %copy-start.5 = (bf16[128,32,64]{0,2,1:T(8,128)(2,1)S(1)}, bf16[128,32,64]{0,2,1:T(8,128)(2,1)}, u32[]{:S(2)}) copy-start(bf16[128,32,64]{0,2,1:T(8,128)(2,1)} %param.13) | copy-start | bytes 1572868
  1.0 3.3 %copy-start = (bf16[8,96,2048]{2,1,0:T(8,128)(2,1)S(1)}, bf16[8,96,2048]{2,1,0:T(8,128)(2,1)}, u32[]{:S(2)}) copy-start(bf16[8,96,2048]{2,1,0:T(8,128)(2,1)} %param.7) | copy-start | bytes 9437188
  1.0 3.3 %copy-start.1 = (bf16[7168,64]{0,1:T(8,128)(2,1)S(1)}, bf16[7168,64]{0,1:T(8,128)(2,1)}, u32[]{:S(2)}) copy-start(bf16[7168,64]{0,1:T(8,128)(2,1)} %param.10) | copy-start | bytes 2752516
  1.0 3.3 %copy-start.2 = (bf16[2048,64]{0,1:T(8,128)(2,1)S(1)}, bf16[2048,64]{0,1:T(8,128)(2,1)}, u32[]{:S(2)}) copy-start(bf16[2048,64]{0,1:T(8,128)(2,1)} %param.9) | copy-start | bytes 786436
  1.3 15.4 %copy-start.3 = (s32[8,96]{1,0:T(8,128)S(1)}, s32[8,96]{1,0:T(8,128)}, u32[]{:S(2)}) copy-start(s32[8,96]{1,0:T(8,128)} %mask_ref.1) | copy-start | bytes 9220
  1.3 15.4 %copy-start.4 = (s32[8]{0:T(128)S(1)}, s32[8]{0:T(128)}, u32[]{:S(2)}) copy-start(s32[8]{0:T(128)} %lengths_ref.3) | copy-start | bytes 100
  1.3 10.5 %collective-permute-start.3 = (bf16[1024,128]{1,0:T(8,128)(2,1)S(1)}, bf16[1024,128]{1,0:T(8,128)(2,1)S(1)}, u32[]{:S(2)}, u32[]{:S(2)}) collective-permute-start(bf16[1024,128]{1,0:T(8,128)(2,1)S(1)} %get-tuple-element.29), channel_id=1, source_target_pairs={{0,2},{2,0},{1,3},{3,1},{4,6},{6,4},{5,7},{7,5},{8,10},{10,8},{9,1... | collective-permute-start | bytes 786440 | tf_op jit(solution)/shard_map/ppermute | solution.py:22
  9.9 6.8 %collective-permute-start = (bf16[768,128]{1,0:T(8,128)(2,1)S(1)}, bf16[768,128]{1,0:T(8,128)(2,1)S(1)}, u32[]{:S(2)}, u32[]{:S(2)}) collective-permute-start(bf16[768,128]{1,0:T(8,128)(2,1)S(1)} %get-tuple-element.27), channel_id=1, source_target_pairs={{0,2},{2,0},{1,3},{3,1},{4,6},{6,4},{5,7},{7,5},{8,10},{10,8},{9,1... | collective-permute-start | bytes 589832 | tf_op jit(solution)/shard_map/ppermute | solution.py:22
  11.8 14.2 %collective-permute-start.4 = (bf16[1024,128]{1,0:T(8,128)(2,1)S(1)}, bf16[1024,128]{1,0:T(8,128)(2,1)S(1)}, u32[]{:S(2)}, u32[]{:S(2)}) collective-permute-start(bf16[1024,128]{1,0:T(8,128)(2,1)S(1)} %get-tuple-element.30.refs_0_), channel_id=1, source_target_pairs={{0,1},{1,0},{2,3},{3,2},{4,5},{5,4},{6,7},{7,6},{8,9},{9,8},{10,11... | collective-permute-start | bytes 786440 | tf_op jit(solution)/shard_map/ppermute | solution.py:22
  11.8 14.2 %collective-permute-start.5 = (bf16[1024,128]{1,0:T(8,128)(2,1)S(1)}, bf16[1024,128]{1,0:T(8,128)(2,1)S(1)}, u32[]{:S(2)}, u32[]{:S(2)}) collective-permute-start(bf16[1024,128]{1,0:T(8,128)(2,1)S(1)} %collective-permute-done.3.refs_1_), channel_id=1, source_target_pairs={{0,1},{1,0},{2,3},{3,2},{4,5},{5,4},{6,7},{7,6},{8,9},{9,8},{10,11... | collective-permute-start | bytes 786440 | tf_op jit(solution)/shard_map/ppermute | solution.py:22
  12.3 17.2 %collective-permute-start.7 = (bf16[1024,128]{1,0:T(8,128)(2,1)S(1)}, bf16[1024,128]{1,0:T(8,128)(2,1)S(1)}, u32[]{:S(2)}, u32[]{:S(2)}) collective-permute-start(bf16[1024,128]{1,0:T(8,128)(2,1)S(1)} %get-tuple-element.30.refs_0_), channel_id=1, source_target_pairs={{0,4},{4,0},{8,12},{12,8},{1,5},{5,1},{9,13},{13,9},{2,6},{6,2},{1... | collective-permute-start | bytes 786440 | tf_op jit(solution)/shard_map/ppermute | solution.py:22
  13.9 15.6 %collective-permute-start.8 = (bf16[1024,128]{1,0:T(8,128)(2,1)S(1)}, bf16[1024,128]{1,0:T(8,128)(2,1)S(1)}, u32[]{:S(2)}, u32[]{:S(2)}) collective-permute-start(bf16[1024,128]{1,0:T(8,128)(2,1)S(1)} %collective-permute-done.3.refs_1_), channel_id=1, source_target_pairs={{0,4},{4,0},{8,12},{12,8},{1,5},{5,1},{9,13},{13,9},{2,6},{6,2},{1... | collective-permute-start | bytes 786440 | tf_op jit(solution)/shard_map/ppermute | solution.py:22
  17.5 1.3 %collective-permute-start.1 = (f32[64,128]{1,0:T(8,128)S(1)}, f32[64,128]{1,0:T(8,128)S(1)}, u32[]{:S(2)}, u32[]{:S(2)}) collective-permute-start(f32[64,128]{1,0:T(8,128)S(1)} %get-tuple-element.28), channel_id=1, source_target_pairs={{0,1},{1,0},{2,3},{3,2},{4,5},{5,4},{6,7},{7,6},{8,9},{9,8},{10,11... | collective-permute-start | bytes 98312 | tf_op jit(solution)/shard_map/ppermute | solution.py:22
  18.8 7.1 %collective-permute-start.2 = (f32[64,128]{1,0:T(8,128)S(1)}, f32[64,128]{1,0:T(8,128)S(1)}, u32[]{:S(2)}, u32[]{:S(2)}) collective-permute-start(f32[64,128]{1,0:T(8,128)S(1)} %add.6), channel_id=1, source_target_pairs={{0,8},{4,12},{8,0},{12,4},{1,9},{5,13},{9,1},{13,5},{2,10},{6,14},... | collective-permute-start | bytes 98312 | tf_op jit(solution)/shard_map/ppermute | solution.py:22
  26.0 5.4 %collective-permute-start.6 = (f32[64,128]{1,0:T(8,128)S(1)}, f32[64,128]{1,0:T(8,128)S(1)}, u32[]{:S(2)}, u32[]{:S(2)}) collective-permute-start(f32[64,128]{1,0:T(8,128)S(1)} %add.7.factor_a_ref), channel_id=1, source_target_pairs={{0,4},{4,0},{8,12},{12,8},{1,5},{5,1},{9,13},{13,9},{2,6},{6,2},{1... | collective-permute-start | bytes 98312 | tf_op jit(solution)/shard_map/ppermute | solution.py:22
  31.4 6.4 %collective-permute-start.9 = (bf16[1024,128]{1,0:T(8,128)(2,1)S(1)}, bf16[1024,128]{1,0:T(8,128)(2,1)S(1)}, u32[]{:S(2)}, u32[]{:S(2)}) collective-permute-start(bf16[1024,128]{1,0:T(8,128)(2,1)S(1)} %collective-permute-done.7.refs_4_), channel_id=1, source_target_pairs={{0,1},{1,0},{2,3},{3,2},{4,5},{5,4},{6,7},{7,6},{8,9},{9,8},{10,11... | collective-permute-start | bytes 786440 | tf_op jit(solution)/shard_map/ppermute | solution.py:22
  31.4 6.4 %collective-permute-start.10 = (bf16[1024,128]{1,0:T(8,128)(2,1)S(1)}, bf16[1024,128]{1,0:T(8,128)(2,1)S(1)}, u32[]{:S(2)}, u32[]{:S(2)}) collective-permute-start(bf16[1024,128]{1,0:T(8,128)(2,1)S(1)} %collective-permute-done.8.refs_5_), channel_id=1, source_target_pairs={{0,1},{1,0},{2,3},{3,2},{4,5},{5,4},{6,7},{7,6},{8,9},{9,8},{10,11... | collective-permute-start | bytes 786440 | tf_op jit(solution)/shard_map/ppermute | solution.py:22
  31.9 5.9 %collective-permute-start.11 = (bf16[4,64,128]{2,1,0:T(8,128)(2,1)S(1)}, bf16[4,64,128]{2,1,0:T(8,128)(2,1)S(1)}, u32[]{:S(2)}, u32[]{:S(2)}) collective-permute-start(bf16[4,64,128]{2,1,0:T(8,128)(2,1)S(1)} %features.1.refs_8_), channel_id=1, source_target_pairs={{0,8},{4,12},{8,0},{12,4},{1,9},{5,13},{9,1},{13,5},{2,10},{6,14},... | collective-permute-start | bytes 196616 | tf_op jit(solution)/shard_map/ppermute | solution.py:22
  39.3 4.6 %collective-permute-start.12 = (f32[2,8,128]{2,1,0:T(8,128)S(1)}, f32[2,8,128]{2,1,0:T(8,128)S(1)}, u32[]{:S(2)}, u32[]{:S(2)}) collective-permute-start(f32[2,8,128]{2,1,0:T(8,128)S(1)} %get-tuple-element.42), channel_id=1, source_target_pairs={{0,8},{4,12},{8,0},{12,4},{1,9},{5,13},{9,1},{13,5},{2,10},{6,14},... | collective-permute-start | bytes 24584 | tf_op jit(solution)/shard_map/ppermute | solution.py:22

commit v7 on v6

--- a/solution.py
+++ b/solution.py
@@ -92,12 +92,27 @@
     )(values)
 
 
-def factors_body(received, lengths_ref, mask_ref, own_ref, *refs):
+def slots_body(out_ref):
+    out_ref[...] = lax.broadcasted_iota(jnp.int32, out_ref.shape, 1)
+
+
+def slots(seq_len):
+    return pl.pallas_call(
+        slots_body,
+        out_shape=jax.ShapeDtypeStruct((1, seq_len), jnp.int32),
+        out_specs=VMEM,
+        compiler_params=pltpu.CompilerParams(vmem_limit_bytes=MIB),
+        cost_estimate=pl.CostEstimate(flops=40960 * MIB, bytes_accessed=4096, transcendentals=0),
+        name="slots",
+    )()
+
+
+def factors_body(received, lengths_ref, positions_ref, mask_ref, own_ref, *refs):
     received_refs = refs[:received]
     factor_ref, rounded_ref, turned_ref = refs[received:]
     examples, seq_len = mask_ref.shape
     rank = factor_ref.shape[0]
-    positions = lax.broadcasted_iota(jnp.int32, (1, seq_len), 1)
+    positions = positions_ref[...]
     total = None
     for example in range(examples):
         rows = pl.ds(example * seq_len, seq_len)
@@ -115,7 +130,7 @@
     factor_ref[...] = jnp.where(lane < rank, total[:rank, :], total[rank:, :])
 
 
-def factors(lengths, mask, own, received):
+def factors(lengths, positions, mask, own, received):
     tokens, width = own.shape
     examples, seq_len = mask.shape
     return pl.pallas_call(
@@ -125,11 +140,11 @@
             jax.ShapeDtypeStruct((tokens, width), bf16),
             jax.ShapeDtypeStruct((examples, width, seq_len), bf16),
         ),
-        in_specs=[SMEM, VMEM, VMEM] + [VMEM] * len(received),
+        in_specs=[SMEM, VMEM, VMEM, VMEM] + [VMEM] * len(received),
         out_specs=(VMEM, VMEM, VMEM),
         compiler_params=pltpu.CompilerParams(vmem_limit_bytes=4 * MIB),
         name="factors",
-    )(lengths, mask, own, *received)
+    )(lengths, positions, mask, own, *received)
 
 
 def features_body(lengths_ref, rounded_ref, turned_ref, feats_ref):
@@ -276,7 +291,7 @@
         out_ref[...] = piece
 
 
-def pack(tests):
+def pack(tests, flops):
     rows, width = tests.shape
     feat_count = lax.axis_size("feat")
     return pl.pallas_call(
@@ -285,7 +300,7 @@
         in_specs=[VMEM],
         out_specs=[VMEM] * feat_count,
         compiler_params=pltpu.CompilerParams(vmem_limit_bytes=8 * MIB),
-        cost_estimate=pl.CostEstimate(flops=40960 * MIB, bytes_accessed=4 * MIB, transcendentals=0),
+        cost_estimate=pl.CostEstimate(flops=flops, bytes_accessed=4 * MIB, transcendentals=0),
         name="pack",
     )(tests)
 
@@ -407,26 +422,26 @@
     x = train_inputs.reshape(tokens, in_width)
     g = train_grads.reshape(tokens, out_width)
     tests = test_feats.transpose(1, 2, 0).reshape(own_rows * test_feats.shape[2], test_feats.shape[0])
-    cut = pack(tests)
+    positions = slots(seq_len)
+    far_tests = xor_permute(tests, "dp", 1)
+    own, sent = project(x, g, after(proj_in.T, positions), proj_out.T, tokens // 3)
+    cut = pack(after(tests, sent), 4 * MIB)
     near = [cut[0]] + [xor_permute(cut[mask], "feat", mask) for mask in range(1, feat_count)]
-    far = [xor_permute(near[0], "dp", 1)]
-    own, sent = project(x, g, after(proj_in.T, cut[0]), proj_out.T, tokens // 3)
-    far += [xor_permute(piece, "dp", 1) for piece in after(tuple(near[1:]), sent)]
     received = [xor_permute(sent, "feat", mask) for mask in range(1, feat_count)]
-    shared = [xor_permute(piece, "test", 1) for piece in after(tuple(near), sent)]
-    factor, rounded, turned = factors(lengths, loss_mask, own, received)
+    cut = pack(after(far_tests, *(sent,)), 4 * MIB)
+    far = [cut[0]] + [xor_permute(cut[mask], "feat", mask) for mask in range(1, feat_count)]
+    factor, rounded, turned = factors(lengths, positions, loss_mask, own, received)
     feats = [features_of(lengths, rounded, turned)]
     even_masks = range(2, dp_count, 2)
     steps = [("test", 1)] + [("dp", m) for m in reversed(masks_of(dp_count))]
     sums = [factor]
     for axis, mask in steps:
-        if len(sums) == 3:
-            sums[-1] = after(sums[-1], *shared)
         if len(sums) == len(steps):
             sums[-1] = after(sums[-1], feats[0])
         other = xor_permute(sums[-1], axis, mask)
         sums.append(sums[-1] + other)
-    pieces = near + shared + far + [xor_permute(piece, "test", 1) for piece in after(tuple(far), *(other,))]
+    shared = [xor_permute(piece, "test", 1) for piece in after(tuple(near), *(sums[2],))]
+    pieces = near + shared + far + [xor_permute(piece, "test", 1) for piece in after(tuple(far[:1]), *(other,))] + [xor_permute(piece, "test", 1) for piece in after(tuple(far[1:]), *(other,))]
     feats += [xor_permute(feats[0], "dp", mask) for mask in even_masks]
     total_tokens = float(tokens * dp_count * test_count)
     grad, in_pair = inverses(total_tokens, sums[-2], other)

time: 44.7 us -> 42.3 us (0.946)
  starting transfers between devices: 17.6 us -> 15.1 us
  local copies, waits for them, and re-layouts: 1.06 us -> 0.02 us
  waiting for transfers between devices: 13.4 us -> 14.3 us
    ppermute x13, starting transfers between devices: 17.6 us -> 15.1 us  [xor_permute(): return lax.ppermute(values, axis, [(i, i ^ mask) for i in range(size)])]
    unnamed x12, local copies, waits for them, and re-layouts: 1.06 us -> 0.02 us
    ppermute x13, waiting for transfers between devices: 13.4 us -> 14.3 us  [xor_permute(): return lax.ppermute(values, axis, [(i, i ^ mask) for i in range(size)])]
  transfers between devices with their start and end apart: 13 -> 13, of which waited for: 6 -> 6; matrix products, arithmetic and copies ran while one was open for 0% -> 0% of each run, Pallas kernels for 22% -> 25%
where the time goes in v7:
time: 42.3 us; the launch traced here: 42.2 us
  starting transfers between devices  15.1 us (36%)
  waiting for transfers between devices  14.3 us (34%)
  Pallas kernels  12.7 us (30%)
    ppermute x13, starting transfers between devices, xor_permute(): return lax.ppermute(values, axis, [(i, i ^ mask) for i in range(size)])  15.1 us
    ppermute x13, waiting for transfers between devices, xor_permute(): return lax.ppermute(values, axis, [(i, i ^ mask) for i in range(size)])  14.3 us
    pallas_call x1, Pallas kernels, project(): pl.pallas_call(functools.partial(project_body, rows), out_shape=(jax.Shap...  5.62 us
    pallas_call x1, Pallas kernels, inverses(): pl.pallas_call(functools.partial(inverses_body, total_tokens), out_shape=...  2.81 us
    pallas_call x1, Pallas kernels, scores_of(): pl.pallas_call(functools.partial(scores_body, len(feats)), out_shape=[jax...  1.52 us
  transfers between devices with their start and end apart: 13, of which 6 were waited for; matrix products, arithmetic and copies ran while one was open for 0% of the time, Pallas kernels for 25%

profile of v7, /device:TPU:0, one launch (start us, length us, event | category | flops | bytes accessed | tf_op | source)
XLA Modules:
  0.0 42.2 jit_solution(15453481675131604593)
XLA Ops:
  0.0 3.1 %collective-permute-start.7 = (bf16[2048,128]{1,0:T(8,128)(2,1)}, bf16[2048,128]{1,0:T(8,128)(2,1)S(1)}, u32[]{:S(2)}, u32[]{:S(2)}) collective-permute-start(bf16[2048,128]{1,0:T(8,128)(2,1)} %bitcast.10), channel_id=1, source_target_pairs={{0,4},{4,0},{8,12},{12,8},{1,5},{5,1},{9,13},{13,9},{2,6},{6,2},{1... | collective-permute-start | bytes 1572872 | tf_op jit(solution)/shard_map/ppermute | solution.py:22
  3.1 5.6 %project.1 = (f32[768,128]{1,0:T(8,128)S(1)}, bf16[768,128]{1,0:T(8,128)(2,1)S(1)}) custom-call(bf16[768,2048]{1,0:T(8,128)(2,1)S(1)} %bitcast.8, bf16[768,7168]{1,0:T(8,128)(2,1)} %bitcast.13, bf16[64,2048]{1,0:T(8,128)(2,1)S(1)} %bitcast.12, bf16[64,7168]{1,0:T(8,128)(2,1)S(1)} %bitcast.9), custom_call_target="tpu_custom_call" | custom-call | flops 905969664 | bytes 15335424 | tf_op jit(solution)/shard_map/project/pallas_call | solution.py:60
  8.8 2.0 %collective-permute-start = (bf16[768,128]{1,0:T(8,128)(2,1)S(1)}, bf16[768,128]{1,0:T(8,128)(2,1)S(1)}, u32[]{:S(2)}, u32[]{:S(2)}) collective-permute-start(bf16[768,128]{1,0:T(8,128)(2,1)S(1)} %get-tuple-element.28), channel_id=1, source_target_pairs={{0,2},{2,0},{1,3},{3,1},{4,6},{6,4},{5,7},{7,5},{8,10},{10,8},{9,1... | collective-permute-start | bytes 589832 | tf_op jit(solution)/shard_map/ppermute | solution.py:22
  10.7 0.2 pack.2
  11.0 0.2 collective-permute-start.4
  11.2 4.1 %collective-permute-done.7.tests_ref = bf16[2048,128]{1,0:T(8,128)(2,1)S(1)} collective-permute-done((bf16[2048,128]{1,0:T(8,128)(2,1)}, bf16[2048,128]{1,0:T(8,128)(2,1)S(1)}, u32[]{:S(2)}, u32[]{:S(2)}) %collective-permute-start.7) | collective-permute-done | bytes 524320 | tf_op jit(solution)/shard_map/ppermute | solution.py:22
  15.2 0.2 pack.3
  15.5 1.7 %collective-permute-start.8 = (bf16[1024,128]{1,0:T(8,128)(2,1)S(1)}, bf16[1024,128]{1,0:T(8,128)(2,1)S(1)}, u32[]{:S(2)}, u32[]{:S(2)}) collective-permute-start(bf16[1024,128]{1,0:T(8,128)(2,1)S(1)} %get-tuple-element.42), channel_id=1, source_target_pairs={{0,2},{2,0},{1,3},{3,1},{4,6},{6,4},{5,7},{7,5},{8,10},{10,8},{9,1... | collective-permute-start | bytes 786440 | tf_op jit(solution)/shard_map/ppermute | solution.py:22
  17.2 0.8 %factors.1 = (f32[64,128]{1,0:T(8,128)S(1)}, bf16[768,128]{1,0:T(8,128)(2,1)S(1)}, bf16[8,128,96]{2,1,0:T(8,128)(2,1)S(1)}) custom-call(s32[8]{0:T(128)S(1)} %copy-done.5, s32[1,96]{1,0:T(1,128)S(1)} %slots.1.positions_ref, s32[8,96]{1,0:T(8,128)S(1)} %copy-done.4, f32[768,128]{1,0:T(8,128)S(1)} %get-tuple-element.27.own_ref, ...), custom_call_target="tpu_custom_call" | custom-call | tf_op jit(solution)/shard_map/factors/pallas_call | solution.py:136
  18.1 1.2 %collective-permute-done.1 = f32[64,128]{1,0:T(8,128)S(1)} collective-permute-done((f32[64,128]{1,0:T(8,128)S(1)}, f32[64,128]{1,0:T(8,128)S(1)}, u32[]{:S(2)}, u32[]{:S(2)}) %collective-permute-start.1) | collective-permute-done | bytes 32800 | tf_op jit(solution)/shard_map/ppermute | solution.py:22
  19.3 2.6 %collective-permute-start.2 = (f32[64,128]{1,0:T(8,128)S(1)}, f32[64,128]{1,0:T(8,128)S(1)}, u32[]{:S(2)}, u32[]{:S(2)}) collective-permute-start(f32[64,128]{1,0:T(8,128)S(1)} %add.6), channel_id=1, source_target_pairs={{0,8},{4,12},{8,0},{12,4},{1,9},{5,13},{9,1},{13,5},{2,10},{6,14},... | collective-permute-start | bytes 98312 | tf_op jit(solution)/shard_map/ppermute | solution.py:22
  21.9 0.8 %features.1.refs_8_ = bf16[4,64,128]{2,1,0:T(8,128)(2,1)S(1)} custom-call(s32[8]{0:T(128)S(1)} %copy-done.5, bf16[768,128]{1,0:T(8,128)(2,1)S(1)} %get-tuple-element.30.rounded_ref, bf16[8,128,96]{2,1,0:T(8,128)(2,1)S(1)} %get-tuple-element.31.turned_ref), custom_call_target="tpu_custom_call" | custom-call | flops 25165824 | bytes 8388608 | tf_op jit(solution)/shard_map/features/pallas_call | solution.py:168
  22.7 1.8 %collective-permute-done.2 = f32[64,128]{1,0:T(8,128)S(1)} collective-permute-done((f32[64,128]{1,0:T(8,128)S(1)}, f32[64,128]{1,0:T(8,128)S(1)}, u32[]{:S(2)}, u32[]{:S(2)}) %collective-permute-start.2) | collective-permute-done | bytes 32800 | tf_op jit(solution)/shard_map/ppermute | solution.py:22
  24.5 1.2 %collective-permute-start.3 = (f32[64,128]{1,0:T(8,128)S(1)}, f32[64,128]{1,0:T(8,128)S(1)}, u32[]{:S(2)}, u32[]{:S(2)}) collective-permute-start(f32[64,128]{1,0:T(8,128)S(1)} %add.7.factor_a_ref), channel_id=1, source_target_pairs={{0,4},{4,0},{8,12},{12,8},{1,5},{5,1},{9,13},{13,9},{2,6},{6,2},{1... | collective-permute-start | bytes 98312 | tf_op jit(solution)/shard_map/ppermute | solution.py:22
  25.7 0.5 %collective-permute-start.6 = (bf16[1024,128]{1,0:T(8,128)(2,1)S(1)}, bf16[1024,128]{1,0:T(8,128)(2,1)S(1)}, u32[]{:S(2)}, u32[]{:S(2)}) collective-permute-start(bf16[1024,128]{1,0:T(8,128)(2,1)S(1)} %collective-permute-done.4.refs_1_), channel_id=1, source_target_pairs={{0,1},{1,0},{2,3},{3,2},{4,5},{5,4},{6,7},{7,6},{8,9},{9,8},{10,11... | collective-permute-start | bytes 786440 | tf_op jit(solution)/shard_map/ppermute | solution.py:22
  26.2 2.2 %collective-permute-done.3.factor_b_ref = f32[64,128]{1,0:T(8,128)S(1)} collective-permute-done((f32[64,128]{1,0:T(8,128)S(1)}, f32[64,128]{1,0:T(8,128)S(1)}, u32[]{:S(2)}, u32[]{:S(2)}) %collective-permute-start.3) | collective-permute-done | bytes 32800 | tf_op jit(solution)/shard_map/ppermute | solution.py:22
  28.4 0.5 %collective-permute-start.10 = (bf16[1024,128]{1,0:T(8,128)(2,1)S(1)}, bf16[1024,128]{1,0:T(8,128)(2,1)S(1)}, u32[]{:S(2)}, u32[]{:S(2)}) collective-permute-start(bf16[1024,128]{1,0:T(8,128)(2,1)S(1)} %collective-permute-done.8.refs_5_), channel_id=1, source_target_pairs={{0,1},{1,0},{2,3},{3,2},{4,5},{5,4},{6,7},{7,6},{8,9},{9,8},{10,11... | collective-permute-start | bytes 786440 | tf_op jit(solution)/shard_map/ppermute | solution.py:22
  28.9 2.2 %collective-permute-start.11 = (bf16[4,64,128]{2,1,0:T(8,128)(2,1)S(1)}, bf16[4,64,128]{2,1,0:T(8,128)(2,1)S(1)}, u32[]{:S(2)}, u32[]{:S(2)}) collective-permute-start(bf16[4,64,128]{2,1,0:T(8,128)(2,1)S(1)} %features.1.refs_8_), channel_id=1, source_target_pairs={{0,8},{4,12},{8,0},{12,4},{1,9},{5,13},{9,1},{13,5},{2,10},{6,14},... | collective-permute-start | bytes 196616 | tf_op jit(solution)/shard_map/ppermute | solution.py:22
  31.2 2.8 %inverses.1 = (bf16[2,64,64]{2,1,0:T(8,128)(2,1)S(1)}, bf16[2,128,128]{2,1,0:T(8,128)(2,1)S(1)}) custom-call(f32[64,128]{1,0:T(8,128)S(1)} %add.7.factor_a_ref, f32[64,128]{1,0:T(8,128)S(1)} %collective-permute-done.3.factor_b_ref), custom_call_target="tpu_custom_call" | custom-call | tf_op jit(solution)/shard_map/inverses/pallas_call | solution.py:263
  34.0 1.4 %collective-permute-done.11.refs_9_ = bf16[4,64,128]{2,1,0:T(8,128)(2,1)S(1)} collective-permute-done((bf16[4,64,128]{2,1,0:T(8,128)(2,1)S(1)}, bf16[4,64,128]{2,1,0:T(8,128)(2,1)S(1)}, u32[]{:S(2)}, u32[]{:S(2)}) %collective-permute-start.11) | collective-permute-done | bytes 65568 | tf_op jit(solution)/shard_map/ppermute | solution.py:22
  35.4 1.5 %scores.1 = (f32[2,8,128]{2,1,0:T(8,128)S(1)}, f32[2,8,128]{2,1,0:T(8,128)S(1)}) custom-call(bf16[2,64,64]{2,1,0:T(8,128)(2,1)S(1)} %get-tuple-element.33.grad_ref, bf16[2,128,128]{2,1,0:T(8,128)(2,1)S(1)} %get-tuple-element.34.in_ref, bf16[1024,128]{1,0:T(8,128)(2,1)S(1)} %get-tuple-element.38.refs_0_, ...), custom_call_target="tpu_custom_call" | custom-call | tf_op jit(solution)/shard_map/scores/pallas_call | solution.py:366
  36.9 1.0 %collective-permute-start.12 = (f32[2,8,128]{2,1,0:T(8,128)S(1)}, f32[2,8,128]{2,1,0:T(8,128)S(1)}, u32[]{:S(2)}, u32[]{:S(2)}) collective-permute-start(f32[2,8,128]{2,1,0:T(8,128)S(1)} %get-tuple-element.46), channel_id=1, source_target_pairs={{0,8},{4,12},{8,0},{12,4},{1,9},{5,13},{9,1},{13,5},{2,10},{6,14},... | collective-permute-start | bytes 24584 | tf_op jit(solution)/shard_map/ppermute | solution.py:22
  37.9 3.6 %collective-permute-done.12.refs_1_ = f32[2,8,128]{2,1,0:T(8,128)S(1)} collective-permute-done((f32[2,8,128]{2,1,0:T(8,128)S(1)}, f32[2,8,128]{2,1,0:T(8,128)S(1)}, u32[]{:S(2)}, u32[]{:S(2)}) %collective-permute-start.12) | collective-permute-done | bytes 8224 | tf_op jit(solution)/shard_map/ppermute | solution.py:22
  41.5 0.7 %finish.1 = f32[64,64]{1,0:T(8,128)} custom-call(f32[2,8,128]{2,1,0:T(8,128)S(1)} %get-tuple-element.45.refs_0_, f32[2,8,128]{2,1,0:T(8,128)S(1)} %collective-permute-done.12.refs_1_), custom_call_target="tpu_custom_call" | custom-call | tf_op jit(solution)/shard_map/finish/pallas_call | solution.py:399
  (25 shorter events, 0.1 us)
Async XLA Ops:
  0.0 3.1 %copy-start = (bf16[8,96,2048]{2,1,0:T(8,128)(2,1)S(1)}, bf16[8,96,2048]{2,1,0:T(8,128)(2,1)}, u32[]{:S(2)}) copy-start(bf16[8,96,2048]{2,1,0:T(8,128)(2,1)} %param.7) | copy-start | bytes 9437188
  0.0 3.1 %copy-start.1 = (bf16[7168,64]{0,1:T(8,128)(2,1)S(1)}, bf16[7168,64]{0,1:T(8,128)(2,1)}, u32[]{:S(2)}) copy-start(bf16[7168,64]{0,1:T(8,128)(2,1)} %param.10) | copy-start | bytes 2752516
  0.0 3.1 %copy-start.3 = (bf16[2048,64]{0,1:T(8,128)(2,1)S(1)}, bf16[2048,64]{0,1:T(8,128)(2,1)}, u32[]{:S(2)}) copy-start(bf16[2048,64]{0,1:T(8,128)(2,1)} %param.9) | copy-start | bytes 786436
  0.0 15.2 %collective-permute-start.7 = (bf16[2048,128]{1,0:T(8,128)(2,1)}, bf16[2048,128]{1,0:T(8,128)(2,1)S(1)}, u32[]{:S(2)}, u32[]{:S(2)}) collective-permute-start(bf16[2048,128]{1,0:T(8,128)(2,1)} %bitcast.10), channel_id=1, source_target_pairs={{0,4},{4,0},{8,12},{12,8},{1,5},{5,1},{9,13},{13,9},{2,6},{6,2},{1... | collective-permute-start | bytes 1572872 | tf_op jit(solution)/shard_map/ppermute | solution.py:22
  3.1 7.6 %copy-start.2 = (bf16[128,32,64]{0,2,1:T(8,128)(2,1)S(1)}, bf16[128,32,64]{0,2,1:T(8,128)(2,1)}, u32[]{:S(2)}) copy-start(bf16[128,32,64]{0,2,1:T(8,128)(2,1)} %param.13) | copy-start | bytes 1572868
  3.1 14.1 %copy-start.4 = (s32[8,96]{1,0:T(8,128)S(1)}, s32[8,96]{1,0:T(8,128)}, u32[]{:S(2)}) copy-start(s32[8,96]{1,0:T(8,128)} %mask_ref.1) | copy-start | bytes 9220
  3.1 14.1 %copy-start.5 = (s32[8]{0:T(128)S(1)}, s32[8]{0:T(128)}, u32[]{:S(2)}) copy-start(s32[8]{0:T(128)} %lengths_ref.3) | copy-start | bytes 100
  8.8 8.4 %collective-permute-start = (bf16[768,128]{1,0:T(8,128)(2,1)S(1)}, bf16[768,128]{1,0:T(8,128)(2,1)S(1)}, u32[]{:S(2)}, u32[]{:S(2)}) collective-permute-start(bf16[768,128]{1,0:T(8,128)(2,1)S(1)} %get-tuple-element.28), channel_id=1, source_target_pairs={{0,2},{2,0},{1,3},{3,1},{4,6},{6,4},{5,7},{7,5},{8,10},{10,8},{9,1... | collective-permute-start | bytes 589832 | tf_op jit(solution)/shard_map/ppermute | solution.py:22
  11.0 14.7 %collective-permute-start.4 = (bf16[1024,128]{1,0:T(8,128)(2,1)S(1)}, bf16[1024,128]{1,0:T(8,128)(2,1)S(1)}, u32[]{:S(2)}, u32[]{:S(2)}) collective-permute-start(bf16[1024,128]{1,0:T(8,128)(2,1)S(1)} %get-tuple-element.37), channel_id=1, source_target_pairs={{0,2},{2,0},{1,3},{3,1},{4,6},{6,4},{5,7},{7,5},{8,10},{10,8},{9,1... | collective-permute-start | bytes 786440 | tf_op jit(solution)/shard_map/ppermute | solution.py:22
  15.5 12.9 %collective-permute-start.8 = (bf16[1024,128]{1,0:T(8,128)(2,1)S(1)}, bf16[1024,128]{1,0:T(8,128)(2,1)S(1)}, u32[]{:S(2)}, u32[]{:S(2)}) collective-permute-start(bf16[1024,128]{1,0:T(8,128)(2,1)S(1)} %get-tuple-element.42), channel_id=1, source_target_pairs={{0,2},{2,0},{1,3},{3,1},{4,6},{6,4},{5,7},{7,5},{8,10},{10,8},{9,1... | collective-permute-start | bytes 786440 | tf_op jit(solution)/shard_map/ppermute | solution.py:22
  18.0 1.3 %collective-permute-start.1 = (f32[64,128]{1,0:T(8,128)S(1)}, f32[64,128]{1,0:T(8,128)S(1)}, u32[]{:S(2)}, u32[]{:S(2)}) collective-permute-start(f32[64,128]{1,0:T(8,128)S(1)} %get-tuple-element.29), channel_id=1, source_target_pairs={{0,1},{1,0},{2,3},{3,2},{4,5},{5,4},{6,7},{7,6},{8,9},{9,8},{10,11... | collective-permute-start | bytes 98312 | tf_op jit(solution)/shard_map/ppermute | solution.py:22
  19.3 5.2 %collective-permute-start.2 = (f32[64,128]{1,0:T(8,128)S(1)}, f32[64,128]{1,0:T(8,128)S(1)}, u32[]{:S(2)}, u32[]{:S(2)}) collective-permute-start(f32[64,128]{1,0:T(8,128)S(1)} %add.6), channel_id=1, source_target_pairs={{0,8},{4,12},{8,0},{12,4},{1,9},{5,13},{9,1},{13,5},{2,10},{6,14},... | collective-permute-start | bytes 98312 | tf_op jit(solution)/shard_map/ppermute | solution.py:22
  24.5 3.9 %collective-permute-start.3 = (f32[64,128]{1,0:T(8,128)S(1)}, f32[64,128]{1,0:T(8,128)S(1)}, u32[]{:S(2)}, u32[]{:S(2)}) collective-permute-start(f32[64,128]{1,0:T(8,128)S(1)} %add.7.factor_a_ref), channel_id=1, source_target_pairs={{0,4},{4,0},{8,12},{12,8},{1,5},{5,1},{9,13},{13,9},{2,6},{6,2},{1... | collective-permute-start | bytes 98312 | tf_op jit(solution)/shard_map/ppermute | solution.py:22
  25.7 9.7 %collective-permute-start.5 = (bf16[1024,128]{1,0:T(8,128)(2,1)S(1)}, bf16[1024,128]{1,0:T(8,128)(2,1)S(1)}, u32[]{:S(2)}, u32[]{:S(2)}) collective-permute-start(bf16[1024,128]{1,0:T(8,128)(2,1)S(1)} %get-tuple-element.38.refs_0_), channel_id=1, source_target_pairs={{0,1},{1,0},{2,3},{3,2},{4,5},{5,4},{6,7},{7,6},{8,9},{9,8},{10,11... | collective-permute-start | bytes 786440 | tf_op jit(solution)/shard_map/ppermute | solution.py:22
  25.7 9.7 %collective-permute-start.6 = (bf16[1024,128]{1,0:T(8,128)(2,1)S(1)}, bf16[1024,128]{1,0:T(8,128)(2,1)S(1)}, u32[]{:S(2)}, u32[]{:S(2)}) collective-permute-start(bf16[1024,128]{1,0:T(8,128)(2,1)S(1)} %collective-permute-done.4.refs_1_), channel_id=1, source_target_pairs={{0,1},{1,0},{2,3},{3,2},{4,5},{5,4},{6,7},{7,6},{8,9},{9,8},{10,11... | collective-permute-start | bytes 786440 | tf_op jit(solution)/shard_map/ppermute | solution.py:22
  28.4 7.0 %collective-permute-start.9 = (bf16[1024,128]{1,0:T(8,128)(2,1)S(1)}, bf16[1024,128]{1,0:T(8,128)(2,1)S(1)}, u32[]{:S(2)}, u32[]{:S(2)}) collective-permute-start(bf16[1024,128]{1,0:T(8,128)(2,1)S(1)} %get-tuple-element.43.refs_4_), channel_id=1, source_target_pairs={{0,1},{1,0},{2,3},{3,2},{4,5},{5,4},{6,7},{7,6},{8,9},{9,8},{10,11... | collective-permute-start | bytes 786440 | tf_op jit(solution)/shard_map/ppermute | solution.py:22
  28.4 7.0 %collective-permute-start.10 = (bf16[1024,128]{1,0:T(8,128)(2,1)S(1)}, bf16[1024,128]{1,0:T(8,128)(2,1)S(1)}, u32[]{:S(2)}, u32[]{:S(2)}) collective-permute-start(bf16[1024,128]{1,0:T(8,128)(2,1)S(1)} %collective-permute-done.8.refs_5_), channel_id=1, source_target_pairs={{0,1},{1,0},{2,3},{3,2},{4,5},{5,4},{6,7},{7,6},{8,9},{9,8},{10,11... | collective-permute-start | bytes 786440 | tf_op jit(solution)/shard_map/ppermute | solution.py:22
  28.9 6.4 %collective-permute-start.11 = (bf16[4,64,128]{2,1,0:T(8,128)(2,1)S(1)}, bf16[4,64,128]{2,1,0:T(8,128)(2,1)S(1)}, u32[]{:S(2)}, u32[]{:S(2)}) collective-permute-start(bf16[4,64,128]{2,1,0:T(8,128)(2,1)S(1)} %features.1.refs_8_), channel_id=1, source_target_pairs={{0,8},{4,12},{8,0},{12,4},{1,9},{5,13},{9,1},{13,5},{2,10},{6,14},... | collective-permute-start | bytes 196616 | tf_op jit(solution)/shard_map/ppermute | solution.py:22
  36.9 4.6 %collective-permute-start.12 = (f32[2,8,128]{2,1,0:T(8,128)S(1)}, f32[2,8,128]{2,1,0:T(8,128)S(1)}, u32[]{:S(2)}, u32[]{:S(2)}) collective-permute-start(f32[2,8,128]{2,1,0:T(8,128)S(1)} %get-tuple-element.46), channel_id=1, source_target_pairs={{0,8},{4,12},{8,0},{12,4},{1,9},{5,13},{9,1},{13,5},{2,10},{6,14},... | collective-permute-start | bytes 24584 | tf_op jit(solution)/shard_map/ppermute | solution.py:22

commit v8 on v7

--- a/solution.py
+++ b/solution.py
@@ -269,7 +269,7 @@
         in_specs=[VMEM, VMEM],
         out_specs=(VMEM, VMEM),
         compiler_params=pltpu.CompilerParams(vmem_limit_bytes=4 * MIB),
-        cost_estimate=pl.CostEstimate(flops=0, bytes_accessed=0, transcendentals=0),
+        cost_estimate=pl.CostEstimate(flops=16384 * MIB, bytes_accessed=0, transcendentals=0),
         name="inverses",
     )(factor_a, factor_b)
 
@@ -305,10 +305,14 @@
     )(tests)
 
 
-def scores_body(blocks, grad_ref, in_ref, *refs):
+def scores_body(blocks, piece_counts, grad_ref, in_ref, *refs):
     feat_count = lax.axis_size("feat")
     feat = lax.axis_index("feat")
-    pieces, refs = refs[: 4 * feat_count], refs[4 * feat_count :]
+    counts, pieces = piece_counts, []
+    for count in counts:
+        rows = refs[0].shape[0] // count
+        pieces += [refs[0].at[pl.ds(rows * i, rows), :] for i in range(count)]
+        refs = refs[1:]
     feats_refs, out_refs, (solved_buf, line_buf) = refs[:blocks], refs[blocks : 2 * blocks], refs[2 * blocks :]
     rank = grad_ref.shape[1]
     pairs = [ref[i] for ref in feats_refs for i in range(ref.shape[0])]
@@ -357,14 +361,14 @@
             out_ref[odd ^ dp_bit, half:, :] = both[count + at * half : count + (at + 1) * half, :]
 
 
-def scores_of(grad, in_pair, pieces, feats):
+def scores_of(grad, in_pair, pieces, piece_counts, feats):
     feat_count = lax.axis_size("feat")
     rank = grad.shape[1]
-    fold, width = pieces[0].shape
+    fold, width = pieces[0].shape[0] // piece_counts[0], pieces[0].shape[1]
     half = feats[0].shape[0]
     count = half * len(feats)
     return pl.pallas_call(
-        functools.partial(scores_body, len(feats)),
+        functools.partial(scores_body, len(feats), piece_counts),
         out_shape=[jax.ShapeDtypeStruct((2, 2 * half, 2 * width // feat_count), f32)] * len(feats),
         in_specs=[VMEM] * (2 + len(pieces) + len(feats)),
         out_specs=[VMEM] * len(feats),
@@ -440,12 +444,15 @@
             sums[-1] = after(sums[-1], feats[0])
         other = xor_permute(sums[-1], axis, mask)
         sums.append(sums[-1] + other)
-    shared = [xor_permute(piece, "test", 1) for piece in after(tuple(near), *(sums[2],))]
-    pieces = near + shared + far + [xor_permute(piece, "test", 1) for piece in after(tuple(far[:1]), *(other,))] + [xor_permute(piece, "test", 1) for piece in after(tuple(far[1:]), *(other,))]
+    pieces, piece_counts = [], []
+    pieces += near + [xor_permute(piece, "test", 1) for piece in after(tuple(near), *(sums[2],))]
+    piece_counts += [1] * (2 * feat_count)
+    pieces += far + [xor_permute(jnp.concatenate(after(tuple(far), *(other,)), axis=0), "test", 1)]
+    piece_counts += [1] * feat_count + [feat_count]
     feats += [xor_permute(feats[0], "dp", mask) for mask in even_masks]
     total_tokens = float(tokens * dp_count * test_count)
     grad, in_pair = inverses(total_tokens, sums[-2], other)
-    blocks = scores_of(grad, in_pair, pieces, feats)
+    blocks = scores_of(grad, in_pair, pieces, piece_counts, feats)
     blocks = [blocks[0]] + [xor_permute(blocks[at + 1], "dp", mask) for at, mask in enumerate(even_masks)]
     return finish(blocks)
 

time: 42.3 us -> 39 us (0.922)
  waiting for transfers between devices: 14.3 us -> 9.93 us
  starting transfers between devices: 15.1 us -> 16 us
    ppermute x13 -> x12, waiting for transfers between devices: 14.3 us -> 9.93 us  [xor_permute(): return lax.ppermute(values, axis, [(i, i ^ mask) for i in range(size)])]
    ppermute x13 -> x12, starting transfers between devices: 15.1 us -> 16 us  [xor_permute(): return lax.ppermute(values, axis, [(i, i ^ mask) for i in range(size)])]
  transfers between devices with their start and end apart: 13 -> 12, of which waited for: 6 -> 4; matrix products, arithmetic and copies ran while one was open for 0% -> 0% of each run, Pallas kernels for 25% -> 27%
where the time goes in v8:
time: 39 us; the launch traced here: 38.8 us
  starting transfers between devices  16 us (41%)
  Pallas kernels  12.7 us (33%)
  waiting for transfers between devices  9.93 us (25%)
    ppermute x12, starting transfers between devices, xor_permute(): return lax.ppermute(values, axis, [(i, i ^ mask) for i in range(size)])  16 us
    ppermute x12, waiting for transfers between devices, xor_permute(): return lax.ppermute(values, axis, [(i, i ^ mask) for i in range(size)])  9.93 us
    pallas_call x1, Pallas kernels, project(): pl.pallas_call(functools.partial(project_body, rows), out_shape=(jax.Shap...  5.62 us
    pallas_call x1, Pallas kernels, inverses(): pl.pallas_call(functools.partial(inverses_body, total_tokens), out_shape=...  2.81 us
    pallas_call x1, Pallas kernels, scores_of(): pl.pallas_call(functools.partial(scores_body, len(feats), piece_counts),...  1.53 us
    pallas_call x1, Pallas kernels, factors(): pl.pallas_call(functools.partial(factors_body, len(received)), out_shape=...  0.84 us
    pallas_call x1, Pallas kernels, features_of(): pl.pallas_call(features_body, out_shape=jax.ShapeDtypeStruct((examples //...  0.79 us
  transfers between devices with their start and end apart: 12, of which 4 were waited for; matrix products, arithmetic and copies ran while one was open for 0% of the time, Pallas kernels for 27%

profile of v8, /device:TPU:0, one launch (start us, length us, event | category | flops | bytes accessed | tf_op | source)
XLA Modules:
  0.0 38.8 jit_solution(14579602196375173820)
XLA Ops:
  0.0 3.1 %collective-permute-start.7 = (bf16[2048,128]{1,0:T(8,128)(2,1)}, bf16[2048,128]{1,0:T(8,128)(2,1)S(1)}, u32[]{:S(2)}, u32[]{:S(2)}) collective-permute-start(bf16[2048,128]{1,0:T(8,128)(2,1)} %bitcast.10), channel_id=1, source_target_pairs={{0,4},{4,0},{8,12},{12,8},{1,5},{5,1},{9,13},{13,9},{2,6},{6,2},{1... | collective-permute-start | bytes 1572872 | tf_op jit(solution)/shard_map/ppermute | solution.py:22
  3.1 5.6 %project.1 = (f32[768,128]{1,0:T(8,128)S(1)}, bf16[768,128]{1,0:T(8,128)(2,1)S(1)}) custom-call(bf16[768,2048]{1,0:T(8,128)(2,1)S(1)} %bitcast.8, bf16[768,7168]{1,0:T(8,128)(2,1)} %bitcast.13, bf16[64,2048]{1,0:T(8,128)(2,1)S(1)} %bitcast.12, bf16[64,7168]{1,0:T(8,128)(2,1)S(1)} %bitcast.9), custom_call_target="tpu_custom_call" | custom-call | flops 905969664 | bytes 15335424 | tf_op jit(solution)/shard_map/project/pallas_call | solution.py:60
  8.8 2.0 %collective-permute-start = (bf16[768,128]{1,0:T(8,128)(2,1)S(1)}, bf16[768,128]{1,0:T(8,128)(2,1)S(1)}, u32[]{:S(2)}, u32[]{:S(2)}) collective-permute-start(bf16[768,128]{1,0:T(8,128)(2,1)S(1)} %get-tuple-element.28), channel_id=1, source_target_pairs={{0,2},{2,0},{1,3},{3,1},{4,6},{6,4},{5,7},{7,5},{8,10},{10,8},{9,1... | collective-permute-start | bytes 589832 | tf_op jit(solution)/shard_map/ppermute | solution.py:22
  10.7 0.2 pack.2
  11.0 0.2 collective-permute-start.4
  11.2 4.1 %collective-permute-done.7.tests_ref = bf16[2048,128]{1,0:T(8,128)(2,1)S(1)} collective-permute-done((bf16[2048,128]{1,0:T(8,128)(2,1)}, bf16[2048,128]{1,0:T(8,128)(2,1)S(1)}, u32[]{:S(2)}, u32[]{:S(2)}) %collective-permute-start.7) | collective-permute-done | bytes 524320 | tf_op jit(solution)/shard_map/ppermute | solution.py:22
  15.2 0.2 pack.3
  15.5 1.7 %collective-permute-start.8 = (bf16[1024,128]{1,0:T(8,128)(2,1)S(1)}, bf16[1024,128]{1,0:T(8,128)(2,1)S(1)}, u32[]{:S(2)}, u32[]{:S(2)}) collective-permute-start(bf16[1024,128]{1,0:T(8,128)(2,1)S(1)} %get-tuple-element.42), channel_id=1, source_target_pairs={{0,2},{2,0},{1,3},{3,1},{4,6},{6,4},{5,7},{7,5},{8,10},{10,8},{9,1... | collective-permute-start | bytes 786440 | tf_op jit(solution)/shard_map/ppermute | solution.py:22
  17.2 0.0 collective-permute-done.refs_0_
  17.2 0.8 %factors.1 = (f32[64,128]{1,0:T(8,128)S(1)}, bf16[768,128]{1,0:T(8,128)(2,1)S(1)}, bf16[8,128,96]{2,1,0:T(8,128)(2,1)S(1)}) custom-call(s32[8]{0:T(128)S(1)} %copy-done.5, s32[1,96]{1,0:T(1,128)S(1)} %slots.1.positions_ref, s32[8,96]{1,0:T(8,128)S(1)} %copy-done.4, f32[768,128]{1,0:T(8,128)S(1)} %get-tuple-element.27.own_ref, ...), custom_call_target="tpu_custom_call" | custom-call | tf_op jit(solution)/shard_map/factors/pallas_call | solution.py:136
  18.0 0.1 collective-permute-start.1
  18.1 1.2 %collective-permute-done.1 = f32[64,128]{1,0:T(8,128)S(1)} collective-permute-done((f32[64,128]{1,0:T(8,128)S(1)}, f32[64,128]{1,0:T(8,128)S(1)}, u32[]{:S(2)}, u32[]{:S(2)}) %collective-permute-start.1) | collective-permute-done | bytes 32800 | tf_op jit(solution)/shard_map/ppermute | solution.py:22
  19.3 2.6 %collective-permute-start.2 = (f32[64,128]{1,0:T(8,128)S(1)}, f32[64,128]{1,0:T(8,128)S(1)}, u32[]{:S(2)}, u32[]{:S(2)}) collective-permute-start(f32[64,128]{1,0:T(8,128)S(1)} %add.6), channel_id=1, source_target_pairs={{0,8},{4,12},{8,0},{12,4},{1,9},{5,13},{9,1},{13,5},{2,10},{6,14},... | collective-permute-start | bytes 98312 | tf_op jit(solution)/shard_map/ppermute | solution.py:22
  21.9 0.8 %features.1.refs_7_ = bf16[4,64,128]{2,1,0:T(8,128)(2,1)S(1)} custom-call(s32[8]{0:T(128)S(1)} %copy-done.5, bf16[768,128]{1,0:T(8,128)(2,1)S(1)} %get-tuple-element.30.rounded_ref, bf16[8,128,96]{2,1,0:T(8,128)(2,1)S(1)} %get-tuple-element.31.turned_ref), custom_call_target="tpu_custom_call" | custom-call | flops 25165824 | bytes 8388608 | tf_op jit(solution)/shard_map/features/pallas_call | solution.py:168
  22.7 1.8 %collective-permute-done.2 = f32[64,128]{1,0:T(8,128)S(1)} collective-permute-done((f32[64,128]{1,0:T(8,128)S(1)}, f32[64,128]{1,0:T(8,128)S(1)}, u32[]{:S(2)}, u32[]{:S(2)}) %collective-permute-start.2) | collective-permute-done | bytes 32800 | tf_op jit(solution)/shard_map/ppermute | solution.py:22
  24.5 1.2 %collective-permute-start.3 = (f32[64,128]{1,0:T(8,128)S(1)}, f32[64,128]{1,0:T(8,128)S(1)}, u32[]{:S(2)}, u32[]{:S(2)}) collective-permute-start(f32[64,128]{1,0:T(8,128)S(1)} %add.7.factor_a_ref), channel_id=1, source_target_pairs={{0,4},{4,0},{8,12},{12,8},{1,5},{5,1},{9,13},{13,9},{2,6},{6,2},{1... | collective-permute-start | bytes 98312 | tf_op jit(solution)/shard_map/ppermute | solution.py:22
  25.7 2.8 %collective-permute-start.10 = (bf16[4,64,128]{2,1,0:T(8,128)(2,1)S(1)}, bf16[4,64,128]{2,1,0:T(8,128)(2,1)S(1)}, u32[]{:S(2)}, u32[]{:S(2)}) collective-permute-start(bf16[4,64,128]{2,1,0:T(8,128)(2,1)S(1)} %features.1.refs_7_), channel_id=1, source_target_pairs={{0,8},{4,12},{8,0},{12,4},{1,9},{5,13},{9,1},{13,5},{2,10},{6,14},... | collective-permute-start | bytes 196616 | tf_op jit(solution)/shard_map/ppermute | solution.py:22
  28.5 0.5 %collective-permute-start.6 = (bf16[1024,128]{1,0:T(8,128)(2,1)S(1)}, bf16[1024,128]{1,0:T(8,128)(2,1)S(1)}, u32[]{:S(2)}, u32[]{:S(2)}) collective-permute-start(bf16[1024,128]{1,0:T(8,128)(2,1)S(1)} %collective-permute-done.4.refs_1_), channel_id=1, source_target_pairs={{0,1},{1,0},{2,3},{3,2},{4,5},{5,4},{6,7},{7,6},{8,9},{9,8},{10,11... | collective-permute-start | bytes 786440 | tf_op jit(solution)/shard_map/ppermute | solution.py:22
  29.1 0.1 collective-permute-start.9
  29.2 2.8 %inverses.1 = (bf16[2,64,64]{2,1,0:T(8,128)(2,1)S(1)}, bf16[2,128,128]{2,1,0:T(8,128)(2,1)S(1)}) custom-call(f32[64,128]{1,0:T(8,128)S(1)} %add.7.factor_a_ref, f32[64,128]{1,0:T(8,128)S(1)} %collective-permute-done.3.factor_b_ref), custom_call_target="tpu_custom_call" | custom-call | flops 17179869184 | tf_op jit(solution)/shard_map/inverses/pallas_call | solution.py:263
  32.0 1.5 %scores.1 = (f32[2,8,128]{2,1,0:T(8,128)S(1)}, f32[2,8,128]{2,1,0:T(8,128)S(1)}) custom-call(bf16[2,64,64]{2,1,0:T(8,128)(2,1)S(1)} %get-tuple-element.33.grad_ref, bf16[2,128,128]{2,1,0:T(8,128)(2,1)S(1)} %get-tuple-element.34.in_ref, bf16[1024,128]{1,0:T(8,128)(2,1)S(1)} %get-tuple-element.38.refs_0_, ...), custom_call_target="tpu_custom_call" | custom-call | tf_op jit(solution)/shard_map/scores/pallas_call | solution.py:370
  33.6 1.7 %collective-permute-start.11 = (f32[2,8,128]{2,1,0:T(8,128)S(1)}, f32[2,8,128]{2,1,0:T(8,128)S(1)}, u32[]{:S(2)}, u32[]{:S(2)}) collective-permute-start(f32[2,8,128]{2,1,0:T(8,128)S(1)} %get-tuple-element.46), channel_id=1, source_target_pairs={{0,8},{4,12},{8,0},{12,4},{1,9},{5,13},{9,1},{13,5},{2,10},{6,14},... | collective-permute-start | bytes 24584 | tf_op jit(solution)/shard_map/ppermute | solution.py:22
  35.3 2.8 %collective-permute-done.11.refs_1_ = f32[2,8,128]{2,1,0:T(8,128)S(1)} collective-permute-done((f32[2,8,128]{2,1,0:T(8,128)S(1)}, f32[2,8,128]{2,1,0:T(8,128)S(1)}, u32[]{:S(2)}, u32[]{:S(2)}) %collective-permute-start.11) | collective-permute-done | bytes 8224 | tf_op jit(solution)/shard_map/ppermute | solution.py:22
  38.1 0.7 %finish.1 = f32[64,64]{1,0:T(8,128)} custom-call(f32[2,8,128]{2,1,0:T(8,128)S(1)} %get-tuple-element.45.refs_0_, f32[2,8,128]{2,1,0:T(8,128)S(1)} %collective-permute-done.11.refs_1_), custom_call_target="tpu_custom_call" | custom-call | tf_op jit(solution)/shard_map/finish/pallas_call | solution.py:403
  (24 shorter events, 0.1 us)
Async XLA Ops:
  0.0 3.1 %copy-start = (bf16[8,96,2048]{2,1,0:T(8,128)(2,1)S(1)}, bf16[8,96,2048]{2,1,0:T(8,128)(2,1)}, u32[]{:S(2)}) copy-start(bf16[8,96,2048]{2,1,0:T(8,128)(2,1)} %param.7) | copy-start | bytes 9437188
  0.0 3.1 %copy-start.1 = (bf16[7168,64]{0,1:T(8,128)(2,1)S(1)}, bf16[7168,64]{0,1:T(8,128)(2,1)}, u32[]{:S(2)}) copy-start(bf16[7168,64]{0,1:T(8,128)(2,1)} %param.10) | copy-start | bytes 2752516
  0.0 3.1 %copy-start.3 = (bf16[2048,64]{0,1:T(8,128)(2,1)S(1)}, bf16[2048,64]{0,1:T(8,128)(2,1)}, u32[]{:S(2)}) copy-start(bf16[2048,64]{0,1:T(8,128)(2,1)} %param.9) | copy-start | bytes 786436
  0.0 15.2 %collective-permute-start.7 = (bf16[2048,128]{1,0:T(8,128)(2,1)}, bf16[2048,128]{1,0:T(8,128)(2,1)S(1)}, u32[]{:S(2)}, u32[]{:S(2)}) collective-permute-start(bf16[2048,128]{1,0:T(8,128)(2,1)} %bitcast.10), channel_id=1, source_target_pairs={{0,4},{4,0},{8,12},{12,8},{1,5},{5,1},{9,13},{13,9},{2,6},{6,2},{1... | collective-permute-start | bytes 1572872 | tf_op jit(solution)/shard_map/ppermute | solution.py:22
  3.1 7.6 %copy-start.2 = (bf16[128,32,64]{0,2,1:T(8,128)(2,1)S(1)}, bf16[128,32,64]{0,2,1:T(8,128)(2,1)}, u32[]{:S(2)}) copy-start(bf16[128,32,64]{0,2,1:T(8,128)(2,1)} %param.13) | copy-start | bytes 1572868
  3.1 14.1 %copy-start.4 = (s32[8,96]{1,0:T(8,128)S(1)}, s32[8,96]{1,0:T(8,128)}, u32[]{:S(2)}) copy-start(s32[8,96]{1,0:T(8,128)} %mask_ref.1) | copy-start | bytes 9220
  3.1 14.1 %copy-start.5 = (s32[8]{0:T(128)S(1)}, s32[8]{0:T(128)}, u32[]{:S(2)}) copy-start(s32[8]{0:T(128)} %lengths_ref.3) | copy-start | bytes 100
  8.8 8.4 %collective-permute-start = (bf16[768,128]{1,0:T(8,128)(2,1)S(1)}, bf16[768,128]{1,0:T(8,128)(2,1)S(1)}, u32[]{:S(2)}, u32[]{:S(2)}) collective-permute-start(bf16[768,128]{1,0:T(8,128)(2,1)S(1)} %get-tuple-element.28), channel_id=1, source_target_pairs={{0,2},{2,0},{1,3},{3,1},{4,6},{6,4},{5,7},{7,5},{8,10},{10,8},{9,1... | collective-permute-start | bytes 589832 | tf_op jit(solution)/shard_map/ppermute | solution.py:22
  11.0 17.6 %collective-permute-start.4 = (bf16[1024,128]{1,0:T(8,128)(2,1)S(1)}, bf16[1024,128]{1,0:T(8,128)(2,1)S(1)}, u32[]{:S(2)}, u32[]{:S(2)}) collective-permute-start(bf16[1024,128]{1,0:T(8,128)(2,1)S(1)} %get-tuple-element.37), channel_id=1, source_target_pairs={{0,2},{2,0},{1,3},{3,1},{4,6},{6,4},{5,7},{7,5},{8,10},{10,8},{9,1... | collective-permute-start | bytes 786440 | tf_op jit(solution)/shard_map/ppermute | solution.py:22
  15.5 13.6 %collective-permute-start.8 = (bf16[1024,128]{1,0:T(8,128)(2,1)S(1)}, bf16[1024,128]{1,0:T(8,128)(2,1)S(1)}, u32[]{:S(2)}, u32[]{:S(2)}) collective-permute-start(bf16[1024,128]{1,0:T(8,128)(2,1)S(1)} %get-tuple-element.42), channel_id=1, source_target_pairs={{0,2},{2,0},{1,3},{3,1},{4,6},{6,4},{5,7},{7,5},{8,10},{10,8},{9,1... | collective-permute-start | bytes 786440 | tf_op jit(solution)/shard_map/ppermute | solution.py:22
  18.0 1.3 %collective-permute-start.1 = (f32[64,128]{1,0:T(8,128)S(1)}, f32[64,128]{1,0:T(8,128)S(1)}, u32[]{:S(2)}, u32[]{:S(2)}) collective-permute-start(f32[64,128]{1,0:T(8,128)S(1)} %get-tuple-element.29), channel_id=1, source_target_pairs={{0,1},{1,0},{2,3},{3,2},{4,5},{5,4},{6,7},{7,6},{8,9},{9,8},{10,11... | collective-permute-start | bytes 98312 | tf_op jit(solution)/shard_map/ppermute | solution.py:22
  19.3 5.2 %collective-permute-start.2 = (f32[64,128]{1,0:T(8,128)S(1)}, f32[64,128]{1,0:T(8,128)S(1)}, u32[]{:S(2)}, u32[]{:S(2)}) collective-permute-start(f32[64,128]{1,0:T(8,128)S(1)} %add.6), channel_id=1, source_target_pairs={{0,8},{4,12},{8,0},{12,4},{1,9},{5,13},{9,1},{13,5},{2,10},{6,14},... | collective-permute-start | bytes 98312 | tf_op jit(solution)/shard_map/ppermute | solution.py:22
  24.5 4.6 %collective-permute-start.3 = (f32[64,128]{1,0:T(8,128)S(1)}, f32[64,128]{1,0:T(8,128)S(1)}, u32[]{:S(2)}, u32[]{:S(2)}) collective-permute-start(f32[64,128]{1,0:T(8,128)S(1)} %add.7.factor_a_ref), channel_id=1, source_target_pairs={{0,4},{4,0},{8,12},{12,8},{1,5},{5,1},{9,13},{13,9},{2,6},{6,2},{1... | collective-permute-start | bytes 98312 | tf_op jit(solution)/shard_map/ppermute | solution.py:22
  25.7 6.3 %collective-permute-start.10 = (bf16[4,64,128]{2,1,0:T(8,128)(2,1)S(1)}, bf16[4,64,128]{2,1,0:T(8,128)(2,1)S(1)}, u32[]{:S(2)}, u32[]{:S(2)}) collective-permute-start(bf16[4,64,128]{2,1,0:T(8,128)(2,1)S(1)} %features.1.refs_7_), channel_id=1, source_target_pairs={{0,8},{4,12},{8,0},{12,4},{1,9},{5,13},{9,1},{13,5},{2,10},{6,14},... | collective-permute-start | bytes 196616 | tf_op jit(solution)/shard_map/ppermute | solution.py:22
  28.5 3.5 %collective-permute-start.5 = (bf16[1024,128]{1,0:T(8,128)(2,1)S(1)}, bf16[1024,128]{1,0:T(8,128)(2,1)S(1)}, u32[]{:S(2)}, u32[]{:S(2)}) collective-permute-start(bf16[1024,128]{1,0:T(8,128)(2,1)S(1)} %get-tuple-element.38.refs_0_), channel_id=1, source_target_pairs={{0,1},{1,0},{2,3},{3,2},{4,5},{5,4},{6,7},{7,6},{8,9},{9,8},{10,11... | collective-permute-start | bytes 786440 | tf_op jit(solution)/shard_map/ppermute | solution.py:22
  28.5 3.5 %collective-permute-start.6 = (bf16[1024,128]{1,0:T(8,128)(2,1)S(1)}, bf16[1024,128]{1,0:T(8,128)(2,1)S(1)}, u32[]{:S(2)}, u32[]{:S(2)}) collective-permute-start(bf16[1024,128]{1,0:T(8,128)(2,1)S(1)} %collective-permute-done.4.refs_1_), channel_id=1, source_target_pairs={{0,1},{1,0},{2,3},{3,2},{4,5},{5,4},{6,7},{7,6},{8,9},{9,8},{10,11... | collective-permute-start | bytes 786440 | tf_op jit(solution)/shard_map/ppermute | solution.py:22
  29.1 2.9 %collective-permute-start.9 = (bf16[2048,128]{1,0:T(8,128)(2,1)S(1)}, bf16[2048,128]{1,0:T(8,128)(2,1)S(1)}, u32[]{:S(2)}, u32[]{:S(2)}) collective-permute-start(bf16[2048,128]{1,0:T(8,128)(2,1)S(1)} %pad_maximum_fusion), channel_id=1, source_target_pairs={{0,1},{1,0},{2,3},{3,2},{4,5},{5,4},{6,7},{7,6},{8,9},{9,8},{10,11... | collective-permute-start | bytes 1572872 | tf_op jit(solution)/shard_map/ppermute | solution.py:22
  33.6 4.6 %collective-permute-start.11 = (f32[2,8,128]{2,1,0:T(8,128)S(1)}, f32[2,8,128]{2,1,0:T(8,128)S(1)}, u32[]{:S(2)}, u32[]{:S(2)}) collective-permute-start(f32[2,8,128]{2,1,0:T(8,128)S(1)} %get-tuple-element.46), channel_id=1, source_target_pairs={{0,8},{4,12},{8,0},{12,4},{1,9},{5,13},{9,1},{13,5},{2,10},{6,14},... | collective-permute-start | bytes 24584 | tf_op jit(solution)/shard_map/ppermute | solution.py:22

commit v9 on v8

--- a/solution.py
+++ b/solution.py
@@ -447,11 +447,12 @@
     pieces, piece_counts = [], []
     pieces += near + [xor_permute(piece, "test", 1) for piece in after(tuple(near), *(sums[2],))]
     piece_counts += [1] * (2 * feat_count)
-    pieces += far + [xor_permute(jnp.concatenate(after(tuple(far), *(other,)), axis=0), "test", 1)]
+    pieces += far + [xor_permute(jnp.concatenate(after(tuple(far), *(sums[2],)), axis=0), "test", 1)]
     piece_counts += [1] * feat_count + [feat_count]
     feats += [xor_permute(feats[0], "dp", mask) for mask in even_masks]
     total_tokens = float(tokens * dp_count * test_count)
     grad, in_pair = inverses(total_tokens, sums[-2], other)
+    pieces = list(lax.optimization_barrier(tuple(pieces)))
     blocks = scores_of(grad, in_pair, pieces, piece_counts, feats)
     blocks = [blocks[0]] + [xor_permute(blocks[at + 1], "dp", mask) for at, mask in enumerate(even_masks)]
     return finish(blocks)

time: 39 us -> 39 us (level)
  starting transfers between devices: 16 us -> 16.4 us
    ppermute x12, starting transfers between devices: 16 us -> 16.4 us  [xor_permute(): return lax.ppermute(values, axis, [(i, i ^ mask) for i in range(size)])]
  transfers between devices with their start and end apart: 12 -> 12, of which waited for: 4 -> 5; matrix products, arithmetic and copies ran while one was open for 0% -> 0% of each run, Pallas kernels for 27% -> 27%
where the time goes in v9:
time: 39 us; the launch traced here: 38.9 us
  starting transfers between devices  16.4 us (42%)
  Pallas kernels  12.7 us (33%)
  waiting for transfers between devices  9.56 us (25%)
    ppermute x12, starting transfers between devices, xor_permute(): return lax.ppermute(values, axis, [(i, i ^ mask) for i in range(size)])  16.4 us
    ppermute x12, waiting for transfers between devices, xor_permute(): return lax.ppermute(values, axis, [(i, i ^ mask) for i in range(size)])  9.56 us
    pallas_call x1, Pallas kernels, project(): pl.pallas_call(functools.partial(project_body, rows), out_shape=(jax.Shap...  5.62 us
    pallas_call x1, Pallas kernels, inverses(): pl.pallas_call(functools.partial(inverses_body, total_tokens), out_shape=...  2.81 us
    pallas_call x1, Pallas kernels, scores_of(): pl.pallas_call(functools.partial(scores_body, len(feats), piece_counts),...  1.52 us
    pallas_call x1, Pallas kernels, factors(): pl.pallas_call(functools.partial(factors_body, len(received)), out_shape=...  0.84 us
    pallas_call x1, Pallas kernels, features_of(): pl.pallas_call(features_body, out_shape=jax.ShapeDtypeStruct((examples //...  0.79 us
  transfers between devices with their start and end apart: 12, of which 5 were waited for; matrix products, arithmetic and copies ran while one was open for 0% of the time, Pallas kernels for 27%

profile of v9, /device:TPU:0, one launch (start us, length us, event | category | flops | bytes accessed | tf_op | source)
XLA Modules:
  0.0 38.9 jit_solution(934711631047312457)
XLA Ops:
  0.0 3.1 %collective-permute-start.7 = (bf16[2048,128]{1,0:T(8,128)(2,1)}, bf16[2048,128]{1,0:T(8,128)(2,1)S(1)}, u32[]{:S(2)}, u32[]{:S(2)}) collective-permute-start(bf16[2048,128]{1,0:T(8,128)(2,1)} %bitcast.10), channel_id=1, source_target_pairs={{0,4},{4,0},{8,12},{12,8},{1,5},{5,1},{9,13},{13,9},{2,6},{6,2},{1... | collective-permute-start | bytes 1572872 | tf_op jit(solution)/shard_map/ppermute | solution.py:22
  3.1 5.6 %project.1 = (f32[768,128]{1,0:T(8,128)S(1)}, bf16[768,128]{1,0:T(8,128)(2,1)S(1)}) custom-call(bf16[768,2048]{1,0:T(8,128)(2,1)S(1)} %bitcast.8, bf16[768,7168]{1,0:T(8,128)(2,1)} %bitcast.13, bf16[64,2048]{1,0:T(8,128)(2,1)S(1)} %bitcast.12, bf16[64,7168]{1,0:T(8,128)(2,1)S(1)} %bitcast.9), custom_call_target="tpu_custom_call" | custom-call | flops 905969664 | bytes 15335424 | tf_op jit(solution)/shard_map/project/pallas_call | solution.py:60
  8.8 2.0 %collective-permute-start = (bf16[768,128]{1,0:T(8,128)(2,1)S(1)}, bf16[768,128]{1,0:T(8,128)(2,1)S(1)}, u32[]{:S(2)}, u32[]{:S(2)}) collective-permute-start(bf16[768,128]{1,0:T(8,128)(2,1)S(1)} %get-tuple-element.35), channel_id=1, source_target_pairs={{0,2},{2,0},{1,3},{3,1},{4,6},{6,4},{5,7},{7,5},{8,10},{10,8},{9,1... | collective-permute-start | bytes 589832 | tf_op jit(solution)/shard_map/ppermute | solution.py:22
  10.7 0.2 pack.2
  11.0 0.2 collective-permute-start.4
  11.2 4.1 %collective-permute-done.7.tests_ref = bf16[2048,128]{1,0:T(8,128)(2,1)S(1)} collective-permute-done((bf16[2048,128]{1,0:T(8,128)(2,1)}, bf16[2048,128]{1,0:T(8,128)(2,1)S(1)}, u32[]{:S(2)}, u32[]{:S(2)}) %collective-permute-start.7) | collective-permute-done | bytes 524320 | tf_op jit(solution)/shard_map/ppermute | solution.py:22
  15.2 0.2 pack.3
  15.5 1.7 %collective-permute-start.8 = (bf16[1024,128]{1,0:T(8,128)(2,1)S(1)}, bf16[1024,128]{1,0:T(8,128)(2,1)S(1)}, u32[]{:S(2)}, u32[]{:S(2)}) collective-permute-start(bf16[1024,128]{1,0:T(8,128)(2,1)S(1)} %get-tuple-element.49), channel_id=1, source_target_pairs={{0,2},{2,0},{1,3},{3,1},{4,6},{6,4},{5,7},{7,5},{8,10},{10,8},{9,1... | collective-permute-start | bytes 786440 | tf_op jit(solution)/shard_map/ppermute | solution.py:22
  17.2 0.8 %factors.1 = (f32[64,128]{1,0:T(8,128)S(1)}, bf16[768,128]{1,0:T(8,128)(2,1)S(1)}, bf16[8,128,96]{2,1,0:T(8,128)(2,1)S(1)}) custom-call(s32[8]{0:T(128)S(1)} %copy-done.5, s32[1,96]{1,0:T(1,128)S(1)} %slots.1.positions_ref, s32[8,96]{1,0:T(8,128)S(1)} %copy-done.4, f32[768,128]{1,0:T(8,128)S(1)} %get-tuple-element.34.own_ref, ...), custom_call_target="tpu_custom_call" | custom-call | tf_op jit(solution)/shard_map/factors/pallas_call | solution.py:136
  18.0 0.1 collective-permute-start.1
  18.1 1.2 %collective-permute-done.1 = f32[64,128]{1,0:T(8,128)S(1)} collective-permute-done((f32[64,128]{1,0:T(8,128)S(1)}, f32[64,128]{1,0:T(8,128)S(1)}, u32[]{:S(2)}, u32[]{:S(2)}) %collective-permute-start.1) | collective-permute-done | bytes 32800 | tf_op jit(solution)/shard_map/ppermute | solution.py:22
  19.3 2.6 %collective-permute-start.2 = (f32[64,128]{1,0:T(8,128)S(1)}, f32[64,128]{1,0:T(8,128)S(1)}, u32[]{:S(2)}, u32[]{:S(2)}) collective-permute-start(f32[64,128]{1,0:T(8,128)S(1)} %add.6), channel_id=1, source_target_pairs={{0,8},{4,12},{8,0},{12,4},{1,9},{5,13},{9,1},{13,5},{2,10},{6,14},... | collective-permute-start | bytes 98312 | tf_op jit(solution)/shard_map/ppermute | solution.py:22
  21.9 0.8 %features.1.refs_7_ = bf16[4,64,128]{2,1,0:T(8,128)(2,1)S(1)} custom-call(s32[8]{0:T(128)S(1)} %copy-done.5, bf16[768,128]{1,0:T(8,128)(2,1)S(1)} %get-tuple-element.37.rounded_ref, bf16[8,128,96]{2,1,0:T(8,128)(2,1)S(1)} %get-tuple-element.38.turned_ref), custom_call_target="tpu_custom_call" | custom-call | flops 25165824 | bytes 8388608 | tf_op jit(solution)/shard_map/features/pallas_call | solution.py:168
  22.7 0.4 %collective-permute-start.10 = (bf16[4,64,128]{2,1,0:T(8,128)(2,1)S(1)}, bf16[4,64,128]{2,1,0:T(8,128)(2,1)S(1)}, u32[]{:S(2)}, u32[]{:S(2)}) collective-permute-start(bf16[4,64,128]{2,1,0:T(8,128)(2,1)S(1)} %features.1.refs_7_), channel_id=1, source_target_pairs={{0,8},{4,12},{8,0},{12,4},{1,9},{5,13},{9,1},{13,5},{2,10},{6,14},... | collective-permute-start | bytes 196616 | tf_op jit(solution)/shard_map/ppermute | solution.py:22
  23.1 1.4 %collective-permute-done.2 = f32[64,128]{1,0:T(8,128)S(1)} collective-permute-done((f32[64,128]{1,0:T(8,128)S(1)}, f32[64,128]{1,0:T(8,128)S(1)}, u32[]{:S(2)}, u32[]{:S(2)}) %collective-permute-start.2) | collective-permute-done | bytes 32800 | tf_op jit(solution)/shard_map/ppermute | solution.py:22
  24.5 2.3 %collective-permute-start.3 = (f32[64,128]{1,0:T(8,128)S(1)}, f32[64,128]{1,0:T(8,128)S(1)}, u32[]{:S(2)}, u32[]{:S(2)}) collective-permute-start(f32[64,128]{1,0:T(8,128)S(1)} %add.7.factor_a_ref), channel_id=1, source_target_pairs={{0,4},{4,0},{8,12},{12,8},{1,5},{5,1},{9,13},{13,9},{2,6},{6,2},{1... | collective-permute-start | bytes 98312 | tf_op jit(solution)/shard_map/ppermute | solution.py:22
  26.8 0.5 %collective-permute-start.6 = (bf16[1024,128]{1,0:T(8,128)(2,1)S(1)}, bf16[1024,128]{1,0:T(8,128)(2,1)S(1)}, u32[]{:S(2)}, u32[]{:S(2)}) collective-permute-start(bf16[1024,128]{1,0:T(8,128)(2,1)S(1)} %collective-permute-done.4.refs_1_), channel_id=1, source_target_pairs={{0,1},{1,0},{2,3},{3,2},{4,5},{5,4},{6,7},{7,6},{8,9},{9,8},{10,11... | collective-permute-start | bytes 786440 | tf_op jit(solution)/shard_map/ppermute | solution.py:22
  27.3 0.1 collective-permute-start.9
  27.4 1.3 %collective-permute-done.3.factor_b_ref = f32[64,128]{1,0:T(8,128)S(1)} collective-permute-done((f32[64,128]{1,0:T(8,128)S(1)}, f32[64,128]{1,0:T(8,128)S(1)}, u32[]{:S(2)}, u32[]{:S(2)}) %collective-permute-start.3) | collective-permute-done | bytes 32800 | tf_op jit(solution)/shard_map/ppermute | solution.py:22
  28.7 2.8 %inverses.1 = (bf16[2,64,64]{2,1,0:T(8,128)(2,1)S(1)}, bf16[2,128,128]{2,1,0:T(8,128)(2,1)S(1)}) custom-call(f32[64,128]{1,0:T(8,128)S(1)} %add.7.factor_a_ref, f32[64,128]{1,0:T(8,128)S(1)} %collective-permute-done.3.factor_b_ref), custom_call_target="tpu_custom_call" | custom-call | flops 17179869184 | tf_op jit(solution)/shard_map/inverses/pallas_call | solution.py:263
  31.5 1.5 %scores.1 = (f32[2,8,128]{2,1,0:T(8,128)S(1)}, f32[2,8,128]{2,1,0:T(8,128)S(1)}) custom-call(bf16[2,64,64]{2,1,0:T(8,128)(2,1)S(1)} %get-tuple-element.40.grad_ref, bf16[2,128,128]{2,1,0:T(8,128)(2,1)S(1)} %get-tuple-element.41.in_ref, bf16[1024,128]{1,0:T(8,128)(2,1)S(1)} %get-tuple-element.52.refs_0_, ...), custom_call_target="tpu_custom_call" | custom-call | tf_op jit(solution)/shard_map/scores/pallas_call | solution.py:370
  33.0 3.5 %collective-permute-start.11 = (f32[2,8,128]{2,1,0:T(8,128)S(1)}, f32[2,8,128]{2,1,0:T(8,128)S(1)}, u32[]{:S(2)}, u32[]{:S(2)}) collective-permute-start(f32[2,8,128]{2,1,0:T(8,128)S(1)} %get-tuple-element.60), channel_id=1, source_target_pairs={{0,8},{4,12},{8,0},{12,4},{1,9},{5,13},{9,1},{13,5},{2,10},{6,14},... | collective-permute-start | bytes 24584 | tf_op jit(solution)/shard_map/ppermute | solution.py:22
  36.6 1.6 %collective-permute-done.11.refs_1_ = f32[2,8,128]{2,1,0:T(8,128)S(1)} collective-permute-done((f32[2,8,128]{2,1,0:T(8,128)S(1)}, f32[2,8,128]{2,1,0:T(8,128)S(1)}, u32[]{:S(2)}, u32[]{:S(2)}) %collective-permute-start.11) | collective-permute-done | bytes 8224 | tf_op jit(solution)/shard_map/ppermute | solution.py:22
  38.2 0.7 %finish.1 = f32[64,64]{1,0:T(8,128)} custom-call(f32[2,8,128]{2,1,0:T(8,128)S(1)} %get-tuple-element.59.refs_0_, f32[2,8,128]{2,1,0:T(8,128)S(1)} %collective-permute-done.11.refs_1_), custom_call_target="tpu_custom_call" | custom-call | tf_op jit(solution)/shard_map/finish/pallas_call | solution.py:403
  (24 shorter events, 0.1 us)
Async XLA Ops:
  0.0 3.1 %copy-start = (bf16[8,96,2048]{2,1,0:T(8,128)(2,1)S(1)}, bf16[8,96,2048]{2,1,0:T(8,128)(2,1)}, u32[]{:S(2)}) copy-start(bf16[8,96,2048]{2,1,0:T(8,128)(2,1)} %param.7) | copy-start | bytes 9437188
  0.0 3.1 %copy-start.1 = (bf16[7168,64]{0,1:T(8,128)(2,1)S(1)}, bf16[7168,64]{0,1:T(8,128)(2,1)}, u32[]{:S(2)}) copy-start(bf16[7168,64]{0,1:T(8,128)(2,1)} %param.10) | copy-start | bytes 2752516
  0.0 3.1 %copy-start.3 = (bf16[2048,64]{0,1:T(8,128)(2,1)S(1)}, bf16[2048,64]{0,1:T(8,128)(2,1)}, u32[]{:S(2)}) copy-start(bf16[2048,64]{0,1:T(8,128)(2,1)} %param.9) | copy-start | bytes 786436
  0.0 15.2 %collective-permute-start.7 = (bf16[2048,128]{1,0:T(8,128)(2,1)}, bf16[2048,128]{1,0:T(8,128)(2,1)S(1)}, u32[]{:S(2)}, u32[]{:S(2)}) collective-permute-start(bf16[2048,128]{1,0:T(8,128)(2,1)} %bitcast.10), channel_id=1, source_target_pairs={{0,4},{4,0},{8,12},{12,8},{1,5},{5,1},{9,13},{13,9},{2,6},{6,2},{1... | collective-permute-start | bytes 1572872 | tf_op jit(solution)/shard_map/ppermute | solution.py:22
  3.1 7.6 %copy-start.2 = (bf16[128,32,64]{0,2,1:T(8,128)(2,1)S(1)}, bf16[128,32,64]{0,2,1:T(8,128)(2,1)}, u32[]{:S(2)}) copy-start(bf16[128,32,64]{0,2,1:T(8,128)(2,1)} %param.13) | copy-start | bytes 1572868
  3.1 14.1 %copy-start.4 = (s32[8,96]{1,0:T(8,128)S(1)}, s32[8,96]{1,0:T(8,128)}, u32[]{:S(2)}) copy-start(s32[8,96]{1,0:T(8,128)} %mask_ref.1) | copy-start | bytes 9220
  3.1 14.1 %copy-start.5 = (s32[8]{0:T(128)S(1)}, s32[8]{0:T(128)}, u32[]{:S(2)}) copy-start(s32[8]{0:T(128)} %lengths_ref.3) | copy-start | bytes 100
  8.8 8.4 %collective-permute-start = (bf16[768,128]{1,0:T(8,128)(2,1)S(1)}, bf16[768,128]{1,0:T(8,128)(2,1)S(1)}, u32[]{:S(2)}, u32[]{:S(2)}) collective-permute-start(bf16[768,128]{1,0:T(8,128)(2,1)S(1)} %get-tuple-element.35), channel_id=1, source_target_pairs={{0,2},{2,0},{1,3},{3,1},{4,6},{6,4},{5,7},{7,5},{8,10},{10,8},{9,1... | collective-permute-start | bytes 589832 | tf_op jit(solution)/shard_map/ppermute | solution.py:22
  11.0 15.8 %collective-permute-start.4 = (bf16[1024,128]{1,0:T(8,128)(2,1)S(1)}, bf16[1024,128]{1,0:T(8,128)(2,1)S(1)}, u32[]{:S(2)}, u32[]{:S(2)}) collective-permute-start(bf16[1024,128]{1,0:T(8,128)(2,1)S(1)} %get-tuple-element.44), channel_id=1, source_target_pairs={{0,2},{2,0},{1,3},{3,1},{4,6},{6,4},{5,7},{7,5},{8,10},{10,8},{9,1... | collective-permute-start | bytes 786440 | tf_op jit(solution)/shard_map/ppermute | solution.py:22
  15.5 11.8 %collective-permute-start.8 = (bf16[1024,128]{1,0:T(8,128)(2,1)S(1)}, bf16[1024,128]{1,0:T(8,128)(2,1)S(1)}, u32[]{:S(2)}, u32[]{:S(2)}) collective-permute-start(bf16[1024,128]{1,0:T(8,128)(2,1)S(1)} %get-tuple-element.49), channel_id=1, source_target_pairs={{0,2},{2,0},{1,3},{3,1},{4,6},{6,4},{5,7},{7,5},{8,10},{10,8},{9,1... | collective-permute-start | bytes 786440 | tf_op jit(solution)/shard_map/ppermute | solution.py:22
  18.0 1.3 %collective-permute-start.1 = (f32[64,128]{1,0:T(8,128)S(1)}, f32[64,128]{1,0:T(8,128)S(1)}, u32[]{:S(2)}, u32[]{:S(2)}) collective-permute-start(f32[64,128]{1,0:T(8,128)S(1)} %get-tuple-element.36), channel_id=1, source_target_pairs={{0,1},{1,0},{2,3},{3,2},{4,5},{5,4},{6,7},{7,6},{8,9},{9,8},{10,11... | collective-permute-start | bytes 98312 | tf_op jit(solution)/shard_map/ppermute | solution.py:22
  19.3 5.2 %collective-permute-start.2 = (f32[64,128]{1,0:T(8,128)S(1)}, f32[64,128]{1,0:T(8,128)S(1)}, u32[]{:S(2)}, u32[]{:S(2)}) collective-permute-start(f32[64,128]{1,0:T(8,128)S(1)} %add.6), channel_id=1, source_target_pairs={{0,8},{4,12},{8,0},{12,4},{1,9},{5,13},{9,1},{13,5},{2,10},{6,14},... | collective-permute-start | bytes 98312 | tf_op jit(solution)/shard_map/ppermute | solution.py:22
  22.7 8.8 %collective-permute-start.10 = (bf16[4,64,128]{2,1,0:T(8,128)(2,1)S(1)}, bf16[4,64,128]{2,1,0:T(8,128)(2,1)S(1)}, u32[]{:S(2)}, u32[]{:S(2)}) collective-permute-start(bf16[4,64,128]{2,1,0:T(8,128)(2,1)S(1)} %features.1.refs_7_), channel_id=1, source_target_pairs={{0,8},{4,12},{8,0},{12,4},{1,9},{5,13},{9,1},{13,5},{2,10},{6,14},... | collective-permute-start | bytes 196616 | tf_op jit(solution)/shard_map/ppermute | solution.py:22
  24.5 4.2 %collective-permute-start.3 = (f32[64,128]{1,0:T(8,128)S(1)}, f32[64,128]{1,0:T(8,128)S(1)}, u32[]{:S(2)}, u32[]{:S(2)}) collective-permute-start(f32[64,128]{1,0:T(8,128)S(1)} %add.7.factor_a_ref), channel_id=1, source_target_pairs={{0,4},{4,0},{8,12},{12,8},{1,5},{5,1},{9,13},{13,9},{2,6},{6,2},{1... | collective-permute-start | bytes 98312 | tf_op jit(solution)/shard_map/ppermute | solution.py:22
  26.8 4.7 %collective-permute-start.5 = (bf16[1024,128]{1,0:T(8,128)(2,1)S(1)}, bf16[1024,128]{1,0:T(8,128)(2,1)S(1)}, u32[]{:S(2)}, u32[]{:S(2)}) collective-permute-start(bf16[1024,128]{1,0:T(8,128)(2,1)S(1)} %get-tuple-element.52.refs_0_), channel_id=1, source_target_pairs={{0,1},{1,0},{2,3},{3,2},{4,5},{5,4},{6,7},{7,6},{8,9},{9,8},{10,11... | collective-permute-start | bytes 786440 | tf_op jit(solution)/shard_map/ppermute | solution.py:22
  26.8 4.7 %collective-permute-start.6 = (bf16[1024,128]{1,0:T(8,128)(2,1)S(1)}, bf16[1024,128]{1,0:T(8,128)(2,1)S(1)}, u32[]{:S(2)}, u32[]{:S(2)}) collective-permute-start(bf16[1024,128]{1,0:T(8,128)(2,1)S(1)} %collective-permute-done.4.refs_1_), channel_id=1, source_target_pairs={{0,1},{1,0},{2,3},{3,2},{4,5},{5,4},{6,7},{7,6},{8,9},{9,8},{10,11... | collective-permute-start | bytes 786440 | tf_op jit(solution)/shard_map/ppermute | solution.py:22
  27.3 4.2 %collective-permute-start.9 = (bf16[2048,128]{1,0:T(8,128)(2,1)S(1)}, bf16[2048,128]{1,0:T(8,128)(2,1)S(1)}, u32[]{:S(2)}, u32[]{:S(2)}) collective-permute-start(bf16[2048,128]{1,0:T(8,128)(2,1)S(1)} %pad_maximum_fusion), channel_id=1, source_target_pairs={{0,1},{1,0},{2,3},{3,2},{4,5},{5,4},{6,7},{7,6},{8,9},{9,8},{10,11... | collective-permute-start | bytes 1572872 | tf_op jit(solution)/shard_map/ppermute | solution.py:22
  33.0 5.2 %collective-permute-start.11 = (f32[2,8,128]{2,1,0:T(8,128)S(1)}, f32[2,8,128]{2,1,0:T(8,128)S(1)}, u32[]{:S(2)}, u32[]{:S(2)}) collective-permute-start(f32[2,8,128]{2,1,0:T(8,128)S(1)} %get-tuple-element.60), channel_id=1, source_target_pairs={{0,8},{4,12},{8,0},{12,4},{1,9},{5,13},{9,1},{13,5},{2,10},{6,14},... | collective-permute-start | bytes 24584 | tf_op jit(solution)/shard_map/ppermute | solution.py:22

commit v10 on v9

--- a/solution.py
+++ b/solution.py
@@ -14,7 +14,7 @@
 VMEM = pl.BlockSpec(memory_space=pltpu.VMEM)
 SMEM = pl.BlockSpec(memory_space=pltpu.SMEM)
 ANY = pl.BlockSpec(memory_space=pl.ANY)
-PROJECT_MIB = 48
+PROJECT_MIB = 40
 
 
 def xor_permute(values, axis, mask):
@@ -30,66 +30,83 @@
     return masks
 
 
-def project_body(rows, x_ref, g_hbm, pin_ref, pout_ref, own_ref, sent_ref, g_buf, sems):
-    steps = x_ref.shape[0] // rows
-    rank = pin_ref.shape[0]
-
-    def g_copy(step):
-        begin = step * rows if isinstance(step, int) else pl.multiple_of(step * rows, rows)
-        block = pl.ds(begin, rows)
-        return pltpu.make_async_copy(g_hbm.at[block, :], g_buf.at[block, :], sems.at[step])
-
-    for step in range(steps):
-        g_copy(step).start()
-    own_ref[:, :rank] = lax.dot_general(x_ref[...], pin_ref[...], NT, preferred_element_type=f32)
-
-    @pl.loop(0, steps)
-    def _(step):
-        g_copy(step).wait()
-        block = pl.ds(pl.multiple_of(step * rows, rows), rows)
+def project_first_body(step, x_ref, g_hbm, pin_ref, pout_ref, own_ref, sent_ref, left_ref, g_ref, g_buf, sems):
+    rows, rank = own_ref.shape[0], pin_ref.shape[0]
+
+    def g_copy(at):
+        begin = at * step if isinstance(at, int) else pl.multiple_of(at * step, step)
+        block = pl.ds(begin, step)
+        return pltpu.make_async_copy(g_hbm.at[block, :], g_buf.at[block, :], sems.at[at])
+
+    for at in range(rows // step):
+        g_copy(at).start()
+    others = pltpu.make_async_copy(g_hbm.at[pl.ds(rows, g_ref.shape[0]), :], g_ref, sems.at[rows // step])
+    others.start()
+    left = lax.dot_general(x_ref[...], pin_ref[...], NT, preferred_element_type=f32)
+    own_ref[:, :rank] = left[:rows, :]
+    left_ref[...] = left[rows:, :]
+
+    @pl.loop(0, rows // step)
+    def _(at):
+        g_copy(at).wait()
+        block = pl.ds(pl.multiple_of(at * step, step), step)
         right = lax.dot_general(g_buf[block, :], pout_ref[...], NT, preferred_element_type=f32)
         both = jnp.concatenate([own_ref[block, :rank], right], axis=1)
         own_ref[block, :] = both
         sent_ref[block, :] = both.astype(bf16)
 
-
-def project(x, g, pin, pout, rows):
+    others.wait()
+
+
+def project_first(x, g, pin, pout, rows, step):
     tokens, in_width = x.shape
     out_width = g.shape[1]
     rank = pin.shape[0]
     return pl.pallas_call(
-        functools.partial(project_body, rows),
+        functools.partial(project_first_body, step),
         out_shape=(
-            jax.ShapeDtypeStruct((tokens, 2 * rank), f32),
-            jax.ShapeDtypeStruct((tokens, 2 * rank), bf16),
+            jax.ShapeDtypeStruct((rows, 2 * rank), f32),
+            jax.ShapeDtypeStruct((rows, 2 * rank), bf16),
+            jax.ShapeDtypeStruct((tokens - rows, rank), f32),
+            jax.ShapeDtypeStruct((tokens - rows, out_width), bf16),
         ),
         in_specs=[VMEM, ANY, VMEM, VMEM],
-        out_specs=(VMEM, VMEM),
-        scratch_shapes=[pltpu.VMEM(g.shape, bf16), pltpu.SemaphoreType.DMA((tokens // rows,))],
+        out_specs=[VMEM] * 4,
+        scratch_shapes=[pltpu.VMEM((rows, out_width), bf16), pltpu.SemaphoreType.DMA((rows // step + 1,))],
         compiler_params=pltpu.CompilerParams(vmem_limit_bytes=PROJECT_MIB * MIB),
         cost_estimate=pl.CostEstimate(
-            flops=2 * tokens * (in_width + out_width) * rank,
+            flops=2 * rows * (in_width + out_width) * rank,
             bytes_accessed=2 * (tokens + rank) * (in_width + out_width),
             transcendentals=0,
         ),
-        name="project",
+        name="project_first",
     )(x, g, pin, pout)
 
 
-def fetch_body(values_ref, out_ref):
-    out_ref[...] = values_ref[...]
-
-
-def fetch(values):
-    return pl.pallas_call(
-        fetch_body,
-        out_shape=jax.ShapeDtypeStruct(values.shape, values.dtype),
-        in_specs=[VMEM],
-        out_specs=VMEM,
-        compiler_params=pltpu.CompilerParams(vmem_limit_bytes=4 * MIB),
-        cost_estimate=pl.CostEstimate(flops=values.size, bytes_accessed=8 * values.size, transcendentals=0),
-        name="fetch",
-    )(values)
+def project_last_body(left_ref, g_ref, pout_ref, own_ref, sent_ref):
+    right = lax.dot_general(g_ref[...], pout_ref[...], NT, preferred_element_type=f32)
+    both = jnp.concatenate([left_ref[...], right], axis=1)
+    own_ref[...] = both
+    sent_ref[...] = both.astype(bf16)
+
+
+def project_last(left, g, pout):
+    rows, out_width = g.shape
+    rank = pout.shape[0]
+    return pl.pallas_call(
+        project_last_body,
+        out_shape=(
+            jax.ShapeDtypeStruct((rows, 2 * rank), f32),
+            jax.ShapeDtypeStruct((rows, 2 * rank), bf16),
+        ),
+        in_specs=[VMEM] * 3,
+        out_specs=[VMEM] * 2,
+        compiler_params=pltpu.CompilerParams(vmem_limit_bytes=16 * MIB),
+        cost_estimate=pl.CostEstimate(
+            flops=2 * rows * out_width * rank, bytes_accessed=2 * (rows + rank) * out_width, transcendentals=0
+        ),
+        name="project_last",
+    )(left, g, pout)
 
 
 def slots_body(out_ref):
@@ -107,18 +124,21 @@
     )()
 
 
-def factors_body(received, lengths_ref, positions_ref, mask_ref, own_ref, *refs):
-    received_refs = refs[:received]
-    factor_ref, rounded_ref, turned_ref = refs[received:]
+def factors_body(parts, lengths_ref, positions_ref, mask_ref, *refs):
+    part_refs = [refs[i * len(refs[:-3]) // parts : (i + 1) * len(refs[:-3]) // parts] for i in range(parts)]
+    factor_ref, rounded_ref, turned_ref = refs[-3:]
     examples, seq_len = mask_ref.shape
     rank = factor_ref.shape[0]
     positions = positions_ref[...]
     total = None
+    begins = [sum(refs_of[0].shape[0] for refs_of in part_refs[:i]) for i in range(parts)]
     for example in range(examples):
         rows = pl.ds(example * seq_len, seq_len)
-        summed = own_ref[rows, :]
-        for ref in received_refs:
-            summed = summed + ref[rows, :].astype(f32)
+        part = max(i for i in range(parts) if begins[i] <= example * seq_len)
+        place = pl.ds(example * seq_len - begins[part], seq_len)
+        summed = part_refs[part][0][place, :]
+        for ref in part_refs[part][1:]:
+            summed = summed + ref[place, :].astype(f32)
         rounded = summed.astype(bf16)
         rounded_ref[rows, :] = rounded
         live = (mask_ref[example : example + 1, :] > 0) & (positions < lengths_ref[example])
@@ -130,21 +150,22 @@
     factor_ref[...] = jnp.where(lane < rank, total[:rank, :], total[rank:, :])
 
 
-def factors(lengths, positions, mask, own, received):
-    tokens, width = own.shape
+def factors(lengths, positions, mask, parts):
+    width = parts[0][0].shape[1]
     examples, seq_len = mask.shape
-    return pl.pallas_call(
-        functools.partial(factors_body, len(received)),
+    values = [value for part in parts for value in part]
+    return pl.pallas_call(
+        functools.partial(factors_body, len(parts)),
         out_shape=(
             jax.ShapeDtypeStruct((width // 2, width), f32),
-            jax.ShapeDtypeStruct((tokens, width), bf16),
+            jax.ShapeDtypeStruct((examples * seq_len, width), bf16),
             jax.ShapeDtypeStruct((examples, width, seq_len), bf16),
         ),
-        in_specs=[SMEM, VMEM, VMEM, VMEM] + [VMEM] * len(received),
+        in_specs=[SMEM, VMEM, VMEM] + [VMEM] * len(values),
         out_specs=(VMEM, VMEM, VMEM),
         compiler_params=pltpu.CompilerParams(vmem_limit_bytes=4 * MIB),
         name="factors",
-    )(lengths, positions, mask, own, *received)
+    )(lengths, positions, mask, *values)
 
 
 def features_body(lengths_ref, rounded_ref, turned_ref, feats_ref):
@@ -428,13 +449,20 @@
     tests = test_feats.transpose(1, 2, 0).reshape(own_rows * test_feats.shape[2], test_feats.shape[0])
     positions = slots(seq_len)
     far_tests = xor_permute(tests, "dp", 1)
-    own, sent = project(x, g, after(proj_in.T, positions), proj_out.T, tokens // 3)
+    first = seq_len * ((5 * examples) // 8)
+    own, sent, left, others = project_first(x, g, after(proj_in.T, positions), proj_out.T, first, first // 2)
+    owns, sents = [own], [sent]
+    own, sent = project_last(left, others, proj_out.T)
+    owns.append(own)
+    sents.append(sent)
+    parts = [
+        [own] + [xor_permute(sent, "feat", mask) for mask in range(1, feat_count)] for own, sent in zip(owns, sents)
+    ]
     cut = pack(after(tests, sent), 4 * MIB)
     near = [cut[0]] + [xor_permute(cut[mask], "feat", mask) for mask in range(1, feat_count)]
-    received = [xor_permute(sent, "feat", mask) for mask in range(1, feat_count)]
-    cut = pack(after(far_tests, *(sent,)), 4 * MIB)
+    factor, rounded, turned = factors(lengths, positions, loss_mask, parts)
+    cut = pack(after(far_tests, *(factor,)), 4 * MIB)
     far = [cut[0]] + [xor_permute(cut[mask], "feat", mask) for mask in range(1, feat_count)]
-    factor, rounded, turned = factors(lengths, positions, loss_mask, own, received)
     feats = [features_of(lengths, rounded, turned)]
     even_masks = range(2, dp_count, 2)
     steps = [("test", 1)] + [("dp", m) for m in reversed(masks_of(dp_count))]

time: 39 us -> 39.3 us (level)
  starting transfers between devices: 16.4 us -> 17.9 us
  waiting for transfers between devices: 9.56 us -> 8.37 us
    ppermute x12 -> x13, starting transfers between devices: 16.4 us -> 17.9 us  [xor_permute(): return lax.ppermute(values, axis, [(i, i ^ mask) for i in range(size)])]
    ppermute x12 -> x13, waiting for transfers between devices: 9.56 us -> 8.37 us  [xor_permute(): return lax.ppermute(values, axis, [(i, i ^ mask) for i in range(size)])]
    pallas_call x2 -> x3, Pallas kernels: 6.46 us -> 6.46 us  [the longest x1 4.35 us: project_first(): pl.pallas_call(functools.partial(project_first_body, step), out_shape=(ja...]
  transfers between devices with their start and end apart: 12 -> 13, of which waited for: 5 -> 5; matrix products, arithmetic and copies ran while one was open for 0% -> 0% of each run, Pallas kernels for 27% -> 27%
where the time goes in v10:
time: 39.3 us; the launch traced here: 39.2 us
  starting transfers between devices  17.9 us (46%)
  Pallas kernels  12.7 us (32%)
  waiting for transfers between devices  8.37 us (21%)
    ppermute x13, starting transfers between devices, xor_permute(): return lax.ppermute(values, axis, [(i, i ^ mask) for i in range(size)])  17.9 us
    ppermute x13, waiting for transfers between devices, xor_permute(): return lax.ppermute(values, axis, [(i, i ^ mask) for i in range(size)])  8.37 us
    pallas_call x1, Pallas kernels, project_first(): pl.pallas_call(functools.partial(project_first_body, step), out_shape=(ja...  4.35 us
    pallas_call x1, Pallas kernels, inverses(): pl.pallas_call(functools.partial(inverses_body, total_tokens), out_shape=...  2.81 us
    pallas_call x1, Pallas kernels, scores_of(): pl.pallas_call(functools.partial(scores_body, len(feats), piece_counts),...  1.52 us
    pallas_call x1, Pallas kernels, project_last(): pl.pallas_call(project_last_body, out_shape=(jax.ShapeDtypeStruct((rows,...  1.27 us
    pallas_call x1, Pallas kernels, factors(): pl.pallas_call(functools.partial(factors_body, len(parts)), out_shape=(ja...  0.84 us
    pallas_call x1, Pallas kernels, features_of(): pl.pallas_call(features_body, out_shape=jax.ShapeDtypeStruct((examples //...  0.79 us
  transfers between devices with their start and end apart: 13, of which 5 were waited for; matrix products, arithmetic and copies ran while one was open for 0% of the time, Pallas kernels for 27%

profile of v10, /device:TPU:0, one launch (start us, length us, event | category | flops | bytes accessed | tf_op | source)
XLA Modules:
  0.0 39.2 jit_solution(10830833664749142590)
XLA Ops:
  0.0 3.1 %collective-permute-start.8 = (bf16[2048,128]{1,0:T(8,128)(2,1)}, bf16[2048,128]{1,0:T(8,128)(2,1)S(1)}, u32[]{:S(2)}, u32[]{:S(2)}) collective-permute-start(bf16[2048,128]{1,0:T(8,128)(2,1)} %bitcast.11), channel_id=1, source_target_pairs={{0,4},{4,0},{8,12},{12,8},{1,5},{5,1},{9,13},{13,9},{2,6},{6,2},{1... | collective-permute-start | bytes 1572872 | tf_op jit(solution)/shard_map/ppermute | solution.py:22
  3.1 4.4 %project_first.1 = (f32[480,128]{1,0:T(8,128)S(1)}, bf16[480,128]{1,0:T(8,128)(2,1)S(1)}, f32[288,64]{1,0:T(8,128)S(1)}, bf16[288,7168]{1,0:T(8,128)(2,1)S(1)}) custom-call(bf16[768,2048]{1,0:T(8,128)(2,1)S(1)} %bitcast.10, bf16[768,7168]{1,0:T(8,128)(2,1)} %bitcast.14, bf16[64,2048]{1,0:T(8,128)(2,1)S(1)} %bitcast.13, bf16[64,7168]{1,0:T(8,128)(2,1)S(1)} %bitcast.8), custom_call_target="tpu_custom_call" | custom-call | flops 566231040 | bytes 15335424 | tf_op jit(solution)/shard_map/project_first/pallas_call | solution.py:65
  7.5 2.1 %collective-permute-start = (bf16[480,128]{1,0:T(8,128)(2,1)S(1)}, bf16[480,128]{1,0:T(8,128)(2,1)S(1)}, u32[]{:S(2)}, u32[]{:S(2)}) collective-permute-start(bf16[480,128]{1,0:T(8,128)(2,1)S(1)} %get-tuple-element.39), channel_id=1, source_target_pairs={{0,2},{2,0},{1,3},{3,1},{4,6},{6,4},{5,7},{7,5},{8,10},{10,8},{9,1... | collective-permute-start | bytes 368648 | tf_op jit(solution)/shard_map/ppermute | solution.py:22
  9.6 1.3 %project_last.1 = (f32[288,128]{1,0:T(8,128)S(1)}, bf16[288,128]{1,0:T(8,128)(2,1)S(1)}) custom-call(f32[288,64]{1,0:T(8,128)S(1)} %get-tuple-element.40.left_ref, bf16[288,7168]{1,0:T(8,128)(2,1)S(1)} %get-tuple-element.41.g_ref, bf16[64,7168]{1,0:T(8,128)(2,1)S(1)} %bitcast.9), custom_call_target="tpu_custom_call" | custom-call | flops 264241152 | bytes 5046272 | tf_op jit(solution)/shard_map/project_last/pallas_call | solution.py:96
  10.9 0.1 collective-permute-start.1
  10.9 0.2 pack.2
  11.2 2.1 %collective-permute-start.5 = (bf16[1024,128]{1,0:T(8,128)(2,1)S(1)}, bf16[1024,128]{1,0:T(8,128)(2,1)S(1)}, u32[]{:S(2)}, u32[]{:S(2)}) collective-permute-start(bf16[1024,128]{1,0:T(8,128)(2,1)S(1)} %get-tuple-element.52), channel_id=1, source_target_pairs={{0,2},{2,0},{1,3},{3,1},{4,6},{6,4},{5,7},{7,5},{8,10},{10,8},{9,1... | collective-permute-start | bytes 786440 | tf_op jit(solution)/shard_map/ppermute | solution.py:22
  13.2 2.9 %collective-permute-done.1.refs_3_ = bf16[288,128]{1,0:T(8,128)(2,1)S(1)} collective-permute-done((bf16[288,128]{1,0:T(8,128)(2,1)S(1)}, bf16[288,128]{1,0:T(8,128)(2,1)S(1)}, u32[]{:S(2)}, u32[]{:S(2)}) %collective-permute-start.1) | collective-permute-done | bytes 73760 | tf_op jit(solution)/shard_map/ppermute | solution.py:22
  16.1 0.8 %factors.1 = (f32[64,128]{1,0:T(8,128)S(1)}, bf16[768,128]{1,0:T(8,128)(2,1)S(1)}, bf16[8,128,96]{2,1,0:T(8,128)(2,1)S(1)}) custom-call(s32[8]{0:T(128)S(1)} %copy-done.5, s32[1,96]{1,0:T(1,128)S(1)} %slots.1.positions_ref, s32[8,96]{1,0:T(8,128)S(1)} %copy-done.4, f32[480,128]{1,0:T(8,128)S(1)} %get-tuple-element.38.refs_0_, ...), custom_call_target="tpu_custom_call" | custom-call | tf_op jit(solution)/shard_map/factors/pallas_call | solution.py:157
  17.0 0.2 pack.3
  17.2 1.2 %collective-permute-start.9 = (bf16[1024,128]{1,0:T(8,128)(2,1)S(1)}, bf16[1024,128]{1,0:T(8,128)(2,1)S(1)}, u32[]{:S(2)}, u32[]{:S(2)}) collective-permute-start(bf16[1024,128]{1,0:T(8,128)(2,1)S(1)} %get-tuple-element.57), channel_id=1, source_target_pairs={{0,2},{2,0},{1,3},{3,1},{4,6},{6,4},{5,7},{7,5},{8,10},{10,8},{9,1... | collective-permute-start | bytes 786440 | tf_op jit(solution)/shard_map/ppermute | solution.py:22
  18.4 1.2 %collective-permute-done.2 = f32[64,128]{1,0:T(8,128)S(1)} collective-permute-done((f32[64,128]{1,0:T(8,128)S(1)}, f32[64,128]{1,0:T(8,128)S(1)}, u32[]{:S(2)}, u32[]{:S(2)}) %collective-permute-start.2) | collective-permute-done | bytes 32800 | tf_op jit(solution)/shard_map/ppermute | solution.py:22
  19.6 2.6 %collective-permute-start.3 = (f32[64,128]{1,0:T(8,128)S(1)}, f32[64,128]{1,0:T(8,128)S(1)}, u32[]{:S(2)}, u32[]{:S(2)}) collective-permute-start(f32[64,128]{1,0:T(8,128)S(1)} %add.6), channel_id=1, source_target_pairs={{0,8},{4,12},{8,0},{12,4},{1,9},{5,13},{9,1},{13,5},{2,10},{6,14},... | collective-permute-start | bytes 98312 | tf_op jit(solution)/shard_map/ppermute | solution.py:22
  22.2 0.8 %features.1.refs_7_ = bf16[4,64,128]{2,1,0:T(8,128)(2,1)S(1)} custom-call(s32[8]{0:T(128)S(1)} %copy-done.5, bf16[768,128]{1,0:T(8,128)(2,1)S(1)} %get-tuple-element.45.rounded_ref, bf16[8,128,96]{2,1,0:T(8,128)(2,1)S(1)} %get-tuple-element.46.turned_ref), custom_call_target="tpu_custom_call" | custom-call | flops 25165824 | bytes 8388608 | tf_op jit(solution)/shard_map/features/pallas_call | solution.py:189
  23.0 0.4 %collective-permute-start.11 = (bf16[4,64,128]{2,1,0:T(8,128)(2,1)S(1)}, bf16[4,64,128]{2,1,0:T(8,128)(2,1)S(1)}, u32[]{:S(2)}, u32[]{:S(2)}) collective-permute-start(bf16[4,64,128]{2,1,0:T(8,128)(2,1)S(1)} %features.1.refs_7_), channel_id=1, source_target_pairs={{0,8},{4,12},{8,0},{12,4},{1,9},{5,13},{9,1},{13,5},{2,10},{6,14},... | collective-permute-start | bytes 196616 | tf_op jit(solution)/shard_map/ppermute | solution.py:22
  23.4 1.4 %collective-permute-done.3 = f32[64,128]{1,0:T(8,128)S(1)} collective-permute-done((f32[64,128]{1,0:T(8,128)S(1)}, f32[64,128]{1,0:T(8,128)S(1)}, u32[]{:S(2)}, u32[]{:S(2)}) %collective-permute-start.3) | collective-permute-done | bytes 32800 | tf_op jit(solution)/shard_map/ppermute | solution.py:22
  24.8 2.3 %collective-permute-start.4 = (f32[64,128]{1,0:T(8,128)S(1)}, f32[64,128]{1,0:T(8,128)S(1)}, u32[]{:S(2)}, u32[]{:S(2)}) collective-permute-start(f32[64,128]{1,0:T(8,128)S(1)} %add.7.factor_a_ref), channel_id=1, source_target_pairs={{0,4},{4,0},{8,12},{12,8},{1,5},{5,1},{9,13},{13,9},{2,6},{6,2},{1... | collective-permute-start | bytes 98312 | tf_op jit(solution)/shard_map/ppermute | solution.py:22
  27.1 0.5 %collective-permute-start.7 = (bf16[1024,128]{1,0:T(8,128)(2,1)S(1)}, bf16[1024,128]{1,0:T(8,128)(2,1)S(1)}, u32[]{:S(2)}, u32[]{:S(2)}) collective-permute-start(bf16[1024,128]{1,0:T(8,128)(2,1)S(1)} %collective-permute-done.5.refs_1_), channel_id=1, source_target_pairs={{0,1},{1,0},{2,3},{3,2},{4,5},{5,4},{6,7},{7,6},{8,9},{9,8},{10,11... | collective-permute-start | bytes 786440 | tf_op jit(solution)/shard_map/ppermute | solution.py:22
  27.7 1.3 %collective-permute-done.4.factor_b_ref = f32[64,128]{1,0:T(8,128)S(1)} collective-permute-done((f32[64,128]{1,0:T(8,128)S(1)}, f32[64,128]{1,0:T(8,128)S(1)}, u32[]{:S(2)}, u32[]{:S(2)}) %collective-permute-start.4) | collective-permute-done | bytes 32800 | tf_op jit(solution)/shard_map/ppermute | solution.py:22
  29.0 2.8 %inverses.1 = (bf16[2,64,64]{2,1,0:T(8,128)(2,1)S(1)}, bf16[2,128,128]{2,1,0:T(8,128)(2,1)S(1)}) custom-call(f32[64,128]{1,0:T(8,128)S(1)} %add.7.factor_a_ref, f32[64,128]{1,0:T(8,128)S(1)} %collective-permute-done.4.factor_b_ref), custom_call_target="tpu_custom_call" | custom-call | flops 17179869184 | tf_op jit(solution)/shard_map/inverses/pallas_call | solution.py:284
  31.8 1.5 %scores.1 = (f32[2,8,128]{2,1,0:T(8,128)S(1)}, f32[2,8,128]{2,1,0:T(8,128)S(1)}) custom-call(bf16[2,64,64]{2,1,0:T(8,128)(2,1)S(1)} %get-tuple-element.48.grad_ref, bf16[2,128,128]{2,1,0:T(8,128)(2,1)S(1)} %get-tuple-element.49.in_ref, bf16[1024,128]{1,0:T(8,128)(2,1)S(1)} %get-tuple-element.60.refs_0_, ...), custom_call_target="tpu_custom_call" | custom-call | tf_op jit(solution)/shard_map/scores/pallas_call | solution.py:391
  33.3 3.5 %collective-permute-start.12 = (f32[2,8,128]{2,1,0:T(8,128)S(1)}, f32[2,8,128]{2,1,0:T(8,128)S(1)}, u32[]{:S(2)}, u32[]{:S(2)}) collective-permute-start(f32[2,8,128]{2,1,0:T(8,128)S(1)} %get-tuple-element.68), channel_id=1, source_target_pairs={{0,8},{4,12},{8,0},{12,4},{1,9},{5,13},{9,1},{13,5},{2,10},{6,14},... | collective-permute-start | bytes 24584 | tf_op jit(solution)/shard_map/ppermute | solution.py:22
  36.9 1.6 %collective-permute-done.12.refs_1_ = f32[2,8,128]{2,1,0:T(8,128)S(1)} collective-permute-done((f32[2,8,128]{2,1,0:T(8,128)S(1)}, f32[2,8,128]{2,1,0:T(8,128)S(1)}, u32[]{:S(2)}, u32[]{:S(2)}) %collective-permute-start.12) | collective-permute-done | bytes 8224 | tf_op jit(solution)/shard_map/ppermute | solution.py:22
  38.5 0.7 %finish.1 = f32[64,64]{1,0:T(8,128)} custom-call(f32[2,8,128]{2,1,0:T(8,128)S(1)} %get-tuple-element.67.refs_0_, f32[2,8,128]{2,1,0:T(8,128)S(1)} %collective-permute-done.12.refs_1_), custom_call_target="tpu_custom_call" | custom-call | tf_op jit(solution)/shard_map/finish/pallas_call | solution.py:424
  (27 shorter events, 0.2 us)
Async XLA Ops:
  0.0 3.1 %copy-start = (bf16[7168,64]{0,1:T(8,128)(2,1)S(1)}, bf16[7168,64]{0,1:T(8,128)(2,1)}, u32[]{:S(2)}) copy-start(bf16[7168,64]{0,1:T(8,128)(2,1)} %param.10) | copy-start | bytes 2752516
  0.0 3.1 %copy-start.1 = (bf16[8,96,2048]{2,1,0:T(8,128)(2,1)S(1)}, bf16[8,96,2048]{2,1,0:T(8,128)(2,1)}, u32[]{:S(2)}) copy-start(bf16[8,96,2048]{2,1,0:T(8,128)(2,1)} %param.7) | copy-start | bytes 9437188
  0.0 3.1 %copy-start.3 = (bf16[2048,64]{0,1:T(8,128)(2,1)S(1)}, bf16[2048,64]{0,1:T(8,128)(2,1)}, u32[]{:S(2)}) copy-start(bf16[2048,64]{0,1:T(8,128)(2,1)} %param.9) | copy-start | bytes 786436
  0.0 17.0 %collective-permute-start.8 = (bf16[2048,128]{1,0:T(8,128)(2,1)}, bf16[2048,128]{1,0:T(8,128)(2,1)S(1)}, u32[]{:S(2)}, u32[]{:S(2)}) collective-permute-start(bf16[2048,128]{1,0:T(8,128)(2,1)} %bitcast.11), channel_id=1, source_target_pairs={{0,4},{4,0},{8,12},{12,8},{1,5},{5,1},{9,13},{13,9},{2,6},{6,2},{1... | collective-permute-start | bytes 1572872 | tf_op jit(solution)/shard_map/ppermute | solution.py:22
  7.5 3.5 %copy-start.2 = (bf16[128,32,64]{0,2,1:T(8,128)(2,1)S(1)}, bf16[128,32,64]{0,2,1:T(8,128)(2,1)}, u32[]{:S(2)}) copy-start(bf16[128,32,64]{0,2,1:T(8,128)(2,1)} %param.13) | copy-start | bytes 1572868
  7.5 8.6 %copy-start.4 = (s32[8,96]{1,0:T(8,128)S(1)}, s32[8,96]{1,0:T(8,128)}, u32[]{:S(2)}) copy-start(s32[8,96]{1,0:T(8,128)} %mask_ref.1) | copy-start | bytes 9220
  7.5 8.6 %copy-start.5 = (s32[8]{0:T(128)S(1)}, s32[8]{0:T(128)}, u32[]{:S(2)}) copy-start(s32[8]{0:T(128)} %lengths_ref.3) | copy-start | bytes 100
  7.5 8.6 %collective-permute-start = (bf16[480,128]{1,0:T(8,128)(2,1)S(1)}, bf16[480,128]{1,0:T(8,128)(2,1)S(1)}, u32[]{:S(2)}, u32[]{:S(2)}) collective-permute-start(bf16[480,128]{1,0:T(8,128)(2,1)S(1)} %get-tuple-element.39), channel_id=1, source_target_pairs={{0,2},{2,0},{1,3},{3,1},{4,6},{6,4},{5,7},{7,5},{8,10},{10,8},{9,1... | collective-permute-start | bytes 368648 | tf_op jit(solution)/shard_map/ppermute | solution.py:22
  10.9 5.3 %collective-permute-start.1 = (bf16[288,128]{1,0:T(8,128)(2,1)S(1)}, bf16[288,128]{1,0:T(8,128)(2,1)S(1)}, u32[]{:S(2)}, u32[]{:S(2)}) collective-permute-start(bf16[288,128]{1,0:T(8,128)(2,1)S(1)} %get-tuple-element.43), channel_id=1, source_target_pairs={{0,2},{2,0},{1,3},{3,1},{4,6},{6,4},{5,7},{7,5},{8,10},{10,8},{9,1... | collective-permute-start | bytes 221192 | tf_op jit(solution)/shard_map/ppermute | solution.py:22
  11.2 15.9 %collective-permute-start.5 = (bf16[1024,128]{1,0:T(8,128)(2,1)S(1)}, bf16[1024,128]{1,0:T(8,128)(2,1)S(1)}, u32[]{:S(2)}, u32[]{:S(2)}) collective-permute-start(bf16[1024,128]{1,0:T(8,128)(2,1)S(1)} %get-tuple-element.52), channel_id=1, source_target_pairs={{0,2},{2,0},{1,3},{3,1},{4,6},{6,4},{5,7},{7,5},{8,10},{10,8},{9,1... | collective-permute-start | bytes 786440 | tf_op jit(solution)/shard_map/ppermute | solution.py:22
  17.2 10.4 %collective-permute-start.9 = (bf16[1024,128]{1,0:T(8,128)(2,1)S(1)}, bf16[1024,128]{1,0:T(8,128)(2,1)S(1)}, u32[]{:S(2)}, u32[]{:S(2)}) collective-permute-start(bf16[1024,128]{1,0:T(8,128)(2,1)S(1)} %get-tuple-element.57), channel_id=1, source_target_pairs={{0,2},{2,0},{1,3},{3,1},{4,6},{6,4},{5,7},{7,5},{8,10},{10,8},{9,1... | collective-permute-start | bytes 786440 | tf_op jit(solution)/shard_map/ppermute | solution.py:22
  18.4 1.2 %collective-permute-start.2 = (f32[64,128]{1,0:T(8,128)S(1)}, f32[64,128]{1,0:T(8,128)S(1)}, u32[]{:S(2)}, u32[]{:S(2)}) collective-permute-start(f32[64,128]{1,0:T(8,128)S(1)} %get-tuple-element.44), channel_id=1, source_target_pairs={{0,1},{1,0},{2,3},{3,2},{4,5},{5,4},{6,7},{7,6},{8,9},{9,8},{10,11... | collective-permute-start | bytes 98312 | tf_op jit(solution)/shard_map/ppermute | solution.py:22
  19.6 5.2 %collective-permute-start.3 = (f32[64,128]{1,0:T(8,128)S(1)}, f32[64,128]{1,0:T(8,128)S(1)}, u32[]{:S(2)}, u32[]{:S(2)}) collective-permute-start(f32[64,128]{1,0:T(8,128)S(1)} %add.6), channel_id=1, source_target_pairs={{0,8},{4,12},{8,0},{12,4},{1,9},{5,13},{9,1},{13,5},{2,10},{6,14},... | collective-permute-start | bytes 98312 | tf_op jit(solution)/shard_map/ppermute | solution.py:22
  23.0 8.8 %collective-permute-start.11 = (bf16[4,64,128]{2,1,0:T(8,128)(2,1)S(1)}, bf16[4,64,128]{2,1,0:T(8,128)(2,1)S(1)}, u32[]{:S(2)}, u32[]{:S(2)}) collective-permute-start(bf16[4,64,128]{2,1,0:T(8,128)(2,1)S(1)} %features.1.refs_7_), channel_id=1, source_target_pairs={{0,8},{4,12},{8,0},{12,4},{1,9},{5,13},{9,1},{13,5},{2,10},{6,14},... | collective-permute-start | bytes 196616 | tf_op jit(solution)/shard_map/ppermute | solution.py:22
  24.8 4.2 %collective-permute-start.4 = (f32[64,128]{1,0:T(8,128)S(1)}, f32[64,128]{1,0:T(8,128)S(1)}, u32[]{:S(2)}, u32[]{:S(2)}) collective-permute-start(f32[64,128]{1,0:T(8,128)S(1)} %add.7.factor_a_ref), channel_id=1, source_target_pairs={{0,4},{4,0},{8,12},{12,8},{1,5},{5,1},{9,13},{13,9},{2,6},{6,2},{1... | collective-permute-start | bytes 98312 | tf_op jit(solution)/shard_map/ppermute | solution.py:22
  27.1 4.7 %collective-permute-start.6 = (bf16[1024,128]{1,0:T(8,128)(2,1)S(1)}, bf16[1024,128]{1,0:T(8,128)(2,1)S(1)}, u32[]{:S(2)}, u32[]{:S(2)}) collective-permute-start(bf16[1024,128]{1,0:T(8,128)(2,1)S(1)} %get-tuple-element.60.refs_0_), channel_id=1, source_target_pairs={{0,1},{1,0},{2,3},{3,2},{4,5},{5,4},{6,7},{7,6},{8,9},{9,8},{10,11... | collective-permute-start | bytes 786440 | tf_op jit(solution)/shard_map/ppermute | solution.py:22
  27.1 4.7 %collective-permute-start.7 = (bf16[1024,128]{1,0:T(8,128)(2,1)S(1)}, bf16[1024,128]{1,0:T(8,128)(2,1)S(1)}, u32[]{:S(2)}, u32[]{:S(2)}) collective-permute-start(bf16[1024,128]{1,0:T(8,128)(2,1)S(1)} %collective-permute-done.5.refs_1_), channel_id=1, source_target_pairs={{0,1},{1,0},{2,3},{3,2},{4,5},{5,4},{6,7},{7,6},{8,9},{9,8},{10,11... | collective-permute-start | bytes 786440 | tf_op jit(solution)/shard_map/ppermute | solution.py:22
  27.6 4.2 %collective-permute-start.10 = (bf16[2048,128]{1,0:T(8,128)(2,1)S(1)}, bf16[2048,128]{1,0:T(8,128)(2,1)S(1)}, u32[]{:S(2)}, u32[]{:S(2)}) collective-permute-start(bf16[2048,128]{1,0:T(8,128)(2,1)S(1)} %pad_maximum_fusion), channel_id=1, source_target_pairs={{0,1},{1,0},{2,3},{3,2},{4,5},{5,4},{6,7},{7,6},{8,9},{9,8},{10,11... | collective-permute-start | bytes 1572872 | tf_op jit(solution)/shard_map/ppermute | solution.py:22
  33.3 5.2 %collective-permute-start.12 = (f32[2,8,128]{2,1,0:T(8,128)S(1)}, f32[2,8,128]{2,1,0:T(8,128)S(1)}, u32[]{:S(2)}, u32[]{:S(2)}) collective-permute-start(f32[2,8,128]{2,1,0:T(8,128)S(1)} %get-tuple-element.68), channel_id=1, source_target_pairs={{0,8},{4,12},{8,0},{12,4},{1,9},{5,13},{9,1},{13,5},{2,10},{6,14},... | collective-permute-start | bytes 24584 | tf_op jit(solution)/shard_map/ppermute | solution.py:22

commit v11 on v8

--- a/solution.py
+++ b/solution.py
@@ -321,9 +321,12 @@
     fold, width = pieces[0].shape
     block = width // feat_count
     dot = functools.partial(jnp.dot, preferred_element_type=f32)
-    for at in range(count):
-        high, low = split(dot(grad_ref[0], pairs[at]) + dot(grad_ref[1], pairs[at]))
-        solved_buf[at * rank : (at + 1) * rank, :] = dot(high, in_ref[0]) + dot(high, in_ref[1]) + dot(low, in_ref[0])
+    both = dot(jnp.concatenate([grad_ref[0], grad_ref[1]], axis=0), jnp.concatenate(pairs, axis=1))
+    solved = both[:rank, :] + both[rank:, :]
+    rows = [solved[:, 2 * rank * at : 2 * rank * (at + 1)] for at in range(count)]
+    high, low = split(jnp.concatenate(rows, axis=0))
+    both = dot(high, jnp.concatenate([in_ref[0], in_ref[1]], axis=1))
+    solved_buf[...] = both[:, : 2 * rank] + both[:, 2 * rank :] + dot(low, in_ref[0])
     lane = lax.broadcasted_iota(jnp.int32, (count, 2 * rank), 1)
     for g in range(0, rank, 2):
         low = solved_buf[pl.ds(g, count, stride=rank), :]

time: 39 us -> 38.6 us (0.990)
  Pallas kernels: 12.7 us -> 12.3 us
where the time goes in v11:
time: 38.6 us; the launch traced here: 38.4 us
  starting transfers between devices  16 us (41%)
  Pallas kernels  12.3 us (32%)
  waiting for transfers between devices  9.93 us (26%)
    ppermute x12, starting transfers between devices, xor_permute(): return lax.ppermute(values, axis, [(i, i ^ mask) for i in range(size)])  16 us
    ppermute x12, waiting for transfers between devices, xor_permute(): return lax.ppermute(values, axis, [(i, i ^ mask) for i in range(size)])  9.93 us
    pallas_call x1, Pallas kernels, project(): pl.pallas_call(functools.partial(project_body, rows), out_shape=(jax.Shap...  5.62 us
    pallas_call x1, Pallas kernels, inverses(): pl.pallas_call(functools.partial(inverses_body, total_tokens), out_shape=...  2.81 us
    pallas_call x1, Pallas kernels, scores_of(): pl.pallas_call(functools.partial(scores_body, len(feats), piece_counts),...  1.15 us
    pallas_call x1, Pallas kernels, factors(): pl.pallas_call(functools.partial(factors_body, len(received)), out_shape=...  0.84 us
    pallas_call x1, Pallas kernels, features_of(): pl.pallas_call(features_body, out_shape=jax.ShapeDtypeStruct((examples //...  0.79 us
  transfers between devices with their start and end apart: 12, of which 4 were waited for; matrix products, arithmetic and copies ran while one was open for 0% of the time, Pallas kernels for 27%

profile of v11, /device:TPU:0, one launch (start us, length us, event | category | flops | bytes accessed | tf_op | source)
XLA Modules:
  0.0 38.4 jit_solution(10397454126093915024)
XLA Ops:
  0.0 3.1 %collective-permute-start.7 = (bf16[2048,128]{1,0:T(8,128)(2,1)}, bf16[2048,128]{1,0:T(8,128)(2,1)S(1)}, u32[]{:S(2)}, u32[]{:S(2)}) collective-permute-start(bf16[2048,128]{1,0:T(8,128)(2,1)} %bitcast.10), channel_id=1, source_target_pairs={{0,4},{4,0},{8,12},{12,8},{1,5},{5,1},{9,13},{13,9},{2,6},{6,2},{1... | collective-permute-start | bytes 1572872 | tf_op jit(solution)/shard_map/ppermute | solution.py:22
  3.1 5.6 %project.1 = (f32[768,128]{1,0:T(8,128)S(1)}, bf16[768,128]{1,0:T(8,128)(2,1)S(1)}) custom-call(bf16[768,2048]{1,0:T(8,128)(2,1)S(1)} %bitcast.8, bf16[768,7168]{1,0:T(8,128)(2,1)} %bitcast.13, bf16[64,2048]{1,0:T(8,128)(2,1)S(1)} %bitcast.12, bf16[64,7168]{1,0:T(8,128)(2,1)S(1)} %bitcast.9), custom_call_target="tpu_custom_call" | custom-call | flops 905969664 | bytes 15335424 | tf_op jit(solution)/shard_map/project/pallas_call | solution.py:60
  8.8 2.0 %collective-permute-start = (bf16[768,128]{1,0:T(8,128)(2,1)S(1)}, bf16[768,128]{1,0:T(8,128)(2,1)S(1)}, u32[]{:S(2)}, u32[]{:S(2)}) collective-permute-start(bf16[768,128]{1,0:T(8,128)(2,1)S(1)} %get-tuple-element.28), channel_id=1, source_target_pairs={{0,2},{2,0},{1,3},{3,1},{4,6},{6,4},{5,7},{7,5},{8,10},{10,8},{9,1... | collective-permute-start | bytes 589832 | tf_op jit(solution)/shard_map/ppermute | solution.py:22
  10.7 0.2 pack.2
  11.0 0.2 collective-permute-start.4
  11.2 4.1 %collective-permute-done.7.tests_ref = bf16[2048,128]{1,0:T(8,128)(2,1)S(1)} collective-permute-done((bf16[2048,128]{1,0:T(8,128)(2,1)}, bf16[2048,128]{1,0:T(8,128)(2,1)S(1)}, u32[]{:S(2)}, u32[]{:S(2)}) %collective-permute-start.7) | collective-permute-done | bytes 524320 | tf_op jit(solution)/shard_map/ppermute | solution.py:22
  15.2 0.2 pack.3
  15.5 1.7 %collective-permute-start.8 = (bf16[1024,128]{1,0:T(8,128)(2,1)S(1)}, bf16[1024,128]{1,0:T(8,128)(2,1)S(1)}, u32[]{:S(2)}, u32[]{:S(2)}) collective-permute-start(bf16[1024,128]{1,0:T(8,128)(2,1)S(1)} %get-tuple-element.42), channel_id=1, source_target_pairs={{0,2},{2,0},{1,3},{3,1},{4,6},{6,4},{5,7},{7,5},{8,10},{10,8},{9,1... | collective-permute-start | bytes 786440 | tf_op jit(solution)/shard_map/ppermute | solution.py:22
  17.2 0.0 collective-permute-done.refs_0_
  17.2 0.8 %factors.1 = (f32[64,128]{1,0:T(8,128)S(1)}, bf16[768,128]{1,0:T(8,128)(2,1)S(1)}, bf16[8,128,96]{2,1,0:T(8,128)(2,1)S(1)}) custom-call(s32[8]{0:T(128)S(1)} %copy-done.5, s32[1,96]{1,0:T(1,128)S(1)} %slots.1.positions_ref, s32[8,96]{1,0:T(8,128)S(1)} %copy-done.4, f32[768,128]{1,0:T(8,128)S(1)} %get-tuple-element.27.own_ref, ...), custom_call_target="tpu_custom_call" | custom-call | tf_op jit(solution)/shard_map/factors/pallas_call | solution.py:136
  18.0 0.1 collective-permute-start.1
  18.1 1.2 %collective-permute-done.1 = f32[64,128]{1,0:T(8,128)S(1)} collective-permute-done((f32[64,128]{1,0:T(8,128)S(1)}, f32[64,128]{1,0:T(8,128)S(1)}, u32[]{:S(2)}, u32[]{:S(2)}) %collective-permute-start.1) | collective-permute-done | bytes 32800 | tf_op jit(solution)/shard_map/ppermute | solution.py:22
  19.3 2.6 %collective-permute-start.2 = (f32[64,128]{1,0:T(8,128)S(1)}, f32[64,128]{1,0:T(8,128)S(1)}, u32[]{:S(2)}, u32[]{:S(2)}) collective-permute-start(f32[64,128]{1,0:T(8,128)S(1)} %add.6), channel_id=1, source_target_pairs={{0,8},{4,12},{8,0},{12,4},{1,9},{5,13},{9,1},{13,5},{2,10},{6,14},... | collective-permute-start | bytes 98312 | tf_op jit(solution)/shard_map/ppermute | solution.py:22
  21.9 0.8 %features.1.refs_7_ = bf16[4,64,128]{2,1,0:T(8,128)(2,1)S(1)} custom-call(s32[8]{0:T(128)S(1)} %copy-done.5, bf16[768,128]{1,0:T(8,128)(2,1)S(1)} %get-tuple-element.30.rounded_ref, bf16[8,128,96]{2,1,0:T(8,128)(2,1)S(1)} %get-tuple-element.31.turned_ref), custom_call_target="tpu_custom_call" | custom-call | flops 25165824 | bytes 8388608 | tf_op jit(solution)/shard_map/features/pallas_call | solution.py:168
  22.7 1.8 %collective-permute-done.2 = f32[64,128]{1,0:T(8,128)S(1)} collective-permute-done((f32[64,128]{1,0:T(8,128)S(1)}, f32[64,128]{1,0:T(8,128)S(1)}, u32[]{:S(2)}, u32[]{:S(2)}) %collective-permute-start.2) | collective-permute-done | bytes 32800 | tf_op jit(solution)/shard_map/ppermute | solution.py:22
  24.5 1.2 %collective-permute-start.3 = (f32[64,128]{1,0:T(8,128)S(1)}, f32[64,128]{1,0:T(8,128)S(1)}, u32[]{:S(2)}, u32[]{:S(2)}) collective-permute-start(f32[64,128]{1,0:T(8,128)S(1)} %add.7.factor_a_ref), channel_id=1, source_target_pairs={{0,4},{4,0},{8,12},{12,8},{1,5},{5,1},{9,13},{13,9},{2,6},{6,2},{1... | collective-permute-start | bytes 98312 | tf_op jit(solution)/shard_map/ppermute | solution.py:22
  25.7 2.8 %collective-permute-start.10 = (bf16[4,64,128]{2,1,0:T(8,128)(2,1)S(1)}, bf16[4,64,128]{2,1,0:T(8,128)(2,1)S(1)}, u32[]{:S(2)}, u32[]{:S(2)}) collective-permute-start(bf16[4,64,128]{2,1,0:T(8,128)(2,1)S(1)} %features.1.refs_7_), channel_id=1, source_target_pairs={{0,8},{4,12},{8,0},{12,4},{1,9},{5,13},{9,1},{13,5},{2,10},{6,14},... | collective-permute-start | bytes 196616 | tf_op jit(solution)/shard_map/ppermute | solution.py:22
  28.5 0.5 %collective-permute-start.6 = (bf16[1024,128]{1,0:T(8,128)(2,1)S(1)}, bf16[1024,128]{1,0:T(8,128)(2,1)S(1)}, u32[]{:S(2)}, u32[]{:S(2)}) collective-permute-start(bf16[1024,128]{1,0:T(8,128)(2,1)S(1)} %collective-permute-done.4.refs_1_), channel_id=1, source_target_pairs={{0,1},{1,0},{2,3},{3,2},{4,5},{5,4},{6,7},{7,6},{8,9},{9,8},{10,11... | collective-permute-start | bytes 786440 | tf_op jit(solution)/shard_map/ppermute | solution.py:22
  29.1 0.1 collective-permute-start.9
  29.2 2.8 %inverses.1 = (bf16[2,64,64]{2,1,0:T(8,128)(2,1)S(1)}, bf16[2,128,128]{2,1,0:T(8,128)(2,1)S(1)}) custom-call(f32[64,128]{1,0:T(8,128)S(1)} %add.7.factor_a_ref, f32[64,128]{1,0:T(8,128)S(1)} %collective-permute-done.3.factor_b_ref), custom_call_target="tpu_custom_call" | custom-call | flops 17179869184 | tf_op jit(solution)/shard_map/inverses/pallas_call | solution.py:263
  32.0 1.1 %scores.1 = (f32[2,8,128]{2,1,0:T(8,128)S(1)}, f32[2,8,128]{2,1,0:T(8,128)S(1)}) custom-call(bf16[2,64,64]{2,1,0:T(8,128)(2,1)S(1)} %get-tuple-element.33.grad_ref, bf16[2,128,128]{2,1,0:T(8,128)(2,1)S(1)} %get-tuple-element.34.in_ref, bf16[1024,128]{1,0:T(8,128)(2,1)S(1)} %get-tuple-element.38.refs_0_, ...), custom_call_target="tpu_custom_call" | custom-call | tf_op jit(solution)/shard_map/scores/pallas_call | solution.py:373
  33.2 1.7 %collective-permute-start.11 = (f32[2,8,128]{2,1,0:T(8,128)S(1)}, f32[2,8,128]{2,1,0:T(8,128)S(1)}, u32[]{:S(2)}, u32[]{:S(2)}) collective-permute-start(f32[2,8,128]{2,1,0:T(8,128)S(1)} %get-tuple-element.46), channel_id=1, source_target_pairs={{0,8},{4,12},{8,0},{12,4},{1,9},{5,13},{9,1},{13,5},{2,10},{6,14},... | collective-permute-start | bytes 24584 | tf_op jit(solution)/shard_map/ppermute | solution.py:22
  34.9 2.8 %collective-permute-done.11.refs_1_ = f32[2,8,128]{2,1,0:T(8,128)S(1)} collective-permute-done((f32[2,8,128]{2,1,0:T(8,128)S(1)}, f32[2,8,128]{2,1,0:T(8,128)S(1)}, u32[]{:S(2)}, u32[]{:S(2)}) %collective-permute-start.11) | collective-permute-done | bytes 8224 | tf_op jit(solution)/shard_map/ppermute | solution.py:22
  37.8 0.7 %finish.1 = f32[64,64]{1,0:T(8,128)} custom-call(f32[2,8,128]{2,1,0:T(8,128)S(1)} %get-tuple-element.45.refs_0_, f32[2,8,128]{2,1,0:T(8,128)S(1)} %collective-permute-done.11.refs_1_), custom_call_target="tpu_custom_call" | custom-call | tf_op jit(solution)/shard_map/finish/pallas_call | solution.py:406
  (24 shorter events, 0.1 us)
Async XLA Ops:
  0.0 3.1 %copy-start = (bf16[8,96,2048]{2,1,0:T(8,128)(2,1)S(1)}, bf16[8,96,2048]{2,1,0:T(8,128)(2,1)}, u32[]{:S(2)}) copy-start(bf16[8,96,2048]{2,1,0:T(8,128)(2,1)} %param.7) | copy-start | bytes 9437188
  0.0 3.1 %copy-start.1 = (bf16[7168,64]{0,1:T(8,128)(2,1)S(1)}, bf16[7168,64]{0,1:T(8,128)(2,1)}, u32[]{:S(2)}) copy-start(bf16[7168,64]{0,1:T(8,128)(2,1)} %param.10) | copy-start | bytes 2752516
  0.0 3.1 %copy-start.3 = (bf16[2048,64]{0,1:T(8,128)(2,1)S(1)}, bf16[2048,64]{0,1:T(8,128)(2,1)}, u32[]{:S(2)}) copy-start(bf16[2048,64]{0,1:T(8,128)(2,1)} %param.9) | copy-start | bytes 786436
  0.0 15.2 %collective-permute-start.7 = (bf16[2048,128]{1,0:T(8,128)(2,1)}, bf16[2048,128]{1,0:T(8,128)(2,1)S(1)}, u32[]{:S(2)}, u32[]{:S(2)}) collective-permute-start(bf16[2048,128]{1,0:T(8,128)(2,1)} %bitcast.10), channel_id=1, source_target_pairs={{0,4},{4,0},{8,12},{12,8},{1,5},{5,1},{9,13},{13,9},{2,6},{6,2},{1... | collective-permute-start | bytes 1572872 | tf_op jit(solution)/shard_map/ppermute | solution.py:22
  3.1 7.6 %copy-start.2 = (bf16[128,32,64]{0,2,1:T(8,128)(2,1)S(1)}, bf16[128,32,64]{0,2,1:T(8,128)(2,1)}, u32[]{:S(2)}) copy-start(bf16[128,32,64]{0,2,1:T(8,128)(2,1)} %param.13) | copy-start | bytes 1572868
  3.1 14.1 %copy-start.4 = (s32[8,96]{1,0:T(8,128)S(1)}, s32[8,96]{1,0:T(8,128)}, u32[]{:S(2)}) copy-start(s32[8,96]{1,0:T(8,128)} %mask_ref.1) | copy-start | bytes 9220
  3.1 14.1 %copy-start.5 = (s32[8]{0:T(128)S(1)}, s32[8]{0:T(128)}, u32[]{:S(2)}) copy-start(s32[8]{0:T(128)} %lengths_ref.3) | copy-start | bytes 100
  8.8 8.4 %collective-permute-start = (bf16[768,128]{1,0:T(8,128)(2,1)S(1)}, bf16[768,128]{1,0:T(8,128)(2,1)S(1)}, u32[]{:S(2)}, u32[]{:S(2)}) collective-permute-start(bf16[768,128]{1,0:T(8,128)(2,1)S(1)} %get-tuple-element.28), channel_id=1, source_target_pairs={{0,2},{2,0},{1,3},{3,1},{4,6},{6,4},{5,7},{7,5},{8,10},{10,8},{9,1... | collective-permute-start | bytes 589832 | tf_op jit(solution)/shard_map/ppermute | solution.py:22
  11.0 17.6 %collective-permute-start.4 = (bf16[1024,128]{1,0:T(8,128)(2,1)S(1)}, bf16[1024,128]{1,0:T(8,128)(2,1)S(1)}, u32[]{:S(2)}, u32[]{:S(2)}) collective-permute-start(bf16[1024,128]{1,0:T(8,128)(2,1)S(1)} %get-tuple-element.37), channel_id=1, source_target_pairs={{0,2},{2,0},{1,3},{3,1},{4,6},{6,4},{5,7},{7,5},{8,10},{10,8},{9,1... | collective-permute-start | bytes 786440 | tf_op jit(solution)/shard_map/ppermute | solution.py:22
  15.5 13.6 %collective-permute-start.8 = (bf16[1024,128]{1,0:T(8,128)(2,1)S(1)}, bf16[1024,128]{1,0:T(8,128)(2,1)S(1)}, u32[]{:S(2)}, u32[]{:S(2)}) collective-permute-start(bf16[1024,128]{1,0:T(8,128)(2,1)S(1)} %get-tuple-element.42), channel_id=1, source_target_pairs={{0,2},{2,0},{1,3},{3,1},{4,6},{6,4},{5,7},{7,5},{8,10},{10,8},{9,1... | collective-permute-start | bytes 786440 | tf_op jit(solution)/shard_map/ppermute | solution.py:22
  18.0 1.3 %collective-permute-start.1 = (f32[64,128]{1,0:T(8,128)S(1)}, f32[64,128]{1,0:T(8,128)S(1)}, u32[]{:S(2)}, u32[]{:S(2)}) collective-permute-start(f32[64,128]{1,0:T(8,128)S(1)} %get-tuple-element.29), channel_id=1, source_target_pairs={{0,1},{1,0},{2,3},{3,2},{4,5},{5,4},{6,7},{7,6},{8,9},{9,8},{10,11... | collective-permute-start | bytes 98312 | tf_op jit(solution)/shard_map/ppermute | solution.py:22
  19.3 5.2 %collective-permute-start.2 = (f32[64,128]{1,0:T(8,128)S(1)}, f32[64,128]{1,0:T(8,128)S(1)}, u32[]{:S(2)}, u32[]{:S(2)}) collective-permute-start(f32[64,128]{1,0:T(8,128)S(1)} %add.6), channel_id=1, source_target_pairs={{0,8},{4,12},{8,0},{12,4},{1,9},{5,13},{9,1},{13,5},{2,10},{6,14},... | collective-permute-start | bytes 98312 | tf_op jit(solution)/shard_map/ppermute | solution.py:22
  24.5 4.6 %collective-permute-start.3 = (f32[64,128]{1,0:T(8,128)S(1)}, f32[64,128]{1,0:T(8,128)S(1)}, u32[]{:S(2)}, u32[]{:S(2)}) collective-permute-start(f32[64,128]{1,0:T(8,128)S(1)} %add.7.factor_a_ref), channel_id=1, source_target_pairs={{0,4},{4,0},{8,12},{12,8},{1,5},{5,1},{9,13},{13,9},{2,6},{6,2},{1... | collective-permute-start | bytes 98312 | tf_op jit(solution)/shard_map/ppermute | solution.py:22
  25.7 6.3 %collective-permute-start.10 = (bf16[4,64,128]{2,1,0:T(8,128)(2,1)S(1)}, bf16[4,64,128]{2,1,0:T(8,128)(2,1)S(1)}, u32[]{:S(2)}, u32[]{:S(2)}) collective-permute-start(bf16[4,64,128]{2,1,0:T(8,128)(2,1)S(1)} %features.1.refs_7_), channel_id=1, source_target_pairs={{0,8},{4,12},{8,0},{12,4},{1,9},{5,13},{9,1},{13,5},{2,10},{6,14},... | collective-permute-start | bytes 196616 | tf_op jit(solution)/shard_map/ppermute | solution.py:22
  28.5 3.5 %collective-permute-start.5 = (bf16[1024,128]{1,0:T(8,128)(2,1)S(1)}, bf16[1024,128]{1,0:T(8,128)(2,1)S(1)}, u32[]{:S(2)}, u32[]{:S(2)}) collective-permute-start(bf16[1024,128]{1,0:T(8,128)(2,1)S(1)} %get-tuple-element.38.refs_0_), channel_id=1, source_target_pairs={{0,1},{1,0},{2,3},{3,2},{4,5},{5,4},{6,7},{7,6},{8,9},{9,8},{10,11... | collective-permute-start | bytes 786440 | tf_op jit(solution)/shard_map/ppermute | solution.py:22
  28.5 3.5 %collective-permute-start.6 = (bf16[1024,128]{1,0:T(8,128)(2,1)S(1)}, bf16[1024,128]{1,0:T(8,128)(2,1)S(1)}, u32[]{:S(2)}, u32[]{:S(2)}) collective-permute-start(bf16[1024,128]{1,0:T(8,128)(2,1)S(1)} %collective-permute-done.4.refs_1_), channel_id=1, source_target_pairs={{0,1},{1,0},{2,3},{3,2},{4,5},{5,4},{6,7},{7,6},{8,9},{9,8},{10,11... | collective-permute-start | bytes 786440 | tf_op jit(solution)/shard_map/ppermute | solution.py:22
  29.1 2.9 %collective-permute-start.9 = (bf16[2048,128]{1,0:T(8,128)(2,1)S(1)}, bf16[2048,128]{1,0:T(8,128)(2,1)S(1)}, u32[]{:S(2)}, u32[]{:S(2)}) collective-permute-start(bf16[2048,128]{1,0:T(8,128)(2,1)S(1)} %pad_maximum_fusion), channel_id=1, source_target_pairs={{0,1},{1,0},{2,3},{3,2},{4,5},{5,4},{6,7},{7,6},{8,9},{9,8},{10,11... | collective-permute-start | bytes 1572872 | tf_op jit(solution)/shard_map/ppermute | solution.py:22
  33.2 4.6 %collective-permute-start.11 = (f32[2,8,128]{2,1,0:T(8,128)S(1)}, f32[2,8,128]{2,1,0:T(8,128)S(1)}, u32[]{:S(2)}, u32[]{:S(2)}) collective-permute-start(f32[2,8,128]{2,1,0:T(8,128)S(1)} %get-tuple-element.46), channel_id=1, source_target_pairs={{0,8},{4,12},{8,0},{12,4},{1,9},{5,13},{9,1},{13,5},{2,10},{6,14},... | collective-permute-start | bytes 24584 | tf_op jit(solution)/shard_map/ppermute | solution.py:22

commit v12 on v11

--- a/solution.py
+++ b/solution.py
@@ -440,7 +440,7 @@
     factor, rounded, turned = factors(lengths, positions, loss_mask, own, received)
     feats = [features_of(lengths, rounded, turned)]
     even_masks = range(2, dp_count, 2)
-    steps = [("test", 1)] + [("dp", m) for m in reversed(masks_of(dp_count))]
+    steps = [("test", 1)] + [("dp", m) for m in masks_of(dp_count)]
     sums = [factor]
     for axis, mask in steps:
         if len(sums) == len(steps):

time: 38.6 us -> 37.6 us (0.974)
  starting transfers between devices: 16 us -> 14.8 us
    ppermute x12, starting transfers between devices: 16 us -> 14.8 us  [xor_permute(): return lax.ppermute(values, axis, [(i, i ^ mask) for i in range(size)])]
  transfers between devices with their start and end apart: 12 -> 12, of which waited for: 4 -> 5; matrix products, arithmetic and copies ran while one was open for 0% -> 0% of each run, Pallas kernels for 27% -> 28%
where the time goes in v12:
time: 37.6 us; the launch traced here: 37.4 us
  starting transfers between devices  14.8 us (39%)
  Pallas kernels  12.3 us (33%)
  waiting for transfers between devices  10.1 us (27%)
    ppermute x12, starting transfers between devices, xor_permute(): return lax.ppermute(values, axis, [(i, i ^ mask) for i in range(size)])  14.8 us
    ppermute x12, waiting for transfers between devices, xor_permute(): return lax.ppermute(values, axis, [(i, i ^ mask) for i in range(size)])  10.1 us
    pallas_call x1, Pallas kernels, project(): pl.pallas_call(functools.partial(project_body, rows), out_shape=(jax.Shap...  5.62 us
    pallas_call x1, Pallas kernels, inverses(): pl.pallas_call(functools.partial(inverses_body, total_tokens), out_shape=...  2.81 us
    pallas_call x1, Pallas kernels, scores_of(): pl.pallas_call(functools.partial(scores_body, len(feats), piece_counts),...  1.15 us
    pallas_call x1, Pallas kernels, factors(): pl.pallas_call(functools.partial(factors_body, len(received)), out_shape=...  0.84 us
    pallas_call x1, Pallas kernels, features_of(): pl.pallas_call(features_body, out_shape=jax.ShapeDtypeStruct((examples //...  0.79 us
  transfers between devices with their start and end apart: 12, of which 5 were waited for; matrix products, arithmetic and copies ran while one was open for 0% of the time, Pallas kernels for 28%

profile of v12, /device:TPU:0, one launch (start us, length us, event | category | flops | bytes accessed | tf_op | source)
XLA Modules:
  0.0 37.4 jit_solution(4204575456767582850)
XLA Ops:
  0.0 3.1 %collective-permute-start.7 = (bf16[2048,128]{1,0:T(8,128)(2,1)}, bf16[2048,128]{1,0:T(8,128)(2,1)S(1)}, u32[]{:S(2)}, u32[]{:S(2)}) collective-permute-start(bf16[2048,128]{1,0:T(8,128)(2,1)} %bitcast.10), channel_id=1, source_target_pairs={{0,4},{4,0},{8,12},{12,8},{1,5},{5,1},{9,13},{13,9},{2,6},{6,2},{1... | collective-permute-start | bytes 1572872 | tf_op jit(solution)/shard_map/ppermute | solution.py:22
  3.1 5.6 %project.1 = (f32[768,128]{1,0:T(8,128)S(1)}, bf16[768,128]{1,0:T(8,128)(2,1)S(1)}) custom-call(bf16[768,2048]{1,0:T(8,128)(2,1)S(1)} %bitcast.8, bf16[768,7168]{1,0:T(8,128)(2,1)} %bitcast.13, bf16[64,2048]{1,0:T(8,128)(2,1)S(1)} %bitcast.12, bf16[64,7168]{1,0:T(8,128)(2,1)S(1)} %bitcast.9), custom_call_target="tpu_custom_call" | custom-call | flops 905969664 | bytes 15335424 | tf_op jit(solution)/shard_map/project/pallas_call | solution.py:60
  8.8 2.0 %collective-permute-start = (bf16[768,128]{1,0:T(8,128)(2,1)S(1)}, bf16[768,128]{1,0:T(8,128)(2,1)S(1)}, u32[]{:S(2)}, u32[]{:S(2)}) collective-permute-start(bf16[768,128]{1,0:T(8,128)(2,1)S(1)} %get-tuple-element.28), channel_id=1, source_target_pairs={{0,2},{2,0},{1,3},{3,1},{4,6},{6,4},{5,7},{7,5},{8,10},{10,8},{9,1... | collective-permute-start | bytes 589832 | tf_op jit(solution)/shard_map/ppermute | solution.py:22
  10.7 0.2 pack.2
  11.0 0.2 collective-permute-start.4
  11.2 4.1 %collective-permute-done.7.tests_ref = bf16[2048,128]{1,0:T(8,128)(2,1)S(1)} collective-permute-done((bf16[2048,128]{1,0:T(8,128)(2,1)}, bf16[2048,128]{1,0:T(8,128)(2,1)S(1)}, u32[]{:S(2)}, u32[]{:S(2)}) %collective-permute-start.7) | collective-permute-done | bytes 524320 | tf_op jit(solution)/shard_map/ppermute | solution.py:22
  15.2 0.2 pack.3
  15.5 1.7 %collective-permute-start.8 = (bf16[1024,128]{1,0:T(8,128)(2,1)S(1)}, bf16[1024,128]{1,0:T(8,128)(2,1)S(1)}, u32[]{:S(2)}, u32[]{:S(2)}) collective-permute-start(bf16[1024,128]{1,0:T(8,128)(2,1)S(1)} %get-tuple-element.42), channel_id=1, source_target_pairs={{0,2},{2,0},{1,3},{3,1},{4,6},{6,4},{5,7},{7,5},{8,10},{10,8},{9,1... | collective-permute-start | bytes 786440 | tf_op jit(solution)/shard_map/ppermute | solution.py:22
  17.2 0.8 %factors.1 = (f32[64,128]{1,0:T(8,128)S(1)}, bf16[768,128]{1,0:T(8,128)(2,1)S(1)}, bf16[8,128,96]{2,1,0:T(8,128)(2,1)S(1)}) custom-call(s32[8]{0:T(128)S(1)} %copy-done.5, s32[1,96]{1,0:T(1,128)S(1)} %slots.1.positions_ref, s32[8,96]{1,0:T(8,128)S(1)} %copy-done.4, f32[768,128]{1,0:T(8,128)S(1)} %get-tuple-element.27.own_ref, ...), custom_call_target="tpu_custom_call" | custom-call | tf_op jit(solution)/shard_map/factors/pallas_call | solution.py:136
  18.0 0.1 collective-permute-start.1
  18.1 1.2 %collective-permute-done.1 = f32[64,128]{1,0:T(8,128)S(1)} collective-permute-done((f32[64,128]{1,0:T(8,128)S(1)}, f32[64,128]{1,0:T(8,128)S(1)}, u32[]{:S(2)}, u32[]{:S(2)}) %collective-permute-start.1) | collective-permute-done | bytes 32800 | tf_op jit(solution)/shard_map/ppermute | solution.py:22
  19.3 1.6 %collective-permute-start.2 = (f32[64,128]{1,0:T(8,128)S(1)}, f32[64,128]{1,0:T(8,128)S(1)}, u32[]{:S(2)}, u32[]{:S(2)}) collective-permute-start(f32[64,128]{1,0:T(8,128)S(1)} %add.6), channel_id=1, source_target_pairs={{0,4},{4,0},{8,12},{12,8},{1,5},{5,1},{9,13},{13,9},{2,6},{6,2},{1... | collective-permute-start | bytes 98312 | tf_op jit(solution)/shard_map/ppermute | solution.py:22
  20.9 0.8 %features.1.refs_7_ = bf16[4,64,128]{2,1,0:T(8,128)(2,1)S(1)} custom-call(s32[8]{0:T(128)S(1)} %copy-done.5, bf16[768,128]{1,0:T(8,128)(2,1)S(1)} %get-tuple-element.30.rounded_ref, bf16[8,128,96]{2,1,0:T(8,128)(2,1)S(1)} %get-tuple-element.31.turned_ref), custom_call_target="tpu_custom_call" | custom-call | flops 25165824 | bytes 8388608 | tf_op jit(solution)/shard_map/features/pallas_call | solution.py:168
  21.7 1.5 %collective-permute-done.2 = f32[64,128]{1,0:T(8,128)S(1)} collective-permute-done((f32[64,128]{1,0:T(8,128)S(1)}, f32[64,128]{1,0:T(8,128)S(1)}, u32[]{:S(2)}, u32[]{:S(2)}) %collective-permute-start.2) | collective-permute-done | bytes 32800 | tf_op jit(solution)/shard_map/ppermute | solution.py:22
  23.2 2.6 %collective-permute-start.3 = (f32[64,128]{1,0:T(8,128)S(1)}, f32[64,128]{1,0:T(8,128)S(1)}, u32[]{:S(2)}, u32[]{:S(2)}) collective-permute-start(f32[64,128]{1,0:T(8,128)S(1)} %add.7.factor_a_ref), channel_id=1, source_target_pairs={{0,8},{4,12},{8,0},{12,4},{1,9},{5,13},{9,1},{13,5},{2,10},{6,14},... | collective-permute-start | bytes 98312 | tf_op jit(solution)/shard_map/ppermute | solution.py:22
  25.8 0.3 collective-permute-start.10
  26.2 0.5 %collective-permute-start.6 = (bf16[1024,128]{1,0:T(8,128)(2,1)S(1)}, bf16[1024,128]{1,0:T(8,128)(2,1)S(1)}, u32[]{:S(2)}, u32[]{:S(2)}) collective-permute-start(bf16[1024,128]{1,0:T(8,128)(2,1)S(1)} %collective-permute-done.4.refs_1_), channel_id=1, source_target_pairs={{0,1},{1,0},{2,3},{3,2},{4,5},{5,4},{6,7},{7,6},{8,9},{9,8},{10,11... | collective-permute-start | bytes 786440 | tf_op jit(solution)/shard_map/ppermute | solution.py:22
  26.7 1.4 %collective-permute-done.3.factor_b_ref = f32[64,128]{1,0:T(8,128)S(1)} collective-permute-done((f32[64,128]{1,0:T(8,128)S(1)}, f32[64,128]{1,0:T(8,128)S(1)}, u32[]{:S(2)}, u32[]{:S(2)}) %collective-permute-start.3) | collective-permute-done | bytes 32800 | tf_op jit(solution)/shard_map/ppermute | solution.py:22
  28.1 0.1 collective-permute-start.9
  28.2 2.8 %inverses.1 = (bf16[2,64,64]{2,1,0:T(8,128)(2,1)S(1)}, bf16[2,128,128]{2,1,0:T(8,128)(2,1)S(1)}) custom-call(f32[64,128]{1,0:T(8,128)S(1)} %add.7.factor_a_ref, f32[64,128]{1,0:T(8,128)S(1)} %collective-permute-done.3.factor_b_ref), custom_call_target="tpu_custom_call" | custom-call | flops 17179869184 | tf_op jit(solution)/shard_map/inverses/pallas_call | solution.py:263
  31.0 1.1 %scores.1 = (f32[2,8,128]{2,1,0:T(8,128)S(1)}, f32[2,8,128]{2,1,0:T(8,128)S(1)}) custom-call(bf16[2,64,64]{2,1,0:T(8,128)(2,1)S(1)} %get-tuple-element.33.grad_ref, bf16[2,128,128]{2,1,0:T(8,128)(2,1)S(1)} %get-tuple-element.34.in_ref, bf16[1024,128]{1,0:T(8,128)(2,1)S(1)} %get-tuple-element.38.refs_0_, ...), custom_call_target="tpu_custom_call" | custom-call | tf_op jit(solution)/shard_map/scores/pallas_call | solution.py:373
  32.2 2.7 %collective-permute-start.11 = (f32[2,8,128]{2,1,0:T(8,128)S(1)}, f32[2,8,128]{2,1,0:T(8,128)S(1)}, u32[]{:S(2)}, u32[]{:S(2)}) collective-permute-start(f32[2,8,128]{2,1,0:T(8,128)S(1)} %get-tuple-element.46), channel_id=1, source_target_pairs={{0,8},{4,12},{8,0},{12,4},{1,9},{5,13},{9,1},{13,5},{2,10},{6,14},... | collective-permute-start | bytes 24584 | tf_op jit(solution)/shard_map/ppermute | solution.py:22
  34.9 1.9 %collective-permute-done.11.refs_1_ = f32[2,8,128]{2,1,0:T(8,128)S(1)} collective-permute-done((f32[2,8,128]{2,1,0:T(8,128)S(1)}, f32[2,8,128]{2,1,0:T(8,128)S(1)}, u32[]{:S(2)}, u32[]{:S(2)}) %collective-permute-start.11) | collective-permute-done | bytes 8224 | tf_op jit(solution)/shard_map/ppermute | solution.py:22
  36.7 0.7 %finish.1 = f32[64,64]{1,0:T(8,128)} custom-call(f32[2,8,128]{2,1,0:T(8,128)S(1)} %get-tuple-element.45.refs_0_, f32[2,8,128]{2,1,0:T(8,128)S(1)} %collective-permute-done.11.refs_1_), custom_call_target="tpu_custom_call" | custom-call | tf_op jit(solution)/shard_map/finish/pallas_call | solution.py:406
  (24 shorter events, 0.1 us)
Async XLA Ops:
  0.0 3.1 %copy-start = (bf16[8,96,2048]{2,1,0:T(8,128)(2,1)S(1)}, bf16[8,96,2048]{2,1,0:T(8,128)(2,1)}, u32[]{:S(2)}) copy-start(bf16[8,96,2048]{2,1,0:T(8,128)(2,1)} %param.7) | copy-start | bytes 9437188
  0.0 3.1 %copy-start.1 = (bf16[7168,64]{0,1:T(8,128)(2,1)S(1)}, bf16[7168,64]{0,1:T(8,128)(2,1)}, u32[]{:S(2)}) copy-start(bf16[7168,64]{0,1:T(8,128)(2,1)} %param.10) | copy-start | bytes 2752516
  0.0 3.1 %copy-start.3 = (bf16[2048,64]{0,1:T(8,128)(2,1)S(1)}, bf16[2048,64]{0,1:T(8,128)(2,1)}, u32[]{:S(2)}) copy-start(bf16[2048,64]{0,1:T(8,128)(2,1)} %param.9) | copy-start | bytes 786436
  0.0 15.2 %collective-permute-start.7 = (bf16[2048,128]{1,0:T(8,128)(2,1)}, bf16[2048,128]{1,0:T(8,128)(2,1)S(1)}, u32[]{:S(2)}, u32[]{:S(2)}) collective-permute-start(bf16[2048,128]{1,0:T(8,128)(2,1)} %bitcast.10), channel_id=1, source_target_pairs={{0,4},{4,0},{8,12},{12,8},{1,5},{5,1},{9,13},{13,9},{2,6},{6,2},{1... | collective-permute-start | bytes 1572872 | tf_op jit(solution)/shard_map/ppermute | solution.py:22
  3.1 7.6 %copy-start.2 = (bf16[128,32,64]{0,2,1:T(8,128)(2,1)S(1)}, bf16[128,32,64]{0,2,1:T(8,128)(2,1)}, u32[]{:S(2)}) copy-start(bf16[128,32,64]{0,2,1:T(8,128)(2,1)} %param.13) | copy-start | bytes 1572868
  3.1 14.1 %copy-start.4 = (s32[8,96]{1,0:T(8,128)S(1)}, s32[8,96]{1,0:T(8,128)}, u32[]{:S(2)}) copy-start(s32[8,96]{1,0:T(8,128)} %mask_ref.1) | copy-start | bytes 9220
  3.1 14.1 %copy-start.5 = (s32[8]{0:T(128)S(1)}, s32[8]{0:T(128)}, u32[]{:S(2)}) copy-start(s32[8]{0:T(128)} %lengths_ref.3) | copy-start | bytes 100
  8.8 8.4 %collective-permute-start = (bf16[768,128]{1,0:T(8,128)(2,1)S(1)}, bf16[768,128]{1,0:T(8,128)(2,1)S(1)}, u32[]{:S(2)}, u32[]{:S(2)}) collective-permute-start(bf16[768,128]{1,0:T(8,128)(2,1)S(1)} %get-tuple-element.28), channel_id=1, source_target_pairs={{0,2},{2,0},{1,3},{3,1},{4,6},{6,4},{5,7},{7,5},{8,10},{10,8},{9,1... | collective-permute-start | bytes 589832 | tf_op jit(solution)/shard_map/ppermute | solution.py:22
  11.0 15.2 %collective-permute-start.4 = (bf16[1024,128]{1,0:T(8,128)(2,1)S(1)}, bf16[1024,128]{1,0:T(8,128)(2,1)S(1)}, u32[]{:S(2)}, u32[]{:S(2)}) collective-permute-start(bf16[1024,128]{1,0:T(8,128)(2,1)S(1)} %get-tuple-element.37), channel_id=1, source_target_pairs={{0,2},{2,0},{1,3},{3,1},{4,6},{6,4},{5,7},{7,5},{8,10},{10,8},{9,1... | collective-permute-start | bytes 786440 | tf_op jit(solution)/shard_map/ppermute | solution.py:22
  15.5 12.6 %collective-permute-start.8 = (bf16[1024,128]{1,0:T(8,128)(2,1)S(1)}, bf16[1024,128]{1,0:T(8,128)(2,1)S(1)}, u32[]{:S(2)}, u32[]{:S(2)}) collective-permute-start(bf16[1024,128]{1,0:T(8,128)(2,1)S(1)} %get-tuple-element.42), channel_id=1, source_target_pairs={{0,2},{2,0},{1,3},{3,1},{4,6},{6,4},{5,7},{7,5},{8,10},{10,8},{9,1... | collective-permute-start | bytes 786440 | tf_op jit(solution)/shard_map/ppermute | solution.py:22
  18.0 1.3 %collective-permute-start.1 = (f32[64,128]{1,0:T(8,128)S(1)}, f32[64,128]{1,0:T(8,128)S(1)}, u32[]{:S(2)}, u32[]{:S(2)}) collective-permute-start(f32[64,128]{1,0:T(8,128)S(1)} %get-tuple-element.29), channel_id=1, source_target_pairs={{0,1},{1,0},{2,3},{3,2},{4,5},{5,4},{6,7},{7,6},{8,9},{9,8},{10,11... | collective-permute-start | bytes 98312 | tf_op jit(solution)/shard_map/ppermute | solution.py:22
  19.3 3.9 %collective-permute-start.2 = (f32[64,128]{1,0:T(8,128)S(1)}, f32[64,128]{1,0:T(8,128)S(1)}, u32[]{:S(2)}, u32[]{:S(2)}) collective-permute-start(f32[64,128]{1,0:T(8,128)S(1)} %add.6), channel_id=1, source_target_pairs={{0,4},{4,0},{8,12},{12,8},{1,5},{5,1},{9,13},{13,9},{2,6},{6,2},{1... | collective-permute-start | bytes 98312 | tf_op jit(solution)/shard_map/ppermute | solution.py:22
  23.2 4.8 %collective-permute-start.3 = (f32[64,128]{1,0:T(8,128)S(1)}, f32[64,128]{1,0:T(8,128)S(1)}, u32[]{:S(2)}, u32[]{:S(2)}) collective-permute-start(f32[64,128]{1,0:T(8,128)S(1)} %add.7.factor_a_ref), channel_id=1, source_target_pairs={{0,8},{4,12},{8,0},{12,4},{1,9},{5,13},{9,1},{13,5},{2,10},{6,14},... | collective-permute-start | bytes 98312 | tf_op jit(solution)/shard_map/ppermute | solution.py:22
  25.8 5.2 %collective-permute-start.10 = (bf16[4,64,128]{2,1,0:T(8,128)(2,1)S(1)}, bf16[4,64,128]{2,1,0:T(8,128)(2,1)S(1)}, u32[]{:S(2)}, u32[]{:S(2)}) collective-permute-start(bf16[4,64,128]{2,1,0:T(8,128)(2,1)S(1)} %features.1.refs_7_), channel_id=1, source_target_pairs={{0,8},{4,12},{8,0},{12,4},{1,9},{5,13},{9,1},{13,5},{2,10},{6,14},... | collective-permute-start | bytes 196616 | tf_op jit(solution)/shard_map/ppermute | solution.py:22
  26.2 4.8 %collective-permute-start.5 = (bf16[1024,128]{1,0:T(8,128)(2,1)S(1)}, bf16[1024,128]{1,0:T(8,128)(2,1)S(1)}, u32[]{:S(2)}, u32[]{:S(2)}) collective-permute-start(bf16[1024,128]{1,0:T(8,128)(2,1)S(1)} %get-tuple-element.38.refs_0_), channel_id=1, source_target_pairs={{0,1},{1,0},{2,3},{3,2},{4,5},{5,4},{6,7},{7,6},{8,9},{9,8},{10,11... | collective-permute-start | bytes 786440 | tf_op jit(solution)/shard_map/ppermute | solution.py:22
  26.2 4.8 %collective-permute-start.6 = (bf16[1024,128]{1,0:T(8,128)(2,1)S(1)}, bf16[1024,128]{1,0:T(8,128)(2,1)S(1)}, u32[]{:S(2)}, u32[]{:S(2)}) collective-permute-start(bf16[1024,128]{1,0:T(8,128)(2,1)S(1)} %collective-permute-done.4.refs_1_), channel_id=1, source_target_pairs={{0,1},{1,0},{2,3},{3,2},{4,5},{5,4},{6,7},{7,6},{8,9},{9,8},{10,11... | collective-permute-start | bytes 786440 | tf_op jit(solution)/shard_map/ppermute | solution.py:22
  28.1 2.9 %collective-permute-start.9 = (bf16[2048,128]{1,0:T(8,128)(2,1)S(1)}, bf16[2048,128]{1,0:T(8,128)(2,1)S(1)}, u32[]{:S(2)}, u32[]{:S(2)}) collective-permute-start(bf16[2048,128]{1,0:T(8,128)(2,1)S(1)} %pad_maximum_fusion), channel_id=1, source_target_pairs={{0,1},{1,0},{2,3},{3,2},{4,5},{5,4},{6,7},{7,6},{8,9},{9,8},{10,11... | collective-permute-start | bytes 1572872 | tf_op jit(solution)/shard_map/ppermute | solution.py:22
  32.2 4.6 %collective-permute-start.11 = (f32[2,8,128]{2,1,0:T(8,128)S(1)}, f32[2,8,128]{2,1,0:T(8,128)S(1)}, u32[]{:S(2)}, u32[]{:S(2)}) collective-permute-start(f32[2,8,128]{2,1,0:T(8,128)S(1)} %get-tuple-element.46), channel_id=1, source_target_pairs={{0,8},{4,12},{8,0},{12,4},{1,9},{5,13},{9,1},{13,5},{2,10},{6,14},... | collective-permute-start | bytes 24584 | tf_op jit(solution)/shard_map/ppermute | solution.py:22

commit v13 on v12

--- a/solution.py
+++ b/solution.py
@@ -107,73 +107,64 @@
     )()
 
 
-def factors_body(received, lengths_ref, positions_ref, mask_ref, own_ref, *refs):
-    received_refs = refs[:received]
-    factor_ref, rounded_ref, turned_ref = refs[received:]
-    examples, seq_len = mask_ref.shape
+def factors_body(live_ref, own_ref, *refs):
+    received_refs, (factor_ref, rounded_ref) = refs[:-2], refs[-2:]
     rank = factor_ref.shape[0]
-    positions = positions_ref[...]
-    total = None
-    for example in range(examples):
-        rows = pl.ds(example * seq_len, seq_len)
-        summed = own_ref[rows, :]
-        for ref in received_refs:
-            summed = summed + ref[rows, :].astype(f32)
-        rounded = summed.astype(bf16)
-        rounded_ref[rows, :] = rounded
-        live = (mask_ref[example : example + 1, :] > 0) & (positions < lengths_ref[example])
-        turned = jnp.where(live, rounded.astype(f32).T, 0.0).astype(bf16)
-        turned_ref[example] = turned
-        products = jnp.dot(turned, rounded, preferred_element_type=f32)
-        total = products if total is None else total + products
+    summed = own_ref[...]
+    for ref in received_refs:
+        summed = summed + ref[...].astype(f32)
+    rounded = summed.astype(bf16)
+    rounded_ref[...] = rounded
+    turned = (rounded.astype(f32).T * live_ref[...]).astype(bf16)
+    total = jnp.dot(turned, rounded, preferred_element_type=f32)
     lane = lax.broadcasted_iota(jnp.int32, (rank, 2 * rank), 1)
     factor_ref[...] = jnp.where(lane < rank, total[:rank, :], total[rank:, :])
 
 
-def factors(lengths, positions, mask, own, received):
+def factors(live, own, received):
     tokens, width = own.shape
-    examples, seq_len = mask.shape
-    return pl.pallas_call(
-        functools.partial(factors_body, len(received)),
+    return pl.pallas_call(
+        factors_body,
         out_shape=(
             jax.ShapeDtypeStruct((width // 2, width), f32),
             jax.ShapeDtypeStruct((tokens, width), bf16),
-            jax.ShapeDtypeStruct((examples, width, seq_len), bf16),
         ),
-        in_specs=[SMEM, VMEM, VMEM, VMEM] + [VMEM] * len(received),
-        out_specs=(VMEM, VMEM, VMEM),
+        in_specs=[VMEM, VMEM] + [VMEM] * len(received),
+        out_specs=(VMEM, VMEM),
         compiler_params=pltpu.CompilerParams(vmem_limit_bytes=4 * MIB),
         name="factors",
-    )(lengths, positions, mask, own, *received)
-
-
-def features_body(lengths_ref, rounded_ref, turned_ref, feats_ref):
+    )(live, own, *received)
+
+
+def features_body(lengths_ref, positions_ref, mask_ref, rounded_ref, feats_ref):
     half, rank, _ = feats_ref.shape
-    examples, _, seq_len = turned_ref.shape
+    seq_len = mask_ref.shape[1]
     lane = lax.broadcasted_iota(jnp.int32, (rank, 2 * rank), 1)
+    positions = positions_ref[...]
 
     def features(example):
-        products = jnp.dot(
-            turned_ref[example, rank:, :], rounded_ref[pl.ds(example * seq_len, seq_len), :], preferred_element_type=f32
-        )
-        return products / lengths_ref[example].astype(f32)
+        rounded = rounded_ref[pl.ds(example * seq_len, seq_len), :]
+        live = (mask_ref[example : example + 1, :] > 0) & (positions < lengths_ref[example])
+        turned = jnp.where(live, rounded.astype(f32).T, 0.0)[rank:, :].astype(bf16)
+        return jnp.dot(turned, rounded, preferred_element_type=f32) / lengths_ref[example].astype(f32)
 
     for pair in range(half):
         other = pltpu.roll(features(half + pair), rank, 1)
         feats_ref[pair] = jnp.where(lane < rank, features(pair), other).astype(bf16)
 
 
-def features_of(lengths, rounded, turned):
-    examples, width, seq_len = turned.shape
+def features_of(lengths, positions, mask, rounded):
+    examples, seq_len = mask.shape
+    width = rounded.shape[1]
     return pl.pallas_call(
         features_body,
         out_shape=jax.ShapeDtypeStruct((examples // 2, width // 2, width), bf16),
-        in_specs=[SMEM, VMEM, VMEM],
+        in_specs=[SMEM, VMEM, VMEM, VMEM],
         out_specs=VMEM,
         compiler_params=pltpu.CompilerParams(vmem_limit_bytes=4 * MIB),
         cost_estimate=pl.CostEstimate(flops=2 * examples * seq_len * width * width, bytes_accessed=8 * MIB, transcendentals=0),
         name="features",
-    )(lengths, rounded, turned)
+    )(lengths, positions, mask, rounded)
 
 
 def split(values):
@@ -435,10 +426,12 @@
     cut = pack(after(tests, sent), 4 * MIB)
     near = [cut[0]] + [xor_permute(cut[mask], "feat", mask) for mask in range(1, feat_count)]
     received = [xor_permute(sent, "feat", mask) for mask in range(1, feat_count)]
-    cut = pack(after(far_tests, *(sent,)), 4 * MIB)
+    slot_numbers = jnp.arange(seq_len, dtype=jnp.int32)
+    live = ((loss_mask > 0) & (slot_numbers[None, :] < lengths[:, None])).astype(f32).reshape(1, tokens)
+    cut = pack(after(far_tests, sent, live), 4 * MIB)
     far = [cut[0]] + [xor_permute(cut[mask], "feat", mask) for mask in range(1, feat_count)]
-    factor, rounded, turned = factors(lengths, positions, loss_mask, own, received)
-    feats = [features_of(lengths, rounded, turned)]
+    factor, rounded = factors(live, own, received)
+    feats = [features_of(lengths, positions, loss_mask, rounded)]
     even_masks = range(2, dp_count, 2)
     steps = [("test", 1)] + [("dp", m) for m in masks_of(dp_count)]
     sums = [factor]

time: 37.6 us -> 37 us (0.984)
  Pallas kernels: 12.3 us -> 11.8 us
    pallas_call x1, Pallas kernels: 0.84 us -> 0.27 us  [factors(): pl.pallas_call(factors_body, out_shape=(jax.ShapeDtypeStruct((width // 2,...]
  transfers between devices with their start and end apart: 12 -> 12, of which waited for: 5 -> 5; matrix products, arithmetic and copies ran while one was open for 0% -> 1% of each run, Pallas kernels for 28% -> 27%
where the time goes in v13:
time: 37 us; the launch traced here: 36.8 us
  starting transfers between devices  14.8 us (40%)
  Pallas kernels  11.8 us (32%)
  waiting for transfers between devices  9.84 us (27%)
    ppermute x12, starting transfers between devices, xor_permute(): return lax.ppermute(values, axis, [(i, i ^ mask) for i in range(size)])  14.8 us
    ppermute x12, waiting for transfers between devices, xor_permute(): return lax.ppermute(values, axis, [(i, i ^ mask) for i in range(size)])  9.84 us
    pallas_call x1, Pallas kernels, project(): pl.pallas_call(functools.partial(project_body, rows), out_shape=(jax.Shap...  5.62 us
    pallas_call x1, Pallas kernels, inverses(): pl.pallas_call(functools.partial(inverses_body, total_tokens), out_shape=...  2.81 us
    pallas_call x1, Pallas kernels, scores_of(): pl.pallas_call(functools.partial(scores_body, len(feats), piece_counts),...  1.15 us
    pallas_call x1, Pallas kernels, features_of(): pl.pallas_call(features_body, out_shape=jax.ShapeDtypeStruct((examples //...  0.87 us
  transfers between devices with their start and end apart: 12, of which 5 were waited for; matrix products, arithmetic and copies ran while one was open for 1% of the time, Pallas kernels for 27%

profile of v13, /device:TPU:0, one launch (start us, length us, event | category | flops | bytes accessed | tf_op | source)
XLA Modules:
  0.0 36.8 jit_solution(1331571113195962497)
XLA Ops:
  0.0 3.1 %collective-permute-start.7 = (bf16[2048,128]{1,0:T(8,128)(2,1)}, bf16[2048,128]{1,0:T(8,128)(2,1)S(1)}, u32[]{:S(2)}, u32[]{:S(2)}) collective-permute-start(bf16[2048,128]{1,0:T(8,128)(2,1)} %bitcast.10), channel_id=1, source_target_pairs={{0,4},{4,0},{8,12},{12,8},{1,5},{5,1},{9,13},{13,9},{2,6},{6,2},{1... | collective-permute-start | bytes 1572872 | tf_op jit(solution)/shard_map/ppermute | solution.py:22
  3.1 5.6 %project.1 = (f32[768,128]{1,0:T(8,128)S(1)}, bf16[768,128]{1,0:T(8,128)(2,1)S(1)}) custom-call(bf16[768,2048]{1,0:T(8,128)(2,1)S(1)} %bitcast.8, bf16[768,7168]{1,0:T(8,128)(2,1)} %bitcast.13, bf16[64,2048]{1,0:T(8,128)(2,1)S(1)} %bitcast.12, bf16[64,7168]{1,0:T(8,128)(2,1)S(1)} %bitcast.9), custom_call_target="tpu_custom_call" | custom-call | flops 905969664 | bytes 15335424 | tf_op jit(solution)/shard_map/project/pallas_call | solution.py:60
  8.8 2.0 %collective-permute-start = (bf16[768,128]{1,0:T(8,128)(2,1)S(1)}, bf16[768,128]{1,0:T(8,128)(2,1)S(1)}, u32[]{:S(2)}, u32[]{:S(2)}) collective-permute-start(bf16[768,128]{1,0:T(8,128)(2,1)S(1)} %get-tuple-element.27), channel_id=1, source_target_pairs={{0,2},{2,0},{1,3},{3,1},{4,6},{6,4},{5,7},{7,5},{8,10},{10,8},{9,1... | collective-permute-start | bytes 589832 | tf_op jit(solution)/shard_map/ppermute | solution.py:22
  10.7 0.2 pack.2
  11.0 0.2 collective-permute-start.4
  11.2 0.1 reshape.25.live_ref
  11.3 3.9 %collective-permute-done.7.tests_ref = bf16[2048,128]{1,0:T(8,128)(2,1)S(1)} collective-permute-done((bf16[2048,128]{1,0:T(8,128)(2,1)}, bf16[2048,128]{1,0:T(8,128)(2,1)S(1)}, u32[]{:S(2)}, u32[]{:S(2)}) %collective-permute-start.7) | collective-permute-done | bytes 524320 | tf_op jit(solution)/shard_map/ppermute | solution.py:22
  15.2 0.2 pack.3
  15.5 1.7 %collective-permute-start.8 = (bf16[1024,128]{1,0:T(8,128)(2,1)S(1)}, bf16[1024,128]{1,0:T(8,128)(2,1)S(1)}, u32[]{:S(2)}, u32[]{:S(2)}) collective-permute-start(bf16[1024,128]{1,0:T(8,128)(2,1)S(1)} %get-tuple-element.40), channel_id=1, source_target_pairs={{0,2},{2,0},{1,3},{3,1},{4,6},{6,4},{5,7},{7,5},{8,10},{10,8},{9,1... | collective-permute-start | bytes 786440 | tf_op jit(solution)/shard_map/ppermute | solution.py:22
  17.2 0.3 factors.1
  17.5 0.1 collective-permute-start.1
  17.5 1.2 %collective-permute-done.1 = f32[64,128]{1,0:T(8,128)S(1)} collective-permute-done((f32[64,128]{1,0:T(8,128)S(1)}, f32[64,128]{1,0:T(8,128)S(1)}, u32[]{:S(2)}, u32[]{:S(2)}) %collective-permute-start.1) | collective-permute-done | bytes 32800 | tf_op jit(solution)/shard_map/ppermute | solution.py:22
  18.7 1.6 %collective-permute-start.2 = (f32[64,128]{1,0:T(8,128)S(1)}, f32[64,128]{1,0:T(8,128)S(1)}, u32[]{:S(2)}, u32[]{:S(2)}) collective-permute-start(f32[64,128]{1,0:T(8,128)S(1)} %add.6), channel_id=1, source_target_pairs={{0,4},{4,0},{8,12},{12,8},{1,5},{5,1},{9,13},{13,9},{2,6},{6,2},{1... | collective-permute-start | bytes 98312 | tf_op jit(solution)/shard_map/ppermute | solution.py:22
  20.3 0.9 %features.1.refs_7_ = bf16[4,64,128]{2,1,0:T(8,128)(2,1)S(1)} custom-call(s32[8]{0:T(128)S(1)} %copy-done.5, s32[1,96]{1,0:T(1,128)S(1)} %slots.1.positions_ref, s32[8,96]{1,0:T(8,128)S(1)} %copy-done.4, bf16[768,128]{1,0:T(8,128)(2,1)S(1)} %get-tuple-element.29.rounded_ref), custom_call_target="tpu_custom_call" | custom-call | flops 25165824 | bytes 8388608 | tf_op jit(solution)/shard_map/features/pallas_call | solution.py:159
  21.2 1.5 %collective-permute-done.2 = f32[64,128]{1,0:T(8,128)S(1)} collective-permute-done((f32[64,128]{1,0:T(8,128)S(1)}, f32[64,128]{1,0:T(8,128)S(1)}, u32[]{:S(2)}, u32[]{:S(2)}) %collective-permute-start.2) | collective-permute-done | bytes 32800 | tf_op jit(solution)/shard_map/ppermute | solution.py:22
  22.7 2.6 %collective-permute-start.3 = (f32[64,128]{1,0:T(8,128)S(1)}, f32[64,128]{1,0:T(8,128)S(1)}, u32[]{:S(2)}, u32[]{:S(2)}) collective-permute-start(f32[64,128]{1,0:T(8,128)S(1)} %add.7.factor_a_ref), channel_id=1, source_target_pairs={{0,8},{4,12},{8,0},{12,4},{1,9},{5,13},{9,1},{13,5},{2,10},{6,14},... | collective-permute-start | bytes 98312 | tf_op jit(solution)/shard_map/ppermute | solution.py:22
  25.2 0.3 collective-permute-start.10
  25.6 0.5 %collective-permute-start.6 = (bf16[1024,128]{1,0:T(8,128)(2,1)S(1)}, bf16[1024,128]{1,0:T(8,128)(2,1)S(1)}, u32[]{:S(2)}, u32[]{:S(2)}) collective-permute-start(bf16[1024,128]{1,0:T(8,128)(2,1)S(1)} %collective-permute-done.4.refs_1_), channel_id=1, source_target_pairs={{0,1},{1,0},{2,3},{3,2},{4,5},{5,4},{6,7},{7,6},{8,9},{9,8},{10,11... | collective-permute-start | bytes 786440 | tf_op jit(solution)/shard_map/ppermute | solution.py:22
  26.1 1.4 %collective-permute-done.3.factor_b_ref = f32[64,128]{1,0:T(8,128)S(1)} collective-permute-done((f32[64,128]{1,0:T(8,128)S(1)}, f32[64,128]{1,0:T(8,128)S(1)}, u32[]{:S(2)}, u32[]{:S(2)}) %collective-permute-start.3) | collective-permute-done | bytes 32800 | tf_op jit(solution)/shard_map/ppermute | solution.py:22
  27.6 2.8 %inverses.1 = (bf16[2,64,64]{2,1,0:T(8,128)(2,1)S(1)}, bf16[2,128,128]{2,1,0:T(8,128)(2,1)S(1)}) custom-call(f32[64,128]{1,0:T(8,128)S(1)} %add.7.factor_a_ref, f32[64,128]{1,0:T(8,128)S(1)} %collective-permute-done.3.factor_b_ref), custom_call_target="tpu_custom_call" | custom-call | flops 17179869184 | tf_op jit(solution)/shard_map/inverses/pallas_call | solution.py:254
  30.4 1.1 %scores.1 = (f32[2,8,128]{2,1,0:T(8,128)S(1)}, f32[2,8,128]{2,1,0:T(8,128)S(1)}) custom-call(bf16[2,64,64]{2,1,0:T(8,128)(2,1)S(1)} %get-tuple-element.31.grad_ref, bf16[2,128,128]{2,1,0:T(8,128)(2,1)S(1)} %get-tuple-element.32.in_ref, bf16[1024,128]{1,0:T(8,128)(2,1)S(1)} %get-tuple-element.36.refs_0_, ...), custom_call_target="tpu_custom_call" | custom-call | tf_op jit(solution)/shard_map/scores/pallas_call | solution.py:364
  31.6 2.7 %collective-permute-start.11 = (f32[2,8,128]{2,1,0:T(8,128)S(1)}, f32[2,8,128]{2,1,0:T(8,128)S(1)}, u32[]{:S(2)}, u32[]{:S(2)}) collective-permute-start(f32[2,8,128]{2,1,0:T(8,128)S(1)} %get-tuple-element.44), channel_id=1, source_target_pairs={{0,8},{4,12},{8,0},{12,4},{1,9},{5,13},{9,1},{13,5},{2,10},{6,14},... | collective-permute-start | bytes 24584 | tf_op jit(solution)/shard_map/ppermute | solution.py:22
  34.3 1.9 %collective-permute-done.11.refs_1_ = f32[2,8,128]{2,1,0:T(8,128)S(1)} collective-permute-done((f32[2,8,128]{2,1,0:T(8,128)S(1)}, f32[2,8,128]{2,1,0:T(8,128)S(1)}, u32[]{:S(2)}, u32[]{:S(2)}) %collective-permute-start.11) | collective-permute-done | bytes 8224 | tf_op jit(solution)/shard_map/ppermute | solution.py:22
  36.2 0.7 %finish.1 = f32[64,64]{1,0:T(8,128)} custom-call(f32[2,8,128]{2,1,0:T(8,128)S(1)} %get-tuple-element.43.refs_0_, f32[2,8,128]{2,1,0:T(8,128)S(1)} %collective-permute-done.11.refs_1_), custom_call_target="tpu_custom_call" | custom-call | tf_op jit(solution)/shard_map/finish/pallas_call | solution.py:397
  (26 shorter events, 0.2 us)
Async XLA Ops:
  0.0 3.1 %copy-start = (bf16[8,96,2048]{2,1,0:T(8,128)(2,1)S(1)}, bf16[8,96,2048]{2,1,0:T(8,128)(2,1)}, u32[]{:S(2)}) copy-start(bf16[8,96,2048]{2,1,0:T(8,128)(2,1)} %param.7) | copy-start | bytes 9437188
  0.0 3.1 %copy-start.1 = (bf16[7168,64]{0,1:T(8,128)(2,1)S(1)}, bf16[7168,64]{0,1:T(8,128)(2,1)}, u32[]{:S(2)}) copy-start(bf16[7168,64]{0,1:T(8,128)(2,1)} %param.10) | copy-start | bytes 2752516
  0.0 3.1 %copy-start.3 = (bf16[2048,64]{0,1:T(8,128)(2,1)S(1)}, bf16[2048,64]{0,1:T(8,128)(2,1)}, u32[]{:S(2)}) copy-start(bf16[2048,64]{0,1:T(8,128)(2,1)} %param.9) | copy-start | bytes 786436
  0.0 15.2 %collective-permute-start.7 = (bf16[2048,128]{1,0:T(8,128)(2,1)}, bf16[2048,128]{1,0:T(8,128)(2,1)S(1)}, u32[]{:S(2)}, u32[]{:S(2)}) collective-permute-start(bf16[2048,128]{1,0:T(8,128)(2,1)} %bitcast.10), channel_id=1, source_target_pairs={{0,4},{4,0},{8,12},{12,8},{1,5},{5,1},{9,13},{13,9},{2,6},{6,2},{1... | collective-permute-start | bytes 1572872 | tf_op jit(solution)/shard_map/ppermute | solution.py:22
  3.1 7.6 %copy-start.2 = (bf16[128,32,64]{0,2,1:T(8,128)(2,1)S(1)}, bf16[128,32,64]{0,2,1:T(8,128)(2,1)}, u32[]{:S(2)}) copy-start(bf16[128,32,64]{0,2,1:T(8,128)(2,1)} %param.13) | copy-start | bytes 1572868
  3.1 8.0 %copy-start.4 = (s32[8,96]{1,0:T(8,128)S(1)}, s32[8,96]{1,0:T(8,128)}, u32[]{:S(2)}) copy-start(s32[8,96]{1,0:T(8,128)} %mask_ref.1) | copy-start | bytes 9220
  3.1 8.0 %copy-start.5 = (s32[8]{0:T(128)S(1)}, s32[8]{0:T(128)}, u32[]{:S(2)}) copy-start(s32[8]{0:T(128)} %lengths_ref.1) | copy-start | bytes 100
  8.8 8.4 %collective-permute-start = (bf16[768,128]{1,0:T(8,128)(2,1)S(1)}, bf16[768,128]{1,0:T(8,128)(2,1)S(1)}, u32[]{:S(2)}, u32[]{:S(2)}) collective-permute-start(bf16[768,128]{1,0:T(8,128)(2,1)S(1)} %get-tuple-element.27), channel_id=1, source_target_pairs={{0,2},{2,0},{1,3},{3,1},{4,6},{6,4},{5,7},{7,5},{8,10},{10,8},{9,1... | collective-permute-start | bytes 589832 | tf_op jit(solution)/shard_map/ppermute | solution.py:22
  11.0 14.6 %collective-permute-start.4 = (bf16[1024,128]{1,0:T(8,128)(2,1)S(1)}, bf16[1024,128]{1,0:T(8,128)(2,1)S(1)}, u32[]{:S(2)}, u32[]{:S(2)}) collective-permute-start(bf16[1024,128]{1,0:T(8,128)(2,1)S(1)} %get-tuple-element.35), channel_id=1, source_target_pairs={{0,2},{2,0},{1,3},{3,1},{4,6},{6,4},{5,7},{7,5},{8,10},{10,8},{9,1... | collective-permute-start | bytes 786440 | tf_op jit(solution)/shard_map/ppermute | solution.py:22
  15.5 12.0 %collective-permute-start.8 = (bf16[1024,128]{1,0:T(8,128)(2,1)S(1)}, bf16[1024,128]{1,0:T(8,128)(2,1)S(1)}, u32[]{:S(2)}, u32[]{:S(2)}) collective-permute-start(bf16[1024,128]{1,0:T(8,128)(2,1)S(1)} %get-tuple-element.40), channel_id=1, source_target_pairs={{0,2},{2,0},{1,3},{3,1},{4,6},{6,4},{5,7},{7,5},{8,10},{10,8},{9,1... | collective-permute-start | bytes 786440 | tf_op jit(solution)/shard_map/ppermute | solution.py:22
  17.5 1.3 %collective-permute-start.1 = (f32[64,128]{1,0:T(8,128)S(1)}, f32[64,128]{1,0:T(8,128)S(1)}, u32[]{:S(2)}, u32[]{:S(2)}) collective-permute-start(f32[64,128]{1,0:T(8,128)S(1)} %get-tuple-element.28), channel_id=1, source_target_pairs={{0,1},{1,0},{2,3},{3,2},{4,5},{5,4},{6,7},{7,6},{8,9},{9,8},{10,11... | collective-permute-start | bytes 98312 | tf_op jit(solution)/shard_map/ppermute | solution.py:22
  18.7 3.9 %collective-permute-start.2 = (f32[64,128]{1,0:T(8,128)S(1)}, f32[64,128]{1,0:T(8,128)S(1)}, u32[]{:S(2)}, u32[]{:S(2)}) collective-permute-start(f32[64,128]{1,0:T(8,128)S(1)} %add.6), channel_id=1, source_target_pairs={{0,4},{4,0},{8,12},{12,8},{1,5},{5,1},{9,13},{13,9},{2,6},{6,2},{1... | collective-permute-start | bytes 98312 | tf_op jit(solution)/shard_map/ppermute | solution.py:22
  22.7 4.8 %collective-permute-start.3 = (f32[64,128]{1,0:T(8,128)S(1)}, f32[64,128]{1,0:T(8,128)S(1)}, u32[]{:S(2)}, u32[]{:S(2)}) collective-permute-start(f32[64,128]{1,0:T(8,128)S(1)} %add.7.factor_a_ref), channel_id=1, source_target_pairs={{0,8},{4,12},{8,0},{12,4},{1,9},{5,13},{9,1},{13,5},{2,10},{6,14},... | collective-permute-start | bytes 98312 | tf_op jit(solution)/shard_map/ppermute | solution.py:22
  25.2 5.2 %collective-permute-start.10 = (bf16[4,64,128]{2,1,0:T(8,128)(2,1)S(1)}, bf16[4,64,128]{2,1,0:T(8,128)(2,1)S(1)}, u32[]{:S(2)}, u32[]{:S(2)}) collective-permute-start(bf16[4,64,128]{2,1,0:T(8,128)(2,1)S(1)} %features.1.refs_7_), channel_id=1, source_target_pairs={{0,8},{4,12},{8,0},{12,4},{1,9},{5,13},{9,1},{13,5},{2,10},{6,14},... | collective-permute-start | bytes 196616 | tf_op jit(solution)/shard_map/ppermute | solution.py:22
  25.6 4.8 %collective-permute-start.5 = (bf16[1024,128]{1,0:T(8,128)(2,1)S(1)}, bf16[1024,128]{1,0:T(8,128)(2,1)S(1)}, u32[]{:S(2)}, u32[]{:S(2)}) collective-permute-start(bf16[1024,128]{1,0:T(8,128)(2,1)S(1)} %get-tuple-element.36.refs_0_), channel_id=1, source_target_pairs={{0,1},{1,0},{2,3},{3,2},{4,5},{5,4},{6,7},{7,6},{8,9},{9,8},{10,11... | collective-permute-start | bytes 786440 | tf_op jit(solution)/shard_map/ppermute | solution.py:22
  25.6 4.8 %collective-permute-start.6 = (bf16[1024,128]{1,0:T(8,128)(2,1)S(1)}, bf16[1024,128]{1,0:T(8,128)(2,1)S(1)}, u32[]{:S(2)}, u32[]{:S(2)}) collective-permute-start(bf16[1024,128]{1,0:T(8,128)(2,1)S(1)} %collective-permute-done.4.refs_1_), channel_id=1, source_target_pairs={{0,1},{1,0},{2,3},{3,2},{4,5},{5,4},{6,7},{7,6},{8,9},{9,8},{10,11... | collective-permute-start | bytes 786440 | tf_op jit(solution)/shard_map/ppermute | solution.py:22
  27.5 2.9 %collective-permute-start.9 = (bf16[2048,128]{1,0:T(8,128)(2,1)S(1)}, bf16[2048,128]{1,0:T(8,128)(2,1)S(1)}, u32[]{:S(2)}, u32[]{:S(2)}) collective-permute-start(bf16[2048,128]{1,0:T(8,128)(2,1)S(1)} %pad_maximum_fusion), channel_id=1, source_target_pairs={{0,1},{1,0},{2,3},{3,2},{4,5},{5,4},{6,7},{7,6},{8,9},{9,8},{10,11... | collective-permute-start | bytes 1572872 | tf_op jit(solution)/shard_map/ppermute | solution.py:22
  31.6 4.6 %collective-permute-start.11 = (f32[2,8,128]{2,1,0:T(8,128)S(1)}, f32[2,8,128]{2,1,0:T(8,128)S(1)}, u32[]{:S(2)}, u32[]{:S(2)}) collective-permute-start(f32[2,8,128]{2,1,0:T(8,128)S(1)} %get-tuple-element.44), channel_id=1, source_target_pairs={{0,8},{4,12},{8,0},{12,4},{1,9},{5,13},{9,1},{13,5},{2,10},{6,14},... | collective-permute-start | bytes 24584 | tf_op jit(solution)/shard_map/ppermute | solution.py:22

commit v14 on v13

--- a/solution.py
+++ b/solution.py
@@ -195,26 +195,25 @@
         for j in range(0, run, 2):
             a, b, c = entry[j][j], entry[j][j + 1], entry[j + 1][j + 1]
             scale = 1.0 / (a * c - b * b)
-            ia, ib, ic = c * scale, -(b * scale), a * scale
             at_first, at_second = column == first + j, column == first + j + 1
-            low = jnp.where(at_first, ia, jnp.where(at_second, ib, ia * rows[j] + ib * rows[j + 1]))
-            high = jnp.where(at_first, ib, jnp.where(at_second, ic, ib * rows[j] + ic * rows[j + 1]))
+            low = jnp.where(at_first, c, jnp.where(at_second, -b, c * rows[j] - b * rows[j + 1]))
+            high = jnp.where(at_first, -b, jnp.where(at_second, a, a * rows[j + 1] - b * rows[j]))
             later = range(j + 2, run)
-            low_entry = {k: ia * entry[j][k] + ib * entry[j + 1][k] for k in later}
-            high_entry = {k: ib * entry[j][k] + ic * entry[j + 1][k] for k in later}
+            low_entry = {k: c * entry[j][k] - b * entry[j + 1][k] for k in later}
+            high_entry = {k: a * entry[j + 1][k] - b * entry[j][k] for k in later}
             for i in range(run):
                 if i in (j, j + 1):
                     continue
                 from_low, from_high = entry[i][j], entry[i][j + 1]
-                rows[i] = jnp.where(at_first | at_second, 0.0, rows[i]) - (from_low * low + from_high * high)
+                rows[i] = jnp.where(at_first | at_second, 0.0, rows[i]) - scale * (from_low * low + from_high * high)
                 for k in later:
                     if j + 1 < i and k < i:
                         entry[i][k] = entry[k][i]
                     else:
-                        entry[i][k] = entry[i][k] - (from_low * low_entry[k] + from_high * high_entry[k])
-            rows[j], rows[j + 1] = low, high
+                        entry[i][k] = entry[i][k] - scale * (from_low * low_entry[k] + from_high * high_entry[k])
+            rows[j], rows[j + 1] = scale * low, scale * high
             for k in later:
-                entry[j][k], entry[j + 1][k] = low_entry[k], high_entry[k]
+                entry[j][k], entry[j + 1][k] = scale * low_entry[k], scale * high_entry[k]
         pivots = (column >= first) & (column < first + run)
         for r in range(len(blocks)):
             if r != p:

time: 37 us -> 37 us (level)
  waiting for transfers between devices: 9.84 us -> 10.5 us
    ppermute x12, waiting for transfers between devices: 9.84 us -> 10.5 us  [xor_permute(): return lax.ppermute(values, axis, [(i, i ^ mask) for i in range(size)])]
  transfers between devices with their start and end apart: 12 -> 12, of which waited for: 5 -> 6; matrix products, arithmetic and copies ran while one was open for 1% -> 1% of each run, Pallas kernels for 27% -> 26%
where the time goes in v14:
time: 37 us; the launch traced here: 36.8 us
  starting transfers between devices  14.5 us (39%)
  Pallas kernels  11.5 us (31%)
  waiting for transfers between devices  10.5 us (28%)
    ppermute x12, starting transfers between devices, xor_permute(): return lax.ppermute(values, axis, [(i, i ^ mask) for i in range(size)])  14.5 us
    ppermute x12, waiting for transfers between devices, xor_permute(): return lax.ppermute(values, axis, [(i, i ^ mask) for i in range(size)])  10.5 us
    pallas_call x1, Pallas kernels, project(): pl.pallas_call(functools.partial(project_body, rows), out_shape=(jax.Shap...  5.62 us
    pallas_call x1, Pallas kernels, inverses(): pl.pallas_call(functools.partial(inverses_body, total_tokens), out_shape=...  2.46 us
    pallas_call x1, Pallas kernels, scores_of(): pl.pallas_call(functools.partial(scores_body, len(feats), piece_counts),...  1.15 us
    pallas_call x1, Pallas kernels, features_of(): pl.pallas_call(features_body, out_shape=jax.ShapeDtypeStruct((examples //...  0.87 us
  transfers between devices with their start and end apart: 12, of which 6 were waited for; matrix products, arithmetic and copies ran while one was open for 1% of the time, Pallas kernels for 26%

profile of v14, /device:TPU:0, one launch (start us, length us, event | category | flops | bytes accessed | tf_op | source)
XLA Modules:
  0.0 36.8 jit_solution(18094698687444576364)
XLA Ops:
  0.0 3.1 %collective-permute-start.7 = (bf16[2048,128]{1,0:T(8,128)(2,1)}, bf16[2048,128]{1,0:T(8,128)(2,1)S(1)}, u32[]{:S(2)}, u32[]{:S(2)}) collective-permute-start(bf16[2048,128]{1,0:T(8,128)(2,1)} %bitcast.10), channel_id=1, source_target_pairs={{0,4},{4,0},{8,12},{12,8},{1,5},{5,1},{9,13},{13,9},{2,6},{6,2},{1... | collective-permute-start | bytes 1572872 | tf_op jit(solution)/shard_map/ppermute | solution.py:22
  3.1 5.6 %project.1 = (f32[768,128]{1,0:T(8,128)S(1)}, bf16[768,128]{1,0:T(8,128)(2,1)S(1)}) custom-call(bf16[768,2048]{1,0:T(8,128)(2,1)S(1)} %bitcast.8, bf16[768,7168]{1,0:T(8,128)(2,1)} %bitcast.13, bf16[64,2048]{1,0:T(8,128)(2,1)S(1)} %bitcast.12, bf16[64,7168]{1,0:T(8,128)(2,1)S(1)} %bitcast.9), custom_call_target="tpu_custom_call" | custom-call | flops 905969664 | bytes 15335424 | tf_op jit(solution)/shard_map/project/pallas_call | solution.py:60
  8.8 2.0 %collective-permute-start = (bf16[768,128]{1,0:T(8,128)(2,1)S(1)}, bf16[768,128]{1,0:T(8,128)(2,1)S(1)}, u32[]{:S(2)}, u32[]{:S(2)}) collective-permute-start(bf16[768,128]{1,0:T(8,128)(2,1)S(1)} %get-tuple-element.27), channel_id=1, source_target_pairs={{0,2},{2,0},{1,3},{3,1},{4,6},{6,4},{5,7},{7,5},{8,10},{10,8},{9,1... | collective-permute-start | bytes 589832 | tf_op jit(solution)/shard_map/ppermute | solution.py:22
  10.7 0.2 pack.2
  11.0 0.2 collective-permute-start.4
  11.2 0.1 reshape.25.live_ref
  11.3 3.9 %collective-permute-done.7.tests_ref = bf16[2048,128]{1,0:T(8,128)(2,1)S(1)} collective-permute-done((bf16[2048,128]{1,0:T(8,128)(2,1)}, bf16[2048,128]{1,0:T(8,128)(2,1)S(1)}, u32[]{:S(2)}, u32[]{:S(2)}) %collective-permute-start.7) | collective-permute-done | bytes 524320 | tf_op jit(solution)/shard_map/ppermute | solution.py:22
  15.2 0.2 pack.3
  15.5 1.7 %collective-permute-start.8 = (bf16[1024,128]{1,0:T(8,128)(2,1)S(1)}, bf16[1024,128]{1,0:T(8,128)(2,1)S(1)}, u32[]{:S(2)}, u32[]{:S(2)}) collective-permute-start(bf16[1024,128]{1,0:T(8,128)(2,1)S(1)} %get-tuple-element.40), channel_id=1, source_target_pairs={{0,2},{2,0},{1,3},{3,1},{4,6},{6,4},{5,7},{7,5},{8,10},{10,8},{9,1... | collective-permute-start | bytes 786440 | tf_op jit(solution)/shard_map/ppermute | solution.py:22
  17.2 0.3 factors.1
  17.5 1.2 %collective-permute-done.1 = f32[64,128]{1,0:T(8,128)S(1)} collective-permute-done((f32[64,128]{1,0:T(8,128)S(1)}, f32[64,128]{1,0:T(8,128)S(1)}, u32[]{:S(2)}, u32[]{:S(2)}) %collective-permute-start.1) | collective-permute-done | bytes 32800 | tf_op jit(solution)/shard_map/ppermute | solution.py:22
  18.7 1.6 %collective-permute-start.2 = (f32[64,128]{1,0:T(8,128)S(1)}, f32[64,128]{1,0:T(8,128)S(1)}, u32[]{:S(2)}, u32[]{:S(2)}) collective-permute-start(f32[64,128]{1,0:T(8,128)S(1)} %add.6), channel_id=1, source_target_pairs={{0,4},{4,0},{8,12},{12,8},{1,5},{5,1},{9,13},{13,9},{2,6},{6,2},{1... | collective-permute-start | bytes 98312 | tf_op jit(solution)/shard_map/ppermute | solution.py:22
  20.3 0.9 %features.1.refs_7_ = bf16[4,64,128]{2,1,0:T(8,128)(2,1)S(1)} custom-call(s32[8]{0:T(128)S(1)} %copy-done.5, s32[1,96]{1,0:T(1,128)S(1)} %slots.1.positions_ref, s32[8,96]{1,0:T(8,128)S(1)} %copy-done.4, bf16[768,128]{1,0:T(8,128)(2,1)S(1)} %get-tuple-element.29.rounded_ref), custom_call_target="tpu_custom_call" | custom-call | flops 25165824 | bytes 8388608 | tf_op jit(solution)/shard_map/features/pallas_call | solution.py:159
  21.2 1.5 %collective-permute-done.2 = f32[64,128]{1,0:T(8,128)S(1)} collective-permute-done((f32[64,128]{1,0:T(8,128)S(1)}, f32[64,128]{1,0:T(8,128)S(1)}, u32[]{:S(2)}, u32[]{:S(2)}) %collective-permute-start.2) | collective-permute-done | bytes 32800 | tf_op jit(solution)/shard_map/ppermute | solution.py:22
  22.7 2.6 %collective-permute-start.3 = (f32[64,128]{1,0:T(8,128)S(1)}, f32[64,128]{1,0:T(8,128)S(1)}, u32[]{:S(2)}, u32[]{:S(2)}) collective-permute-start(f32[64,128]{1,0:T(8,128)S(1)} %add.7.factor_a_ref), channel_id=1, source_target_pairs={{0,8},{4,12},{8,0},{12,4},{1,9},{5,13},{9,1},{13,5},{2,10},{6,14},... | collective-permute-start | bytes 98312 | tf_op jit(solution)/shard_map/ppermute | solution.py:22
  25.2 0.3 collective-permute-start.10
  25.6 0.5 %collective-permute-start.6 = (bf16[1024,128]{1,0:T(8,128)(2,1)S(1)}, bf16[1024,128]{1,0:T(8,128)(2,1)S(1)}, u32[]{:S(2)}, u32[]{:S(2)}) collective-permute-start(bf16[1024,128]{1,0:T(8,128)(2,1)S(1)} %collective-permute-done.4.refs_1_), channel_id=1, source_target_pairs={{0,1},{1,0},{2,3},{3,2},{4,5},{5,4},{6,7},{7,6},{8,9},{9,8},{10,11... | collective-permute-start | bytes 786440 | tf_op jit(solution)/shard_map/ppermute | solution.py:22
  26.1 1.4 %collective-permute-done.3.factor_b_ref = f32[64,128]{1,0:T(8,128)S(1)} collective-permute-done((f32[64,128]{1,0:T(8,128)S(1)}, f32[64,128]{1,0:T(8,128)S(1)}, u32[]{:S(2)}, u32[]{:S(2)}) %collective-permute-start.3) | collective-permute-done | bytes 32800 | tf_op jit(solution)/shard_map/ppermute | solution.py:22
  27.6 2.5 %inverses.1 = (bf16[2,64,64]{2,1,0:T(8,128)(2,1)S(1)}, bf16[2,128,128]{2,1,0:T(8,128)(2,1)S(1)}) custom-call(f32[64,128]{1,0:T(8,128)S(1)} %add.7.factor_a_ref, f32[64,128]{1,0:T(8,128)S(1)} %collective-permute-done.3.factor_b_ref), custom_call_target="tpu_custom_call" | custom-call | flops 17179869184 | tf_op jit(solution)/shard_map/inverses/pallas_call | solution.py:253
  30.0 0.4 collective-permute-done.10.refs_8_
  30.4 1.1 %scores.1 = (f32[2,8,128]{2,1,0:T(8,128)S(1)}, f32[2,8,128]{2,1,0:T(8,128)S(1)}) custom-call(bf16[2,64,64]{2,1,0:T(8,128)(2,1)S(1)} %get-tuple-element.31.grad_ref, bf16[2,128,128]{2,1,0:T(8,128)(2,1)S(1)} %get-tuple-element.32.in_ref, bf16[1024,128]{1,0:T(8,128)(2,1)S(1)} %get-tuple-element.36.refs_0_, ...), custom_call_target="tpu_custom_call" | custom-call | tf_op jit(solution)/shard_map/scores/pallas_call | solution.py:363
  31.6 2.4 %collective-permute-start.11 = (f32[2,8,128]{2,1,0:T(8,128)S(1)}, f32[2,8,128]{2,1,0:T(8,128)S(1)}, u32[]{:S(2)}, u32[]{:S(2)}) collective-permute-start(f32[2,8,128]{2,1,0:T(8,128)S(1)} %get-tuple-element.44), channel_id=1, source_target_pairs={{0,8},{4,12},{8,0},{12,4},{1,9},{5,13},{9,1},{13,5},{2,10},{6,14},... | collective-permute-start | bytes 24584 | tf_op jit(solution)/shard_map/ppermute | solution.py:22
  33.9 2.2 %collective-permute-done.11.refs_1_ = f32[2,8,128]{2,1,0:T(8,128)S(1)} collective-permute-done((f32[2,8,128]{2,1,0:T(8,128)S(1)}, f32[2,8,128]{2,1,0:T(8,128)S(1)}, u32[]{:S(2)}, u32[]{:S(2)}) %collective-permute-start.11) | collective-permute-done | bytes 8224 | tf_op jit(solution)/shard_map/ppermute | solution.py:22
  36.1 0.7 %finish.1 = f32[64,64]{1,0:T(8,128)} custom-call(f32[2,8,128]{2,1,0:T(8,128)S(1)} %get-tuple-element.43.refs_0_, f32[2,8,128]{2,1,0:T(8,128)S(1)} %collective-permute-done.11.refs_1_), custom_call_target="tpu_custom_call" | custom-call | tf_op jit(solution)/shard_map/finish/pallas_call | solution.py:396
  (26 shorter events, 0.3 us)
Async XLA Ops:
  0.0 3.1 %copy-start = (bf16[8,96,2048]{2,1,0:T(8,128)(2,1)S(1)}, bf16[8,96,2048]{2,1,0:T(8,128)(2,1)}, u32[]{:S(2)}) copy-start(bf16[8,96,2048]{2,1,0:T(8,128)(2,1)} %param.7) | copy-start | bytes 9437188
  0.0 3.1 %copy-start.1 = (bf16[7168,64]{0,1:T(8,128)(2,1)S(1)}, bf16[7168,64]{0,1:T(8,128)(2,1)}, u32[]{:S(2)}) copy-start(bf16[7168,64]{0,1:T(8,128)(2,1)} %param.10) | copy-start | bytes 2752516
  0.0 3.1 %copy-start.3 = (bf16[2048,64]{0,1:T(8,128)(2,1)S(1)}, bf16[2048,64]{0,1:T(8,128)(2,1)}, u32[]{:S(2)}) copy-start(bf16[2048,64]{0,1:T(8,128)(2,1)} %param.9) | copy-start | bytes 786436
  0.0 15.2 %collective-permute-start.7 = (bf16[2048,128]{1,0:T(8,128)(2,1)}, bf16[2048,128]{1,0:T(8,128)(2,1)S(1)}, u32[]{:S(2)}, u32[]{:S(2)}) collective-permute-start(bf16[2048,128]{1,0:T(8,128)(2,1)} %bitcast.10), channel_id=1, source_target_pairs={{0,4},{4,0},{8,12},{12,8},{1,5},{5,1},{9,13},{13,9},{2,6},{6,2},{1... | collective-permute-start | bytes 1572872 | tf_op jit(solution)/shard_map/ppermute | solution.py:22
  3.1 7.6 %copy-start.2 = (bf16[128,32,64]{0,2,1:T(8,128)(2,1)S(1)}, bf16[128,32,64]{0,2,1:T(8,128)(2,1)}, u32[]{:S(2)}) copy-start(bf16[128,32,64]{0,2,1:T(8,128)(2,1)} %param.13) | copy-start | bytes 1572868
  3.1 8.0 %copy-start.4 = (s32[8,96]{1,0:T(8,128)S(1)}, s32[8,96]{1,0:T(8,128)}, u32[]{:S(2)}) copy-start(s32[8,96]{1,0:T(8,128)} %mask_ref.1) | copy-start | bytes 9220
  3.1 8.0 %copy-start.5 = (s32[8]{0:T(128)S(1)}, s32[8]{0:T(128)}, u32[]{:S(2)}) copy-start(s32[8]{0:T(128)} %lengths_ref.1) | copy-start | bytes 100
  8.8 8.4 %collective-permute-start = (bf16[768,128]{1,0:T(8,128)(2,1)S(1)}, bf16[768,128]{1,0:T(8,128)(2,1)S(1)}, u32[]{:S(2)}, u32[]{:S(2)}) collective-permute-start(bf16[768,128]{1,0:T(8,128)(2,1)S(1)} %get-tuple-element.27), channel_id=1, source_target_pairs={{0,2},{2,0},{1,3},{3,1},{4,6},{6,4},{5,7},{7,5},{8,10},{10,8},{9,1... | collective-permute-start | bytes 589832 | tf_op jit(solution)/shard_map/ppermute | solution.py:22
  11.0 14.6 %collective-permute-start.4 = (bf16[1024,128]{1,0:T(8,128)(2,1)S(1)}, bf16[1024,128]{1,0:T(8,128)(2,1)S(1)}, u32[]{:S(2)}, u32[]{:S(2)}) collective-permute-start(bf16[1024,128]{1,0:T(8,128)(2,1)S(1)} %get-tuple-element.35), channel_id=1, source_target_pairs={{0,2},{2,0},{1,3},{3,1},{4,6},{6,4},{5,7},{7,5},{8,10},{10,8},{9,1... | collective-permute-start | bytes 786440 | tf_op jit(solution)/shard_map/ppermute | solution.py:22
  15.5 12.0 %collective-permute-start.8 = (bf16[1024,128]{1,0:T(8,128)(2,1)S(1)}, bf16[1024,128]{1,0:T(8,128)(2,1)S(1)}, u32[]{:S(2)}, u32[]{:S(2)}) collective-permute-start(bf16[1024,128]{1,0:T(8,128)(2,1)S(1)} %get-tuple-element.40), channel_id=1, source_target_pairs={{0,2},{2,0},{1,3},{3,1},{4,6},{6,4},{5,7},{7,5},{8,10},{10,8},{9,1... | collective-permute-start | bytes 786440 | tf_op jit(solution)/shard_map/ppermute | solution.py:22
  17.5 1.3 %collective-permute-start.1 = (f32[64,128]{1,0:T(8,128)S(1)}, f32[64,128]{1,0:T(8,128)S(1)}, u32[]{:S(2)}, u32[]{:S(2)}) collective-permute-start(f32[64,128]{1,0:T(8,128)S(1)} %get-tuple-element.28), channel_id=1, source_target_pairs={{0,1},{1,0},{2,3},{3,2},{4,5},{5,4},{6,7},{7,6},{8,9},{9,8},{10,11... | collective-permute-start | bytes 98312 | tf_op jit(solution)/shard_map/ppermute | solution.py:22
  18.7 3.9 %collective-permute-start.2 = (f32[64,128]{1,0:T(8,128)S(1)}, f32[64,128]{1,0:T(8,128)S(1)}, u32[]{:S(2)}, u32[]{:S(2)}) collective-permute-start(f32[64,128]{1,0:T(8,128)S(1)} %add.6), channel_id=1, source_target_pairs={{0,4},{4,0},{8,12},{12,8},{1,5},{5,1},{9,13},{13,9},{2,6},{6,2},{1... | collective-permute-start | bytes 98312 | tf_op jit(solution)/shard_map/ppermute | solution.py:22
  22.7 4.8 %collective-permute-start.3 = (f32[64,128]{1,0:T(8,128)S(1)}, f32[64,128]{1,0:T(8,128)S(1)}, u32[]{:S(2)}, u32[]{:S(2)}) collective-permute-start(f32[64,128]{1,0:T(8,128)S(1)} %add.7.factor_a_ref), channel_id=1, source_target_pairs={{0,8},{4,12},{8,0},{12,4},{1,9},{5,13},{9,1},{13,5},{2,10},{6,14},... | collective-permute-start | bytes 98312 | tf_op jit(solution)/shard_map/ppermute | solution.py:22
  25.2 5.2 %collective-permute-start.10 = (bf16[4,64,128]{2,1,0:T(8,128)(2,1)S(1)}, bf16[4,64,128]{2,1,0:T(8,128)(2,1)S(1)}, u32[]{:S(2)}, u32[]{:S(2)}) collective-permute-start(bf16[4,64,128]{2,1,0:T(8,128)(2,1)S(1)} %features.1.refs_7_), channel_id=1, source_target_pairs={{0,8},{4,12},{8,0},{12,4},{1,9},{5,13},{9,1},{13,5},{2,10},{6,14},... | collective-permute-start | bytes 196616 | tf_op jit(solution)/shard_map/ppermute | solution.py:22
  25.6 4.8 %collective-permute-start.5 = (bf16[1024,128]{1,0:T(8,128)(2,1)S(1)}, bf16[1024,128]{1,0:T(8,128)(2,1)S(1)}, u32[]{:S(2)}, u32[]{:S(2)}) collective-permute-start(bf16[1024,128]{1,0:T(8,128)(2,1)S(1)} %get-tuple-element.36.refs_0_), channel_id=1, source_target_pairs={{0,1},{1,0},{2,3},{3,2},{4,5},{5,4},{6,7},{7,6},{8,9},{9,8},{10,11... | collective-permute-start | bytes 786440 | tf_op jit(solution)/shard_map/ppermute | solution.py:22
  25.6 4.8 %collective-permute-start.6 = (bf16[1024,128]{1,0:T(8,128)(2,1)S(1)}, bf16[1024,128]{1,0:T(8,128)(2,1)S(1)}, u32[]{:S(2)}, u32[]{:S(2)}) collective-permute-start(bf16[1024,128]{1,0:T(8,128)(2,1)S(1)} %collective-permute-done.4.refs_1_), channel_id=1, source_target_pairs={{0,1},{1,0},{2,3},{3,2},{4,5},{5,4},{6,7},{7,6},{8,9},{9,8},{10,11... | collective-permute-start | bytes 786440 | tf_op jit(solution)/shard_map/ppermute | solution.py:22
  27.5 2.9 %collective-permute-start.9 = (bf16[2048,128]{1,0:T(8,128)(2,1)S(1)}, bf16[2048,128]{1,0:T(8,128)(2,1)S(1)}, u32[]{:S(2)}, u32[]{:S(2)}) collective-permute-start(bf16[2048,128]{1,0:T(8,128)(2,1)S(1)} %pad_maximum_fusion), channel_id=1, source_target_pairs={{0,1},{1,0},{2,3},{3,2},{4,5},{5,4},{6,7},{7,6},{8,9},{9,8},{10,11... | collective-permute-start | bytes 1572872 | tf_op jit(solution)/shard_map/ppermute | solution.py:22
  31.6 4.6 %collective-permute-start.11 = (f32[2,8,128]{2,1,0:T(8,128)S(1)}, f32[2,8,128]{2,1,0:T(8,128)S(1)}, u32[]{:S(2)}, u32[]{:S(2)}) collective-permute-start(f32[2,8,128]{2,1,0:T(8,128)S(1)} %get-tuple-element.44), channel_id=1, source_target_pairs={{0,8},{4,12},{8,0},{12,4},{1,9},{5,13},{9,1},{13,5},{2,10},{6,14},... | collective-permute-start | bytes 24584 | tf_op jit(solution)/shard_map/ppermute | solution.py:22

commit v15 on v14

--- a/solution.py
+++ b/solution.py
@@ -432,17 +432,17 @@
     factor, rounded = factors(live, own, received)
     feats = [features_of(lengths, positions, loss_mask, rounded)]
     even_masks = range(2, dp_count, 2)
-    steps = [("test", 1)] + [("dp", m) for m in masks_of(dp_count)]
+    steps = [("dp", m) for m in masks_of(dp_count)] + [("test", 1)]
     sums = [factor]
     for axis, mask in steps:
-        if len(sums) == len(steps):
+        if len(sums) == 3:
             sums[-1] = after(sums[-1], feats[0])
         other = xor_permute(sums[-1], axis, mask)
         sums.append(sums[-1] + other)
     pieces, piece_counts = [], []
     pieces += near + [xor_permute(piece, "test", 1) for piece in after(tuple(near), *(sums[2],))]
     piece_counts += [1] * (2 * feat_count)
-    pieces += far + [xor_permute(jnp.concatenate(after(tuple(far), *(other,)), axis=0), "test", 1)]
+    pieces += far + [xor_permute(jnp.concatenate(after(tuple(far), *(sums[2],)), axis=0), "test", 1)]
     piece_counts += [1] * feat_count + [feat_count]
     feats += [xor_permute(feats[0], "dp", mask) for mask in even_masks]
     total_tokens = float(tokens * dp_count * test_count)

time: 37 us -> 36.7 us (level)
  waiting for transfers between devices: 10.5 us -> 9.73 us
  starting transfers between devices: 14.5 us -> 15.1 us
    ppermute x12, waiting for transfers between devices: 10.5 us -> 9.73 us  [xor_permute(): return lax.ppermute(values, axis, [(i, i ^ mask) for i in range(size)])]
    ppermute x12, starting transfers between devices: 14.5 us -> 15.1 us  [xor_permute(): return lax.ppermute(values, axis, [(i, i ^ mask) for i in range(size)])]
  transfers between devices with their start and end apart: 12 -> 12, of which waited for: 6 -> 5; matrix products, arithmetic and copies ran while one was open for 1% -> 1% of each run, Pallas kernels for 26% -> 26%
where the time goes in v15:
time: 36.7 us; the launch traced here: 36.6 us
  starting transfers between devices  15.1 us (41%)
  Pallas kernels  11.5 us (31%)
  waiting for transfers between devices  9.73 us (27%)
    ppermute x12, starting transfers between devices, xor_permute(): return lax.ppermute(values, axis, [(i, i ^ mask) for i in range(size)])  15.1 us
    ppermute x12, waiting for transfers between devices, xor_permute(): return lax.ppermute(values, axis, [(i, i ^ mask) for i in range(size)])  9.73 us
    pallas_call x1, Pallas kernels, project(): pl.pallas_call(functools.partial(project_body, rows), out_shape=(jax.Shap...  5.62 us
    pallas_call x1, Pallas kernels, inverses(): pl.pallas_call(functools.partial(inverses_body, total_tokens), out_shape=...  2.46 us
    pallas_call x1, Pallas kernels, scores_of(): pl.pallas_call(functools.partial(scores_body, len(feats), piece_counts),...  1.15 us
    pallas_call x1, Pallas kernels, features_of(): pl.pallas_call(features_body, out_shape=jax.ShapeDtypeStruct((examples //...  0.87 us
  transfers between devices with their start and end apart: 12, of which 5 were waited for; matrix products, arithmetic and copies ran while one was open for 1% of the time, Pallas kernels for 26%

profile of v15, /device:TPU:0, one launch (start us, length us, event | category | flops | bytes accessed | tf_op | source)
XLA Modules:
  0.0 36.6 jit_solution(6549100364105432081)
XLA Ops:
  0.0 3.1 %collective-permute-start.7 = (bf16[2048,128]{1,0:T(8,128)(2,1)}, bf16[2048,128]{1,0:T(8,128)(2,1)S(1)}, u32[]{:S(2)}, u32[]{:S(2)}) collective-permute-start(bf16[2048,128]{1,0:T(8,128)(2,1)} %bitcast.10), channel_id=1, source_target_pairs={{0,4},{4,0},{8,12},{12,8},{1,5},{5,1},{9,13},{13,9},{2,6},{6,2},{1... | collective-permute-start | bytes 1572872 | tf_op jit(solution)/shard_map/ppermute | solution.py:22
  3.1 5.6 %project.1 = (f32[768,128]{1,0:T(8,128)S(1)}, bf16[768,128]{1,0:T(8,128)(2,1)S(1)}) custom-call(bf16[768,2048]{1,0:T(8,128)(2,1)S(1)} %bitcast.8, bf16[768,7168]{1,0:T(8,128)(2,1)} %bitcast.13, bf16[64,2048]{1,0:T(8,128)(2,1)S(1)} %bitcast.12, bf16[64,7168]{1,0:T(8,128)(2,1)S(1)} %bitcast.9), custom_call_target="tpu_custom_call" | custom-call | flops 905969664 | bytes 15335424 | tf_op jit(solution)/shard_map/project/pallas_call | solution.py:60
  8.8 2.0 %collective-permute-start = (bf16[768,128]{1,0:T(8,128)(2,1)S(1)}, bf16[768,128]{1,0:T(8,128)(2,1)S(1)}, u32[]{:S(2)}, u32[]{:S(2)}) collective-permute-start(bf16[768,128]{1,0:T(8,128)(2,1)S(1)} %get-tuple-element.27), channel_id=1, source_target_pairs={{0,2},{2,0},{1,3},{3,1},{4,6},{6,4},{5,7},{7,5},{8,10},{10,8},{9,1... | collective-permute-start | bytes 589832 | tf_op jit(solution)/shard_map/ppermute | solution.py:22
  10.7 0.2 pack.2
  11.0 0.2 collective-permute-start.4
  11.2 0.1 reshape.25.live_ref
  11.3 3.9 %collective-permute-done.7.tests_ref = bf16[2048,128]{1,0:T(8,128)(2,1)S(1)} collective-permute-done((bf16[2048,128]{1,0:T(8,128)(2,1)}, bf16[2048,128]{1,0:T(8,128)(2,1)S(1)}, u32[]{:S(2)}, u32[]{:S(2)}) %collective-permute-start.7) | collective-permute-done | bytes 524320 | tf_op jit(solution)/shard_map/ppermute | solution.py:22
  15.2 0.2 pack.3
  15.5 1.7 %collective-permute-start.8 = (bf16[1024,128]{1,0:T(8,128)(2,1)S(1)}, bf16[1024,128]{1,0:T(8,128)(2,1)S(1)}, u32[]{:S(2)}, u32[]{:S(2)}) collective-permute-start(bf16[1024,128]{1,0:T(8,128)(2,1)S(1)} %get-tuple-element.40), channel_id=1, source_target_pairs={{0,2},{2,0},{1,3},{3,1},{4,6},{6,4},{5,7},{7,5},{8,10},{10,8},{9,1... | collective-permute-start | bytes 786440 | tf_op jit(solution)/shard_map/ppermute | solution.py:22
  17.2 0.3 factors.1
  17.5 1.6 %collective-permute-start.1 = (f32[64,128]{1,0:T(8,128)S(1)}, f32[64,128]{1,0:T(8,128)S(1)}, u32[]{:S(2)}, u32[]{:S(2)}) collective-permute-start(f32[64,128]{1,0:T(8,128)S(1)} %get-tuple-element.28), channel_id=1, source_target_pairs={{0,4},{4,0},{8,12},{12,8},{1,5},{5,1},{9,13},{13,9},{2,6},{6,2},{1... | collective-permute-start | bytes 98312 | tf_op jit(solution)/shard_map/ppermute | solution.py:22
  19.1 2.3 %collective-permute-done.1 = f32[64,128]{1,0:T(8,128)S(1)} collective-permute-done((f32[64,128]{1,0:T(8,128)S(1)}, f32[64,128]{1,0:T(8,128)S(1)}, u32[]{:S(2)}, u32[]{:S(2)}) %collective-permute-start.1) | collective-permute-done | bytes 32800 | tf_op jit(solution)/shard_map/ppermute | solution.py:22
  21.4 2.6 %collective-permute-start.2 = (f32[64,128]{1,0:T(8,128)S(1)}, f32[64,128]{1,0:T(8,128)S(1)}, u32[]{:S(2)}, u32[]{:S(2)}) collective-permute-start(f32[64,128]{1,0:T(8,128)S(1)} %add.6), channel_id=1, source_target_pairs={{0,8},{4,12},{8,0},{12,4},{1,9},{5,13},{9,1},{13,5},{2,10},{6,14},... | collective-permute-start | bytes 98312 | tf_op jit(solution)/shard_map/ppermute | solution.py:22
  24.0 0.9 %features.1.refs_7_ = bf16[4,64,128]{2,1,0:T(8,128)(2,1)S(1)} custom-call(s32[8]{0:T(128)S(1)} %copy-done.5, s32[1,96]{1,0:T(1,128)S(1)} %slots.1.positions_ref, s32[8,96]{1,0:T(8,128)S(1)} %copy-done.4, bf16[768,128]{1,0:T(8,128)(2,1)S(1)} %get-tuple-element.29.rounded_ref), custom_call_target="tpu_custom_call" | custom-call | flops 25165824 | bytes 8388608 | tf_op jit(solution)/shard_map/features/pallas_call | solution.py:159
  24.9 0.4 %collective-permute-start.10 = (bf16[4,64,128]{2,1,0:T(8,128)(2,1)S(1)}, bf16[4,64,128]{2,1,0:T(8,128)(2,1)S(1)}, u32[]{:S(2)}, u32[]{:S(2)}) collective-permute-start(bf16[4,64,128]{2,1,0:T(8,128)(2,1)S(1)} %features.1.refs_7_), channel_id=1, source_target_pairs={{0,8},{4,12},{8,0},{12,4},{1,9},{5,13},{9,1},{13,5},{2,10},{6,14},... | collective-permute-start | bytes 196616 | tf_op jit(solution)/shard_map/ppermute | solution.py:22
  25.3 1.2 %collective-permute-done.2 = f32[64,128]{1,0:T(8,128)S(1)} collective-permute-done((f32[64,128]{1,0:T(8,128)S(1)}, f32[64,128]{1,0:T(8,128)S(1)}, u32[]{:S(2)}, u32[]{:S(2)}) %collective-permute-start.2) | collective-permute-done | bytes 32800 | tf_op jit(solution)/shard_map/ppermute | solution.py:22
  26.5 0.5 %collective-permute-start.5 = (bf16[1024,128]{1,0:T(8,128)(2,1)S(1)}, bf16[1024,128]{1,0:T(8,128)(2,1)S(1)}, u32[]{:S(2)}, u32[]{:S(2)}) collective-permute-start(bf16[1024,128]{1,0:T(8,128)(2,1)S(1)} %get-tuple-element.36.refs_0_), channel_id=1, source_target_pairs={{0,1},{1,0},{2,3},{3,2},{4,5},{5,4},{6,7},{7,6},{8,9},{9,8},{10,11... | collective-permute-start | bytes 786440 | tf_op jit(solution)/shard_map/ppermute | solution.py:22
  27.0 0.1 collective-permute-start.6
  27.1 0.5 %collective-permute-start.9 = (bf16[2048,128]{1,0:T(8,128)(2,1)S(1)}, bf16[2048,128]{1,0:T(8,128)(2,1)S(1)}, u32[]{:S(2)}, u32[]{:S(2)}) collective-permute-start(bf16[2048,128]{1,0:T(8,128)(2,1)S(1)} %pad_maximum_fusion), channel_id=1, source_target_pairs={{0,1},{1,0},{2,3},{3,2},{4,5},{5,4},{6,7},{7,6},{8,9},{9,8},{10,11... | collective-permute-start | bytes 1572872 | tf_op jit(solution)/shard_map/ppermute | solution.py:22
  27.7 2.5 %inverses.1 = (bf16[2,64,64]{2,1,0:T(8,128)(2,1)S(1)}, bf16[2,128,128]{2,1,0:T(8,128)(2,1)S(1)}) custom-call(f32[64,128]{1,0:T(8,128)S(1)} %add.7.factor_a_ref, f32[64,128]{1,0:T(8,128)S(1)} %collective-permute-done.3.factor_b_ref), custom_call_target="tpu_custom_call" | custom-call | flops 17179869184 | tf_op jit(solution)/shard_map/inverses/pallas_call | solution.py:253
  30.2 1.1 %scores.1 = (f32[2,8,128]{2,1,0:T(8,128)S(1)}, f32[2,8,128]{2,1,0:T(8,128)S(1)}) custom-call(bf16[2,64,64]{2,1,0:T(8,128)(2,1)S(1)} %get-tuple-element.31.grad_ref, bf16[2,128,128]{2,1,0:T(8,128)(2,1)S(1)} %get-tuple-element.32.in_ref, bf16[1024,128]{1,0:T(8,128)(2,1)S(1)} %get-tuple-element.36.refs_0_, ...), custom_call_target="tpu_custom_call" | custom-call | tf_op jit(solution)/shard_map/scores/pallas_call | solution.py:363
  31.3 2.4 %collective-permute-start.11 = (f32[2,8,128]{2,1,0:T(8,128)S(1)}, f32[2,8,128]{2,1,0:T(8,128)S(1)}, u32[]{:S(2)}, u32[]{:S(2)}) collective-permute-start(f32[2,8,128]{2,1,0:T(8,128)S(1)} %get-tuple-element.44), channel_id=1, source_target_pairs={{0,8},{4,12},{8,0},{12,4},{1,9},{5,13},{9,1},{13,5},{2,10},{6,14},... | collective-permute-start | bytes 24584 | tf_op jit(solution)/shard_map/ppermute | solution.py:22
  33.7 2.2 %collective-permute-done.11.refs_1_ = f32[2,8,128]{2,1,0:T(8,128)S(1)} collective-permute-done((f32[2,8,128]{2,1,0:T(8,128)S(1)}, f32[2,8,128]{2,1,0:T(8,128)S(1)}, u32[]{:S(2)}, u32[]{:S(2)}) %collective-permute-start.11) | collective-permute-done | bytes 8224 | tf_op jit(solution)/shard_map/ppermute | solution.py:22
  35.9 0.7 %finish.1 = f32[64,64]{1,0:T(8,128)} custom-call(f32[2,8,128]{2,1,0:T(8,128)S(1)} %get-tuple-element.43.refs_0_, f32[2,8,128]{2,1,0:T(8,128)S(1)} %collective-permute-done.11.refs_1_), custom_call_target="tpu_custom_call" | custom-call | tf_op jit(solution)/shard_map/finish/pallas_call | solution.py:396
  (26 shorter events, 0.2 us)
Async XLA Ops:
  0.0 3.1 %copy-start = (bf16[8,96,2048]{2,1,0:T(8,128)(2,1)S(1)}, bf16[8,96,2048]{2,1,0:T(8,128)(2,1)}, u32[]{:S(2)}) copy-start(bf16[8,96,2048]{2,1,0:T(8,128)(2,1)} %param.7) | copy-start | bytes 9437188
  0.0 3.1 %copy-start.1 = (bf16[7168,64]{0,1:T(8,128)(2,1)S(1)}, bf16[7168,64]{0,1:T(8,128)(2,1)}, u32[]{:S(2)}) copy-start(bf16[7168,64]{0,1:T(8,128)(2,1)} %param.10) | copy-start | bytes 2752516
  0.0 3.1 %copy-start.3 = (bf16[2048,64]{0,1:T(8,128)(2,1)S(1)}, bf16[2048,64]{0,1:T(8,128)(2,1)}, u32[]{:S(2)}) copy-start(bf16[2048,64]{0,1:T(8,128)(2,1)} %param.9) | copy-start | bytes 786436
  0.0 15.2 %collective-permute-start.7 = (bf16[2048,128]{1,0:T(8,128)(2,1)}, bf16[2048,128]{1,0:T(8,128)(2,1)S(1)}, u32[]{:S(2)}, u32[]{:S(2)}) collective-permute-start(bf16[2048,128]{1,0:T(8,128)(2,1)} %bitcast.10), channel_id=1, source_target_pairs={{0,4},{4,0},{8,12},{12,8},{1,5},{5,1},{9,13},{13,9},{2,6},{6,2},{1... | collective-permute-start | bytes 1572872 | tf_op jit(solution)/shard_map/ppermute | solution.py:22
  3.1 7.6 %copy-start.2 = (bf16[128,32,64]{0,2,1:T(8,128)(2,1)S(1)}, bf16[128,32,64]{0,2,1:T(8,128)(2,1)}, u32[]{:S(2)}) copy-start(bf16[128,32,64]{0,2,1:T(8,128)(2,1)} %param.13) | copy-start | bytes 1572868
  3.1 8.0 %copy-start.4 = (s32[8,96]{1,0:T(8,128)S(1)}, s32[8,96]{1,0:T(8,128)}, u32[]{:S(2)}) copy-start(s32[8,96]{1,0:T(8,128)} %mask_ref.1) | copy-start | bytes 9220
  3.1 8.0 %copy-start.5 = (s32[8]{0:T(128)S(1)}, s32[8]{0:T(128)}, u32[]{:S(2)}) copy-start(s32[8]{0:T(128)} %lengths_ref.1) | copy-start | bytes 100
  8.8 8.4 %collective-permute-start = (bf16[768,128]{1,0:T(8,128)(2,1)S(1)}, bf16[768,128]{1,0:T(8,128)(2,1)S(1)}, u32[]{:S(2)}, u32[]{:S(2)}) collective-permute-start(bf16[768,128]{1,0:T(8,128)(2,1)S(1)} %get-tuple-element.27), channel_id=1, source_target_pairs={{0,2},{2,0},{1,3},{3,1},{4,6},{6,4},{5,7},{7,5},{8,10},{10,8},{9,1... | collective-permute-start | bytes 589832 | tf_op jit(solution)/shard_map/ppermute | solution.py:22
  11.0 15.5 %collective-permute-start.4 = (bf16[1024,128]{1,0:T(8,128)(2,1)S(1)}, bf16[1024,128]{1,0:T(8,128)(2,1)S(1)}, u32[]{:S(2)}, u32[]{:S(2)}) collective-permute-start(bf16[1024,128]{1,0:T(8,128)(2,1)S(1)} %get-tuple-element.35), channel_id=1, source_target_pairs={{0,2},{2,0},{1,3},{3,1},{4,6},{6,4},{5,7},{7,5},{8,10},{10,8},{9,1... | collective-permute-start | bytes 786440 | tf_op jit(solution)/shard_map/ppermute | solution.py:22
  15.5 11.6 %collective-permute-start.8 = (bf16[1024,128]{1,0:T(8,128)(2,1)S(1)}, bf16[1024,128]{1,0:T(8,128)(2,1)S(1)}, u32[]{:S(2)}, u32[]{:S(2)}) collective-permute-start(bf16[1024,128]{1,0:T(8,128)(2,1)S(1)} %get-tuple-element.40), channel_id=1, source_target_pairs={{0,2},{2,0},{1,3},{3,1},{4,6},{6,4},{5,7},{7,5},{8,10},{10,8},{9,1... | collective-permute-start | bytes 786440 | tf_op jit(solution)/shard_map/ppermute | solution.py:22
  17.5 4.0 %collective-permute-start.1 = (f32[64,128]{1,0:T(8,128)S(1)}, f32[64,128]{1,0:T(8,128)S(1)}, u32[]{:S(2)}, u32[]{:S(2)}) collective-permute-start(f32[64,128]{1,0:T(8,128)S(1)} %get-tuple-element.28), channel_id=1, source_target_pairs={{0,4},{4,0},{8,12},{12,8},{1,5},{5,1},{9,13},{13,9},{2,6},{6,2},{1... | collective-permute-start | bytes 98312 | tf_op jit(solution)/shard_map/ppermute | solution.py:22
  21.4 5.1 %collective-permute-start.2 = (f32[64,128]{1,0:T(8,128)S(1)}, f32[64,128]{1,0:T(8,128)S(1)}, u32[]{:S(2)}, u32[]{:S(2)}) collective-permute-start(f32[64,128]{1,0:T(8,128)S(1)} %add.6), channel_id=1, source_target_pairs={{0,8},{4,12},{8,0},{12,4},{1,9},{5,13},{9,1},{13,5},{2,10},{6,14},... | collective-permute-start | bytes 98312 | tf_op jit(solution)/shard_map/ppermute | solution.py:22
  24.9 5.3 %collective-permute-start.10 = (bf16[4,64,128]{2,1,0:T(8,128)(2,1)S(1)}, bf16[4,64,128]{2,1,0:T(8,128)(2,1)S(1)}, u32[]{:S(2)}, u32[]{:S(2)}) collective-permute-start(bf16[4,64,128]{2,1,0:T(8,128)(2,1)S(1)} %features.1.refs_7_), channel_id=1, source_target_pairs={{0,8},{4,12},{8,0},{12,4},{1,9},{5,13},{9,1},{13,5},{2,10},{6,14},... | collective-permute-start | bytes 196616 | tf_op jit(solution)/shard_map/ppermute | solution.py:22
  26.5 1.2 %collective-permute-start.3 = (f32[64,128]{1,0:T(8,128)S(1)}, f32[64,128]{1,0:T(8,128)S(1)}, u32[]{:S(2)}, u32[]{:S(2)}) collective-permute-start(f32[64,128]{1,0:T(8,128)S(1)} %add.7.factor_a_ref), channel_id=1, source_target_pairs={{0,1},{1,0},{2,3},{3,2},{4,5},{5,4},{6,7},{7,6},{8,9},{9,8},{10,11... | collective-permute-start | bytes 98312 | tf_op jit(solution)/shard_map/ppermute | solution.py:22
  26.5 3.7 %collective-permute-start.5 = (bf16[1024,128]{1,0:T(8,128)(2,1)S(1)}, bf16[1024,128]{1,0:T(8,128)(2,1)S(1)}, u32[]{:S(2)}, u32[]{:S(2)}) collective-permute-start(bf16[1024,128]{1,0:T(8,128)(2,1)S(1)} %get-tuple-element.36.refs_0_), channel_id=1, source_target_pairs={{0,1},{1,0},{2,3},{3,2},{4,5},{5,4},{6,7},{7,6},{8,9},{9,8},{10,11... | collective-permute-start | bytes 786440 | tf_op jit(solution)/shard_map/ppermute | solution.py:22
  27.0 3.2 %collective-permute-start.6 = (bf16[1024,128]{1,0:T(8,128)(2,1)S(1)}, bf16[1024,128]{1,0:T(8,128)(2,1)S(1)}, u32[]{:S(2)}, u32[]{:S(2)}) collective-permute-start(bf16[1024,128]{1,0:T(8,128)(2,1)S(1)} %collective-permute-done.4.refs_1_), channel_id=1, source_target_pairs={{0,1},{1,0},{2,3},{3,2},{4,5},{5,4},{6,7},{7,6},{8,9},{9,8},{10,11... | collective-permute-start | bytes 786440 | tf_op jit(solution)/shard_map/ppermute | solution.py:22
  27.1 3.1 %collective-permute-start.9 = (bf16[2048,128]{1,0:T(8,128)(2,1)S(1)}, bf16[2048,128]{1,0:T(8,128)(2,1)S(1)}, u32[]{:S(2)}, u32[]{:S(2)}) collective-permute-start(bf16[2048,128]{1,0:T(8,128)(2,1)S(1)} %pad_maximum_fusion), channel_id=1, source_target_pairs={{0,1},{1,0},{2,3},{3,2},{4,5},{5,4},{6,7},{7,6},{8,9},{9,8},{10,11... | collective-permute-start | bytes 1572872 | tf_op jit(solution)/shard_map/ppermute | solution.py:22
  31.3 4.6 %collective-permute-start.11 = (f32[2,8,128]{2,1,0:T(8,128)S(1)}, f32[2,8,128]{2,1,0:T(8,128)S(1)}, u32[]{:S(2)}, u32[]{:S(2)}) collective-permute-start(f32[2,8,128]{2,1,0:T(8,128)S(1)} %get-tuple-element.44), channel_id=1, source_target_pairs={{0,8},{4,12},{8,0},{12,4},{1,9},{5,13},{9,1},{13,5},{2,10},{6,14},... | collective-permute-start | bytes 24584 | tf_op jit(solution)/shard_map/ppermute | solution.py:22

commit v16 on v15

--- a/solution.py
+++ b/solution.py
@@ -323,7 +323,7 @@
         high = solved_buf[pl.ds(g + 1, count, stride=rank), :]
         first = jnp.where(lane < rank, low, pltpu.roll(high, rank, 1))
         second = jnp.where(lane < rank, pltpu.roll(low, rank, 1), high)
-        line = jnp.concatenate([first, second], axis=0).astype(bf16)
+        line = jnp.concatenate([first, second], axis=0)
         step = min(fold, 2 * rank)
         for begin in range(0, 2 * rank, step):
             at = (g * rank + begin) // fold
@@ -332,7 +332,7 @@
     lines = []
     for mask in range(feat_count):
         owner = feat ^ mask
-        lines.append(jnp.concatenate([line_buf[owner, j] for j in range(feat_count)], axis=0))
+        lines.append(jnp.concatenate([line_buf[owner, j] for j in range(feat_count)], axis=0).astype(bf16))
     is_first = lax.axis_index("test") == 0
     odd = lax.rem(lax.axis_index("dp"), 2)
     for dp_bit in range(2):
@@ -367,7 +367,7 @@
         out_specs=[VMEM] * len(feats),
         scratch_shapes=[
             pltpu.VMEM((count * rank, 2 * rank), f32),
-            pltpu.VMEM((feat_count, feat_count, 2 * count, fold), bf16),
+            pltpu.VMEM((feat_count, feat_count, 2 * count, fold), f32),
         ],
         compiler_params=pltpu.CompilerParams(vmem_limit_bytes=16 * MIB),
         name="scores",
@@ -447,8 +447,9 @@
     feats += [xor_permute(feats[0], "dp", mask) for mask in even_masks]
     total_tokens = float(tokens * dp_count * test_count)
     grad, in_pair = inverses(total_tokens, sums[-2], other)
-    blocks = scores_of(grad, in_pair, pieces, piece_counts, feats)
-    blocks = [blocks[0]] + [xor_permute(blocks[at + 1], "dp", mask) for at, mask in enumerate(even_masks)]
+    blocks = scores_of(grad, in_pair, pieces, piece_counts, feats[1:])
+    blocks = [xor_permute(block, "dp", mask) for block, mask in zip(blocks, even_masks)]
+    blocks = [*scores_of(grad, in_pair, pieces, piece_counts, feats[:1]), *blocks]
     return finish(blocks)
 
 

time: 36.7 us -> 36.6 us (level)
  waiting for transfers between devices: 9.73 us -> 8.74 us
  Pallas kernels: 11.5 us -> 12.3 us
    ppermute x12, waiting for transfers between devices: 9.73 us -> 8.74 us  [xor_permute(): return lax.ppermute(values, axis, [(i, i ^ mask) for i in range(size)])]
    pallas_call x1 -> x2, Pallas kernels: 1.15 us -> 1.98 us  [scores_of(): pl.pallas_call(functools.partial(scores_body, len(feats), piece_counts),...]
  transfers between devices with their start and end apart: 12 -> 12, of which waited for: 5 -> 5; matrix products, arithmetic and copies ran while one was open for 1% -> 1% of each run, Pallas kernels for 26% -> 29%
where the time goes in v16:
time: 36.6 us; the launch traced here: 36.5 us
  starting transfers between devices  15.1 us (41%)
  Pallas kernels  12.3 us (34%)
  waiting for transfers between devices  8.74 us (24%)
    ppermute x12, starting transfers between devices, xor_permute(): return lax.ppermute(values, axis, [(i, i ^ mask) for i in range(size)])  15.1 us
    ppermute x12, waiting for transfers between devices, xor_permute(): return lax.ppermute(values, axis, [(i, i ^ mask) for i in range(size)])  8.74 us
    pallas_call x1, Pallas kernels, project(): pl.pallas_call(functools.partial(project_body, rows), out_shape=(jax.Shap...  5.62 us
    pallas_call x1, Pallas kernels, inverses(): pl.pallas_call(functools.partial(inverses_body, total_tokens), out_shape=...  2.46 us
    pallas_call x2, Pallas kernels, scores_of(): pl.pallas_call(functools.partial(scores_body, len(feats), piece_counts),...  1.98 us
    pallas_call x1, Pallas kernels, features_of(): pl.pallas_call(features_body, out_shape=jax.ShapeDtypeStruct((examples //...  0.87 us
  transfers between devices with their start and end apart: 12, of which 5 were waited for; matrix products, arithmetic and copies ran while one was open for 1% of the time, Pallas kernels for 29%

profile of v16, /device:TPU:0, one launch (start us, length us, event | category | flops | bytes accessed | tf_op | source)
XLA Modules:
  0.0 36.5 jit_solution(10700234373042186495)
XLA Ops:
  0.0 3.1 %collective-permute-start.7 = (bf16[2048,128]{1,0:T(8,128)(2,1)}, bf16[2048,128]{1,0:T(8,128)(2,1)S(1)}, u32[]{:S(2)}, u32[]{:S(2)}) collective-permute-start(bf16[2048,128]{1,0:T(8,128)(2,1)} %bitcast.10), channel_id=1, source_target_pairs={{0,4},{4,0},{8,12},{12,8},{1,5},{5,1},{9,13},{13,9},{2,6},{6,2},{1... | collective-permute-start | bytes 1572872 | tf_op jit(solution)/shard_map/ppermute | solution.py:22
  3.1 5.6 %project.1 = (f32[768,128]{1,0:T(8,128)S(1)}, bf16[768,128]{1,0:T(8,128)(2,1)S(1)}) custom-call(bf16[768,2048]{1,0:T(8,128)(2,1)S(1)} %bitcast.8, bf16[768,7168]{1,0:T(8,128)(2,1)} %bitcast.13, bf16[64,2048]{1,0:T(8,128)(2,1)S(1)} %bitcast.12, bf16[64,7168]{1,0:T(8,128)(2,1)S(1)} %bitcast.9), custom_call_target="tpu_custom_call" | custom-call | flops 905969664 | bytes 15335424 | tf_op jit(solution)/shard_map/project/pallas_call | solution.py:60
  8.8 2.0 %collective-permute-start = (bf16[768,128]{1,0:T(8,128)(2,1)S(1)}, bf16[768,128]{1,0:T(8,128)(2,1)S(1)}, u32[]{:S(2)}, u32[]{:S(2)}) collective-permute-start(bf16[768,128]{1,0:T(8,128)(2,1)S(1)} %get-tuple-element.25), channel_id=1, source_target_pairs={{0,2},{2,0},{1,3},{3,1},{4,6},{6,4},{5,7},{7,5},{8,10},{10,8},{9,1... | collective-permute-start | bytes 589832 | tf_op jit(solution)/shard_map/ppermute | solution.py:22
  10.7 0.2 pack.2
  11.0 0.2 collective-permute-start.4
  11.2 0.1 reshape.25.live_ref
  11.3 3.9 %collective-permute-done.7.tests_ref = bf16[2048,128]{1,0:T(8,128)(2,1)S(1)} collective-permute-done((bf16[2048,128]{1,0:T(8,128)(2,1)}, bf16[2048,128]{1,0:T(8,128)(2,1)S(1)}, u32[]{:S(2)}, u32[]{:S(2)}) %collective-permute-start.7) | collective-permute-done | bytes 524320 | tf_op jit(solution)/shard_map/ppermute | solution.py:22
  15.2 0.2 pack.3
  15.5 1.7 %collective-permute-start.8 = (bf16[1024,128]{1,0:T(8,128)(2,1)S(1)}, bf16[1024,128]{1,0:T(8,128)(2,1)S(1)}, u32[]{:S(2)}, u32[]{:S(2)}) collective-permute-start(bf16[1024,128]{1,0:T(8,128)(2,1)S(1)} %get-tuple-element.38), channel_id=1, source_target_pairs={{0,2},{2,0},{1,3},{3,1},{4,6},{6,4},{5,7},{7,5},{8,10},{10,8},{9,1... | collective-permute-start | bytes 786440 | tf_op jit(solution)/shard_map/ppermute | solution.py:22
  17.2 0.3 factors.1
  17.5 1.6 %collective-permute-start.1 = (f32[64,128]{1,0:T(8,128)S(1)}, f32[64,128]{1,0:T(8,128)S(1)}, u32[]{:S(2)}, u32[]{:S(2)}) collective-permute-start(f32[64,128]{1,0:T(8,128)S(1)} %get-tuple-element.26), channel_id=1, source_target_pairs={{0,4},{4,0},{8,12},{12,8},{1,5},{5,1},{9,13},{13,9},{2,6},{6,2},{1... | collective-permute-start | bytes 98312 | tf_op jit(solution)/shard_map/ppermute | solution.py:22
  19.1 2.3 %collective-permute-done.1 = f32[64,128]{1,0:T(8,128)S(1)} collective-permute-done((f32[64,128]{1,0:T(8,128)S(1)}, f32[64,128]{1,0:T(8,128)S(1)}, u32[]{:S(2)}, u32[]{:S(2)}) %collective-permute-start.1) | collective-permute-done | bytes 32800 | tf_op jit(solution)/shard_map/ppermute | solution.py:22
  21.4 2.6 %collective-permute-start.2 = (f32[64,128]{1,0:T(8,128)S(1)}, f32[64,128]{1,0:T(8,128)S(1)}, u32[]{:S(2)}, u32[]{:S(2)}) collective-permute-start(f32[64,128]{1,0:T(8,128)S(1)} %add.6), channel_id=1, source_target_pairs={{0,8},{4,12},{8,0},{12,4},{1,9},{5,13},{9,1},{13,5},{2,10},{6,14},... | collective-permute-start | bytes 98312 | tf_op jit(solution)/shard_map/ppermute | solution.py:22
  24.0 0.9 %features.1.refs_7_ = bf16[4,64,128]{2,1,0:T(8,128)(2,1)S(1)} custom-call(s32[8]{0:T(128)S(1)} %copy-done.5, s32[1,96]{1,0:T(1,128)S(1)} %slots.1.positions_ref, s32[8,96]{1,0:T(8,128)S(1)} %copy-done.4, bf16[768,128]{1,0:T(8,128)(2,1)S(1)} %get-tuple-element.27.rounded_ref), custom_call_target="tpu_custom_call" | custom-call | flops 25165824 | bytes 8388608 | tf_op jit(solution)/shard_map/features/pallas_call | solution.py:159
  24.9 0.4 %collective-permute-start.10 = (bf16[4,64,128]{2,1,0:T(8,128)(2,1)S(1)}, bf16[4,64,128]{2,1,0:T(8,128)(2,1)S(1)}, u32[]{:S(2)}, u32[]{:S(2)}) collective-permute-start(bf16[4,64,128]{2,1,0:T(8,128)(2,1)S(1)} %features.1.refs_7_), channel_id=1, source_target_pairs={{0,8},{4,12},{8,0},{12,4},{1,9},{5,13},{9,1},{13,5},{2,10},{6,14},... | collective-permute-start | bytes 196616 | tf_op jit(solution)/shard_map/ppermute | solution.py:22
  25.3 1.2 %collective-permute-done.2 = f32[64,128]{1,0:T(8,128)S(1)} collective-permute-done((f32[64,128]{1,0:T(8,128)S(1)}, f32[64,128]{1,0:T(8,128)S(1)}, u32[]{:S(2)}, u32[]{:S(2)}) %collective-permute-start.2) | collective-permute-done | bytes 32800 | tf_op jit(solution)/shard_map/ppermute | solution.py:22
  26.5 0.5 %collective-permute-start.5 = (bf16[1024,128]{1,0:T(8,128)(2,1)S(1)}, bf16[1024,128]{1,0:T(8,128)(2,1)S(1)}, u32[]{:S(2)}, u32[]{:S(2)}) collective-permute-start(bf16[1024,128]{1,0:T(8,128)(2,1)S(1)} %get-tuple-element.34.refs_0_), channel_id=1, source_target_pairs={{0,1},{1,0},{2,3},{3,2},{4,5},{5,4},{6,7},{7,6},{8,9},{9,8},{10,11... | collective-permute-start | bytes 786440 | tf_op jit(solution)/shard_map/ppermute | solution.py:22
  27.1 0.5 %collective-permute-start.9 = (bf16[2048,128]{1,0:T(8,128)(2,1)S(1)}, bf16[2048,128]{1,0:T(8,128)(2,1)S(1)}, u32[]{:S(2)}, u32[]{:S(2)}) collective-permute-start(bf16[2048,128]{1,0:T(8,128)(2,1)S(1)} %pad_maximum_fusion), channel_id=1, source_target_pairs={{0,1},{1,0},{2,3},{3,2},{4,5},{5,4},{6,7},{7,6},{8,9},{9,8},{10,11... | collective-permute-start | bytes 1572872 | tf_op jit(solution)/shard_map/ppermute | solution.py:22
  27.7 2.5 %inverses.1 = (bf16[2,64,64]{2,1,0:T(8,128)(2,1)S(1)}, bf16[2,128,128]{2,1,0:T(8,128)(2,1)S(1)}) custom-call(f32[64,128]{1,0:T(8,128)S(1)} %add.7.factor_a_ref, f32[64,128]{1,0:T(8,128)S(1)} %collective-permute-done.3.factor_b_ref), custom_call_target="tpu_custom_call" | custom-call | flops 17179869184 | tf_op jit(solution)/shard_map/inverses/pallas_call | solution.py:253
  30.2 1.0 %scores.3 = f32[2,8,128]{2,1,0:T(8,128)S(1)} custom-call(bf16[2,64,64]{2,1,0:T(8,128)(2,1)S(1)} %get-tuple-element.29.grad_ref, bf16[2,128,128]{2,1,0:T(8,128)(2,1)S(1)} %get-tuple-element.30.in_ref, bf16[1024,128]{1,0:T(8,128)(2,1)S(1)} %get-tuple-element.34.refs_0_, bf16[1024,128]{1,0:T(8,128)(2,1)S(1)} %collective-permute-done.4.refs_1_, ...), custom_call_target="tpu_custom_call" | custom-call | tf_op jit(solution)/shard_map/scores/pallas_call | solution.py:363
  31.2 2.4 %collective-permute-start.11 = (f32[2,8,128]{2,1,0:T(8,128)S(1)}, f32[2,8,128]{2,1,0:T(8,128)S(1)}, u32[]{:S(2)}, u32[]{:S(2)}) collective-permute-start(f32[2,8,128]{2,1,0:T(8,128)S(1)} %scores.3), channel_id=1, source_target_pairs={{0,8},{4,12},{8,0},{12,4},{1,9},{5,13},{9,1},{13,5},{2,10},{6,14},... | collective-permute-start | bytes 24584 | tf_op jit(solution)/shard_map/ppermute | solution.py:22
  33.6 1.0 %scores.2.refs_0_ = f32[2,8,128]{2,1,0:T(8,128)S(1)} custom-call(bf16[2,64,64]{2,1,0:T(8,128)(2,1)S(1)} %get-tuple-element.29.grad_ref, bf16[2,128,128]{2,1,0:T(8,128)(2,1)S(1)} %get-tuple-element.30.in_ref, bf16[1024,128]{1,0:T(8,128)(2,1)S(1)} %get-tuple-element.34.refs_0_, bf16[1024,128]{1,0:T(8,128)(2,1)S(1)} %collective-permute-done.4.refs_1_, ...), custom_call_target="tpu_custom_call" | custom-call | tf_op jit(solution)/shard_map/scores/pallas_call | solution.py:363
  34.6 1.2 %collective-permute-done.11.refs_1_ = f32[2,8,128]{2,1,0:T(8,128)S(1)} collective-permute-done((f32[2,8,128]{2,1,0:T(8,128)S(1)}, f32[2,8,128]{2,1,0:T(8,128)S(1)}, u32[]{:S(2)}, u32[]{:S(2)}) %collective-permute-start.11) | collective-permute-done | bytes 8224 | tf_op jit(solution)/shard_map/ppermute | solution.py:22
  35.8 0.7 %finish.1 = f32[64,64]{1,0:T(8,128)} custom-call(f32[2,8,128]{2,1,0:T(8,128)S(1)} %scores.2.refs_0_, f32[2,8,128]{2,1,0:T(8,128)S(1)} %collective-permute-done.11.refs_1_), custom_call_target="tpu_custom_call" | custom-call | tf_op jit(solution)/shard_map/finish/pallas_call | solution.py:396
  (27 shorter events, 0.3 us)
Async XLA Ops:
  0.0 3.1 %copy-start = (bf16[8,96,2048]{2,1,0:T(8,128)(2,1)S(1)}, bf16[8,96,2048]{2,1,0:T(8,128)(2,1)}, u32[]{:S(2)}) copy-start(bf16[8,96,2048]{2,1,0:T(8,128)(2,1)} %param.7) | copy-start | bytes 9437188
  0.0 3.1 %copy-start.1 = (bf16[7168,64]{0,1:T(8,128)(2,1)S(1)}, bf16[7168,64]{0,1:T(8,128)(2,1)}, u32[]{:S(2)}) copy-start(bf16[7168,64]{0,1:T(8,128)(2,1)} %param.10) | copy-start | bytes 2752516
  0.0 3.1 %copy-start.3 = (bf16[2048,64]{0,1:T(8,128)(2,1)S(1)}, bf16[2048,64]{0,1:T(8,128)(2,1)}, u32[]{:S(2)}) copy-start(bf16[2048,64]{0,1:T(8,128)(2,1)} %param.9) | copy-start | bytes 786436
  0.0 15.2 %collective-permute-start.7 = (bf16[2048,128]{1,0:T(8,128)(2,1)}, bf16[2048,128]{1,0:T(8,128)(2,1)S(1)}, u32[]{:S(2)}, u32[]{:S(2)}) collective-permute-start(bf16[2048,128]{1,0:T(8,128)(2,1)} %bitcast.10), channel_id=1, source_target_pairs={{0,4},{4,0},{8,12},{12,8},{1,5},{5,1},{9,13},{13,9},{2,6},{6,2},{1... | collective-permute-start | bytes 1572872 | tf_op jit(solution)/shard_map/ppermute | solution.py:22
  3.1 7.6 %copy-start.2 = (bf16[128,32,64]{0,2,1:T(8,128)(2,1)S(1)}, bf16[128,32,64]{0,2,1:T(8,128)(2,1)}, u32[]{:S(2)}) copy-start(bf16[128,32,64]{0,2,1:T(8,128)(2,1)} %param.13) | copy-start | bytes 1572868
  3.1 8.0 %copy-start.4 = (s32[8,96]{1,0:T(8,128)S(1)}, s32[8,96]{1,0:T(8,128)}, u32[]{:S(2)}) copy-start(s32[8,96]{1,0:T(8,128)} %mask_ref.1) | copy-start | bytes 9220
  3.1 8.0 %copy-start.5 = (s32[8]{0:T(128)S(1)}, s32[8]{0:T(128)}, u32[]{:S(2)}) copy-start(s32[8]{0:T(128)} %lengths_ref.1) | copy-start | bytes 100
  8.8 8.4 %collective-permute-start = (bf16[768,128]{1,0:T(8,128)(2,1)S(1)}, bf16[768,128]{1,0:T(8,128)(2,1)S(1)}, u32[]{:S(2)}, u32[]{:S(2)}) collective-permute-start(bf16[768,128]{1,0:T(8,128)(2,1)S(1)} %get-tuple-element.25), channel_id=1, source_target_pairs={{0,2},{2,0},{1,3},{3,1},{4,6},{6,4},{5,7},{7,5},{8,10},{10,8},{9,1... | collective-permute-start | bytes 589832 | tf_op jit(solution)/shard_map/ppermute | solution.py:22
  11.0 15.5 %collective-permute-start.4 = (bf16[1024,128]{1,0:T(8,128)(2,1)S(1)}, bf16[1024,128]{1,0:T(8,128)(2,1)S(1)}, u32[]{:S(2)}, u32[]{:S(2)}) collective-permute-start(bf16[1024,128]{1,0:T(8,128)(2,1)S(1)} %get-tuple-element.33), channel_id=1, source_target_pairs={{0,2},{2,0},{1,3},{3,1},{4,6},{6,4},{5,7},{7,5},{8,10},{10,8},{9,1... | collective-permute-start | bytes 786440 | tf_op jit(solution)/shard_map/ppermute | solution.py:22
  15.5 11.6 %collective-permute-start.8 = (bf16[1024,128]{1,0:T(8,128)(2,1)S(1)}, bf16[1024,128]{1,0:T(8,128)(2,1)S(1)}, u32[]{:S(2)}, u32[]{:S(2)}) collective-permute-start(bf16[1024,128]{1,0:T(8,128)(2,1)S(1)} %get-tuple-element.38), channel_id=1, source_target_pairs={{0,2},{2,0},{1,3},{3,1},{4,6},{6,4},{5,7},{7,5},{8,10},{10,8},{9,1... | collective-permute-start | bytes 786440 | tf_op jit(solution)/shard_map/ppermute | solution.py:22
  17.5 4.0 %collective-permute-start.1 = (f32[64,128]{1,0:T(8,128)S(1)}, f32[64,128]{1,0:T(8,128)S(1)}, u32[]{:S(2)}, u32[]{:S(2)}) collective-permute-start(f32[64,128]{1,0:T(8,128)S(1)} %get-tuple-element.26), channel_id=1, source_target_pairs={{0,4},{4,0},{8,12},{12,8},{1,5},{5,1},{9,13},{13,9},{2,6},{6,2},{1... | collective-permute-start | bytes 98312 | tf_op jit(solution)/shard_map/ppermute | solution.py:22
  21.4 5.1 %collective-permute-start.2 = (f32[64,128]{1,0:T(8,128)S(1)}, f32[64,128]{1,0:T(8,128)S(1)}, u32[]{:S(2)}, u32[]{:S(2)}) collective-permute-start(f32[64,128]{1,0:T(8,128)S(1)} %add.6), channel_id=1, source_target_pairs={{0,8},{4,12},{8,0},{12,4},{1,9},{5,13},{9,1},{13,5},{2,10},{6,14},... | collective-permute-start | bytes 98312 | tf_op jit(solution)/shard_map/ppermute | solution.py:22
  24.9 5.3 %collective-permute-start.10 = (bf16[4,64,128]{2,1,0:T(8,128)(2,1)S(1)}, bf16[4,64,128]{2,1,0:T(8,128)(2,1)S(1)}, u32[]{:S(2)}, u32[]{:S(2)}) collective-permute-start(bf16[4,64,128]{2,1,0:T(8,128)(2,1)S(1)} %features.1.refs_7_), channel_id=1, source_target_pairs={{0,8},{4,12},{8,0},{12,4},{1,9},{5,13},{9,1},{13,5},{2,10},{6,14},... | collective-permute-start | bytes 196616 | tf_op jit(solution)/shard_map/ppermute | solution.py:22
  26.5 1.2 %collective-permute-start.3 = (f32[64,128]{1,0:T(8,128)S(1)}, f32[64,128]{1,0:T(8,128)S(1)}, u32[]{:S(2)}, u32[]{:S(2)}) collective-permute-start(f32[64,128]{1,0:T(8,128)S(1)} %add.7.factor_a_ref), channel_id=1, source_target_pairs={{0,1},{1,0},{2,3},{3,2},{4,5},{5,4},{6,7},{7,6},{8,9},{9,8},{10,11... | collective-permute-start | bytes 98312 | tf_op jit(solution)/shard_map/ppermute | solution.py:22
  26.5 3.7 %collective-permute-start.5 = (bf16[1024,128]{1,0:T(8,128)(2,1)S(1)}, bf16[1024,128]{1,0:T(8,128)(2,1)S(1)}, u32[]{:S(2)}, u32[]{:S(2)}) collective-permute-start(bf16[1024,128]{1,0:T(8,128)(2,1)S(1)} %get-tuple-element.34.refs_0_), channel_id=1, source_target_pairs={{0,1},{1,0},{2,3},{3,2},{4,5},{5,4},{6,7},{7,6},{8,9},{9,8},{10,11... | collective-permute-start | bytes 786440 | tf_op jit(solution)/shard_map/ppermute | solution.py:22
  27.0 3.2 %collective-permute-start.6 = (bf16[1024,128]{1,0:T(8,128)(2,1)S(1)}, bf16[1024,128]{1,0:T(8,128)(2,1)S(1)}, u32[]{:S(2)}, u32[]{:S(2)}) collective-permute-start(bf16[1024,128]{1,0:T(8,128)(2,1)S(1)} %collective-permute-done.4.refs_1_), channel_id=1, source_target_pairs={{0,1},{1,0},{2,3},{3,2},{4,5},{5,4},{6,7},{7,6},{8,9},{9,8},{10,11... | collective-permute-start | bytes 786440 | tf_op jit(solution)/shard_map/ppermute | solution.py:22
  27.1 3.1 %collective-permute-start.9 = (bf16[2048,128]{1,0:T(8,128)(2,1)S(1)}, bf16[2048,128]{1,0:T(8,128)(2,1)S(1)}, u32[]{:S(2)}, u32[]{:S(2)}) collective-permute-start(bf16[2048,128]{1,0:T(8,128)(2,1)S(1)} %pad_maximum_fusion), channel_id=1, source_target_pairs={{0,1},{1,0},{2,3},{3,2},{4,5},{5,4},{6,7},{7,6},{8,9},{9,8},{10,11... | collective-permute-start | bytes 1572872 | tf_op jit(solution)/shard_map/ppermute | solution.py:22
  31.2 4.6 %collective-permute-start.11 = (f32[2,8,128]{2,1,0:T(8,128)S(1)}, f32[2,8,128]{2,1,0:T(8,128)S(1)}, u32[]{:S(2)}, u32[]{:S(2)}) collective-permute-start(f32[2,8,128]{2,1,0:T(8,128)S(1)} %scores.3), channel_id=1, source_target_pairs={{0,8},{4,12},{8,0},{12,4},{1,9},{5,13},{9,1},{13,5},{2,10},{6,14},... | collective-permute-start | bytes 24584 | tf_op jit(solution)/shard_map/ppermute | solution.py:22
